TPU v7x, 32 devices: a whole 2x2x4 slice. The times are simulated.
32 devices in a mesh: seq: 8 (over z, y), exp: 4 (over x, core).
Axes of the slice: x: 2, y: 2, z: 4, core: 2. Of those that a mesh axis runs over, the one named last changes fastest.
Arguments:
- hidden_in: bfloat16 [4, 3072, 768], P('exp', 'seq'), may hold values from -6 to 6
- memory: bfloat16 [4, 1024, 768], P('exp', 'seq'), may hold values from -6 to 6
- proj_in: bfloat16 [6, 768, 768], replicated, may hold values from -0.21875 to 0.21875
- proj_out: bfloat16 [2, 768, 768], replicated, may hold values from -0.625 to 0.625
- norm_gains: bfloat16 [3, 768], replicated, may hold values from 0.5 to 1.5
- rel_bias: float32 [32, 12], replicated, may hold values from -4 to 4
- router: bfloat16 [768, 8], replicated, may hold values from -0.109375 to 0.109375
- expert_choice: int32 [4, 3072, 1], P('exp', 'seq'), may hold values from 0 to 7
- expert_in: bfloat16 [8, 768, 3072], P('exp', None, 'seq'), may hold values from -0.21875 to 0.21875
- expert_out: bfloat16 [8, 768, 3072], P('exp', None, 'seq'), may hold values from -1.5 to 1.5
- cotangent: bfloat16 [4, 3072, 768], P('exp', 'seq'), may hold values from -6 to 6
Outputs:
- output: bfloat16 [4, 3072, 768], P('exp', 'seq')
- grad_in: bfloat16 [4, 3072, 768], P('exp', 'seq')
- grad_memory: bfloat16 [4, 1024, 768], P('exp', 'seq')
- grad_proj_in: float32 [6, 768, 768], replicated
- grad_proj_out: float32 [2, 768, 768], replicated
- grad_gains: float32 [3, 768], replicated
- grad_rel_bias: float32 [32, 12], replicated
- grad_router: float32 [768, 8], replicated
- grad_expert_in: float32 [8, 768, 3072], P('exp', None, 'seq')
- grad_expert_out: float32 [8, 768, 3072], P('exp', None, 'seq')
- expert_tally: int32 [4, 8, 2, 8], P('exp', 'seq')
Inputs may be any that keep to these rules, and one draw needn't show every extreme that they name: `expert_choice`: each token names one expert; every expert is named by some token.
All inputs are finite; a program needn't handle non-finite values.
Results may differ from a plain program's by a relative error of at most 0.03.
Values may be sent and summed in bfloat16 or wider, within the bound.
A program may use at most 320 MiB of HBM per device.

v0:
```python
import jax
import jax.numpy as jnp
from jax import lax
from jax.sharding import PartitionSpec as P

D = 768
HEADS = 12
HEAD_DIM = 64
NBUCKET = 32
MAXDIST = 128


norm_eps = 1e-06
masked_score = -1e30
highest = lax.Precision.HIGHEST


def bucket_edges():
    half_count = NBUCKET // 2
    thresholds = []
    for bucket_number in range(1, NBUCKET):
        if bucket_number < half_count:
            thresholds.append(bucket_number)
        else:
            thresholds.append(
                int(
                    half_count
                    * (MAXDIST / half_count) ** ((bucket_number - half_count) / half_count)
                )
            )
    return thresholds


def rms_apply(values, gain_row):
    return (
        values * lax.rsqrt(jnp.mean(values * values, axis=-1, keepdims=True) + norm_eps) * gain_row
    )


def rms_backward(values, gain_row, upstream):
    _, pullback = jax.vjp(rms_apply, values, gain_row)
    return pullback(upstream)


def gelu_backward(pre_act, upstream):
    _, pullback = jax.vjp(jax.nn.gelu, pre_act)
    return pullback(upstream)[0]


def heads_of(matrix):
    return matrix.reshape(matrix.shape[0], HEADS, HEAD_DIM)


def relative_terms(bias_table, query_start, key_start, query_count, key_count):
    distance = (
        query_start
        - key_start
        + jnp.arange(query_count, dtype=jnp.int32)[:, None]
        - jnp.arange(key_count, dtype=jnp.int32)[None, :]
    )
    bucket_grid = jnp.zeros(distance.shape, jnp.int32)
    rel_terms = jnp.broadcast_to(
        bias_table[0][:, None, None], (bias_table.shape[1], query_count, key_count)
    )
    for bucket_number, threshold in enumerate(bucket_edges()):
        reached = distance >= threshold
        bucket_grid = bucket_grid + reached.astype(jnp.int32)
        rel_terms = jnp.where(
            reached[None], bias_table[bucket_number + 1][:, None, None], rel_terms
        )
    allowed = distance >= 0
    return (rel_terms, allowed, bucket_grid)


def split_blocks(key_rows, value_rows):
    key_total = key_rows.shape[0]
    block_width = 512
    block_shape = (key_total // block_width, block_width, HEADS, HEAD_DIM)
    offsets = jnp.arange(key_total // block_width, dtype=jnp.int32) * block_width
    return (key_rows.reshape(block_shape), value_rows.reshape(block_shape), offsets)


def attend_forward(queries, key_rows, value_rows, bias_table, query_start, causal):
    query_count = queries.shape[0]
    key_stack, value_stack, offsets = split_blocks(key_rows, value_rows)
    block_width = key_stack.shape[1]
    scale_factor = HEAD_DIM ** (-0.5)

    def block_step(state_in, inputs):
        key_block, value_block, offset = inputs

        def compute(unused):
            running_max, denom_sum, weighted = state_in
            scores = (
                jnp.einsum("qhd,khd->hqk", queries, key_block, preferred_element_type=jnp.float32)
                * scale_factor
            )
            if causal:
                rel_terms, allowed, _ = relative_terms(
                    bias_table, query_start, offset, query_count, block_width
                )
                scores = jnp.where(allowed[None], scores + rel_terms, masked_score)
            new_max = jnp.maximum(running_max, jnp.max(scores, axis=-1))
            weights = jnp.exp(scores - new_max[..., None])
            if causal:
                weights = jnp.where(allowed[None], weights, 0.0)
            factor = jnp.exp(running_max - new_max)
            denom_sum = denom_sum * factor + jnp.sum(weights, axis=-1)
            weighted = weighted * factor[..., None] + jnp.einsum(
                "hqk,khd->hqd",
                weights.astype(jnp.bfloat16),
                value_block,
                preferred_element_type=jnp.float32,
            )
            return (new_max, denom_sum, weighted)

        if causal:
            state_out = lax.cond(
                offset < query_start + query_count, compute, lambda unused: state_in, None
            )
        else:
            state_out = compute(None)
        return (state_out, None)

    initial = (
        jnp.full((HEADS, query_count), masked_score, jnp.float32),
        jnp.zeros((HEADS, query_count), jnp.float32),
        jnp.zeros((HEADS, query_count, HEAD_DIM), jnp.float32),
    )
    (running_max, denom_sum, weighted), _ = lax.scan(
        block_step, initial, (key_stack, value_stack, offsets)
    )
    attended = (
        (weighted / denom_sum[..., None]).transpose(1, 0, 2).reshape(query_count, HEADS * HEAD_DIM)
    )
    return (attended, running_max + jnp.log(denom_sum))


def attend_backward(
    queries, key_rows, value_rows, bias_table, query_start, causal, grad_out, logsum, row_delta
):
    query_count = queries.shape[0]
    key_total = key_rows.shape[0]
    key_stack, value_stack, offsets = split_blocks(key_rows, value_rows)
    block_width = key_stack.shape[1]
    scale_factor = HEAD_DIM ** (-0.5)
    bucket_ids = jnp.arange(NBUCKET, dtype=jnp.int32)

    def block_step(state_in, inputs):
        key_block, value_block, offset = inputs

        def compute(unused):
            grad_query, grad_table = state_in
            scores = (
                jnp.einsum("qhd,khd->hqk", queries, key_block, preferred_element_type=jnp.float32)
                * scale_factor
            )
            if causal:
                rel_terms, allowed, bucket_grid = relative_terms(
                    bias_table, query_start, offset, query_count, block_width
                )
                scores = scores + rel_terms
            block_probs = jnp.exp(scores - logsum[..., None])
            if causal:
                block_probs = jnp.where(allowed[None], block_probs, 0.0)
            grad_probs = jnp.einsum(
                "qhd,khd->hqk", grad_out, value_block, preferred_element_type=jnp.float32
            )
            grad_scores = (block_probs * (grad_probs - row_delta[..., None])).astype(jnp.bfloat16)
            grad_query = (
                grad_query
                + jnp.einsum(
                    "hqk,khd->qhd", grad_scores, key_block, preferred_element_type=jnp.float32
                )
                * scale_factor
            )
            if causal:
                grid_onehot = (bucket_grid[..., None] == bucket_ids).astype(jnp.bfloat16)
                grad_table = grad_table + jnp.einsum(
                    "hqk,qkb->bh", grad_scores, grid_onehot, preferred_element_type=jnp.float32
                )
            grad_value = jnp.einsum(
                "hqk,qhd->khd",
                block_probs.astype(jnp.bfloat16),
                grad_out,
                preferred_element_type=jnp.float32,
            )
            grad_key = (
                jnp.einsum("hqk,qhd->khd", grad_scores, queries, preferred_element_type=jnp.float32)
                * scale_factor
            )
            return ((grad_query, grad_table), (grad_key, grad_value))

        def skip(unused):
            empty = jnp.zeros((block_width, HEADS, HEAD_DIM), jnp.float32)
            return (state_in, (empty, empty))

        if causal:
            return lax.cond(offset < query_start + query_count, compute, skip, None)
        return compute(None)

    initial = (
        jnp.zeros((query_count, HEADS, HEAD_DIM), jnp.float32),
        jnp.zeros((NBUCKET, HEADS), jnp.float32),
    )
    (grad_query, grad_table), kv_terms = lax.scan(
        block_step, initial, (key_stack, value_stack, offsets)
    )
    grad_keys, grad_values = kv_terms
    return (
        grad_query.reshape(query_count, HEADS * HEAD_DIM),
        grad_keys.reshape(key_total, HEADS * HEAD_DIM),
        grad_values.reshape(key_total, HEADS * HEAD_DIM),
        grad_table,
    )


def project(source, matrix):
    return jnp.dot(source, matrix, preferred_element_type=jnp.float32).astype(jnp.bfloat16)


def weight_grad(source, upstream):
    return jnp.einsum("td,te->de", source, upstream, preferred_element_type=jnp.float32)


def input_grad(upstream, matrix):
    return jnp.einsum("te,de->td", upstream, matrix, preferred_element_type=jnp.float32)


def body(
    hidden_in,
    memory,
    proj_in,
    proj_out,
    norm_gains,
    rel_bias,
    router,
    expert_choice,
    expert_in,
    expert_out,
    cotangent,
):
    tokens = hidden_in[0].astype(jnp.float32)
    memory_rows = memory[0]
    memory_count = memory_rows.shape[0]
    gain_rows = norm_gains.astype(jnp.float32)
    token_count = tokens.shape[0]
    query_start = lax.axis_index("seq") * token_count
    normed_self = rms_apply(tokens, gain_rows[0]).astype(jnp.bfloat16)
    queries = project(normed_self, proj_in[0])
    key_local = project(normed_self, proj_in[1])
    value_local = project(normed_self, proj_in[2])
    memory_keys = project(memory_rows, proj_in[4])
    memory_values = project(memory_rows, proj_in[5])
    key_all, value_all, memory_key_all, memory_value_all = (
        lax.all_gather(key_local, "seq", axis=0, tiled=True),
        lax.all_gather(value_local, "seq", axis=0, tiled=True),
        lax.all_gather(memory_keys, "seq", axis=0, tiled=True),
        lax.all_gather(memory_values, "seq", axis=0, tiled=True),
    )
    attended_self, logsum_self = attend_forward(
        heads_of(queries), key_all, value_all, rel_bias, query_start, True
    )
    attended_self_low = attended_self.astype(jnp.bfloat16)
    after_self = tokens + jnp.dot(
        attended_self_low, proj_out[0], preferred_element_type=jnp.float32
    )
    normed_cross = rms_apply(after_self, gain_rows[1]).astype(jnp.bfloat16)
    cross_queries = project(normed_cross, proj_in[3])
    attended_cross, logsum_cross = attend_forward(
        heads_of(cross_queries), memory_key_all, memory_value_all, rel_bias, query_start, False
    )
    attended_cross_low = attended_cross.astype(jnp.bfloat16)
    after_cross = after_self + jnp.dot(
        attended_cross_low, proj_out[1], preferred_element_type=jnp.float32
    )
    mixed_low = rms_apply(after_cross, gain_rows[2]).astype(jnp.bfloat16)
    softmax_probs = jax.nn.softmax(
        jnp.dot(mixed_low, router, preferred_element_type=jnp.float32), axis=-1
    )
    expert_count = router.shape[1]
    local_experts = expert_in.shape[0]
    capacity = max(2, 5 * token_count // (4 * expert_count))
    chosen = expert_choice[0, :, 0]
    onehot_int = (chosen[:, None] == jnp.arange(expert_count, dtype=jnp.int32)[None, :]).astype(
        jnp.int32
    )
    onehot = onehot_int.astype(jnp.float32)
    gate_prob = jnp.sum(softmax_probs * onehot, axis=-1)
    slot_index = jnp.sum(jnp.cumsum(onehot_int, axis=0) * onehot_int, axis=-1) - 1
    is_kept = slot_index < capacity
    slot_onehot = (
        (slot_index[:, None] == jnp.arange(capacity, dtype=jnp.int32)[None, :]) & is_kept[:, None]
    ).astype(jnp.float32)
    dispatch = (
        (onehot[:, :, None] * slot_onehot[:, None, :])
        .reshape(token_count, expert_count * capacity)
        .astype(jnp.bfloat16)
    )
    dispatched = jnp.sum(onehot_int * is_kept[:, None].astype(jnp.int32), axis=0)
    tally_counts = jnp.stack(
        [dispatched, jnp.sum(onehot_int, axis=0) - dispatched], axis=0
    ).reshape(1, 1, 2, expert_count)
    sent_rows = (
        jnp.einsum("tx,td->xd", dispatch, mixed_low, preferred_element_type=jnp.float32)
        .astype(jnp.bfloat16)
        .reshape(expert_count, capacity, D)
    )
    received = lax.all_to_all(sent_rows, "exp", split_axis=0, concat_axis=1, tiled=True)
    in_piece = lax.all_gather(expert_in, "seq", axis=2, tiled=True)
    out_piece = lax.all_gather(expert_out, "seq", axis=2, tiled=True)
    pre_act = jnp.einsum("erd,edf->erf", received, in_piece, preferred_element_type=jnp.float32)
    act_low = jax.nn.gelu(pre_act).astype(jnp.bfloat16)
    summed = jnp.einsum("erf,edf->erd", act_low, out_piece, preferred_element_type=jnp.float32)
    forward_pre_all = pre_act
    forward_act_all = act_low
    summed, pre_all, act_all = (summed, forward_pre_all, forward_act_all)
    returned = lax.all_to_all(
        summed.astype(jnp.bfloat16), "exp", split_axis=1, concat_axis=0, tiled=True
    ).reshape(expert_count * capacity, D)
    combined = jnp.dot(dispatch, returned, preferred_element_type=jnp.float32)
    output = (after_cross + gate_prob[:, None] * combined).astype(jnp.bfloat16)
    grad_top = cotangent[0].astype(jnp.float32)
    scaled = (gate_prob[:, None] * grad_top).astype(jnp.bfloat16)
    grad_gate = jnp.sum(grad_top * combined, axis=-1)
    grad_slots = (
        jnp.einsum("tx,td->xd", dispatch, scaled, preferred_element_type=jnp.float32)
        .astype(jnp.bfloat16)
        .reshape(expert_count, capacity, D)
    )
    grad_result = lax.all_to_all(grad_slots, "exp", split_axis=0, concat_axis=1, tiled=True)
    in_piece = lax.all_gather(expert_in, "seq", axis=2, tiled=True)
    out_piece = lax.all_gather(expert_out, "seq", axis=2, tiled=True)
    pre_act = pre_all
    grad_act = jnp.einsum(
        "erd,edf->erf", grad_result, out_piece, preferred_element_type=jnp.float32
    )
    grad_pre = gelu_backward(pre_act, grad_act).astype(jnp.bfloat16)
    grad_rows = jnp.einsum("erf,edf->erd", grad_pre, in_piece, preferred_element_type=jnp.float32)
    backward_grad_pre_all = grad_pre
    grad_rows, grad_pre_all = (grad_rows, backward_grad_pre_all)
    act_low = act_all
    grad_pre = grad_pre_all
    term_in = jnp.einsum("erd,erf->fed", received, grad_pre, preferred_element_type=jnp.float32)
    term_out = jnp.einsum("erd,erf->fed", grad_result, act_low, preferred_element_type=jnp.float32)
    terms_own = lax.psum_scatter(
        jnp.concatenate([term_in, term_out], axis=1).astype(jnp.bfloat16),
        "seq",
        scatter_dimension=0,
        tiled=True,
    ).astype(jnp.float32)
    grad_expert_in = terms_own[:, :local_experts].transpose(1, 2, 0)
    grad_expert_out = terms_own[:, local_experts:].transpose(1, 2, 0)
    grad_routed = lax.all_to_all(
        grad_rows.astype(jnp.bfloat16), "exp", split_axis=1, concat_axis=0, tiled=True
    ).reshape(expert_count * capacity, D)
    grad_mixed = jnp.dot(dispatch, grad_routed, preferred_element_type=jnp.float32)
    grad_logits = softmax_probs * (onehot - gate_prob[:, None]) * grad_gate[:, None]
    grad_router = jnp.einsum(
        "td,te->de", mixed_low.astype(jnp.float32), grad_logits, precision=highest
    )
    grad_mixed = grad_mixed + jnp.einsum(
        "te,de->td", grad_logits, router.astype(jnp.float32), precision=highest
    )
    grad_cross_part, grad_gain_mix = rms_backward(after_cross, gain_rows[2], grad_mixed)
    grad_after_cross = grad_top + grad_cross_part
    grad_cross_low = grad_after_cross.astype(jnp.bfloat16)
    grad_out_cross = weight_grad(attended_cross_low, grad_cross_low)
    grad_attended_cross = input_grad(grad_cross_low, proj_out[1]).astype(jnp.bfloat16)
    delta_cross = jnp.sum(
        heads_of(grad_attended_cross).astype(jnp.float32) * heads_of(attended_cross), axis=-1
    ).T
    grad_cross_query, grad_memory_keys, grad_memory_values, _ = attend_backward(
        heads_of(cross_queries),
        memory_key_all,
        memory_value_all,
        rel_bias,
        query_start,
        False,
        heads_of(grad_attended_cross),
        logsum_cross,
        delta_cross,
    )
    grad_cross_query = grad_cross_query.astype(jnp.bfloat16)
    grad_query_cross = weight_grad(normed_cross, grad_cross_query)
    grad_self_part, grad_gain_cross = rms_backward(
        after_self, gain_rows[1], input_grad(grad_cross_query, proj_in[3])
    )
    grad_after_self = grad_after_cross + grad_self_part
    grad_self_low = grad_after_self.astype(jnp.bfloat16)
    grad_out_self = weight_grad(attended_self_low, grad_self_low)
    grad_attended_self = input_grad(grad_self_low, proj_out[0]).astype(jnp.bfloat16)
    delta_self = jnp.sum(
        heads_of(grad_attended_self).astype(jnp.float32) * heads_of(attended_self), axis=-1
    ).T
    grad_self_query, grad_keys, grad_values, grad_table = attend_backward(
        heads_of(queries),
        key_all,
        value_all,
        rel_bias,
        query_start,
        True,
        heads_of(grad_attended_self),
        logsum_self,
        delta_self,
    )
    grad_self_query = grad_self_query.astype(jnp.bfloat16)
    grad_key_own, grad_value_own, grad_memkey_own, grad_memvalue_own = (
        lax.psum_scatter(
            grad_keys.astype(jnp.bfloat16), "seq", scatter_dimension=0, tiled=True
        ).astype(jnp.float32),
        lax.psum_scatter(
            grad_values.astype(jnp.bfloat16), "seq", scatter_dimension=0, tiled=True
        ).astype(jnp.float32),
        lax.psum_scatter(
            grad_memory_keys.astype(jnp.bfloat16), "seq", scatter_dimension=0, tiled=True
        ).astype(jnp.float32),
        lax.psum_scatter(
            grad_memory_values.astype(jnp.bfloat16), "seq", scatter_dimension=0, tiled=True
        ).astype(jnp.float32),
    )
    grad_key_own = grad_key_own.astype(jnp.bfloat16)
    grad_value_own = grad_value_own.astype(jnp.bfloat16)
    grad_memkey_own = grad_memkey_own.astype(jnp.bfloat16)
    grad_memvalue_own = grad_memvalue_own.astype(jnp.bfloat16)
    grad_memory = (
        input_grad(grad_memkey_own, proj_in[4]) + input_grad(grad_memvalue_own, proj_in[5])
    ).astype(jnp.bfloat16)
    grad_normed_self = (
        input_grad(grad_self_query, proj_in[0])
        + input_grad(grad_key_own, proj_in[1])
        + input_grad(grad_value_own, proj_in[2])
    )
    grad_token_part, grad_gain_self = rms_backward(tokens, gain_rows[0], grad_normed_self)
    grad_in = (grad_after_self + grad_token_part).astype(jnp.bfloat16)
    grad_proj_in = jnp.stack(
        [
            weight_grad(normed_self, grad_self_query),
            weight_grad(normed_self, grad_key_own),
            weight_grad(normed_self, grad_value_own),
            grad_query_cross,
            weight_grad(memory_rows, grad_memkey_own),
            weight_grad(memory_rows, grad_memvalue_own),
        ]
    )
    grad_proj_out = jnp.stack([grad_out_self, grad_out_cross])
    grad_gains = jnp.stack([grad_gain_self, grad_gain_cross, grad_gain_mix])
    grad_proj_in, grad_proj_out, grad_gains, grad_rel_bias, grad_router = lax.psum(
        (grad_proj_in, grad_proj_out, grad_gains, grad_table, grad_router), ("seq", "exp")
    )
    return (
        output.reshape(1, token_count, D),
        grad_in.reshape(1, token_count, D),
        grad_memory.reshape(1, memory_count, D),
        grad_proj_in,
        grad_proj_out,
        grad_gains,
        grad_rel_bias,
        grad_router,
        grad_expert_in,
        grad_expert_out,
        tally_counts,
    )


def solution(mesh):
    placed = (
        P("exp", "seq", None),
        P("exp", "seq", None),
        P(),
        P(),
        P(),
        P(),
        P(),
        P("exp", "seq", None),
        P("exp", None, "seq"),
        P("exp", None, "seq"),
        P("exp", "seq", None),
    )
    return jax.shard_map(
        body,
        mesh=mesh,
        in_specs=placed,
        out_specs=(
            P("exp", "seq", None),
            P("exp", "seq", None),
            P("exp", "seq", None),
            P(),
            P(),
            P(),
            P(),
            P(),
            P("exp", None, "seq"),
            P("exp", None, "seq"),
            P("exp", "seq", None, None),
        ),
        check_vma=False,
    )
```

profile of v0, /device:TPU:25, one launch (start us, length us, event | category | flops | bytes accessed | tf_op | source)
XLA Modules:
  0.0 2236.8 jit_solution(14791899676010954966)
XLA Ops:
  27.0 27.8 %all-gather.11.cloned.1.call-done = bf16[1024,768]{1,0:T(8,128)(2,1)} async-done(((bf16[128,768]{1,0:T(8,128)(2,1)}), bf16[1024,768]{1,0:T(8,128)(2,1)}) %all-gather.11.cloned.1.call-update) | async-done | bytes 1572880 | tf_op jit(solution)/shard_map/all_gather | solution.py:258
  59.2 41.4 %all-gather.13.cloned.1.call-done = bf16[1024,768]{1,0:T(8,128)(2,1)} async-done(((bf16[128,768]{1,0:T(8,128)(2,1)}), bf16[1024,768]{1,0:T(8,128)(2,1)}) %all-gather.13.cloned.1.call-update) | async-done | bytes 1572880 | tf_op jit(solution)/shard_map/all_gather | solution.py:259
  105.0 76.6 %all-gather.7.cloned.1.call-done = bf16[3072,768]{1,0:T(8,128)(2,1)} async-done(((bf16[384,768]{1,0:T(8,128)(2,1)}), bf16[3072,768]{1,0:T(8,128)(2,1)}) %all-gather.7.cloned.1.call-update) | async-done | bytes 4718608 | tf_op jit(solution)/shard_map/all_gather | solution.py:256
  210.0 52.2 %all-gather.9.cloned.1.call-done = bf16[3072,768]{1,0:T(8,128)(2,1)} async-done(((bf16[384,768]{1,0:T(8,128)(2,1)}), bf16[3072,768]{1,0:T(8,128)(2,1)}) %all-gather.9.cloned.1.call-update) | async-done | bytes 4718608 | tf_op jit(solution)/shard_map/all_gather | solution.py:257
  291.9 282.8 %while.63 = (s32[]{:T(128)}, f32[12,384]{1,0:T(8,128)S(1)}, f32[12,384]{1,0:T(8,128)S(1)}, f32[12,384,64]{1,2,0:T(8,128)}, s32[6]{0:T(128)}, /*index=5*/s32[]{:T...) while((s32[]{:T(128)}, f32[12,384]{1,0:T(8,128)S(1)}, ...), condition=%wide.region_6.7_spmd, body=%wide.region_1.6_spmd.sunk | while | flops 707798400 | bytes 46127968 | solution.py:130
  313.5 41.0 %conditional.5 = ((f32[12,384]{1,0:T(8,128)S(1)}, f32[12,384]{1,0:T(8,128)S(1)}, f32[12,384,64]{1,2,0:T(8,128)})) conditional(s32[]{:T(128)} %convert_element_type.792, (f32[12,384]{1,0:T(8,128)S(1)}, f32[12,384]{1,0:T(8,128)S(1)}, f32[12,384,64]{1,2,0:T(8,128)}) %tuple.271, (s32[]{:T(128)}, s32[]{:T(128)}, bf16[6,512,12,64]{1,3,2,0:T(8,128)(2,1)}, ...), branch_computations={%region_2.2_spmd, %region_3.5_spmd} | conditional | flops 707798400 | bytes 46127712 | solution.py:118
  356.5 40.6 %conditional.5 = ((f32[12,384]{1,0:T(8,128)S(1)}, f32[12,384]{1,0:T(8,128)S(1)}, f32[12,384,64]{1,2,0:T(8,128)})) conditional(s32[]{:T(128)} %convert_element_type.792, (f32[12,384]{1,0:T(8,128)S(1)}, f32[12,384]{1,0:T(8,128)S(1)}, f32[12,384,64]{1,2,0:T(8,128)}) %tuple.271, (s32[]{:T(128)}, s32[]{:T(128)}, bf16[6,512,12,64]{1,3,2,0:T(8,128)(2,1)}, ...), branch_computations={%region_2.2_spmd, %region_3.5_spmd} | conditional | flops 707798400 | bytes 46127712 | solution.py:118
  399.2 40.7 %conditional.5 = ((f32[12,384]{1,0:T(8,128)S(1)}, f32[12,384]{1,0:T(8,128)S(1)}, f32[12,384,64]{1,2,0:T(8,128)})) conditional(s32[]{:T(128)} %convert_element_type.792, (f32[12,384]{1,0:T(8,128)S(1)}, f32[12,384]{1,0:T(8,128)S(1)}, f32[12,384,64]{1,2,0:T(8,128)}) %tuple.271, (s32[]{:T(128)}, s32[]{:T(128)}, bf16[6,512,12,64]{1,3,2,0:T(8,128)(2,1)}, ...), branch_computations={%region_2.2_spmd, %region_3.5_spmd} | conditional | flops 707798400 | bytes 46127712 | solution.py:118
  441.9 40.7 %conditional.5 = ((f32[12,384]{1,0:T(8,128)S(1)}, f32[12,384]{1,0:T(8,128)S(1)}, f32[12,384,64]{1,2,0:T(8,128)})) conditional(s32[]{:T(128)} %convert_element_type.792, (f32[12,384]{1,0:T(8,128)S(1)}, f32[12,384]{1,0:T(8,128)S(1)}, f32[12,384,64]{1,2,0:T(8,128)}) %tuple.271, (s32[]{:T(128)}, s32[]{:T(128)}, bf16[6,512,12,64]{1,3,2,0:T(8,128)(2,1)}, ...), branch_computations={%region_2.2_spmd, %region_3.5_spmd} | conditional | flops 707798400 | bytes 46127712 | solution.py:118
  484.6 40.6 %conditional.5 = ((f32[12,384]{1,0:T(8,128)S(1)}, f32[12,384]{1,0:T(8,128)S(1)}, f32[12,384,64]{1,2,0:T(8,128)})) conditional(s32[]{:T(128)} %convert_element_type.792, (f32[12,384]{1,0:T(8,128)S(1)}, f32[12,384]{1,0:T(8,128)S(1)}, f32[12,384,64]{1,2,0:T(8,128)}) %tuple.271, (s32[]{:T(128)}, s32[]{:T(128)}, bf16[6,512,12,64]{1,3,2,0:T(8,128)(2,1)}, ...), branch_computations={%region_2.2_spmd, %region_3.5_spmd} | conditional | flops 707798400 | bytes 46127712 | solution.py:118
  527.3 40.7 %conditional.5 = ((f32[12,384]{1,0:T(8,128)S(1)}, f32[12,384]{1,0:T(8,128)S(1)}, f32[12,384,64]{1,2,0:T(8,128)})) conditional(s32[]{:T(128)} %convert_element_type.792, (f32[12,384]{1,0:T(8,128)S(1)}, f32[12,384]{1,0:T(8,128)S(1)}, f32[12,384,64]{1,2,0:T(8,128)}) %tuple.271, (s32[]{:T(128)}, s32[]{:T(128)}, bf16[6,512,12,64]{1,3,2,0:T(8,128)(2,1)}, ...), branch_computations={%region_2.2_spmd, %region_3.5_spmd} | conditional | flops 707798400 | bytes 46127712 | solution.py:118
  584.0 32.1 %while.65 = (s32[]{:T(128)}, f32[12,384]{1,0:T(8,128)}, f32[12,384]{1,0:T(8,128)}, f32[12,384,64]{1,2,0:T(8,128)S(1)}, bf16[2,512,12,64]{1,3,2,0:T(8,128)(2,1)S(...) while((s32[]{:T(128)}, f32[12,384]{1,0:T(8,128)}, ...), condition=%wide.region_11.12_spmd.clone, body=%wide.region_8.11_spmd.clone.sunk | while | flops 623761920 | bytes 71098600 | solution.py:130
  727.2 38.3 %while.66 = (s32[]{:T(128)}, f32[384,12,64]{0,2,1:T(8,128)}, bf16[2,512,12,64]{1,3,2,0:T(8,128)(2,1)}, bf16[2,512,12,64]{1,3,2,0:T(8,128)(2,1)}, bf16[2,512,12,6...) while((s32[]{:T(128)}, f32[384,12,64]{0,2,1:T(8,128)}, ...), condition=%wide.region_23.24_spmd.clone, body=%wide.region_22.23_spmd.clone.sunk | while | flops 1530101760 | bytes 147136816 | solution.py:206
  777.0 449.1 %while.64 = (s32[]{:T(128)}, f32[384,12,64]{0,2,1:T(8,128)}, f32[32,12]{0,1:T(8,128)S(1)}, bf16[6,512,12,64]{1,3,2,0:T(8,128)(2,1)}, bf16[6,512,12,64]{1,3,2,0:T...) while((s32[]{:T(128)}, f32[384,12,64]{0,2,1:T(8,128)}, ...), condition=%wide.region_29.30_spmd.clone, body=%wide.region_26.29_spmd.clone.sunk | while | flops 1785398016 | bytes 75549312 | solution.py:206
  779.1 58.2 %conditional.6 = (f32[384,12,64]{0,2,1:T(8,128)}, f32[32,12]{0,1:T(8,128)S(1)}, bf16[1,512,12,64]{1,3,2,0:T(8,128)(2,1)S(1)}, bf16[1,512,12,64]{1,3,2,0:T(8,128)(2,1)S(1)}) conditional(s32[]{:T(128)} %convert_element_type.793, (f32[384,12,64]{0,2,1:T(8,128)}, f32[32,12]{0,1:T(8,128)S(1)}) %tuple.275, (s32[]{:T(128)}, s32[]{:T(128)}, ...), branch_computations={%region_27.27_spmd, %region_28.28_spmd} | conditional | flops 1785398016 | bytes 72402640 | solution.py:199
  784.6 28.2 %fusion.59 = f32[12,384,512]{1,2,0:T(8,128)} fusion(f32[12,384]{1,0:T(8,128)S(1)} %get-tuple-element.501, f32[12]{0:T(128)S(1)} %get-tuple-element.929, f32[12]{0:T(128)S(1)} %get-tuple-element.930, f32[12]{0:T(128)S(1)} %get-tuple-element.931, f32[12]{0:T(128)S(1)} %get-tuple-element.932, f32[12]{0:T(128)S(1)} %get-tuple-element.933, ...), kind=kOutput, calls=%fused_computation.95 | convolution fusion | flops 384565248 | bytes 17125376 | tf_op jit(solution)/shard_map/while/body/eval_jaxpr/cond/branch_1_fun/qhd,khd->hqk/dot_general | solution.py:155
  848.8 66.7 %conditional.6 = (f32[384,12,64]{0,2,1:T(8,128)}, f32[32,12]{0,1:T(8,128)S(1)}, bf16[1,512,12,64]{1,3,2,0:T(8,128)(2,1)S(1)}, bf16[1,512,12,64]{1,3,2,0:T(8,128)(2,1)S(1)}) conditional(s32[]{:T(128)} %convert_element_type.793, (f32[384,12,64]{0,2,1:T(8,128)}, f32[32,12]{0,1:T(8,128)S(1)}) %tuple.275, (s32[]{:T(128)}, s32[]{:T(128)}, ...), branch_computations={%region_27.27_spmd, %region_28.28_spmd} | conditional | flops 1785398016 | bytes 72402640 | solution.py:199
  854.3 36.5 %fusion.59 = f32[12,384,512]{1,2,0:T(8,128)} fusion(f32[12,384]{1,0:T(8,128)S(1)} %get-tuple-element.501, f32[12]{0:T(128)S(1)} %get-tuple-element.929, f32[12]{0:T(128)S(1)} %get-tuple-element.930, f32[12]{0:T(128)S(1)} %get-tuple-element.931, f32[12]{0:T(128)S(1)} %get-tuple-element.932, f32[12]{0:T(128)S(1)} %get-tuple-element.933, ...), kind=kOutput, calls=%fused_computation.95 | convolution fusion | flops 384565248 | bytes 17125376 | tf_op jit(solution)/shard_map/while/body/eval_jaxpr/cond/branch_1_fun/qhd,khd->hqk/dot_general | solution.py:155
  926.8 58.2 %conditional.6 = (f32[384,12,64]{0,2,1:T(8,128)}, f32[32,12]{0,1:T(8,128)S(1)}, bf16[1,512,12,64]{1,3,2,0:T(8,128)(2,1)S(1)}, bf16[1,512,12,64]{1,3,2,0:T(8,128)(2,1)S(1)}) conditional(s32[]{:T(128)} %convert_element_type.793, (f32[384,12,64]{0,2,1:T(8,128)}, f32[32,12]{0,1:T(8,128)S(1)}) %tuple.275, (s32[]{:T(128)}, s32[]{:T(128)}, ...), branch_computations={%region_27.27_spmd, %region_28.28_spmd} | conditional | flops 1785398016 | bytes 72402640 | solution.py:199
  932.4 28.2 %fusion.59 = f32[12,384,512]{1,2,0:T(8,128)} fusion(f32[12,384]{1,0:T(8,128)S(1)} %get-tuple-element.501, f32[12]{0:T(128)S(1)} %get-tuple-element.929, f32[12]{0:T(128)S(1)} %get-tuple-element.930, f32[12]{0:T(128)S(1)} %get-tuple-element.931, f32[12]{0:T(128)S(1)} %get-tuple-element.932, f32[12]{0:T(128)S(1)} %get-tuple-element.933, ...), kind=kOutput, calls=%fused_computation.95 | convolution fusion | flops 384565248 | bytes 17125376 | tf_op jit(solution)/shard_map/while/body/eval_jaxpr/cond/branch_1_fun/qhd,khd->hqk/dot_general | solution.py:155
  996.6 66.7 %conditional.6 = (f32[384,12,64]{0,2,1:T(8,128)}, f32[32,12]{0,1:T(8,128)S(1)}, bf16[1,512,12,64]{1,3,2,0:T(8,128)(2,1)S(1)}, bf16[1,512,12,64]{1,3,2,0:T(8,128)(2,1)S(1)}) conditional(s32[]{:T(128)} %convert_element_type.793, (f32[384,12,64]{0,2,1:T(8,128)}, f32[32,12]{0,1:T(8,128)S(1)}) %tuple.275, (s32[]{:T(128)}, s32[]{:T(128)}, ...), branch_computations={%region_27.27_spmd, %region_28.28_spmd} | conditional | flops 1785398016 | bytes 72402640 | solution.py:199
  1002.1 36.5 %fusion.59 = f32[12,384,512]{1,2,0:T(8,128)} fusion(f32[12,384]{1,0:T(8,128)S(1)} %get-tuple-element.501, f32[12]{0:T(128)S(1)} %get-tuple-element.929, f32[12]{0:T(128)S(1)} %get-tuple-element.930, f32[12]{0:T(128)S(1)} %get-tuple-element.931, f32[12]{0:T(128)S(1)} %get-tuple-element.932, f32[12]{0:T(128)S(1)} %get-tuple-element.933, ...), kind=kOutput, calls=%fused_computation.95 | convolution fusion | flops 384565248 | bytes 17125376 | tf_op jit(solution)/shard_map/while/body/eval_jaxpr/cond/branch_1_fun/qhd,khd->hqk/dot_general | solution.py:155
  1074.6 58.2 %conditional.6 = (f32[384,12,64]{0,2,1:T(8,128)}, f32[32,12]{0,1:T(8,128)S(1)}, bf16[1,512,12,64]{1,3,2,0:T(8,128)(2,1)S(1)}, bf16[1,512,12,64]{1,3,2,0:T(8,128)(2,1)S(1)}) conditional(s32[]{:T(128)} %convert_element_type.793, (f32[384,12,64]{0,2,1:T(8,128)}, f32[32,12]{0,1:T(8,128)S(1)}) %tuple.275, (s32[]{:T(128)}, s32[]{:T(128)}, ...), branch_computations={%region_27.27_spmd, %region_28.28_spmd} | conditional | flops 1785398016 | bytes 72402640 | solution.py:199
  1080.1 28.2 %fusion.59 = f32[12,384,512]{1,2,0:T(8,128)} fusion(f32[12,384]{1,0:T(8,128)S(1)} %get-tuple-element.501, f32[12]{0:T(128)S(1)} %get-tuple-element.929, f32[12]{0:T(128)S(1)} %get-tuple-element.930, f32[12]{0:T(128)S(1)} %get-tuple-element.931, f32[12]{0:T(128)S(1)} %get-tuple-element.932, f32[12]{0:T(128)S(1)} %get-tuple-element.933, ...), kind=kOutput, calls=%fused_computation.95 | convolution fusion | flops 384565248 | bytes 17125376 | tf_op jit(solution)/shard_map/while/body/eval_jaxpr/cond/branch_1_fun/qhd,khd->hqk/dot_general | solution.py:155
  1144.3 66.7 %conditional.6 = (f32[384,12,64]{0,2,1:T(8,128)}, f32[32,12]{0,1:T(8,128)S(1)}, bf16[1,512,12,64]{1,3,2,0:T(8,128)(2,1)S(1)}, bf16[1,512,12,64]{1,3,2,0:T(8,128)(2,1)S(1)}) conditional(s32[]{:T(128)} %convert_element_type.793, (f32[384,12,64]{0,2,1:T(8,128)}, f32[32,12]{0,1:T(8,128)S(1)}) %tuple.275, (s32[]{:T(128)}, s32[]{:T(128)}, ...), branch_computations={%region_27.27_spmd, %region_28.28_spmd} | conditional | flops 1785398016 | bytes 72402640 | solution.py:199
  1149.8 36.5 %fusion.59 = f32[12,384,512]{1,2,0:T(8,128)} fusion(f32[12,384]{1,0:T(8,128)S(1)} %get-tuple-element.501, f32[12]{0:T(128)S(1)} %get-tuple-element.929, f32[12]{0:T(128)S(1)} %get-tuple-element.930, f32[12]{0:T(128)S(1)} %get-tuple-element.931, f32[12]{0:T(128)S(1)} %get-tuple-element.932, f32[12]{0:T(128)S(1)} %get-tuple-element.933, ...), kind=kOutput, calls=%fused_computation.95 | convolution fusion | flops 384565248 | bytes 17125376 | tf_op jit(solution)/shard_map/while/body/eval_jaxpr/cond/branch_1_fun/qhd,khd->hqk/dot_general | solution.py:155
  1353.6 95.5 %reduce-scatter.18.cloned.1.call-done = bf16[384,768]{1,0:T(8,128)(2,1)} async-done(((bf16[3072,768]{1,0:T(8,128)(2,1)}), bf16[384,768]{1,0:T(8,128)(2,1)}) %reduce-scatter.18.cloned.1.call-update) | async-done | bytes 589840
  1454.8 61.9 %reduce-scatter.20.cloned.1.call-done = bf16[128,768]{1,0:T(8,128)(2,1)} async-done(((bf16[1024,768]{1,0:T(8,128)(2,1)}), bf16[128,768]{1,0:T(8,128)(2,1)}) %reduce-scatter.20.cloned.1.call-update) | async-done | bytes 196624
  1519.5 65.1 %reduce-scatter.22.cloned.1.call-done = bf16[128,768]{1,0:T(8,128)(2,1)} async-done(((bf16[1024,768]{1,0:T(8,128)(2,1)}), bf16[128,768]{1,0:T(8,128)(2,1)}) %reduce-scatter.22.cloned.1.call-update) | async-done | bytes 196624
  1600.0 45.4 %all-reduce = (f32[3,768]{1,0:T(4,128)}, f32[32,12]{0,1:T(8,128)}, f32[768,8]{0,1:T(8,128)}) all-reduce(f32[3,768]{1,0:T(4,128)S(1)} %pad_maximum_fusion.2, f32[32,12]{0,1:T(8,128)S(1)} %get-tuple-element.564, f32[768,8]{0,1:T(8,128)S(1)} %fusion.266), channel_id=1, replica_groups=mesh['seq'=8,'exp'=4] {'seq','exp'}, use_global_device_ids=true, to_apply=%region_40.41 | all-reduce | flops 8832 | bytes 70656 | tf_op jit(solution)/shard_map/psum | solution.py:448
  1646.6 255.6 %reduce-scatter.14.cloned.1.call-done = bf16[384,4,768]{2,0,1:T(8,128)(2,1)} async-done(((bf16[3072,4,768]{2,0,1:T(8,128)(2,1)}), bf16[384,4,768]{2,0,1:T(8,128)(2,1)}) %reduce-scatter.14.cloned.1.call-update) | async-done | bytes 2359312 | tf_op jit(solution)/shard_map/reduce_scatter | solution.py:346
  1911.1 301.8 %all-reduce.4.cloned.1.call-done = (f32[6,768,768]{2,1,0:T(8,128)}, f32[2,768,768]{2,1,0:T(8,128)}) async-done(((f32[6,768,768]{2,1,0:T(8,128)}, f32[2,768,768]{2,1,0:T(8,128)}), (f32[6,768,768]{2,1,0:T(8,128)}, f32[2,768,768]{2,1,0:T(8,128)})) %all-reduce.4.cloned.1.call-update) | async-done | bytes 18874384 | tf_op jit(solution)/shard_map/psum | solution.py:448
  (571 shorter events, 903.3 us)
Async XLA Ops:
  7.2 47.6 %all-gather.11.cloned.1.call-start = ((), (), s32[]{:S(2)}) async-start(), calls=%async_computation.11 | async-start | bytes 1769472 | tf_op jit(solution)/shard_map/all_gather | solution.py:258
  10.4 90.2 %all-gather.13.cloned.1.call-start = ((), (), s32[]{:S(2)}) async-start(), calls=%async_computation.12 | async-start | bytes 1769472 | tf_op jit(solution)/shard_map/all_gather | solution.py:259
  12.8 168.8 %all-gather.7.cloned.1.call-start = ((), (), s32[]{:S(2)}) async-start(), calls=%async_computation.9 | async-start | bytes 5308416 | tf_op jit(solution)/shard_map/all_gather | solution.py:256
  16.5 245.8 %all-gather.9.cloned.1.call-start = ((), (), s32[]{:S(2)}) async-start(), calls=%async_computation.10 | async-start | bytes 5308416 | tf_op jit(solution)/shard_map/all_gather | solution.py:257
  19.3 640.3 %all-gather.15.cloned.1.call-start = ((), (), s32[]{:S(2)}) async-start(), calls=%async_computation.13 | async-start | bytes 10616832 | tf_op jit(solution)/shard_map/all_gather | solution.py:310
  19.9 648.3 %all-gather.17.cloned.1.call-start = ((), (), s32[]{:S(2)}) async-start(), calls=%async_computation.14 | async-start | bytes 10616832 | tf_op jit(solution)/shard_map/all_gather | solution.py:311
  616.1 24.6 %copy-start.6 = (f32[12,384,64]{1,2,0:T(8,128)}, f32[12,384,64]{1,2,0:T(8,128)S(1)}, u32[]{:S(2)}) copy-start(f32[12,384,64]{1,2,0:T(8,128)S(1)} %get-tuple-element.554) | copy-start | bytes 3538948
  621.7 10.6 copy-start.65
  625.1 15.6 all-to-all-start
  631.2 86.9 %copy-start.62 = (f32[384,8]{0,1:T(8,128)}, f32[384,8]{0,1:T(8,128)S(1)}, u32[]{:S(2)}) copy-start(f32[384,8]{0,1:T(8,128)S(1)} %get-tuple-element.1071) | copy-start | bytes 36868
  640.7 16.1 all-to-all-start.2
  647.9 20.3 copy-start.18
  668.2 8.9 copy-start.22
  681.3 14.6 all-to-all-start.3
  694.3 7.9 copy-start.35
  694.3 7.9 copy-start.48
  694.3 10.7 copy-start.26
  695.9 15.4 all-to-all-start.1
  700.9 649.3 %reduce-scatter.16.cloned.1.call-start = ((), (), s32[]{:S(2)}) async-start(), calls=%async_computation.16 | async-start | bytes 5308416
  727.2 39.8 %copy-start.76 = (f32[768]{0:T(1024)S(1)}, f32[768]{0:T(1024)}, u32[]{:S(2)}) copy-start(f32[768]{0:T(1024)} %get-tuple-element.827) | copy-start | bytes 9220
  727.2 39.8 %copy-start.91 = (f32[384]{0:T(512)S(1)}, f32[384]{0:T(512)}, u32[]{:S(2)}) copy-start(f32[384]{0:T(512)} %copy-done.90) | copy-start | bytes 4612
  733.9 9.4 copy-start.3
  752.8 9.7 copy-start.3
  1256.5 192.5 %reduce-scatter.18.cloned.1.call-start = ((), (), s32[]{:S(2)}) async-start(), calls=%async_computation.17 | async-start | bytes 5308416
  1287.2 229.5 %reduce-scatter.20.cloned.1.call-start = ((), (), s32[]{:S(2)}) async-start(), calls=%async_computation.18 | async-start | bytes 1769472
  1292.2 292.5 %reduce-scatter.22.cloned.1.call-start = ((), (), s32[]{:S(2)}) async-start(), calls=%async_computation.19 | async-start | bytes 1769472
  1295.9 606.3 %reduce-scatter.14.cloned.1.call-start = ((), (), s32[]{:S(2)}) async-start(), calls=%async_computation.15 | async-start | bytes 21233664 | tf_op jit(solution)/shard_map/reduce_scatter | solution.py:346
  1323.2 889.7 %all-reduce.4.cloned.1.call-start = ((), (), s32[]{:S(2)}) async-start(), calls=%async_computation.20 | async-start | bytes 37748736 | tf_op jit(solution)/shard_map/psum | solution.py:448
  1331.7 120.8 %copy-start.21 = (f32[384,768]{1,0:T(8,128)S(1)}, f32[384,768]{1,0:T(8,128)}, u32[]{:S(2)}) copy-start(f32[384,768]{1,0:T(8,128)} %copy-done.19) | copy-start | bytes 3538948
  1331.7 120.8 %copy-start.77 = (f32[768]{0:T(1024)S(1)}, f32[768]{0:T(1024)}, u32[]{:S(2)}) copy-start(f32[768]{0:T(1024)} %get-tuple-element.827) | copy-start | bytes 9220
  1331.7 120.8 %copy-start.92 = (f32[384]{0:T(512)S(1)}, f32[384]{0:T(512)}, u32[]{:S(2)}) copy-start(f32[384]{0:T(512)} %copy-done.90) | copy-start | bytes 4612
  1597.7 47.7 %copy-start.94 = (f32[384]{0:T(512)S(1)}, f32[384]{0:T(512)}, u32[]{:S(2)}) copy-start(f32[384]{0:T(512)} %copy-done.93) | copy-start | bytes 4612
  (101 other events, 342.4 us)
Sparse Core Ops, SparseCore 0:
  10.8 43.9 all-gather.10
  57.6 42.9 all-gather.12
  103.4 78.1 all-gather.6
  184.2 78.0 all-gather.8
  264.2 136.3 all-gather.14
  402.4 136.3 all-gather.16
  1256.6 93.5 reduce-scatter.15
  1353.8 95.1 reduce-scatter.17
  1453.0 63.6 reduce-scatter.19
  1520.9 63.6 reduce-scatter.21
  1588.5 313.5 reduce-scatter.13
  1909.0 303.8 all-reduce.3
where the time goes:
time: 2250 us; the launch traced here: 2240 us
  waiting for transfers between devices  1010 us (45%)
  matrix products  676 us (30%)
  local copies, waits for them, and re-layouts  232 us (10%)
  other arithmetic  134 us (6%)
  loops' own time  100 us (4%)
  blocking collectives  45.4 us (2%)
    dot_general x16, matrix products, compute(): jnp.einsum('qhd,khd->hqk', queries, key_block, preferred_element_type=jnp...  369 us
    psum x1, waiting for transfers between devices, body(): lax.psum((grad_proj_in, grad_proj_out, grad_gains, grad_table, grad_route...  302 us
    reduce_scatter x1, waiting for transfers between devices, body(): lax.psum_scatter(jnp.concatenate([term_in, term_out], axis=1).astype(jnp....  256 us
    unnamed x16, waiting for transfers between devices  242 us
    unnamed x200, local copies, waits for them, and re-layouts  100 us
    all_gather x1, waiting for transfers between devices, body(): lax.all_gather(key_local, 'seq', axis=0, tiled=True)  76.6 us
    ge x12, other arithmetic, relative_terms(): allowed = distance >= 0  59.4 us
    another operation x2, loops' own time, attend_backward(): lax.scan(block_step, initial, (key_stack, value_stack, offsets))  59.1 us
  transfers between devices with their start and end apart: 16, of which 14 were waited for; matrix products, arithmetic and copies ran while one was open for 23% of the time, Pallas kernels for 0%

commit v1 on v0

v1 whole, which is shorter than its diff:
```python
import functools
import math

import jax
import jax.numpy as jnp
from jax import lax
from jax.experimental import pallas as pl
from jax.experimental.pallas import tpu as pltpu
from jax.sharding import PartitionSpec as P

D = 768
HEADS = 12
HEAD_DIM = 64
NBUCKET = 32
MAXDIST = 128
TILE = 128
PAIRS = HEADS * HEAD_DIM // TILE

MESH = pl.DeviceIdType.MESH
ANY = pl.BlockSpec(memory_space=pl.ANY)
SMEM = pl.BlockSpec(memory_space=pltpu.SMEM)

norm_eps = 1e-06
masked_score = -1e30
highest = lax.Precision.HIGHEST
log2e = 1.0 / math.log(2.0)
scale_factor = HEAD_DIM ** (-0.5)


def bucket_edges():
    half_count = NBUCKET // 2
    thresholds = []
    for bucket_number in range(1, NBUCKET):
        if bucket_number < half_count:
            thresholds.append(bucket_number)
        else:
            thresholds.append(
                int(
                    half_count
                    * (MAXDIST / half_count) ** ((bucket_number - half_count) / half_count)
                )
            )
    return thresholds


def rms_apply(values, gain_row):
    return (
        values * lax.rsqrt(jnp.mean(values * values, axis=-1, keepdims=True) + norm_eps) * gain_row
    )


def rms_backward(values, gain_row, upstream):
    _, pullback = jax.vjp(rms_apply, values, gain_row)
    return pullback(upstream)


def seq_cycle(n):
    cols = n // 4
    if n % 4 or cols < 2:
        return list(range(n))
    order = [0]
    for row in range(4):
        span = range(1, cols) if row % 2 == 0 else range(cols - 1, 0, -1)
        order += [row * cols + col for col in span]
    return order + [3 * cols, 2 * cols, cols]


def chip_cycle(n, chips):
    order = seq_cycle(n)
    if chips == 1:
        return [(place, 0) for place in order]
    cycle = [(order[0], 0)]
    for row in range(n):
        span = range(1, chips) if row % 2 == 0 else range(chips - 1, 0, -1)
        cycle += [(order[row], chip) for chip in span]
    return cycle + [(order[row], 0) for row in range(n - 1, 0, -1)]


def look_up(index, table):
    value = jnp.int32(table[0])
    for number, entry in enumerate(table[1:], 1):
        value = jnp.where(index == number, jnp.int32(entry), value)
    return value


def greet(others):
    barrier = pltpu.get_barrier_semaphore()
    for other in others:
        pl.semaphore_signal(barrier, inc=1, device_id=other, device_id_type=MESH)
    pl.semaphore_wait(barrier, len(others))


def seq_ring(n):
    order = seq_cycle(n)
    pos = look_up(lax.axis_index("seq"), [order.index(i) for i in range(n)])

    def at(place):
        return look_up(lax.rem(place + 4 * n, n), order)

    return pos, at, ({"seq": at(pos + 1)}, {"seq": at(pos - 1)})


def gather_kernel(n, parts, count, *refs):
    sources, outs = refs[:count], refs[count : 2 * count]
    own_sem, send_sem, recv_sem = refs[2 * count :]
    pos, at, sides = seq_ring(n)
    me = at(pos)
    greet(sides)
    own = [
        pltpu.make_async_copy(sources[a], outs[a].at[me], own_sem.at[a]) for a in range(count)
    ]
    for copy in own:
        copy.start()
    started, latest = [], {}
    for step in range(n - 1):
        for a in range(count):
            rows = sources[a].shape[0] // 2 // parts
            for part in range(parts):
                for way in range(2):
                    if step:
                        latest[a, way, part].wait_recv()
                    block = at(pos - step) if way == 0 else at(pos + step)
                    span = pl.ds((way * parts + part) * rows, rows)
                    copy = pltpu.make_async_remote_copy(
                        src_ref=outs[a].at[block, span] if step else sources[a].at[span],
                        dst_ref=outs[a].at[block, span],
                        send_sem=send_sem.at[a, way, step, part],
                        recv_sem=recv_sem.at[a, way, step, part],
                        device_id=sides[way],
                        device_id_type=MESH,
                    )
                    copy.start()
                    started.append(copy)
                    latest[a, way, part] = copy
    for copy in latest.values():
        copy.wait_recv()
    for copy in started:
        copy.wait_send()
    for copy in own:
        copy.wait()


def ring_gather(arrays, n, number, parts=2):
    count = len(arrays)
    copies = (count, 2, n - 1, parts)
    return pl.pallas_call(
        functools.partial(gather_kernel, n, parts, count),
        out_shape=[jax.ShapeDtypeStruct((n,) + a.shape, a.dtype) for a in arrays],
        in_specs=[ANY] * count,
        out_specs=[ANY] * count,
        scratch_shapes=[
            pltpu.SemaphoreType.DMA((count,)),
            pltpu.SemaphoreType.DMA(copies),
            pltpu.SemaphoreType.DMA(copies),
        ],
        compiler_params=pltpu.CompilerParams(collective_id=number, has_side_effects=True),
        name="ring_gather",
    )(*arrays)


def scatter_kernel(n, parts, count, *refs):
    sources, outs = refs[:count], refs[count : 2 * count]
    own_bufs, got_bufs = refs[2 * count : 3 * count], refs[3 * count : 4 * count]
    own_sem, send_sem, recv_sem = refs[4 * count :]
    pos, at, sides = seq_ring(n)
    greet(sides)
    lanes = [(a, part, way) for a in range(count) for part in range(parts) for way in range(2)]

    def span(a, part, way):
        rows = sources[a].shape[1] // 2 // parts
        return pl.ds((way * parts + part) * rows, rows)

    def block(way, step):
        return at(pos - 1 - step) if way == 0 else at(pos + 1 + step)

    def send(lane, step, source):
        a, part, way = lane
        copy = pltpu.make_async_remote_copy(
            src_ref=source,
            dst_ref=got_bufs[a].at[way, step, part],
            send_sem=send_sem.at[a, way, step, part],
            recv_sem=recv_sem.at[a, way, step, part],
            device_id=sides[way],
            device_id_type=MESH,
        )
        copy.start()
        return copy

    latest, started, own = {}, [], {}
    for lane in lanes:
        a, part, way = lane
        latest[lane] = send(lane, 0, sources[a].at[block(way, 0), span(a, part, way)])
        started.append(latest[lane])
    for step in range(1, n):
        for lane in lanes:
            a, part, way = lane
            own[lane, step] = pltpu.make_async_copy(
                sources[a].at[block(way, step), span(a, part, way)],
                own_bufs[a].at[way, step - 1, part],
                own_sem.at[a, way, step - 1, part],
            )
            own[lane, step].start()
    for step in range(1, n):
        for lane in lanes:
            a, part, way = lane
            own[lane, step].wait()
            latest[lane].wait_recv()
            total = got_bufs[a][way, step - 1, part].astype(jnp.float32) + own_bufs[a][
                way, step - 1, part
            ].astype(jnp.float32)
            if step == n - 1:
                outs[a][span(a, part, way)] = total.astype(outs[a].dtype)
            else:
                got_bufs[a][way, step - 1, part] = total.astype(got_bufs[a].dtype)
                latest[lane] = send(lane, step, got_bufs[a].at[way, step - 1, part])
                started.append(latest[lane])
    for copy in started:
        copy.wait_send()


def ring_scatter(arrays, n, number, out_dtype, parts=2):
    count = len(arrays)
    copies = (count, 2, n - 1, parts)
    bufs = [
        pltpu.VMEM((2, n - 1, parts, a.shape[1] // 2 // parts, a.shape[2]), a.dtype)
        for a in arrays
    ]
    return pl.pallas_call(
        functools.partial(scatter_kernel, n, parts, count),
        out_shape=[jax.ShapeDtypeStruct(a.shape[1:], out_dtype) for a in arrays],
        in_specs=[ANY] * count,
        out_specs=[pl.BlockSpec(memory_space=pltpu.VMEM)] * count,
        scratch_shapes=bufs + bufs + [pltpu.SemaphoreType.DMA(copies)] * 3,
        compiler_params=pltpu.CompilerParams(
            collective_id=number, has_side_effects=True, vmem_limit_bytes=58 << 20
        ),
        name="ring_scatter",
    )(*arrays)


def total_kernel(n, chips, x_ref, out_ref, mine, twin, got, own_sem, twin_sem, ring_sem, back_sem):
    cycle = chip_cycle(n, chips)
    length = len(cycle)
    seq, exp = lax.axis_index("seq"), lax.axis_index("exp")
    core = lax.rem(exp, 2)
    places = [cycle.index((i // chips, i % chips)) for i in range(length)]
    pos = look_up(seq * chips + exp // 2, places)

    def device(place):
        place = lax.rem(place + length, length)
        return {
            "seq": look_up(place, [c[0] for c in cycle]),
            "exp": look_up(place, [c[1] for c in cycle]) * 2 + core,
        }

    def block(way, step):
        place = pos - 1 - step if way == 0 else pos + 1 + step
        return lax.rem(place + 2 * length, length)

    peer = {"exp": exp + 1 - 2 * core}
    sides = (device(pos + 1), device(pos - 1))
    greet((peer,) + sides)
    rows = x_ref.shape[2] // 2
    spans = (pl.ds(0, rows), pl.ds(rows, rows))
    started = []

    def push(source, target, sems, index, to):
        copy = pltpu.make_async_remote_copy(
            src_ref=source,
            dst_ref=target,
            send_sem=sems.at[(0,) + index],
            recv_sem=sems.at[(1,) + index],
            device_id=to,
            device_id_type=MESH,
        )
        copy.start()
        started.append(copy)
        return copy

    pairs, own = {}, {}
    for step in range(length):
        for way in range(2):
            where = block(way, step)
            pairs[way, step] = push(
                x_ref.at[1 - core, where, spans[way]], twin.at[way, step], twin_sem, (way, step), peer
            )
            own[way, step] = pltpu.make_async_copy(
                x_ref.at[core, where, spans[way]], mine.at[way, step], own_sem.at[way, step]
            )
            own[way, step].start()
    latest = {}
    for step in range(length):
        for way in range(2):
            own[way, step].wait()
            pairs[way, step].wait_recv()
            total = mine[way, step].astype(jnp.float32) + twin[way, step].astype(jnp.float32)
            if step:
                latest[way].wait_recv()
                total = total + got[way, step - 1].astype(jnp.float32)
            mine[way, step] = total.astype(mine.dtype)
            if step < length - 1:
                latest[way] = push(
                    mine.at[way, step], got.at[way, step], ring_sem, (0, way, step), sides[way]
                )
    keep = []
    for step in range(length):
        for way in range(2):
            if step:
                latest[way].wait_recv()
            where = lax.rem(pos - step + length, length) if way == 0 else lax.rem(pos + step, length)
            target = out_ref.at[core, where, spans[way]]
            source = target if step else mine.at[way, length - 1]
            if step < length - 1:
                latest[way] = push(source, target, ring_sem, (1, way, step), sides[way])
            pairs[way, step] = push(source, target, back_sem, (way, step), peer)
            if step == 0:
                copy = pltpu.make_async_copy(source, target, own_sem.at[way, 0])
                copy.start()
                keep.append(copy)
    for copy in keep:
        copy.wait()
    for copy in pairs.values():
        copy.wait_recv()
    for copy in started:
        copy.wait_send()


def total_everywhere(rows_in, n, m, number):
    chips = m // 2
    length = n * chips
    rows, cols = rows_in.shape
    each = rows // (2 * length)
    if m % 2 or rows % (2 * length * 32):
        return lax.psum(rows_in, ("seq", "exp"))
    x = rows_in.reshape(2, length, each, cols)
    buf = pltpu.VMEM((2, length, each // 2, cols), x.dtype)
    return pl.pallas_call(
        functools.partial(total_kernel, n, chips),
        out_shape=jax.ShapeDtypeStruct(x.shape, x.dtype),
        in_specs=[ANY],
        out_specs=ANY,
        scratch_shapes=[
            buf,
            buf,
            buf,
            pltpu.SemaphoreType.DMA((2, length)),
            pltpu.SemaphoreType.DMA((2, 2, length)),
            pltpu.SemaphoreType.DMA((2, 2, 2, length)),
            pltpu.SemaphoreType.DMA((2, 2, length)),
        ],
        compiler_params=pltpu.CompilerParams(
            collective_id=number, has_side_effects=True, vmem_limit_bytes=58 << 20
        ),
        name="total_everywhere",
    )(x).reshape(rows, cols)


def dot_last(a, b):
    return lax.dot_general(a, b, (((1,), (1,)), ((), ())), preferred_element_type=jnp.float32)


def dot_first(a, b):
    return lax.dot_general(a, b, (((0,), (0,)), ((), ())), preferred_element_type=jnp.float32)


def dot_plain(a, b):
    return jnp.dot(a, b, preferred_element_type=jnp.float32)


def head_masks(dtype):
    low = lax.broadcasted_iota(jnp.int32, (1, TILE), 1) < HEAD_DIM
    first = jnp.where(low, 1.0, 0.0).astype(jnp.float32)
    return first.astype(dtype), (1.0 - first).astype(dtype)


def split_heads(pair):
    return jnp.concatenate([pair * mask for mask in head_masks(pair.dtype)], axis=0)


def own_bias(tiles, count):
    rows = []
    for r in range(count):
        row = []
        for c in range(count):
            if c == r:
                row.append(tiles[:, TILE:])
            elif c == r - 1:
                row.append(tiles[:, :TILE])
            else:
                row.append(jnp.full((TILE, TILE), 0.0 if c < r else masked_score, jnp.float32))
        rows.append(jnp.concatenate(row, axis=1))
    return jnp.concatenate(rows, axis=0)


def attend_kernel(causal, block, s_ref, q_ref, k_ref, v_ref, *refs):
    if causal:
        tile_ref, low_ref, wide_ref, lse_ref, acc_ref, top_ref = refs
    else:
        low_ref, wide_ref, lse_ref, acc_ref, top_ref = refs
    rows = q_ref.shape[0]
    both = split_heads(q_ref[...])
    masks = head_masks(v_ref.dtype)

    def visit(start, bias, first):
        keys = k_ref[pl.ds(start, block), :]
        values = v_ref[pl.ds(start, block), :]
        t = dot_last(both, keys) * (scale_factor * log2e)
        if bias is not None:
            t = t + bias
        top = jnp.max(t, axis=1, keepdims=True)
        if not first:
            before = top_ref[...]
            top = jnp.maximum(before, top)
            fade = jnp.exp2(before - top)
        top_ref[...] = top
        p = jnp.exp2(t - top).astype(values.dtype)
        for h in range(2):
            part = dot_plain(p[h * rows : (h + 1) * rows], values * masks[h] + masks[1 - h])
            if first:
                acc_ref[h] = part
            else:
                acc_ref[h] = acc_ref[h] * fade[h * rows : (h + 1) * rows] + part

    if causal:
        s = s_ref[0]
        count = rows // TILE
        visit(
            pl.multiple_of(s * block, block),
            jnp.concatenate([own_bias(tile_ref[h], count) for h in range(2)], axis=0),
            True,
        )

        @pl.when(s > 0)
        def _():
            edge = []
            for h in range(2):
                top_row = jnp.concatenate(
                    [jnp.zeros((TILE, rows - TILE), jnp.float32), tile_ref[h][:, :TILE]], axis=1
                )
                edge += [top_row, jnp.zeros((rows - TILE, rows), jnp.float32)]
            visit(pl.multiple_of((s - 1) * block, block), jnp.concatenate(edge, axis=0), False)

        def far(j, carry):
            visit(pl.multiple_of(j * block, block), None, False)
            return carry

        lax.fori_loop(0, s - 1, far, 0)
    else:
        for j in range(k_ref.shape[0] // block):
            visit(j * block, None, j == 0)
    low = lax.broadcasted_iota(jnp.int32, (rows, TILE), 1) < HEAD_DIM
    acc0, acc1 = acc_ref[0], acc_ref[1]
    wide = jnp.where(
        low,
        acc0 / pltpu.roll(acc0, HEAD_DIM, 1),
        acc1 / pltpu.roll(acc1, HEAD_DIM, 1),
    )
    wide_ref[...] = wide
    low_ref[...] = wide.astype(low_ref.dtype)
    lse0 = top_ref[:rows] + jnp.log2(acc0[:, HEAD_DIM : HEAD_DIM + 1])
    lse1 = top_ref[rows:] + jnp.log2(acc1[:, :1])
    turned = jnp.where(low, lse0, lse1).T
    lse_ref[0] = jnp.concatenate([turned[:1], turned[HEAD_DIM : HEAD_DIM + 1]], axis=0)


def attend(seq_at, queries, keys, values, tiles):
    rows, total = queries.shape[0], keys.shape[0]
    causal = tiles is not None
    block = rows if causal else math.gcd(total, 512)
    pair = pl.BlockSpec((rows, TILE), lambda g: (0, g))
    long = pl.BlockSpec((total, TILE), lambda g: (0, g))
    extra, specs = [], []
    if causal:
        extra, specs = [tiles], [pl.BlockSpec((2,) + tiles.shape[1:], lambda g: (g, 0, 0))]
    return pl.pallas_call(
        functools.partial(attend_kernel, causal, block),
        grid=(PAIRS,),
        out_shape=[
            jax.ShapeDtypeStruct((rows, D), jnp.bfloat16),
            jax.ShapeDtypeStruct((rows, D), jnp.float32),
            jax.ShapeDtypeStruct((PAIRS, 2, rows), jnp.float32),
        ],
        in_specs=[SMEM, pair, long, long] + specs,
        out_specs=[pair, pair, pl.BlockSpec((1, 2, rows), lambda g: (g, 0, 0))],
        scratch_shapes=[
            pltpu.VMEM((2, rows, TILE), jnp.float32),
            pltpu.VMEM((2 * rows, 1), jnp.float32),
        ],
        compiler_params=pltpu.CompilerParams(vmem_limit_bytes=48 << 20),
        name="attend_self" if causal else "attend_cross",
    )(seq_at, queries, keys, values, *extra)


def attend_back_kernel(causal, block, s_ref, q_ref, k_ref, v_ref, up_ref, wide_ref, lse_ref, *refs):
    if causal:
        tile_ref, dq_ref, dk_ref, dv_ref, near_ref, sum_ref, acc_ref = refs
    else:
        dq_ref, dk_ref, dv_ref, acc_ref = refs
    rows = q_ref.shape[0]
    both = split_heads(q_ref[...])
    up = up_ref[...]
    up_both = split_heads(up)
    turned = (up.astype(jnp.float32) * wide_ref[...]).T
    delta = jnp.concatenate(
        [
            jnp.sum(turned[:HEAD_DIM], axis=0, keepdims=True),
            jnp.sum(turned[HEAD_DIM:], axis=0, keepdims=True),
        ],
        axis=1,
    )
    lse = jnp.concatenate([lse_ref[0, :1], lse_ref[0, 1:]], axis=1)
    ones = jnp.ones((16, block), k_ref.dtype)

    def visit(start, bias, first):
        keys = k_ref[pl.ds(start, block), :]
        values = v_ref[pl.ds(start, block), :]
        t = dot_last(keys, both) * (scale_factor * log2e)
        if bias is not None:
            t = t + bias
        p = jnp.exp2(t - lse)
        ds = (p * (dot_last(values, up_both) - delta)).astype(keys.dtype)
        dv_ref[pl.ds(start, block), :] = dot_plain(p.astype(keys.dtype), up_both).astype(
            dv_ref.dtype
        )
        dk_ref[pl.ds(start, block), :] = (dot_plain(ds, both) * scale_factor).astype(dk_ref.dtype)
        part = dot_plain(jnp.concatenate([keys.T, ones], axis=0), ds)
        if first:
            acc_ref[...] = part
        else:
            acc_ref[...] += part
        return ds

    if causal:
        s = s_ref[0]
        count = rows // TILE
        ds = visit(
            pl.multiple_of(s * block, block),
            jnp.concatenate([own_bias(tile_ref[h], count).T for h in range(2)], axis=1),
            True,
        )
        for h in range(2):
            same = before = jnp.zeros((TILE, TILE), jnp.float32)
            for r in range(count):
                columns = slice(h * rows + r * TILE, h * rows + (r + 1) * TILE)
                same = same + ds[r * TILE : (r + 1) * TILE, columns].astype(jnp.float32)
                if r:
                    before = before + ds[(r - 1) * TILE : r * TILE, columns].astype(jnp.float32)
            near_ref[h, :TILE] = before
            near_ref[h, TILE:] = same

        @pl.when(s > 0)
        def _():
            edge = []
            for h in range(2):
                first_rows = jnp.concatenate(
                    [jnp.zeros((rows - TILE, TILE), jnp.float32), tile_ref[h][:, :TILE].T], axis=0
                )
                edge += [first_rows, jnp.zeros((rows, rows - TILE), jnp.float32)]
            ds = visit(pl.multiple_of((s - 1) * block, block), jnp.concatenate(edge, axis=1), False)
            for h in range(2):
                near_ref[h, :TILE] += ds[rows - TILE :, h * rows : h * rows + TILE].astype(
                    jnp.float32
                )

        def far(j, carry):
            visit(pl.multiple_of(j * block, block), None, False)
            return carry

        lax.fori_loop(0, s - 1, far, 0)

        def beyond(j, carry):
            start = pl.multiple_of(j * block, block)
            dk_ref[pl.ds(start, block), :] = jnp.zeros((block, TILE), dk_ref.dtype)
            dv_ref[pl.ds(start, block), :] = jnp.zeros((block, TILE), dv_ref.dtype)
            return carry

        lax.fori_loop(s + 1, k_ref.shape[0] // block, beyond, 0)
        sum_ref[0] = jnp.concatenate(
            [acc_ref[TILE : TILE + 1, :rows], acc_ref[TILE : TILE + 1, rows:]], axis=0
        )
    else:
        for j in range(k_ref.shape[0] // block):
            visit(j * block, None, j == 0)
    dq = jnp.concatenate([acc_ref[:HEAD_DIM, :rows], acc_ref[HEAD_DIM:TILE, rows:]], axis=0)
    dq_ref[...] = (dq.T * scale_factor).astype(dq_ref.dtype)


def attend_back(seq_at, queries, keys, values, upstream, wide, lse, tiles):
    rows, total = queries.shape[0], keys.shape[0]
    causal = tiles is not None
    block = rows if causal else math.gcd(total, 512)
    pair = pl.BlockSpec((rows, TILE), lambda g: (0, g))
    long = pl.BlockSpec((total, TILE), lambda g: (0, g))
    line = pl.BlockSpec((1, 2, rows), lambda g: (g, 0, 0))
    extra, specs, shapes, out_specs = [], [], [], []
    if causal:
        extra, specs = [tiles], [pl.BlockSpec((2,) + tiles.shape[1:], lambda g: (g, 0, 0))]
        shapes = [
            jax.ShapeDtypeStruct((HEADS, 2 * TILE, TILE), jnp.float32),
            jax.ShapeDtypeStruct((PAIRS, 2, rows), jnp.float32),
        ]
        out_specs = [pl.BlockSpec((2, 2 * TILE, TILE), lambda g: (g, 0, 0)), line]
    return pl.pallas_call(
        functools.partial(attend_back_kernel, causal, block),
        grid=(PAIRS,),
        out_shape=[
            jax.ShapeDtypeStruct((rows, D), jnp.bfloat16),
            jax.ShapeDtypeStruct((total, D), jnp.bfloat16),
            jax.ShapeDtypeStruct((total, D), jnp.bfloat16),
        ]
        + shapes,
        in_specs=[SMEM, pair, long, long, pair, pair, line] + specs,
        out_specs=[pair, long, long] + out_specs,
        scratch_shapes=[pltpu.VMEM((TILE + 16, 2 * rows), jnp.float32)],
        compiler_params=pltpu.CompilerParams(vmem_limit_bytes=48 << 20),
        name="attend_self_back" if causal else "attend_cross_back",
    )(seq_at, queries, keys, values, upstream, wide, lse, *extra)


def bias_tiles(bias_table):
    distance = (
        TILE
        + jnp.arange(TILE, dtype=jnp.int32)[:, None]
        - jnp.arange(2 * TILE, dtype=jnp.int32)[None, :]
    )
    table = (bias_table - bias_table[NBUCKET - 1 :]) * log2e
    terms = jnp.broadcast_to(table[0][:, None, None], (HEADS, TILE, 2 * TILE))
    for number, threshold in enumerate(bucket_edges()):
        terms = jnp.where((distance >= threshold)[None], table[number + 1][:, None, None], terms)
    return jnp.where((distance >= 0)[None], terms, masked_score)


def bias_gradient(near, sums):
    distance = (
        TILE
        + jnp.arange(TILE, dtype=jnp.int32)[None, :]
        - jnp.arange(2 * TILE, dtype=jnp.int32)[:, None]
    )
    bucket = jnp.zeros(distance.shape, jnp.int32)
    for threshold in bucket_edges():
        bucket = bucket + (distance >= threshold).astype(jnp.int32)
    onehot = (
        bucket.reshape(-1)[None, :] == jnp.arange(NBUCKET, dtype=jnp.int32)[:, None]
    ).astype(jnp.float32)
    flat = near.reshape(HEADS, -1)
    table = lax.dot_general(
        onehot, flat, (((1,), (1,)), ((), ())), precision=highest
    )
    far = jnp.sum(sums, axis=-1).reshape(HEADS) - jnp.sum(flat, axis=-1)
    last = jnp.arange(NBUCKET, dtype=jnp.int32)[:, None] == NBUCKET - 1
    return table + jnp.where(last, far[None, :], 0.0)


def expert_kernel(rows_ref, in_ref, out_ref, part_ref, gin_ref, gout_ref):
    tokens = rows_ref[0, :, :D]
    upstream = rows_ref[0, :, D:]
    up_map, down_map = in_ref[0], out_ref[0]
    u = dot_plain(tokens, up_map)
    square = u * u
    slope = math.sqrt(2.0 / math.pi)
    bend = jnp.tanh(slope * (u + 0.044715 * (square * u)))
    half = 0.5 * (1.0 + bend)
    act = (u * half).astype(tokens.dtype)
    rise = half + 0.5 * u * (1.0 - bend * bend) * (slope * (1.0 + 3 * 0.044715 * square))
    du = (dot_plain(upstream, down_map) * rise).astype(tokens.dtype)
    part_ref[0, :, :D] = dot_last(act, down_map).astype(part_ref.dtype)
    part_ref[0, :, D:] = dot_last(du, up_map).astype(part_ref.dtype)
    gin, gout = dot_first(tokens, du), dot_first(upstream, act)

    @pl.when(pl.program_id(1) == 0)
    def _():
        gin_ref[0] = gin
        gout_ref[0] = gout

    @pl.when(pl.program_id(1) > 0)
    def _():
        gin_ref[0] += gin
        gout_ref[0] += gout


def run_experts(gathered, expert_in, expert_out):
    n, rows, width = gathered.shape
    count, _, hidden = expert_in.shape
    each = rows // count
    block = pl.BlockSpec((1, each, width), lambda e, s: (s, e, 0))
    weight = pl.BlockSpec((1, D, hidden), lambda e, s: (e, 0, 0))
    grad = jax.ShapeDtypeStruct(expert_in.shape, jnp.float32)
    return pl.pallas_call(
        expert_kernel,
        grid=(count, n),
        out_shape=[jax.ShapeDtypeStruct(gathered.shape, gathered.dtype), grad, grad],
        in_specs=[block, weight, weight],
        out_specs=[block, weight, weight],
        compiler_params=pltpu.CompilerParams(vmem_limit_bytes=48 << 20),
        name="run_experts",
    )(gathered, expert_in, expert_out)


def project(source, matrix):
    return jnp.dot(source, matrix, preferred_element_type=jnp.float32).astype(jnp.bfloat16)


def weight_grad(source, upstream):
    return jnp.einsum("td,te->de", source, upstream, preferred_element_type=jnp.float32).astype(
        jnp.bfloat16
    )


def input_grad(upstream, matrix):
    return jnp.einsum("te,de->td", upstream, matrix, preferred_element_type=jnp.float32)


def body(
    n,
    m,
    hidden_in,
    memory,
    proj_in,
    proj_out,
    norm_gains,
    rel_bias,
    router,
    expert_choice,
    expert_in,
    expert_out,
    cotangent,
):
    tokens = hidden_in[0].astype(jnp.float32)
    memory_rows = memory[0]
    memory_count = memory_rows.shape[0]
    gain_rows = norm_gains.astype(jnp.float32)
    token_count = tokens.shape[0]
    seq_at = lax.axis_index("seq").astype(jnp.int32).reshape(1)
    normed_self = rms_apply(tokens, gain_rows[0]).astype(jnp.bfloat16)
    tiles = bias_tiles(rel_bias)

    normed_all, memory_all = ring_gather([normed_self, memory_rows], n, 1)
    normed_all = normed_all.reshape(n * token_count, D)
    memory_all = memory_all.reshape(n * memory_count, D)
    queries = project(normed_self, proj_in[0])
    key_all = project(normed_all, proj_in[1])
    value_all = project(normed_all, proj_in[2])
    memory_key_all = project(memory_all, proj_in[4])
    memory_value_all = project(memory_all, proj_in[5])
    attended_self_low, attended_self, lse_self = attend(
        seq_at, queries, key_all, value_all, tiles
    )
    after_self = tokens + jnp.dot(
        attended_self_low, proj_out[0], preferred_element_type=jnp.float32
    )

    normed_cross = rms_apply(after_self, gain_rows[1]).astype(jnp.bfloat16)
    cross_queries = project(normed_cross, proj_in[3])
    attended_cross_low, attended_cross, lse_cross = attend(
        seq_at, cross_queries, memory_key_all, memory_value_all, None
    )
    after_cross = after_self + jnp.dot(
        attended_cross_low, proj_out[1], preferred_element_type=jnp.float32
    )

    mixed_low = rms_apply(after_cross, gain_rows[2]).astype(jnp.bfloat16)
    softmax_probs = jax.nn.softmax(
        jnp.dot(mixed_low, router, preferred_element_type=jnp.float32), axis=-1
    )
    expert_count = router.shape[1]
    local_experts = expert_in.shape[0]
    capacity = max(2, 5 * token_count // (4 * expert_count))
    chosen = expert_choice[0, :, 0]
    onehot_int = (chosen[:, None] == jnp.arange(expert_count, dtype=jnp.int32)[None, :]).astype(
        jnp.int32
    )
    onehot = onehot_int.astype(jnp.float32)
    gate_prob = jnp.sum(softmax_probs * onehot, axis=-1)
    slot_index = jnp.sum(jnp.cumsum(onehot_int, axis=0) * onehot_int, axis=-1) - 1
    is_kept = slot_index < capacity
    place = jnp.where(is_kept, chosen * capacity + slot_index, -1)
    dispatch = (
        place[:, None] == jnp.arange(expert_count * capacity, dtype=jnp.int32)[None, :]
    ).astype(jnp.bfloat16)
    dispatched = jnp.sum(onehot_int * is_kept[:, None].astype(jnp.int32), axis=0)
    tally_counts = jnp.stack(
        [dispatched, jnp.sum(onehot_int, axis=0) - dispatched], axis=0
    ).reshape(1, 1, 2, expert_count)

    grad_top = cotangent[0].astype(jnp.float32)
    scaled = (gate_prob[:, None] * grad_top).astype(jnp.bfloat16)
    sent_rows = (
        jnp.einsum(
            "tx,td->xd",
            dispatch,
            jnp.concatenate([mixed_low, scaled], axis=1),
            preferred_element_type=jnp.float32,
        )
        .astype(jnp.bfloat16)
        .reshape(expert_count, capacity, 2 * D)
    )
    received = lax.all_to_all(sent_rows, "exp", split_axis=0, concat_axis=1, tiled=True)
    (gathered,) = ring_gather([received.reshape(local_experts * m * capacity, 2 * D)], n, 2)
    parts, grad_expert_in, grad_expert_out = run_experts(gathered, expert_in, expert_out)
    (summed,) = ring_scatter([parts], n, 3, jnp.bfloat16)
    returned = lax.all_to_all(
        summed.reshape(local_experts, m * capacity, 2 * D),
        "exp",
        split_axis=1,
        concat_axis=0,
        tiled=True,
    ).reshape(expert_count * capacity, 2 * D)
    routed = jnp.dot(dispatch, returned, preferred_element_type=jnp.float32)
    combined, grad_mixed = routed[:, :D], routed[:, D:]
    output = (after_cross + gate_prob[:, None] * combined).astype(jnp.bfloat16)

    grad_gate = jnp.sum(grad_top * combined, axis=-1)
    grad_logits = softmax_probs * (onehot - gate_prob[:, None]) * grad_gate[:, None]
    grad_router = jnp.einsum(
        "td,te->de", mixed_low.astype(jnp.float32), grad_logits, precision=highest
    )
    grad_mixed = grad_mixed + jnp.einsum(
        "te,de->td", grad_logits, router.astype(jnp.float32), precision=highest
    )
    grad_cross_part, grad_gain_mix = rms_backward(after_cross, gain_rows[2], grad_mixed)
    grad_after_cross = grad_top + grad_cross_part

    grad_cross_low = grad_after_cross.astype(jnp.bfloat16)
    grad_out_cross = weight_grad(attended_cross_low, grad_cross_low)
    grad_attended_cross = input_grad(grad_cross_low, proj_out[1]).astype(jnp.bfloat16)
    grad_cross_query, grad_memory_keys, grad_memory_values = attend_back(
        seq_at,
        cross_queries,
        memory_key_all,
        memory_value_all,
        grad_attended_cross,
        attended_cross,
        lse_cross,
        None,
    )
    grad_query_cross = weight_grad(normed_cross, grad_cross_query)
    grad_self_part, grad_gain_cross = rms_backward(
        after_self, gain_rows[1], input_grad(grad_cross_query, proj_in[3])
    )
    grad_after_self = grad_after_cross + grad_self_part
    grad_memory_part = (
        input_grad(grad_memory_keys, proj_in[4]) + input_grad(grad_memory_values, proj_in[5])
    ).astype(jnp.bfloat16)

    grad_self_low = grad_after_self.astype(jnp.bfloat16)
    grad_out_self = weight_grad(attended_self_low, grad_self_low)
    grad_attended_self = input_grad(grad_self_low, proj_out[0]).astype(jnp.bfloat16)
    grad_self_query, grad_keys, grad_values, near, sums = attend_back(
        seq_at,
        queries,
        key_all,
        value_all,
        grad_attended_self,
        attended_self,
        lse_self,
        tiles,
    )
    grad_table = bias_gradient(near, sums)
    grad_normed_part = (
        input_grad(grad_keys, proj_in[1]) + input_grad(grad_values, proj_in[2])
    ).astype(jnp.bfloat16)
    grad_normed_own, grad_memory = ring_scatter(
        [
            grad_normed_part.reshape(n, token_count, D),
            grad_memory_part.reshape(n, memory_count, D),
        ],
        n,
        4,
        jnp.float32,
    )
    grad_normed_self = input_grad(grad_self_query, proj_in[0]) + grad_normed_own
    grad_token_part, grad_gain_self = rms_backward(tokens, gain_rows[0], grad_normed_self)
    grad_in = (grad_after_self + grad_token_part).astype(jnp.bfloat16)

    grads = jnp.stack(
        [
            weight_grad(normed_self, grad_self_query),
            weight_grad(normed_all, grad_keys),
            weight_grad(normed_all, grad_values),
            grad_query_cross,
            weight_grad(memory_all, grad_memory_keys),
            weight_grad(memory_all, grad_memory_values),
            grad_out_self,
            grad_out_cross,
        ]
    )
    grads = total_everywhere(grads.reshape(-1, D), n, m, 5).reshape(-1, D, D).astype(jnp.float32)
    grad_gains = jnp.stack([grad_gain_self, grad_gain_cross, grad_gain_mix])
    small = lax.psum(
        jnp.concatenate([grad_gains.reshape(-1), grad_table.reshape(-1), grad_router.reshape(-1)]),
        ("seq", "exp"),
    )
    ends = (grad_gains.size, grad_gains.size + grad_table.size)
    return (
        output.reshape(1, token_count, D),
        grad_in.reshape(1, token_count, D),
        grad_memory.astype(jnp.bfloat16).reshape(1, memory_count, D),
        grads[:6],
        grads[6:],
        small[: ends[0]].reshape(grad_gains.shape),
        small[ends[0] : ends[1]].reshape(grad_table.shape),
        small[ends[1] :].reshape(grad_router.shape),
        grad_expert_in,
        grad_expert_out,
        tally_counts,
    )


def solution(mesh):
    rows = P("exp", "seq", None)
    hidden = P("exp", None, "seq")
    return jax.shard_map(
        functools.partial(body, mesh.shape["seq"], mesh.shape["exp"]),
        mesh=mesh,
        in_specs=(rows, rows, P(), P(), P(), P(), P(), rows, hidden, hidden, rows),
        out_specs=(
            rows,
            rows,
            rows,
            P(),
            P(),
            P(),
            P(),
            P(),
            hidden,
            hidden,
            P("exp", "seq", None, None),
        ),
        check_vma=False,
    )
```

time: 2250 us -> 942 us (0.42)
  waiting for transfers between devices: 1010 us -> 36.2 us
  Pallas kernels: 0 us -> 687 us
  matrix products: 676 us -> 84.7 us
  local copies, waits for them, and re-layouts: 232 us -> 50.4 us
  other arithmetic: 134 us -> 22.6 us
  loops' own time: 100 us -> 0 us
    pallas_call x0 -> x10, Pallas kernels: none -> 687 us  [the longest x2 183 us: ring_gather(): pl.pallas_call(functools.partial(gather_kernel, n, parts, count), out_sha...]
    dot_general x72 -> x3, matrix products: 617 us -> 7.8 us  [the longest x1 3.21 us: body(): jnp.einsum('tx,td->xd', dispatch, jnp.concatenate([mixed_low, scaled], ax...]
    psum x1 -> x0, waiting for transfers between devices: 302 us -> none  [body(): lax.psum((grad_proj_in, grad_proj_out, grad_gains, grad_table, grad_route...]
    reduce_scatter x1 -> x0, waiting for transfers between devices: 256 us -> none  [body(): lax.psum_scatter(jnp.concatenate([term_in, term_out], axis=1).astype(jnp....]
    unnamed x16 -> x0, waiting for transfers between devices: 242 us -> none
    all_gather x6 -> x0, waiting for transfers between devices: 198 us -> none  [the longest x1 76.6 us: body(): lax.all_gather(key_local, 'seq', axis=0, tiled=True)]
    another operation x16 -> x0, loops' own time: 100 us -> none  [the longest x2 59.1 us: attend_backward(): lax.scan(block_step, initial, (key_stack, value_stack, offsets))]
    unnamed x200 -> x148, local copies, waits for them, and re-layouts: 100 us -> 20.4 us
  transfers between devices with their start and end apart: 16 -> 2, of which waited for: 14 -> 2; matrix products, arithmetic and copies ran while one was open for 23% -> 0% of each run, Pallas kernels for 0% -> 0%
where the time goes in v1:
time: 942 us; the launch traced here: 935 us
  Pallas kernels  687 us (73%)
  matrix products  84.7 us (9%)
  local copies, waits for them, and re-layouts  50.4 us (5%)
  blocking collectives  40 us (4%)
  waiting for transfers between devices  36.2 us (4%)
  other arithmetic  22.6 us (2%)
  starting transfers between devices  12.5 us (1%)
    pallas_call x2, Pallas kernels, ring_gather(): pl.pallas_call(functools.partial(gather_kernel, n, parts, count), out_sha...  183 us
    pallas_call x2, Pallas kernels, ring_scatter(): pl.pallas_call(functools.partial(scatter_kernel, n, parts, count), out_sh...  182 us
    pallas_call x1, Pallas kernels, total_everywhere(): pl.pallas_call(functools.partial(total_kernel, n, chips), out_shape=jax.S...  162 us
    pallas_call x2, Pallas kernels, attend(): pl.pallas_call(functools.partial(attend_kernel, causal, block), grid=(PAI...  72.6 us
    pallas_call x2, Pallas kernels, attend_back(): pl.pallas_call(functools.partial(attend_back_kernel, causal, block), grid...  57.6 us
    psum x1, blocking collectives, body(): lax.psum(jnp.concatenate([grad_gains.reshape(-1), grad_table.reshape(-1),...  40 us
    pallas_call x1, Pallas kernels, run_experts(): pl.pallas_call(expert_kernel, grid=(count, n), out_shape=[jax.ShapeDtypeS...  29 us
    dot_general x8, matrix products, input_grad(): jnp.einsum('te,de->td', upstream, matrix, preferred_element_type=jnp.floa...  28.6 us
  transfers between devices with their start and end apart: 2, of which 2 were waited for; matrix products, arithmetic and copies ran while one was open for 0% of the time, Pallas kernels for 0%

profile of v1, /device:TPU:25, one launch (start us, length us, event | category | flops | bytes accessed | tf_op | source)
XLA Modules:
  0.0 935.4 jit_solution(15388199927159324687)
XLA Ops:
  9.2 62.0 %ring_gather.2 = (bf16[8,384,768]{2,1,0:T(8,128)(2,1)}, bf16[8,128,768]{2,1,0:T(8,128)(2,1)}) custom-call(bf16[384,768]{1,0:T(8,128)(2,1)} %fusion.25.refs_0_, bf16[128,768]{1,0:T(8,128)(2,1)} %bitcast.273), custom_call_target="tpu_custom_call" | custom-call | tf_op jit(solution)/shard_map/ring_gather/pallas_call | solution.py:146
  71.2 8.8 convolution_convert_fusion.v_ref
  80.0 7.1 convolution_convert_fusion.1.k_ref
  90.1 2.6 convolution_convert_fusion.4.k_ref
  94.1 7.5 select_select_fusion.refs_0_
  102.7 58.6 %attend_self.1 = (bf16[384,768]{1,0:T(8,128)(2,1)S(1)}, f32[384,768]{1,0:T(8,128)S(1)}, f32[6,2,384]{2,1,0:T(2,128)S(1)}) custom-call(s32[1]{0:T(128)} %bitcast.1.s_ref, bf16[384,768]{1,0:T(8,128)(2,1)S(1)} %copy-done.4, bf16[3072,768]{1,0:T(8,128)(2,1)} %convolution_convert_fusion.1.k_ref, bf16[3072,768]{1,0:T(8,128)(2,1)} %convolution_convert_fusion.v_ref, ...), custom_call_target="tpu_custom_call" | custom-call | tf_op jit(solution)/shard_map/attend_self/pallas_call | solution.py:475
  164.9 14.0 %attend_cross.1 = (bf16[384,768]{1,0:T(8,128)(2,1)S(1)}, f32[384,768]{1,0:T(8,128)S(1)}, f32[6,2,384]{2,1,0:T(2,128)S(1)}) custom-call(s32[1]{0:T(128)} %bitcast.1.s_ref, bf16[384,768]{1,0:T(8,128)(2,1)S(1)} %convolution_convert_fusion.15.q_ref, bf16[1024,768]{1,0:T(8,128)(2,1)S(1)} %copy-done.3, bf16[1024,768]{1,0:T(8,128)(2,1)S(1)} %convolution_convert_fusion.3.v_ref), custom_call_target="tpu_custom_call" | custom-call | tf_op jit(solution)/shard_map/attend_cross/pallas_call | solution.py:475
  184.3 3.2 convolution_convert_fusion.2
  189.9 5.5 all-to-all-start
  195.6 19.0 %all-to-all-done = bf16[8,60,1536]{2,1,0:T(8,128)(2,1)S(1)} async-done(((bf16[8,60,1536]{2,1,0:T(8,128)(2,1)}), bf16[8,60,1536]{2,1,0:T(8,128)(2,1)S(1)}, u32[]{:S(2)}, u32[]{:S(2)}) %all-to-all-start) | async-done | bytes 1474592 | tf_op jit(solution)/shard_map/all_to_all | solution.py:797
  217.8 121.2 %ring_gather.3.rows_ref = bf16[8,480,1536]{2,1,0:T(8,128)(2,1)} custom-call(bf16[480,1536]{1,0:T(8,128)(2,1)} %reshape.1099.refs_0_), custom_call_target="tpu_custom_call" | custom-call | tf_op jit(solution)/shard_map/ring_gather/pallas_call | solution.py:146
  340.3 29.0 %run_experts.1 = (bf16[8,480,1536]{2,1,0:T(8,128)(2,1)}, f32[2,768,384]{2,1,0:T(8,128)}, f32[2,768,384]{2,1,0:T(8,128)}) custom-call(bf16[8,480,1536]{2,1,0:T(8,128)(2,1)} %ring_gather.3.rows_ref, bf16[2,768,384]{2,1,0:T(8,128)(2,1)S(1)} %copy-done.10, bf16[2,768,384]{2,1,0:T(8,128)(2,1)S(1)} %copy-done.11), custom_call_target="tpu_custom_call" | custom-call | tf_op jit(solution)/shard_map/run_experts/pallas_call | solution.py:688
  369.3 113.6 %ring_scatter.2 = bf16[480,1536]{1,0:T(8,128)(2,1)} custom-call(bf16[8,480,1536]{2,1,0:T(8,128)(2,1)} %get-tuple-element.36.refs_0_), custom_call_target="tpu_custom_call" | custom-call | tf_op jit(solution)/shard_map/ring_scatter/pallas_call | solution.py:228
  483.0 4.0 copy.24
  487.0 7.0 all-to-all-start.1
  495.0 17.2 %all-to-all-done.1 = bf16[2,240,1536]{2,0,1:T(2,128)(2,1)} async-done(((bf16[2,240,1536]{2,0,1:T(2,128)(2,1)}), bf16[2,240,1536]{2,0,1:T(2,128)(2,1)}, u32[]{:S(2)}, u32[]{:S(2)}) %all-to-all-start.1) | async-done | bytes 1474592 | tf_op jit(solution)/shard_map/all_to_all | solution.py:801
  523.1 15.1 %attend_cross_back.1 = (bf16[384,768]{1,0:T(8,128)(2,1)S(1)}, bf16[1024,768]{1,0:T(8,128)(2,1)S(1)}, bf16[1024,768]{1,0:T(8,128)(2,1)S(1)}) custom-call(s32[1]{0:T(128)} %bitcast.1.s_ref, bf16[384,768]{1,0:T(8,128)(2,1)S(1)} %copy-done.9, bf16[1024,768]{1,0:T(8,128)(2,1)} %convolution_convert_fusion.4.k_ref, bf16[1024,768]{1,0:T(8,128)(2,1)} %copy-done.2, ...), custom_call_target="tpu_custom_call" | custom-call | tf_op jit(solution)/shard_map/attend_cross_back/pallas_call | solution.py:603
  538.2 3.0 multiply_reduce_fusion.1
  543.5 42.4 %attend_self_back.1 = (bf16[384,768]{1,0:T(8,128)(2,1)S(1)}, bf16[3072,768]{1,0:T(8,128)(2,1)}, bf16[3072,768]{1,0:T(8,128)(2,1)}, f32[12,256,128]{2,1,0:T(8,128)S(1)}, f32[6,2,384]{2,1,0:T(2,128)S(1)}) custom-call(s32[1]{0:T(128)} %bitcast.1.s_ref, bf16[384,768]{1,0:T(8,128)(2,1)S(1)} %copy-done.5, bf16[3072,768]{1,0:T(8,128)(2,1)} %convolution_convert_fusion.1.k_ref, ...), custom_call_target="tpu_custom_call" | custom-call | tf_op jit(solution)/shard_map/attend_self_back/pallas_call | solution.py:603
  589.3 3.5 fusion.43
  593.3 6.7 fusion.53
  600.0 2.6 add_convert_fusion.1
  602.6 8.0 add_convert_fusion
  610.6 68.7 %ring_scatter.3 = (f32[384,768]{1,0:T(8,128)}, f32[128,768]{1,0:T(8,128)}) custom-call(bf16[8,384,768]{2,1,0:T(8,128)(2,1)} %bitcast.271, bf16[8,128,768]{2,1,0:T(8,128)(2,1)} %bitcast.272), custom_call_target="tpu_custom_call" | custom-call | tf_op jit(solution)/shard_map/ring_scatter/pallas_call | solution.py:228
  679.3 3.5 fusion.26
  683.0 2.8 copy.32
  688.6 40.0 %psum.7 = f32[8832]{0:T(1024)S(1)} all-reduce(f32[8832]{0:T(1024)S(1)} %pad_maximum_fusion), channel_id=1, replica_groups=mesh['seq'=8,'exp'=4] {'seq','exp'}, use_global_device_ids=true, to_apply=%region_18.19 | all-reduce | flops 8832 | bytes 70656 | tf_op jit(solution)/shard_map/psum | solution.py:889
  729.5 8.1 fusion.22
  737.6 6.4 fusion.24
  751.2 3.7 copy-done.34
  754.9 162.4 %total_everywhere.1 = bf16[2,16,192,768]{3,2,1,0:T(8,128)(2,1)} custom-call(bf16[2,16,192,768]{3,2,1,0:T(8,128)(2,1)} %bitcast.265), custom_call_target="tpu_custom_call" | custom-call | tf_op jit(solution)/shard_map/total_everywhere/pallas_call | solution.py:337
  917.3 9.7 %slice.277 = f32[6,768,768]{2,1,0:T(8,128)} slice(bf16[8,768,768]{2,1,0:T(8,128)(2,1)} %bitcast.263), slice={[0:6], [0:768], [0:768]} | slice | bytes 28311552 | tf_op jit(solution)/shard_map/slice | solution.py:898
  (233 shorter events, 66.5 us)
Async XLA Ops:
  0.6 180.7 %copy-start = (bf16[768,8]{0,1:T(8,128)(2,1)S(1)}, bf16[768,8]{0,1:T(8,128)(2,1)}, u32[]{:S(2)}) copy-start(bf16[768,8]{0,1:T(8,128)(2,1)} %param.17) | copy-start | bytes 36868
  0.7 92.0 %copy-start.57 = (s32[128]{0:T(128)}, s32[128]{0:T(128)S(1)}, u32[]{:S(2)}) copy-start(s32[128]{0:T(128)S(1)} %iota_add_fusion) | copy-start | bytes 1540
  5.8 81.4 %copy-start.50 = (f32[768]{0:T(1024)}, f32[768]{0:T(1024)S(1)}, u32[]{:S(2)}) copy-start(f32[768]{0:T(1024)S(1)} %get-tuple-element.72) | copy-start | bytes 9220
  7.0 72.9 %copy-start.54 = (f32[384]{0:T(512)}, f32[384]{0:T(512)S(1)}, u32[]{:S(2)}) copy-start(f32[384]{0:T(512)S(1)} %fusion.27) | copy-start | bytes 4612
  7.1 80.1 %copy-start.52 = (f32[384]{0:T(512)}, f32[384]{0:T(512)S(1)}, u32[]{:S(2)}) copy-start(f32[384]{0:T(512)S(1)} %fusion.169) | copy-start | bytes 4612
  71.2 8.8 copy-start.60
  71.2 16.0 %slice-start.1 = ((s8[7077888]{0:T(1024)(128)(4,1)}), s8[4194304]{0:T(1024)(128)(4,1)S(1)}, s32[]{:S(2)}) async-start(s8[7077888]{0:T(1024)(128)(4,1)} %bitcast.277), calls=%async_computation.3 | async-start | bytes 8388608
  80.0 7.2 copy-start.35
  80.0 7.2 slice-start.2
  90.1 74.8 %copy-start.2 = (bf16[1024,768]{1,0:T(8,128)(2,1)}, bf16[1024,768]{1,0:T(8,128)(2,1)S(1)}, u32[]{:S(2)}) copy-start(bf16[1024,768]{1,0:T(8,128)(2,1)S(1)} %convolution_convert_fusion.3.v_ref) | copy-start | bytes 4718596
  102.7 58.6 %copy-start.36 = (bf16[1,384,768]{2,1,0:T(8,128)(2,1)S(1)}, bf16[1,384,768]{2,1,0:T(8,128)(2,1)}, u32[]{:S(2)}) copy-start(bf16[1,384,768]{2,1,0:T(8,128)(2,1)} %param.11) | copy-start | bytes 1769476
  102.7 58.6 %copy-start.39 = (bf16[2,768,768]{2,1,0:T(8,128)(2,1)S(1)}, bf16[2,768,768]{2,1,0:T(8,128)(2,1)}, u32[]{:S(2)}) copy-start(bf16[2,768,768]{2,1,0:T(8,128)(2,1)} %param.14) | copy-start | bytes 7077892
  162.5 16.5 %copy-start.44 = (f32[384,768]{1,0:T(8,128)}, f32[384,768]{1,0:T(8,128)S(1)}, u32[]{:S(2)}) copy-start(f32[384,768]{1,0:T(8,128)S(1)} %get-tuple-element.142) | copy-start | bytes 3538948
  164.9 14.1 %copy-start.8 = (bf16[384,768]{1,0:T(8,128)(2,1)}, bf16[384,768]{1,0:T(8,128)(2,1)S(1)}, u32[]{:S(2)}) copy-start(bf16[384,768]{1,0:T(8,128)(2,1)S(1)} %convolution_convert_fusion.15.q_ref) | copy-start | bytes 1769476
  189.9 24.7 %all-to-all-start = ((bf16[8,60,1536]{2,1,0:T(8,128)(2,1)}), bf16[8,60,1536]{2,1,0:T(8,128)(2,1)S(1)}, u32[]{:S(2)}, u32[]{:S(2)}) async-start(bf16[8,60,1536]{2,1,0:T(8,128)(2,1)} %reshape.1098), calls=%async_computation | async-start | bytes 3145728 | tf_op jit(solution)/shard_map/all_to_all | solution.py:797
  217.8 121.2 %copy-start.10 = (bf16[2,768,384]{2,1,0:T(8,128)(2,1)S(1)}, bf16[2,768,384]{2,1,0:T(8,128)(2,1)}, u32[]{:S(2)}) copy-start(bf16[2,768,384]{2,1,0:T(8,128)(2,1)} %in_ref.1) | copy-start | bytes 3538948
  487.0 7.6 copy-start.58
  487.0 25.2 %all-to-all-start.1 = ((bf16[2,240,1536]{2,0,1:T(2,128)(2,1)}), bf16[2,240,1536]{2,0,1:T(2,128)(2,1)}, u32[]{:S(2)}, u32[]{:S(2)}) async-start(bf16[2,240,1536]{2,0,1:T(2,128)(2,1)} %copy.24), calls=%async_computation.1 | async-start | bytes 2949120 | tf_op jit(solution)/shard_map/all_to_all | solution.py:801
  521.2 20.1 %copy-start.32 = (f32[384,768]{1,0:T(8,128)}, f32[384,768]{1,0:T(8,128)S(1)}, u32[]{:S(2)}) copy-start(f32[384,768]{1,0:T(8,128)S(1)} %convert_add_fusion) | copy-start | bytes 3538948
  523.1 15.2 %copy-start.45 = (f32[384,768]{1,0:T(8,128)S(1)}, f32[384,768]{1,0:T(8,128)}, u32[]{:S(2)}) copy-start(f32[384,768]{1,0:T(8,128)} %copy-done.44) | copy-start | bytes 3538948
  589.3 13.3 %slice-start.5 = ((s8[4718592]{0:T(1024)(128)(4,1)}), s8[4194304]{0:T(1024)(128)(4,1)S(1)}, s32[]{:S(2)}) async-start(s8[4718592]{0:T(1024)(128)(4,1)} %bitcast.285), calls=%async_computation.7 | async-start | bytes 8388608
  593.3 6.7 copy-start.19
  593.3 9.3 slice-start.6
  610.6 68.7 %copy-start.26 = (bf16[384,768]{1,0:T(8,128)(2,1)S(1)}, bf16[384,768]{1,0:T(8,128)(2,1)}, u32[]{:S(2)}) copy-start(bf16[384,768]{1,0:T(8,128)(2,1)} %copy-done.25) | copy-start | bytes 1769476
  610.6 68.7 %copy-start.37 = (bf16[1,384,768]{2,1,0:T(8,128)(2,1)S(1)}, bf16[1,384,768]{2,1,0:T(8,128)(2,1)}, u32[]{:S(2)}) copy-start(bf16[1,384,768]{2,1,0:T(8,128)(2,1)} %param.11) | copy-start | bytes 1769476
  610.6 68.7 %copy-start.51 = (f32[768]{0:T(1024)S(1)}, f32[768]{0:T(1024)}, u32[]{:S(2)}) copy-start(f32[768]{0:T(1024)} %copy-done.50) | copy-start | bytes 9220
  610.6 68.7 %copy-start.53 = (f32[384]{0:T(512)S(1)}, f32[384]{0:T(512)}, u32[]{:S(2)}) copy-start(f32[384]{0:T(512)} %copy-done.52) | copy-start | bytes 4612
  685.9 42.7 %copy-start.47 = (bf16[384,768]{1,0:T(8,128)(2,1)S(1)}, bf16[384,768]{1,0:T(8,128)(2,1)}, u32[]{:S(2)}) copy-start(bf16[384,768]{1,0:T(8,128)(2,1)} %fusion.25.refs_0_) | copy-start | bytes 1769476
  728.6 8.9 slice-start.7
  729.4 8.1 slice-start.8
  737.6 6.4 copy-start.24
  917.3 9.7 %copy-start.27 = (bf16[2,16,192,768]{3,2,1,0:T(8,128)(2,1)S(1)}, bf16[2,16,192,768]{3,2,1,0:T(8,128)(2,1)}, u32[]{:S(2)}) copy-start(bf16[2,16,192,768]{3,2,1,0:T(8,128)(2,1)} %total_everywhere.1) | copy-start | bytes 28311556
  (43 other events, 100.0 us)

commit v2 on v1

--- a/solution.py
+++ b/solution.py
@@ -238,7 +238,11 @@
     )(*arrays)
 
 
-def total_kernel(n, chips, x_ref, out_ref, mine, twin, got, own_sem, twin_sem, ring_sem, back_sem):
+def total_kernel(n, chips, parts, *refs):
+    count = len(parts)
+    xs, outs = refs[:count], refs[count : 2 * count]
+    mines, twins, gots = (refs[(2 + i) * count : (3 + i) * count] for i in range(3))
+    own_sem, twin_sem, ring_sem, back_sem = refs[5 * count :]
     cycle = chip_cycle(n, chips)
     length = len(cycle)
     seq, exp = lax.axis_index("seq"), lax.axis_index("exp")
@@ -260,8 +264,7 @@
     peer = {"exp": exp + 1 - 2 * core}
     sides = (device(pos + 1), device(pos - 1))
     greet((peer,) + sides)
-    rows = x_ref.shape[2] // 2
-    spans = (pl.ds(0, rows), pl.ds(rows, rows))
+    lanes = [(a, part, way) for a in range(count) for part in range(parts[a]) for way in range(2)]
     started = []
 
     def push(source, target, sems, index, to):
@@ -277,44 +280,65 @@
         started.append(copy)
         return copy
 
-    pairs, own = {}, {}
+    def spans(lane):
+        a, part, way = lane
+        half = xs[a].shape[2] // 2
+        rows = half // parts[a]
+        return pl.ds(part * rows, rows), pl.ds(way * half + part * rows, rows)
+
+    pairs, own, latest = {}, {}, {}
     for step in range(length):
-        for way in range(2):
+        for lane in lanes:
+            a, part, way = lane
+            near, wide = spans(lane)
             where = block(way, step)
-            pairs[way, step] = push(
-                x_ref.at[1 - core, where, spans[way]], twin.at[way, step], twin_sem, (way, step), peer
+            pairs[lane, step] = push(
+                xs[a].at[1 - core, where, wide],
+                twins[a].at[way, step, near],
+                twin_sem,
+                lane + (step,),
+                peer,
             )
-            own[way, step] = pltpu.make_async_copy(
-                x_ref.at[core, where, spans[way]], mine.at[way, step], own_sem.at[way, step]
+            own[lane, step] = pltpu.make_async_copy(
+                xs[a].at[core, where, wide], mines[a].at[way, step, near], own_sem.at[lane + (step,)]
             )
-            own[way, step].start()
-    latest = {}
+            own[lane, step].start()
     for step in range(length):
-        for way in range(2):
-            own[way, step].wait()
-            pairs[way, step].wait_recv()
-            total = mine[way, step].astype(jnp.float32) + twin[way, step].astype(jnp.float32)
+        for lane in lanes:
+            a, part, way = lane
+            near, wide = spans(lane)
+            own[lane, step].wait()
+            pairs[lane, step].wait_recv()
+            total = mines[a][way, step, near].astype(jnp.float32) + twins[a][
+                way, step, near
+            ].astype(jnp.float32)
             if step:
-                latest[way].wait_recv()
-                total = total + got[way, step - 1].astype(jnp.float32)
-            mine[way, step] = total.astype(mine.dtype)
+                latest[lane].wait_recv()
+                total = total + gots[a][way, step - 1, near].astype(jnp.float32)
+            mines[a][way, step, near] = total.astype(mines[a].dtype)
             if step < length - 1:
-                latest[way] = push(
-                    mine.at[way, step], got.at[way, step], ring_sem, (0, way, step), sides[way]
+                latest[lane] = push(
+                    mines[a].at[way, step, near],
+                    gots[a].at[way, step, near],
+                    ring_sem,
+                    (0,) + lane + (step,),
+                    sides[way],
                 )
     keep = []
     for step in range(length):
-        for way in range(2):
+        for lane in lanes:
+            a, part, way = lane
+            near, wide = spans(lane)
             if step:
-                latest[way].wait_recv()
-            where = lax.rem(pos - step + length, length) if way == 0 else lax.rem(pos + step, length)
-            target = out_ref.at[core, where, spans[way]]
-            source = target if step else mine.at[way, length - 1]
+                latest[lane].wait_recv()
+            where = lax.rem(pos - step + length if way == 0 else pos + step, length)
+            target = outs[a].at[core, where, wide]
+            source = target if step else mines[a].at[way, length - 1, near]
             if step < length - 1:
-                latest[way] = push(source, target, ring_sem, (1, way, step), sides[way])
-            pairs[way, step] = push(source, target, back_sem, (way, step), peer)
+                latest[lane] = push(source, target, ring_sem, (1,) + lane + (step,), sides[way])
+            pairs[lane, step] = push(source, target, back_sem, lane + (step,), peer)
             if step == 0:
-                copy = pltpu.make_async_copy(source, target, own_sem.at[way, 0])
+                copy = pltpu.make_async_copy(source, target, own_sem.at[lane + (0,)])
                 copy.start()
                 keep.append(copy)
     for copy in keep:
@@ -325,34 +349,99 @@
         copy.wait_send()
 
 
-def total_everywhere(rows_in, n, m, number):
+def total_everywhere(rows_in, small, n, m, number):
     chips = m // 2
     length = n * chips
     rows, cols = rows_in.shape
-    each = rows // (2 * length)
-    if m % 2 or rows % (2 * length * 32):
-        return lax.psum(rows_in, ("seq", "exp"))
-    x = rows_in.reshape(2, length, each, cols)
-    buf = pltpu.VMEM((2, length, each // 2, cols), x.dtype)
-    return pl.pallas_call(
-        functools.partial(total_kernel, n, chips),
-        out_shape=jax.ShapeDtypeStruct(x.shape, x.dtype),
-        in_specs=[ANY],
-        out_specs=ANY,
-        scratch_shapes=[
-            buf,
-            buf,
-            buf,
-            pltpu.SemaphoreType.DMA((2, length)),
-            pltpu.SemaphoreType.DMA((2, 2, length)),
-            pltpu.SemaphoreType.DMA((2, 2, 2, length)),
-            pltpu.SemaphoreType.DMA((2, 2, length)),
+    lanes_of = TILE * 8
+    parts = (3, 1)
+    if m % 2 or rows % (4 * length * parts[0] * 16) or small.size > 4 * length * lanes_of:
+        return lax.psum((rows_in, small), ("seq", "exp"))
+    padded = jnp.pad(small, (0, 4 * length * lanes_of - small.size))
+    arrays = [
+        rows_in.reshape(2, length, rows // (2 * length), cols),
+        padded.reshape(2, length, 16, TILE),
+    ]
+    bufs = [pltpu.VMEM((2, length, x.shape[2] // 2, x.shape[3]), x.dtype) for x in arrays]
+    sems = (len(arrays), max(parts), 2, length)
+    big, little = pl.pallas_call(
+        functools.partial(total_kernel, n, chips, parts),
+        out_shape=[jax.ShapeDtypeStruct(x.shape, x.dtype) for x in arrays],
+        in_specs=[ANY] * 2,
+        out_specs=[ANY] * 2,
+        scratch_shapes=bufs * 3
+        + [
+            pltpu.SemaphoreType.DMA(sems),
+            pltpu.SemaphoreType.DMA((2,) + sems),
+            pltpu.SemaphoreType.DMA((2, 2) + sems),
+            pltpu.SemaphoreType.DMA((2,) + sems),
         ],
         compiler_params=pltpu.CompilerParams(
             collective_id=number, has_side_effects=True, vmem_limit_bytes=58 << 20
         ),
         name="total_everywhere",
-    )(x).reshape(rows, cols)
+    )(*arrays)
+    return big.reshape(rows, cols), little.reshape(-1)[: small.size]
+
+
+QUAD = 4
+
+
+def quad_moves(n):
+    ring = (0, 1, 3, 2)
+    step = lambda i, by: i - i % QUAD + ring[(ring.index(i % QUAD) + by) % QUAD]
+    return [(i, step(i, 1)) for i in range(n)], [(i, step(i, -1)) for i in range(n)]
+
+
+def spread_kernel(n, m, back, x_ref, out_ref, own_sem, send_sem, recv_sem):
+    seq, exp = lax.axis_index("seq"), lax.axis_index("exp")
+    groups = n // QUAD
+    moves = [(g, k) for g in reversed(range(groups)) for k in range(m) if g or k]
+
+    def target(g, k):
+        shift = n - g * QUAD if back else g * QUAD
+        return lax.rem(seq + shift, n), lax.rem(exp + k, m)
+
+    greet([dict(zip(("seq", "exp"), target(g, k))) for g, k in moves])
+    started = []
+    for g, k in moves:
+        to_seq, to_exp = target(g, k)
+        copy = pltpu.make_async_remote_copy(
+            src_ref=x_ref.at[g, to_exp] if back else x_ref.at[to_exp],
+            dst_ref=out_ref.at[g, exp],
+            send_sem=send_sem.at[g, k],
+            recv_sem=recv_sem.at[g, k],
+            device_id={"seq": to_seq, "exp": to_exp},
+            device_id_type=MESH,
+        )
+        copy.start()
+        started.append(copy)
+    own = pltpu.make_async_copy(
+        x_ref.at[0, exp] if back else x_ref.at[exp], out_ref.at[0, exp], own_sem
+    )
+    own.start()
+    for copy in started:
+        copy.wait_recv()
+    for copy in started:
+        copy.wait_send()
+    own.wait()
+
+
+def spread(x, n, m, back, number):
+    groups = n // QUAD
+    return pl.pallas_call(
+        functools.partial(spread_kernel, n, m, back),
+        out_shape=jax.ShapeDtypeStruct((groups,) + x.shape[-3:], x.dtype),
+        in_specs=[ANY],
+        out_specs=ANY,
+        scratch_shapes=[
+            pltpu.SemaphoreType.DMA,
+            pltpu.SemaphoreType.DMA((groups, m)),
+            pltpu.SemaphoreType.DMA((groups, m)),
+        ],
+        compiler_params=pltpu.CompilerParams(collective_id=number, has_side_effects=True),
+        name="spread_back" if back else "spread",
+    )(x)
 
 
 def dot_last(a, b):
@@ -392,6 +481,16 @@
     return jnp.concatenate(rows, axis=0)
 
 
+def edge_bias(tile_ref, rows):
+    edge = []
+    for h in range(2):
+        first = jnp.concatenate(
+            [jnp.zeros((rows - TILE, TILE), jnp.float32), tile_ref[h][:, :TILE].T], axis=0
+        )
+        edge += [first, jnp.zeros((rows, rows - TILE), jnp.float32)]
+    return jnp.concatenate(edge, axis=1)
+
+
 def attend_kernel(causal, block, s_ref, q_ref, k_ref, v_ref, *refs):
     if causal:
         tile_ref, low_ref, wide_ref, lse_ref, acc_ref, top_ref = refs
@@ -399,46 +498,39 @@
         low_ref, wide_ref, lse_ref, acc_ref, top_ref = refs
     rows = q_ref.shape[0]
     both = split_heads(q_ref[...])
-    masks = head_masks(v_ref.dtype)
+    ones = jnp.ones((16, block), v_ref.dtype)
 
     def visit(start, bias, first):
         keys = k_ref[pl.ds(start, block), :]
         values = v_ref[pl.ds(start, block), :]
-        t = dot_last(both, keys) * (scale_factor * log2e)
+        t = dot_last(keys, both) * (scale_factor * log2e)
         if bias is not None:
             t = t + bias
-        top = jnp.max(t, axis=1, keepdims=True)
+        top = jnp.max(t, axis=0, keepdims=True)
         if not first:
             before = top_ref[...]
             top = jnp.maximum(before, top)
             fade = jnp.exp2(before - top)
         top_ref[...] = top
         p = jnp.exp2(t - top).astype(values.dtype)
-        for h in range(2):
-            part = dot_plain(p[h * rows : (h + 1) * rows], values * masks[h] + masks[1 - h])
-            if first:
-                acc_ref[h] = part
-            else:
-                acc_ref[h] = acc_ref[h] * fade[h * rows : (h + 1) * rows] + part
+        part = dot_plain(jnp.concatenate([values.T, ones], axis=0), p)
+        if first:
+            acc_ref[...] = part
+        else:
+            acc_ref[...] = acc_ref[...] * fade + part
 
     if causal:
         s = s_ref[0]
         count = rows // TILE
         visit(
             pl.multiple_of(s * block, block),
-            jnp.concatenate([own_bias(tile_ref[h], count) for h in range(2)], axis=0),
+            jnp.concatenate([own_bias(tile_ref[h], count).T for h in range(2)], axis=1),
             True,
         )
 
         @pl.when(s > 0)
         def _():
-            edge = []
-            for h in range(2):
-                top_row = jnp.concatenate(
-                    [jnp.zeros((TILE, rows - TILE), jnp.float32), tile_ref[h][:, :TILE]], axis=1
-                )
-                edge += [top_row, jnp.zeros((rows - TILE, rows), jnp.float32)]
-            visit(pl.multiple_of((s - 1) * block, block), jnp.concatenate(edge, axis=0), False)
+            visit(pl.multiple_of((s - 1) * block, block), edge_bias(tile_ref, rows), False)
 
         def far(j, carry):
             visit(pl.multiple_of(j * block, block), None, False)
@@ -448,19 +540,18 @@
     else:
         for j in range(k_ref.shape[0] // block):
             visit(j * block, None, j == 0)
-    low = lax.broadcasted_iota(jnp.int32, (rows, TILE), 1) < HEAD_DIM
-    acc0, acc1 = acc_ref[0], acc_ref[1]
-    wide = jnp.where(
-        low,
-        acc0 / pltpu.roll(acc0, HEAD_DIM, 1),
-        acc1 / pltpu.roll(acc1, HEAD_DIM, 1),
-    )
+    sums = acc_ref[TILE : TILE + 1, :]
+    wide = jnp.concatenate(
+        [
+            acc_ref[:HEAD_DIM, :rows] / sums[:, :rows],
+            acc_ref[HEAD_DIM:TILE, rows:] / sums[:, rows:],
+        ],
+        axis=0,
+    ).T
     wide_ref[...] = wide
     low_ref[...] = wide.astype(low_ref.dtype)
-    lse0 = top_ref[:rows] + jnp.log2(acc0[:, HEAD_DIM : HEAD_DIM + 1])
-    lse1 = top_ref[rows:] + jnp.log2(acc1[:, :1])
-    turned = jnp.where(low, lse0, lse1).T
-    lse_ref[0] = jnp.concatenate([turned[:1], turned[HEAD_DIM : HEAD_DIM + 1]], axis=0)
+    lse = top_ref[...] + jnp.log2(sums)
+    lse_ref[0] = jnp.concatenate([lse[:, :rows], lse[:, rows:]], axis=0)
 
 
 def attend(seq_at, queries, keys, values, tiles):
@@ -483,8 +574,8 @@
         in_specs=[SMEM, pair, long, long] + specs,
         out_specs=[pair, pair, pl.BlockSpec((1, 2, rows), lambda g: (g, 0, 0))],
         scratch_shapes=[
-            pltpu.VMEM((2, rows, TILE), jnp.float32),
-            pltpu.VMEM((2 * rows, 1), jnp.float32),
+            pltpu.VMEM((TILE + 16, 2 * rows), jnp.float32),
+            pltpu.VMEM((1, 2 * rows), jnp.float32),
         ],
         compiler_params=pltpu.CompilerParams(vmem_limit_bytes=48 << 20),
         name="attend_self" if causal else "attend_cross",
@@ -550,13 +641,7 @@
 
         @pl.when(s > 0)
         def _():
-            edge = []
-            for h in range(2):
-                first_rows = jnp.concatenate(
-                    [jnp.zeros((rows - TILE, TILE), jnp.float32), tile_ref[h][:, :TILE].T], axis=0
-                )
-                edge += [first_rows, jnp.zeros((rows, rows - TILE), jnp.float32)]
-            ds = visit(pl.multiple_of((s - 1) * block, block), jnp.concatenate(edge, axis=1), False)
+            ds = visit(pl.multiple_of((s - 1) * block, block), edge_bias(tile_ref, rows), False)
             for h in range(2):
                 near_ref[h, :TILE] += ds[rows - TILE :, h * rows : h * rows + TILE].astype(
                     jnp.float32
@@ -651,49 +736,51 @@
     return table + jnp.where(last, far[None, :], 0.0)
 
 
-def expert_kernel(rows_ref, in_ref, out_ref, part_ref, gin_ref, gout_ref):
-    tokens = rows_ref[0, :, :D]
-    upstream = rows_ref[0, :, D:]
-    up_map, down_map = in_ref[0], out_ref[0]
-    u = dot_plain(tokens, up_map)
-    square = u * u
+def expert_kernel(*refs):
+    rows_ref, maps = refs[0], refs[1 : 1 + 2 * QUAD]
+    part_ref, grads = refs[1 + 2 * QUAD], refs[2 + 2 * QUAD :]
+    shape = rows_ref.shape
+    rows = rows_ref[...].reshape(shape[0] * shape[1] * shape[2], shape[3])
+    tokens, upstream = rows[:, :D], rows[:, D:]
     slope = math.sqrt(2.0 / math.pi)
-    bend = jnp.tanh(slope * (u + 0.044715 * (square * u)))
-    half = 0.5 * (1.0 + bend)
-    act = (u * half).astype(tokens.dtype)
-    rise = half + 0.5 * u * (1.0 - bend * bend) * (slope * (1.0 + 3 * 0.044715 * square))
-    du = (dot_plain(upstream, down_map) * rise).astype(tokens.dtype)
-    part_ref[0, :, :D] = dot_last(act, down_map).astype(part_ref.dtype)
-    part_ref[0, :, D:] = dot_last(du, up_map).astype(part_ref.dtype)
-    gin, gout = dot_first(tokens, du), dot_first(upstream, act)
-
-    @pl.when(pl.program_id(1) == 0)
-    def _():
-        gin_ref[0] = gin
-        gout_ref[0] = gout
-
-    @pl.when(pl.program_id(1) > 0)
-    def _():
-        gin_ref[0] += gin
-        gout_ref[0] += gout
-
-
-def run_experts(gathered, expert_in, expert_out):
-    n, rows, width = gathered.shape
-    count, _, hidden = expert_in.shape
-    each = rows // count
-    block = pl.BlockSpec((1, each, width), lambda e, s: (s, e, 0))
-    weight = pl.BlockSpec((1, D, hidden), lambda e, s: (e, 0, 0))
-    grad = jax.ShapeDtypeStruct(expert_in.shape, jnp.float32)
+    result = back = None
+    for j in range(QUAD):
+        up_map, down_map = maps[2 * j][0], maps[2 * j + 1][0]
+        u = dot_plain(tokens, up_map)
+        square = u * u
+        bend = jnp.tanh(slope * (u + 0.044715 * (square * u)))
+        half = 0.5 * (1.0 + bend)
+        act = (u * half).astype(tokens.dtype)
+        rise = half + 0.5 * u * (1.0 - bend * bend) * (slope * (1.0 + 3 * 0.044715 * square))
+        du = (dot_plain(upstream, down_map) * rise).astype(tokens.dtype)
+        y, dn = dot_last(act, down_map), dot_last(du, up_map)
+        result = y if result is None else result + y
+        back = dn if back is None else back + dn
+        for ref, left, right in ((grads[2 * j], tokens, du), (grads[2 * j + 1], upstream, act)):
+            ref[0] = dot_first(left, right).astype(ref.dtype)
+    part_ref[...] = (
+        jnp.concatenate([result, back], axis=1).astype(part_ref.dtype).reshape(part_ref.shape)
+    )
+
+
+def run_experts(rows, maps):
+    groups, m, slots, width = rows.shape
+    count, _, hidden = maps[0].shape
+    block = pl.BlockSpec((groups, m, slots // count, width), lambda e: (0, 0, e, 0))
+    weight = pl.BlockSpec((1, D, hidden), lambda e: (e, 0, 0))
     return pl.pallas_call(
         expert_kernel,
-        grid=(count, n),
-        out_shape=[jax.ShapeDtypeStruct(gathered.shape, gathered.dtype), grad, grad],
-        in_specs=[block, weight, weight],
-        out_specs=[block, weight, weight],
-        compiler_params=pltpu.CompilerParams(vmem_limit_bytes=48 << 20),
+        grid=(count,),
+        out_shape=[jax.ShapeDtypeStruct(rows.shape, rows.dtype)]
+        + [
+            jax.ShapeDtypeStruct(w.shape, jnp.float32 if i < 2 else jnp.bfloat16)
+            for i, w in enumerate(maps)
+        ],
+        in_specs=[block] + [weight] * len(maps),
+        out_specs=[block] + [weight] * len(maps),
+        compiler_params=pltpu.CompilerParams(vmem_limit_bytes=58 << 20),
         name="run_experts",
-    )(gathered, expert_in, expert_out)
+    )(rows, *maps)
 
 
 def project(source, matrix):
@@ -735,6 +822,13 @@
     tiles = bias_tiles(rel_bias)
 
     normed_all, memory_all = ring_gather([normed_self, memory_rows], n, 1)
+    to_next, to_last = quad_moves(n)
+    in_own, out_own, normed_all = lax.optimization_barrier((expert_in, expert_out, normed_all))
+    in_last, out_last = (lax.ppermute(w, "seq", to_next) for w in (in_own, out_own))
+    in_next, out_next = (lax.ppermute(w, "seq", to_last) for w in (in_own, out_own))
+    in_far = lax.ppermute(in_last, "seq", to_next)
+    out_far = lax.ppermute(out_next, "seq", to_last)
+    maps = [in_own, out_own, in_last, out_last, in_next, out_next, in_far, out_far]
     normed_all = normed_all.reshape(n * token_count, D)
     memory_all = memory_all.reshape(n * memory_count, D)
     queries = project(normed_self, proj_in[0])
@@ -773,9 +867,10 @@
     gate_prob = jnp.sum(softmax_probs * onehot, axis=-1)
     slot_index = jnp.sum(jnp.cumsum(onehot_int, axis=0) * onehot_int, axis=-1) - 1
     is_kept = slot_index < capacity
-    place = jnp.where(is_kept, chosen * capacity + slot_index, -1)
+    slots = -(-capacity // 16) * 16
+    place = jnp.where(is_kept, chosen * slots + slot_index, -1)
     dispatch = (
-        place[:, None] == jnp.arange(expert_count * capacity, dtype=jnp.int32)[None, :]
+        place[:, None] == jnp.arange(expert_count * slots, dtype=jnp.int32)[None, :]
     ).astype(jnp.bfloat16)
     dispatched = jnp.sum(onehot_int * is_kept[:, None].astype(jnp.int32), axis=0)
     tally_counts = jnp.stack(
@@ -792,19 +887,20 @@
             preferred_element_type=jnp.float32,
         )
         .astype(jnp.bfloat16)
-        .reshape(expert_count, capacity, 2 * D)
-    )
-    received = lax.all_to_all(sent_rows, "exp", split_axis=0, concat_axis=1, tiled=True)
-    (gathered,) = ring_gather([received.reshape(local_experts * m * capacity, 2 * D)], n, 2)
-    parts, grad_expert_in, grad_expert_out = run_experts(gathered, expert_in, expert_out)
-    (summed,) = ring_scatter([parts], n, 3, jnp.bfloat16)
-    returned = lax.all_to_all(
-        summed.reshape(local_experts, m * capacity, 2 * D),
-        "exp",
-        split_axis=1,
-        concat_axis=0,
-        tiled=True,
-    ).reshape(expert_count * capacity, 2 * D)
+        .reshape(m, local_experts * slots, 2 * D)
+    )
+    received = spread(sent_rows, n, m, False, 2)
+    parts, *terms = run_experts(received, maps)
+    returned = spread(parts, n, m, True, 3)
+    returned = jnp.sum(returned.astype(jnp.float32), axis=0).astype(jnp.bfloat16)
+    returned = returned.reshape(expert_count * slots, 2 * D)
+    gin_own, gout_own, gin_last, gout_last, gin_next, gout_next, gin_far, gout_far = terms
+    gin_next = gin_next + lax.ppermute(gin_far, "seq", to_next)
+    gout_last = gout_last + lax.ppermute(gout_far, "seq", to_last)
+    gin_next, gout_next = (lax.ppermute(w, "seq", to_next) for w in (gin_next, gout_next))
+    gin_last, gout_last = (lax.ppermute(w, "seq", to_last) for w in (gin_last, gout_last))
+    grad_expert_in = gin_own + gin_last.astype(jnp.float32) + gin_next.astype(jnp.float32)
+    grad_expert_out = gout_own + gout_last.astype(jnp.float32) + gout_next.astype(jnp.float32)
     routed = jnp.dot(dispatch, returned, preferred_element_type=jnp.float32)
     combined, grad_mixed = routed[:, :D], routed[:, D:]
     output = (after_cross + gate_prob[:, None] * combined).astype(jnp.bfloat16)
@@ -884,12 +980,15 @@
             grad_out_cross,
         ]
     )
-    grads = total_everywhere(grads.reshape(-1, D), n, m, 5).reshape(-1, D, D).astype(jnp.float32)
     grad_gains = jnp.stack([grad_gain_self, grad_gain_cross, grad_gain_mix])
-    small = lax.psum(
+    grads, small = total_everywhere(
+        grads.reshape(-1, D),
         jnp.concatenate([grad_gains.reshape(-1), grad_table.reshape(-1), grad_router.reshape(-1)]),
-        ("seq", "exp"),
-    )
+        n,
+        m,
+        5,
+    )
+    grads = grads.reshape(-1, D, D).astype(jnp.float32)
     ends = (grad_gains.size, grad_gains.size + grad_table.size)
     return (
         output.reshape(1, token_count, D),

time: 942 us -> 795 us (0.84)
  Pallas kernels: 687 us -> 578 us
  blocking collectives: 40 us -> 0 us
  local copies, waits for them, and re-layouts: 50.4 us -> 35 us
  waiting for transfers between devices: 36.2 us -> 20.9 us
  other arithmetic: 22.6 us -> 36.8 us
  starting transfers between devices: 12.5 us -> 22.5 us
    pallas_call x2 -> x4, Pallas kernels: 191 us -> 322 us  [the longest x1 153 us: total_everywhere(): pl.pallas_call(functools.partial(total_kernel, n, chips, parts), out_shap...]
    pallas_call x2 -> x1, Pallas kernels: 183 us -> 62 us  [ring_gather(): pl.pallas_call(functools.partial(gather_kernel, n, parts, count), out_sha...]
    pallas_call x2 -> x1, Pallas kernels: 182 us -> 91.1 us  [ring_scatter(): pl.pallas_call(functools.partial(scatter_kernel, n, parts, count), out_sh...]
    psum x1 -> x0, blocking collectives: 40 us -> none  [body(): lax.psum(jnp.concatenate([grad_gains.reshape(-1), grad_table.reshape(-1),...]
    all_to_all x2 -> x0, waiting for transfers between devices: 36.2 us -> none  [the longest x1 19 us: body(): lax.all_to_all(sent_rows, 'exp', split_axis=0, concat_axis=1, tiled=True)]
    pallas_call x2, Pallas kernels: 72.6 us -> 45.1 us  [attend(): pl.pallas_call(functools.partial(attend_kernel, causal, block), grid=(PAI...]
    ppermute x0 -> x12, starting transfers between devices: none -> 22.5 us  [the longest x1 11.2 us: body(): gout_last = gout_last + lax.ppermute(gout_far, 'seq', to_last)]
    ppermute x0 -> x12, waiting for transfers between devices: none -> 20.9 us  [the longest x4 15.1 us: body(): lax.ppermute(w, 'seq', to_last)]
  transfers between devices with their start and end apart: 2 -> 12, of which waited for: 2 -> 2; matrix products, arithmetic and copies ran while one was open for 0% -> 17% of each run, Pallas kernels for 0% -> 46%
where the time goes in v2:
time: 795 us; the launch traced here: 786 us
  Pallas kernels  578 us (73%)
  matrix products  90.8 us (11%)
  other arithmetic  36.8 us (5%)
  local copies, waits for them, and re-layouts  35 us (4%)
  starting transfers between devices  22.5 us (3%)
  waiting for transfers between devices  20.9 us (3%)
    pallas_call x1, Pallas kernels, total_everywhere(): pl.pallas_call(functools.partial(total_kernel, n, chips, parts), out_shap...  153 us
    pallas_call x2, Pallas kernels, spread(): pl.pallas_call(functools.partial(spread_kernel, n, m, back), out_shape=ja...  141 us
    pallas_call x1, Pallas kernels, ring_scatter(): pl.pallas_call(functools.partial(scatter_kernel, n, parts, count), out_sh...  91.1 us
    pallas_call x1, Pallas kernels, ring_gather(): pl.pallas_call(functools.partial(gather_kernel, n, parts, count), out_sha...  62 us
    pallas_call x2, Pallas kernels, attend_back(): pl.pallas_call(functools.partial(attend_back_kernel, causal, block), grid...  57.5 us
    pallas_call x2, Pallas kernels, attend(): pl.pallas_call(functools.partial(attend_kernel, causal, block), grid=(PAI...  45.1 us
    dot_general x8, matrix products, weight_grad(): jnp.einsum('td,te->de', source, upstream, preferred_element_type=jnp.floa...  30.2 us
    pallas_call x1, Pallas kernels, run_experts(): pl.pallas_call(expert_kernel, grid=(count,), out_shape=[jax.ShapeDtypeStr...  28.3 us
  transfers between devices with their start and end apart: 12, of which 2 were waited for; matrix products, arithmetic and copies ran while one was open for 17% of the time, Pallas kernels for 46%

profile of v2, /device:TPU:25, one launch (start us, length us, event | category | flops | bytes accessed | tf_op | source)
XLA Modules:
  0.0 786.0 jit_solution(12020933080283056636)
XLA Ops:
  5.4 62.0 %ring_gather.1 = (bf16[8,384,768]{2,1,0:T(8,128)(2,1)}, bf16[8,128,768]{2,1,0:T(8,128)(2,1)}) custom-call(bf16[384,768]{1,0:T(8,128)(2,1)} %fusion.25.refs_0_, bf16[128,768]{1,0:T(8,128)(2,1)} %bitcast.273), custom_call_target="tpu_custom_call" | custom-call | tf_op jit(solution)/shard_map/ring_gather/pallas_call | solution.py:146
  72.7 9.2 %convolution_convert_fusion.v_ref = bf16[3072,768]{1,0:T(8,128)(2,1)} fusion(bf16[3072,768]{1,0:T(8,128)(2,1)} %bitcast.281, bf16[6,768,768]{2,1,0:T(8,128)(2,1)} %param.13), kind=kOutput, calls=%fused_computation.1 | convolution fusion | flops 3626237952 | bytes 10616832 | tf_op jit(solution)/shard_map/dot_general | solution.py:787
  81.9 5.7 convolution_convert_fusion.1.k_ref
  94.5 7.5 select_select_fusion.refs_0_
  103.0 34.7 %attend_self.1 = (bf16[384,768]{1,0:T(8,128)(2,1)S(1)}, f32[384,768]{1,0:T(8,128)S(1)}, f32[6,2,384]{2,1,0:T(2,128)S(1)}) custom-call(s32[1]{0:T(128)} %bitcast.1.s_ref, bf16[384,768]{1,0:T(8,128)(2,1)S(1)} %copy-done.4, bf16[3072,768]{1,0:T(8,128)(2,1)} %convolution_convert_fusion.1.k_ref, bf16[3072,768]{1,0:T(8,128)(2,1)} %convolution_convert_fusion.v_ref, ...), custom_call_target="tpu_custom_call" | custom-call | tf_op jit(solution)/shard_map/attend_self/pallas_call | solution.py:566
  141.4 10.4 %attend_cross.1 = (bf16[384,768]{1,0:T(8,128)(2,1)S(1)}, f32[384,768]{1,0:T(8,128)S(1)}, f32[6,2,384]{2,1,0:T(2,128)S(1)}) custom-call(s32[1]{0:T(128)} %bitcast.1.s_ref, bf16[384,768]{1,0:T(8,128)(2,1)S(1)} %convolution_convert_fusion.15.q_ref, bf16[1024,768]{1,0:T(8,128)(2,1)S(1)} %copy-done.3, bf16[1024,768]{1,0:T(8,128)(2,1)S(1)} %convolution_convert_fusion.3.v_ref), custom_call_target="tpu_custom_call" | custom-call | tf_op jit(solution)/shard_map/attend_cross/pallas_call | solution.py:566
  158.6 5.9 collective-permute-start.5
  164.5 72.7 %spread.1.refs_0_ = bf16[2,4,128,1536]{3,2,1,0:T(8,128)(2,1)} custom-call(bf16[4,128,1536]{2,1,0:T(8,128)(2,1)} %bitcast.268), custom_call_target="tpu_custom_call" | custom-call | tf_op jit(solution)/shard_map/spread/pallas_call | solution.py:432
  238.2 28.3 %run_experts.1 = (bf16[2,4,128,1536]{3,2,1,0:T(8,128)(2,1)}, f32[2,768,384]{2,1,0:T(8,128)}, f32[2,768,384]{2,1,0:T(8,128)}, bf16[2,768,384]{2,1,0:T(8,128)(2,1)...) custom-call(bf16[2,4,128,1536]{3,2,1,0:T(8,128)(2,1)} %spread.1.refs, ...), custom_call_target="tpu_custom_call" | custom-call | tf_op jit(solution)/shard_map/run_experts/pallas_call | solution.py:771
  266.5 68.2 %spread_back.1 = bf16[2,4,128,1536]{3,2,1,0:T(8,128)(2,1)} custom-call(bf16[2,4,128,1536]{3,2,1,0:T(8,128)(2,1)} %get-tuple-element.50.x_ref), custom_call_target="tpu_custom_call" | custom-call | tf_op jit(solution)/shard_map/spread_back/pallas_call | solution.py:432
  334.7 4.1 reduce_sum.176
  346.8 15.1 %attend_cross_back.1 = (bf16[384,768]{1,0:T(8,128)(2,1)S(1)}, bf16[1024,768]{1,0:T(8,128)(2,1)S(1)}, bf16[1024,768]{1,0:T(8,128)(2,1)S(1)}) custom-call(s32[1]{0:T(128)} %bitcast.1.s_ref, bf16[384,768]{1,0:T(8,128)(2,1)S(1)} %copy-done.9, bf16[1024,768]{1,0:T(8,128)(2,1)} %convolution_convert_fusion.4.k_ref, bf16[1024,768]{1,0:T(8,128)(2,1)} %copy-done.2, ...), custom_call_target="tpu_custom_call" | custom-call | tf_op jit(solution)/shard_map/attend_cross_back/pallas_call | solution.py:688
  362.0 3.0 multiply_reduce_fusion.1
  367.2 42.4 %attend_self_back.1 = (bf16[384,768]{1,0:T(8,128)(2,1)S(1)}, bf16[3072,768]{1,0:T(8,128)(2,1)}, bf16[3072,768]{1,0:T(8,128)(2,1)}, f32[12,256,128]{2,1,0:T(8,128)S(1)}, f32[6,2,384]{2,1,0:T(2,128)S(1)}) custom-call(s32[1]{0:T(128)} %bitcast.1.s_ref, bf16[384,768]{1,0:T(8,128)(2,1)S(1)} %copy-done.5, bf16[3072,768]{1,0:T(8,128)(2,1)} %convolution_convert_fusion.1.k_ref, ...), custom_call_target="tpu_custom_call" | custom-call | tf_op jit(solution)/shard_map/attend_self_back/pallas_call | solution.py:688
  413.0 11.2 %collective-permute-start.9 = (bf16[2,768,384]{2,1,0:T(8,128)(2,1)}, bf16[2,768,384]{2,1,0:T(8,128)(2,1)}, u32[]{:S(2)}, u32[]{:S(2)}) collective-permute-start(bf16[2,768,384]{2,1,0:T(8,128)(2,1)} %get-tuple-element.73), channel_id=1, source_target_pairs={{0,8},{4,0},{8,12},{12,4},{16,24},{20,16},{24,28},{28,20},{1,9},{5... | collective-permute-start | bytes 3538952 | tf_op jit(solution)/shard_map/ppermute | solution.py:899
  424.6 2.8 fusion.43
  428.1 6.3 fusion.53
  436.3 2.7 add_convert_fusion.1
  438.9 8.0 %add_convert_fusion = bf16[3072,768]{1,0:T(8,128)(2,1)} fusion(f32[3072,768]{1,0:T(8,128)} %fusion.53, bf16[3072,768]{1,0:T(8,128)(2,1)S(1)} %bitcast.288, bf16[6,768,768]{2,1,0:T(8,128)(2,1)S(1)} %bitcast.280), kind=kOutput, calls=%fused_computation | convolution fusion | flops 3628597248 | bytes 20054016 | tf_op jit(solution)/shard_map/te,de->td/dot_general | solution.py:797
  446.9 91.1 %ring_scatter.1 = (f32[384,768]{1,0:T(8,128)}, f32[128,768]{1,0:T(8,128)}) custom-call(bf16[8,384,768]{2,1,0:T(8,128)(2,1)} %bitcast.267, bf16[8,128,768]{2,1,0:T(8,128)(2,1)} %bitcast.269), custom_call_target="tpu_custom_call" | custom-call | tf_op jit(solution)/shard_map/ring_scatter/pallas_call | solution.py:228
  538.1 3.4 fusion.26
  541.8 2.8 copy.28
  547.3 8.7 %fusion.22 = bf16[8,768,768]{2,1,0:T(8,128)(2,1)} fusion(bf16[8,768,768]{2,1,0:T(8,128)(2,1)} %fusion.14, bf16[3072,768]{1,0:T(8,128)(2,1)} %bitcast.282, bf16[3072,768]{1,0:T(8,128)(2,1)} %get-tuple-element.57), kind=kOutput, calls=%fused_computation.52 | convolution fusion | flops 3624468480 | bytes 10616832 | tf_op jit(solution)/shard_map/td,te->de/dot_general | solution.py:791
  556.0 9.0 %fusion.24 = bf16[8,768,768]{2,1,0:T(8,128)(2,1)} fusion(bf16[8,768,768]{2,1,0:T(8,128)(2,1)} %fusion.22, bf16[3072,768]{1,0:T(8,128)(2,1)} %bitcast.283, bf16[3072,768]{1,0:T(8,128)(2,1)} %get-tuple-element.58), kind=kOutput, calls=%fused_computation.54 | convolution fusion | flops 3624468480 | bytes 10616832 | tf_op jit(solution)/shard_map/td,te->de/dot_general | solution.py:791
  572.6 2.7 add.447
  579.7 153.3 %total_everywhere.1 = (bf16[2,16,192,768]{3,2,1,0:T(8,128)(2,1)}, f32[2,16,16,128]{3,2,1,0:T(8,128)}) custom-call(bf16[2,16,192,768]{3,2,1,0:T(8,128)(2,1)} %bitcast.263, f32[2,16,16,128]{3,2,1,0:T(8,128)} %bitcast.270), custom_call_target="tpu_custom_call" | custom-call | tf_op jit(solution)/shard_map/total_everywhere/pallas_call | solution.py:367
  733.0 9.7 %slice.269 = f32[6,768,768]{2,1,0:T(8,128)} slice(bf16[8,768,768]{2,1,0:T(8,128)(2,1)} %bitcast.261), slice={[0:6], [0:768], [0:768]} | slice | bytes 28311552 | tf_op jit(solution)/shard_map/slice | solution.py:997
  745.3 3.6 slice.229
  758.2 3.6 convert_add_fusion
  761.8 15.1 %collective-permute-done.6 = bf16[2,768,384]{2,1,0:T(8,128)(2,1)} collective-permute-done((bf16[2,768,384]{2,1,0:T(8,128)(2,1)}, bf16[2,768,384]{2,1,0:T(8,128)(2,1)}, u32[]{:S(2)}, u32[]{:S(2)}) %collective-permute-start.6) | collective-permute-done | bytes 1179680 | tf_op jit(solution)/shard_map/ppermute | solution.py:901
  776.9 5.8 collective-permute-done.8
  782.7 3.1 convert_add_fusion.1
  (245 shorter events, 72.3 us)
Async XLA Ops:
  0.6 154.0 %copy-start = (bf16[768,8]{0,1:T(8,128)(2,1)S(1)}, bf16[768,8]{0,1:T(8,128)(2,1)}, u32[]{:S(2)}) copy-start(bf16[768,8]{0,1:T(8,128)(2,1)} %param.17) | copy-start | bytes 36868
  0.7 69.7 %copy-start.50 = (f32[32,12]{0,1:T(8,128)S(1)}, f32[32,12]{0,1:T(8,128)}, u32[]{:S(2)}) copy-start(f32[32,12]{0,1:T(8,128)} %param.16) | copy-start | bytes 4612
  2.0 85.6 %copy-start.48 = (f32[768]{0:T(1024)}, f32[768]{0:T(1024)S(1)}, u32[]{:S(2)}) copy-start(f32[768]{0:T(1024)S(1)} %get-tuple-element.94) | copy-start | bytes 9220
  3.3 78.6 %copy-start.53 = (f32[384]{0:T(512)}, f32[384]{0:T(512)S(1)}, u32[]{:S(2)}) copy-start(f32[384]{0:T(512)S(1)} %fusion.27) | copy-start | bytes 4612
  3.3 84.3 %copy-start.51 = (f32[384]{0:T(512)}, f32[384]{0:T(512)S(1)}, u32[]{:S(2)}) copy-start(f32[384]{0:T(512)S(1)} %fusion.169) | copy-start | bytes 4612
  67.4 91.2 %collective-permute-start.3 = (bf16[2,768,384]{2,1,0:T(8,128)(2,1)}, bf16[2,768,384]{2,1,0:T(8,128)(2,1)}, u32[]{:S(2)}, u32[]{:S(2)}) collective-permute-start(bf16[2,768,384]{2,1,0:T(8,128)(2,1)} %refs_2_), channel_id=1, source_target_pairs={{0,8},{4,0},{8,12},{12,4},{16,24},{20,16},{24,28},{28,20},{1,9},{5... | collective-permute-start | bytes 3538952 | tf_op jit(solution)/shard_map/ppermute | solution.py:828
  68.7 169.5 %collective-permute-start.1 = (bf16[2,768,384]{2,1,0:T(8,128)(2,1)}, bf16[2,768,384]{2,1,0:T(8,128)(2,1)}, u32[]{:S(2)}, u32[]{:S(2)}) collective-permute-start(bf16[2,768,384]{2,1,0:T(8,128)(2,1)} %refs_2_), channel_id=1, source_target_pairs={{0,4},{4,12},{8,0},{12,8},{16,20},{20,28},{24,16},{28,24},{1,5},{5... | collective-permute-start | bytes 3538952 | tf_op jit(solution)/shard_map/ppermute | solution.py:827
  68.9 89.7 %collective-permute-start = (bf16[2,768,384]{2,1,0:T(8,128)(2,1)}, bf16[2,768,384]{2,1,0:T(8,128)(2,1)}, u32[]{:S(2)}, u32[]{:S(2)}) collective-permute-start(bf16[2,768,384]{2,1,0:T(8,128)(2,1)} %refs_1_), channel_id=1, source_target_pairs={{0,4},{4,12},{8,0},{12,8},{16,20},{20,28},{24,16},{28,24},{1,5},{5... | collective-permute-start | bytes 3538952 | tf_op jit(solution)/shard_map/ppermute | solution.py:827
  70.1 168.1 %collective-permute-start.2 = (bf16[2,768,384]{2,1,0:T(8,128)(2,1)}, bf16[2,768,384]{2,1,0:T(8,128)(2,1)}, u32[]{:S(2)}, u32[]{:S(2)}) collective-permute-start(bf16[2,768,384]{2,1,0:T(8,128)(2,1)} %refs_1_), channel_id=1, source_target_pairs={{0,8},{4,0},{8,12},{12,4},{16,24},{20,16},{24,28},{28,20},{1,9},{5... | collective-permute-start | bytes 3538952 | tf_op jit(solution)/shard_map/ppermute | solution.py:828
  70.4 22.7 %copy-start.56 = (s32[128]{0:T(128)}, s32[128]{0:T(128)S(1)}, u32[]{:S(2)}) copy-start(s32[128]{0:T(128)S(1)} %iota_add_fusion) | copy-start | bytes 1540
  70.6 11.2 %slice-start.4 = ((s8[4718592]{0:T(1024)(128)(4,1)}), s8[4194304]{0:T(1024)(128)(4,1)S(1)}, s32[]{:S(2)}) async-start(s8[4718592]{0:T(1024)(128)(4,1)} %bitcast.284), calls=%async_computation.4 | async-start | bytes 8388608
  90.5 50.9 %copy-start.2 = (bf16[1024,768]{1,0:T(8,128)(2,1)}, bf16[1024,768]{1,0:T(8,128)(2,1)S(1)}, u32[]{:S(2)}) copy-start(bf16[1024,768]{1,0:T(8,128)(2,1)S(1)} %convolution_convert_fusion.3.v_ref) | copy-start | bytes 4718596
  103.0 34.7 %copy-start.31 = (bf16[1,384,768]{2,1,0:T(8,128)(2,1)S(1)}, bf16[1,384,768]{2,1,0:T(8,128)(2,1)}, u32[]{:S(2)}) copy-start(bf16[1,384,768]{2,1,0:T(8,128)(2,1)} %param.11) | copy-start | bytes 1769476
  103.0 34.7 %copy-start.33 = (bf16[2,768,768]{2,1,0:T(8,128)(2,1)S(1)}, bf16[2,768,768]{2,1,0:T(8,128)(2,1)}, u32[]{:S(2)}) copy-start(bf16[2,768,768]{2,1,0:T(8,128)(2,1)} %param.14) | copy-start | bytes 7077892
  139.0 12.9 %copy-start.38 = (f32[384,768]{1,0:T(8,128)}, f32[384,768]{1,0:T(8,128)S(1)}, u32[]{:S(2)}) copy-start(f32[384,768]{1,0:T(8,128)S(1)} %get-tuple-element.164) | copy-start | bytes 3538948
  158.5 79.6 %collective-permute-start.4 = (bf16[2,768,384]{2,1,0:T(8,128)(2,1)}, bf16[2,768,384]{2,1,0:T(8,128)(2,1)}, u32[]{:S(2)}, u32[]{:S(2)}) collective-permute-start(bf16[2,768,384]{2,1,0:T(8,128)(2,1)} %collective-permute-done.refs_3_), channel_id=1, source_target_pairs={{0,4},{4,12},{8,0},{12,8},{16,20},{20,28},{24,16},{28,24},{1,5},{5... | collective-permute-start | bytes 3538952 | tf_op jit(solution)/shard_map/ppermute | solution.py:829
  158.6 79.6 %collective-permute-start.5 = (bf16[2,768,384]{2,1,0:T(8,128)(2,1)}, bf16[2,768,384]{2,1,0:T(8,128)(2,1)}, u32[]{:S(2)}, u32[]{:S(2)}) collective-permute-start(bf16[2,768,384]{2,1,0:T(8,128)(2,1)} %collective-permute-done.3.refs_6_), channel_id=1, source_target_pairs={{0,8},{4,0},{8,12},{12,4},{16,24},{20,16},{24,28},{28,20},{1,9},{5... | collective-permute-start | bytes 3538952 | tf_op jit(solution)/shard_map/ppermute | solution.py:830
  164.5 73.3 %copy-start.57 = (s32[128]{0:T(128)S(1)}, s32[128]{0:T(128)}, u32[]{:S(2)}) copy-start(s32[128]{0:T(128)} %copy-done.56) | copy-start | bytes 1540
  344.9 20.1 %copy-start.28 = (f32[384,768]{1,0:T(8,128)}, f32[384,768]{1,0:T(8,128)S(1)}, u32[]{:S(2)}) copy-start(f32[384,768]{1,0:T(8,128)S(1)} %convert_add_fusion.2) | copy-start | bytes 3538948
  346.8 15.2 %copy-start.39 = (f32[384,768]{1,0:T(8,128)S(1)}, f32[384,768]{1,0:T(8,128)}, u32[]{:S(2)}) copy-start(f32[384,768]{1,0:T(8,128)} %copy-done.38) | copy-start | bytes 3538948
  410.6 13.9 %copy-start.19 = (bf16[1024,768]{1,0:T(8,128)(2,1)S(1)}, bf16[1024,768]{1,0:T(8,128)(2,1)}, u32[]{:S(2)}) copy-start(bf16[1024,768]{1,0:T(8,128)(2,1)} %copy-done.18) | copy-start | bytes 4718596
  410.6 16.8 %slice-start.2 = ((s8[7077888]{0:T(1024)(128)(4,1)}), s8[4194304]{0:T(1024)(128)(4,1)S(1)}, s32[]{:S(2)}) async-start(s8[7077888]{0:T(1024)(128)(4,1)} %bitcast.279), calls=%async_computation.2 | async-start | bytes 8388608
  413.0 159.6 %collective-permute-start.9 = (bf16[2,768,384]{2,1,0:T(8,128)(2,1)}, bf16[2,768,384]{2,1,0:T(8,128)(2,1)}, u32[]{:S(2)}, u32[]{:S(2)}) collective-permute-start(bf16[2,768,384]{2,1,0:T(8,128)(2,1)} %get-tuple-element.73), channel_id=1, source_target_pairs={{0,8},{4,0},{8,12},{12,4},{16,24},{20,16},{24,28},{28,20},{1,9},{5... | collective-permute-start | bytes 3538952 | tf_op jit(solution)/shard_map/ppermute | solution.py:899
  424.2 333.4 %collective-permute-start.11 = (bf16[2,768,384]{2,1,0:T(8,128)(2,1)}, bf16[2,768,384]{2,1,0:T(8,128)(2,1)}, u32[]{:S(2)}, u32[]{:S(2)}) collective-permute-start(bf16[2,768,384]{2,1,0:T(8,128)(2,1)} %get-tuple-element.74), channel_id=1, source_target_pairs={{0,4},{4,12},{8,0},{12,8},{16,20},{20,28},{24,16},{28,24},{1,5},{5... | collective-permute-start | bytes 3538952 | tf_op jit(solution)/shard_map/ppermute | solution.py:900
  424.2 328.5 %collective-permute-start.7 = (bf16[2,768,384]{2,1,0:T(8,128)(2,1)}, bf16[2,768,384]{2,1,0:T(8,128)(2,1)}, u32[]{:S(2)}, u32[]{:S(2)}) collective-permute-start(bf16[2,768,384]{2,1,0:T(8,128)(2,1)} %get-tuple-element.70), channel_id=1, source_target_pairs={{0,4},{4,12},{8,0},{12,8},{16,20},{20,28},{24,16},{28,24},{1,5},{5... | collective-permute-start | bytes 3538952 | tf_op jit(solution)/shard_map/ppermute | solution.py:898
  446.9 91.2 %copy-start.32 = (bf16[1,384,768]{2,1,0:T(8,128)(2,1)S(1)}, bf16[1,384,768]{2,1,0:T(8,128)(2,1)}, u32[]{:S(2)}) copy-start(bf16[1,384,768]{2,1,0:T(8,128)(2,1)} %param.11) | copy-start | bytes 1769476
  446.9 91.2 %copy-start.49 = (f32[768]{0:T(1024)S(1)}, f32[768]{0:T(1024)}, u32[]{:S(2)}) copy-start(f32[768]{0:T(1024)} %copy-done.48) | copy-start | bytes 9220
  446.9 91.2 %copy-start.52 = (f32[384]{0:T(512)S(1)}, f32[384]{0:T(512)}, u32[]{:S(2)}) copy-start(f32[384]{0:T(512)} %copy-done.51) | copy-start | bytes 4612
  575.4 182.2 %collective-permute-start.10 = (bf16[2,768,384]{2,1,0:T(8,128)(2,1)}, bf16[2,768,384]{2,1,0:T(8,128)(2,1)}, u32[]{:S(2)}, u32[]{:S(2)}) collective-permute-start(bf16[2,768,384]{2,1,0:T(8,128)(2,1)} %add.447), channel_id=1, source_target_pairs={{0,8},{4,0},{8,12},{12,4},{16,24},{20,16},{24,28},{28,20},{1,9},{5... | collective-permute-start | bytes 3538952 | tf_op jit(solution)/shard_map/ppermute | solution.py:901
  748.9 28.0 %collective-permute-start.6 = (bf16[2,768,384]{2,1,0:T(8,128)(2,1)}, bf16[2,768,384]{2,1,0:T(8,128)(2,1)}, u32[]{:S(2)}, u32[]{:S(2)}) collective-permute-start(bf16[2,768,384]{2,1,0:T(8,128)(2,1)} %get-tuple-element.68), channel_id=1, source_target_pairs={{0,8},{4,0},{8,12},{12,4},{16,24},{20,16},{24,28},{28,20},{1,9},{5... | collective-permute-start | bytes 3538952 | tf_op jit(solution)/shard_map/ppermute | solution.py:901
  754.7 27.9 %collective-permute-start.8 = (bf16[2,768,384]{2,1,0:T(8,128)(2,1)S(1)}, bf16[2,768,384]{2,1,0:T(8,128)(2,1)S(1)}, u32[]{:S(2)}, u32[]{:S(2)}) collective-permute-start(bf16[2,768,384]{2,1,0:T(8,128)(2,1)S(1)} %add.445), channel_id=1, source_target_pairs={{0,4},{4,12},{8,0},{12,8},{16,20},{20,28},{24,16},{28,24},{1,5},{5... | collective-permute-start | bytes 3538952 | tf_op jit(solution)/shard_map/ppermute | solution.py:900
  758.2 24.5 %copy-start.41 = (f32[2,768,384]{2,1,0:T(8,128)S(1)}, f32[2,768,384]{2,1,0:T(8,128)}, u32[]{:S(2)}) copy-start(f32[2,768,384]{2,1,0:T(8,128)} %get-tuple-element.67) | copy-start | bytes 7077892
  (50 other events, 176.3 us)

commit v3 on v2

--- a/solution.py
+++ b/solution.py
@@ -54,6 +54,10 @@
     return pullback(upstream)
 
 
+def cost(us):
+    return pl.CostEstimate(flops=us * 10**9, bytes_accessed=0, transcendentals=0)
+
+
 def seq_cycle(n):
     cols = n // 4
     if n % 4 or cols < 2:
@@ -63,17 +67,6 @@
         span = range(1, cols) if row % 2 == 0 else range(cols - 1, 0, -1)
         order += [row * cols + col for col in span]
     return order + [3 * cols, 2 * cols, cols]
-
-
-def chip_cycle(n, chips):
-    order = seq_cycle(n)
-    if chips == 1:
-        return [(place, 0) for place in order]
-    cycle = [(order[0], 0)]
-    for row in range(n):
-        span = range(1, chips) if row % 2 == 0 else range(chips - 1, 0, -1)
-        cycle += [(order[row], chip) for chip in span]
-    return cycle + [(order[row], 0) for row in range(n - 1, 0, -1)]
 
 
 def look_up(index, table):
@@ -154,6 +147,7 @@
             pltpu.SemaphoreType.DMA(copies),
         ],
         compiler_params=pltpu.CompilerParams(collective_id=number, has_side_effects=True),
+        cost_estimate=cost(60),
         name="ring_gather",
     )(*arrays)
 
@@ -238,33 +232,19 @@
     )(*arrays)
 
 
-def total_kernel(n, chips, parts, *refs):
-    count = len(parts)
-    xs, outs = refs[:count], refs[count : 2 * count]
-    mines, twins, gots = (refs[(2 + i) * count : (3 + i) * count] for i in range(3))
-    own_sem, twin_sem, ring_sem, back_sem = refs[5 * count :]
-    cycle = chip_cycle(n, chips)
-    length = len(cycle)
-    seq, exp = lax.axis_index("seq"), lax.axis_index("exp")
-    core = lax.rem(exp, 2)
-    places = [cycle.index((i // chips, i % chips)) for i in range(length)]
-    pos = look_up(seq * chips + exp // 2, places)
-
-    def device(place):
-        place = lax.rem(place + length, length)
-        return {
-            "seq": look_up(place, [c[0] for c in cycle]),
-            "exp": look_up(place, [c[1] for c in cycle]) * 2 + core,
-        }
-
-    def block(way, step):
-        place = pos - 1 - step if way == 0 else pos + 1 + step
-        return lax.rem(place + 2 * length, length)
-
-    peer = {"exp": exp + 1 - 2 * core}
-    sides = (device(pos + 1), device(pos - 1))
-    greet((peer,) + sides)
-    lanes = [(a, part, way) for a in range(count) for part in range(parts[a]) for way in range(2)]
+def finish_kernel(n, counts, *refs):
+    few, many = counts
+    refs = list(refs)
+    take = lambda count: [refs.pop(0) for _ in range(count)]
+    blocks, xs, sums, outs = take(few), take(many), take(few), take(many)
+    own_bufs, got_bufs = take(few), take(few)
+    mines, twins, crosses, gots = take(many), take(many), take(many), take(many)
+    near_sem, far_sem, own_sem, pair_sem, cross_sem, ring_sem = refs
+    pos, at, sides = seq_ring(n)
+    exp = lax.axis_index("exp")
+    core, chip = lax.rem(exp, 2), exp // 2
+    peer, over = {"exp": exp + 1 - 2 * core}, {"exp": core + 2 * (1 - chip)}
+    greet(sides + (peer, over))
     started = []
 
     def push(source, target, sems, index, to):
@@ -280,108 +260,194 @@
         started.append(copy)
         return copy
 
-    def spans(lane):
-        a, part, way = lane
-        half = xs[a].shape[2] // 2
-        rows = half // parts[a]
-        return pl.ds(part * rows, rows), pl.ds(way * half + part * rows, rows)
-
-    pairs, own, latest = {}, {}, {}
-    for step in range(length):
+    def block(way, step):
+        return at(pos - 1 - step) if way == 0 else at(pos + 1 + step)
+
+    def fetch(source, target, sem):
+        copy = pltpu.make_async_copy(source, target, sem)
+        copy.start()
+        return copy
+
+    add = lambda *terms: functools.reduce(lambda u, v: u + v, [t.astype(jnp.float32) for t in terms])
+    ways = range(2)
+    lanes = [(a, way) for a in range(many) for way in ways]
+    rings = [(a, way) for a in range(few) for way in ways]
+
+    def span(ref, way):
+        half = ref.shape[-2] // 2
+        return pl.ds(way * half, half)
+
+    pairs, own, crossing, ring = {}, {}, {}, {}
+    for side in range(2):
+        for step in range(n):
+            for lane in lanes:
+                a, way = lane
+                place = chip if side else 1 - chip
+                where, rows = block(way, step), span(xs[a], way)
+                pairs[side, lane, step] = push(
+                    xs[a].at[1 - core, place, where, rows],
+                    twins[a].at[side, way, step],
+                    pair_sem,
+                    (0, side) + lane + (step,),
+                    peer,
+                )
+                own[side, lane, step] = fetch(
+                    xs[a].at[core, place, where, rows],
+                    mines[a].at[side, way, step],
+                    own_sem.at[(side,) + lane + (step,)],
+                )
+        if side == 0:
+            for lane in rings:
+                a, way = lane
+                ring[lane] = push(
+                    blocks[a].at[block(way, 0), span(blocks[a], way)],
+                    got_bufs[a].at[way, 0],
+                    far_sem,
+                    lane + (0,),
+                    sides[way],
+                )
+            near = {
+                (lane, step): fetch(
+                    blocks[lane[0]].at[block(lane[1], step), span(blocks[lane[0]], lane[1])],
+                    own_bufs[lane[0]].at[lane[1], step - 1],
+                    near_sem.at[lane + (step - 1,)],
+                )
+                for step in range(1, n)
+                for lane in rings
+            }
+
+    def scatter(step):
+        for lane in rings:
+            a, way = lane
+            near[lane, step].wait()
+            ring[lane].wait_recv()
+            total = add(got_bufs[a][way, step - 1], own_bufs[a][way, step - 1])
+            if step == n - 1:
+                sums[a][span(sums[a], way)] = total.astype(sums[a].dtype)
+            else:
+                got_bufs[a][way, step - 1] = total.astype(got_bufs[a].dtype)
+                ring[lane] = push(
+                    got_bufs[a].at[way, step - 1],
+                    got_bufs[a].at[way, step],
+                    far_sem,
+                    lane + (step,),
+                    sides[way],
+                )
+
+    for step in range(n):
         for lane in lanes:
-            a, part, way = lane
-            near, wide = spans(lane)
-            where = block(way, step)
-            pairs[lane, step] = push(
-                xs[a].at[1 - core, where, wide],
-                twins[a].at[way, step, near],
-                twin_sem,
-                lane + (step,),
-                peer,
+            a, way = lane
+            own[0, lane, step].wait()
+            pairs[0, lane, step].wait_recv()
+            mines[a][0, way, step] = add(mines[a][0, way, step], twins[a][0, way, step]).astype(
+                mines[a].dtype
             )
-            own[lane, step] = pltpu.make_async_copy(
-                xs[a].at[core, where, wide], mines[a].at[way, step, near], own_sem.at[lane + (step,)]
+            crossing[lane, step] = push(
+                mines[a].at[0, way, step],
+                crosses[a].at[way, step],
+                cross_sem,
+                (0,) + lane + (step,),
+                over,
             )
-            own[lane, step].start()
-    for step in range(length):
+        if step == n // 2:
+            scatter(1)
+    latest = {}
+    for step in range(n):
         for lane in lanes:
-            a, part, way = lane
-            near, wide = spans(lane)
-            own[lane, step].wait()
-            pairs[lane, step].wait_recv()
-            total = mines[a][way, step, near].astype(jnp.float32) + twins[a][
-                way, step, near
-            ].astype(jnp.float32)
+            a, way = lane
+            own[1, lane, step].wait()
+            pairs[1, lane, step].wait_recv()
+            crossing[lane, step].wait_recv()
+            terms = [mines[a][1, way, step], twins[a][1, way, step], crosses[a][way, step]]
             if step:
                 latest[lane].wait_recv()
-                total = total + gots[a][way, step - 1, near].astype(jnp.float32)
-            mines[a][way, step, near] = total.astype(mines[a].dtype)
-            if step < length - 1:
+                terms.append(gots[a][way, step - 1])
+            mines[a][1, way, step] = add(*terms).astype(mines[a].dtype)
+            if step < n - 1:
                 latest[lane] = push(
-                    mines[a].at[way, step, near],
-                    gots[a].at[way, step, near],
+                    mines[a].at[1, way, step],
+                    gots[a].at[way, step],
                     ring_sem,
                     (0,) + lane + (step,),
                     sides[way],
                 )
-    keep = []
-    for step in range(length):
+        if 2 <= step + 2 < n:
+            scatter(step + 2)
+    keep, done = [], []
+
+    def hand_on(step):
         for lane in lanes:
-            a, part, way = lane
-            near, wide = spans(lane)
+            a, way = lane
+            crossing[lane, step].wait_recv()
+            where = at(pos - step) if way == 0 else at(pos + step)
+            place = outs[a].at[core, 1 - chip, where, span(outs[a], way)]
+            done.append(push(place, place, pair_sem, (1, 1) + lane + (step,), peer))
+
+    for step in range(n):
+        for lane in lanes:
+            a, way = lane
             if step:
                 latest[lane].wait_recv()
-            where = lax.rem(pos - step + length if way == 0 else pos + step, length)
-            target = outs[a].at[core, where, wide]
-            source = target if step else mines[a].at[way, length - 1, near]
-            if step < length - 1:
+            where = at(pos - step) if way == 0 else at(pos + step)
+            target = outs[a].at[core, chip, where, span(outs[a], way)]
+            source = target if step else mines[a].at[1, way, n - 1]
+            if step < n - 1:
                 latest[lane] = push(source, target, ring_sem, (1,) + lane + (step,), sides[way])
-            pairs[lane, step] = push(source, target, back_sem, lane + (step,), peer)
+            crossing[lane, step] = push(source, target, cross_sem, (1,) + lane + (step,), over)
+            done.append(push(source, target, pair_sem, (1, 0) + lane + (step,), peer))
             if step == 0:
-                copy = pltpu.make_async_copy(source, target, own_sem.at[lane + (0,)])
-                copy.start()
-                keep.append(copy)
+                keep.append(fetch(source, target, own_sem.at[(0,) + lane + (0,)]))
+        if step:
+            hand_on(step - 1)
+    hand_on(n - 1)
     for copy in keep:
         copy.wait()
-    for copy in pairs.values():
+    for copy in done:
         copy.wait_recv()
     for copy in started:
         copy.wait_send()
 
 
-def total_everywhere(rows_in, small, n, m, number):
-    chips = m // 2
-    length = n * chips
+def finish(blocks, rows_in, small, n, m, number):
     rows, cols = rows_in.shape
-    lanes_of = TILE * 8
-    parts = (3, 1)
-    if m % 2 or rows % (4 * length * parts[0] * 16) or small.size > 4 * length * lanes_of:
-        return lax.psum((rows_in, small), ("seq", "exp"))
-    padded = jnp.pad(small, (0, 4 * length * lanes_of - small.size))
-    arrays = [
-        rows_in.reshape(2, length, rows // (2 * length), cols),
-        padded.reshape(2, length, 16, TILE),
-    ]
-    bufs = [pltpu.VMEM((2, length, x.shape[2] // 2, x.shape[3]), x.dtype) for x in arrays]
-    sems = (len(arrays), max(parts), 2, length)
-    big, little = pl.pallas_call(
-        functools.partial(total_kernel, n, chips, parts),
-        out_shape=[jax.ShapeDtypeStruct(x.shape, x.dtype) for x in arrays],
-        in_specs=[ANY] * 2,
-        out_specs=[ANY] * 2,
-        scratch_shapes=bufs * 3
+    each = rows // (4 * n)
+    if m != 4 or rows % (4 * n * 32) or small.size > 4 * n * 16 * TILE:
+        return (
+            ring_scatter(blocks, n, number, jnp.float32),
+            *lax.psum((rows_in, small), ("seq", "exp")),
+        )
+    padded = jnp.pad(small, (0, 4 * n * 16 * TILE - small.size))
+    arrays = [rows_in.reshape(2, 2, n, each, cols), padded.reshape(2, 2, n, 16, TILE)]
+    few, many = len(blocks), len(arrays)
+    halves = [(x.shape[-2] // 2, x.shape[-1], x.dtype) for x in blocks + arrays]
+    ring_bufs = [pltpu.VMEM((2, n - 1, r, c), t) for r, c, t in halves[:few]]
+    two = [pltpu.VMEM((2, 2, n, r, c), t) for r, c, t in halves[few:]]
+    one = [pltpu.VMEM((2, n, r, c), t) for r, c, t in halves[few:]]
+    dma = pltpu.SemaphoreType.DMA
+    results = pl.pallas_call(
+        functools.partial(finish_kernel, n, (few, many)),
+        out_shape=[jax.ShapeDtypeStruct(x.shape[1:], jnp.float32) for x in blocks]
+        + [jax.ShapeDtypeStruct(x.shape, x.dtype) for x in arrays],
+        in_specs=[ANY] * (few + many),
+        out_specs=[pl.BlockSpec(memory_space=pltpu.VMEM)] * few + [ANY] * many,
+        scratch_shapes=ring_bufs * 2
+        + two * 2
+        + one * 2
         + [
-            pltpu.SemaphoreType.DMA(sems),
-            pltpu.SemaphoreType.DMA((2,) + sems),
-            pltpu.SemaphoreType.DMA((2, 2) + sems),
-            pltpu.SemaphoreType.DMA((2,) + sems),
+            dma((few, 2, n)),
+            dma((2, few, 2, n)),
+            dma((2, many, 2, n)),
+            dma((2, 2, 2, many, 2, n)),
+            dma((2, 2, many, 2, n)),
+            dma((2, 2, many, 2, n)),
         ],
         compiler_params=pltpu.CompilerParams(
             collective_id=number, has_side_effects=True, vmem_limit_bytes=58 << 20
         ),
-        name="total_everywhere",
-    )(*arrays)
-    return big.reshape(rows, cols), little.reshape(-1)[: small.size]
+        cost_estimate=cost(120),
+        name="finish",
+    )(*blocks, *arrays)
+    return results[:few], results[few].reshape(rows, cols), results[-1].reshape(-1)[: small.size]
 
 
 QUAD = 4
@@ -440,6 +506,7 @@
             pltpu.SemaphoreType.DMA((groups, m)),
         ],
         compiler_params=pltpu.CompilerParams(collective_id=number, has_side_effects=True),
+        cost_estimate=cost(70),
         name="spread_back" if back else "spread",
     )(x)
 
@@ -578,6 +645,7 @@
             pltpu.VMEM((1, 2 * rows), jnp.float32),
         ],
         compiler_params=pltpu.CompilerParams(vmem_limit_bytes=48 << 20),
+        cost_estimate=cost(40 if causal else 10),
         name="attend_self" if causal else "attend_cross",
     )(seq_at, queries, keys, values, *extra)
 
@@ -698,6 +766,7 @@
         out_specs=[pair, long, long] + out_specs,
         scratch_shapes=[pltpu.VMEM((TILE + 16, 2 * rows), jnp.float32)],
         compiler_params=pltpu.CompilerParams(vmem_limit_bytes=48 << 20),
+        cost_estimate=cost(48 if causal else 15),
         name="attend_self_back" if causal else "attend_cross_back",
     )(seq_at, queries, keys, values, upstream, wide, lse, *extra)
 
@@ -779,6 +848,7 @@
         in_specs=[block] + [weight] * len(maps),
         out_specs=[block] + [weight] * len(maps),
         compiler_params=pltpu.CompilerParams(vmem_limit_bytes=58 << 20),
+        cost_estimate=cost(28),
         name="run_experts",
     )(rows, *maps)
 
@@ -826,9 +896,6 @@
     in_own, out_own, normed_all = lax.optimization_barrier((expert_in, expert_out, normed_all))
     in_last, out_last = (lax.ppermute(w, "seq", to_next) for w in (in_own, out_own))
     in_next, out_next = (lax.ppermute(w, "seq", to_last) for w in (in_own, out_own))
-    in_far = lax.ppermute(in_last, "seq", to_next)
-    out_far = lax.ppermute(out_next, "seq", to_last)
-    maps = [in_own, out_own, in_last, out_last, in_next, out_next, in_far, out_far]
     normed_all = normed_all.reshape(n * token_count, D)
     memory_all = memory_all.reshape(n * memory_count, D)
     queries = project(normed_self, proj_in[0])
@@ -839,6 +906,11 @@
     attended_self_low, attended_self, lse_self = attend(
         seq_at, queries, key_all, value_all, tiles
     )
+    attended_self_low, in_last, out_next = lax.optimization_barrier(
+        (attended_self_low, in_last, out_next)
+    )
+    in_far = lax.ppermute(in_last, "seq", to_next)
+    out_far = lax.ppermute(out_next, "seq", to_last)
     after_self = tokens + jnp.dot(
         attended_self_low, proj_out[0], preferred_element_type=jnp.float32
     )
@@ -889,18 +961,20 @@
         .astype(jnp.bfloat16)
         .reshape(m, local_experts * slots, 2 * D)
     )
+    sent_rows, in_far, out_far = lax.optimization_barrier((sent_rows, in_far, out_far))
+    maps = [in_own, out_own, in_last, out_last, in_next, out_next, in_far, out_far]
     received = spread(sent_rows, n, m, False, 2)
     parts, *terms = run_experts(received, maps)
     returned = spread(parts, n, m, True, 3)
+    gin_own, gout_own, gin_last, gout_last, gin_next, gout_next, gin_far, gout_far = terms
+    gin_far = lax.ppermute(gin_far, "seq", to_next)
+    gout_far = lax.ppermute(gout_far, "seq", to_last)
+    returned, gin_far, gout_far = lax.optimization_barrier((returned, gin_far, gout_far))
+    gin_next, gout_last = gin_next + gin_far, gout_last + gout_far
+    gin_next, gout_next = (lax.ppermute(w, "seq", to_next) for w in (gin_next, gout_next))
+    gin_last, gout_last = (lax.ppermute(w, "seq", to_last) for w in (gin_last, gout_last))
     returned = jnp.sum(returned.astype(jnp.float32), axis=0).astype(jnp.bfloat16)
     returned = returned.reshape(expert_count * slots, 2 * D)
-    gin_own, gout_own, gin_last, gout_last, gin_next, gout_next, gin_far, gout_far = terms
-    gin_next = gin_next + lax.ppermute(gin_far, "seq", to_next)
-    gout_last = gout_last + lax.ppermute(gout_far, "seq", to_last)
-    gin_next, gout_next = (lax.ppermute(w, "seq", to_next) for w in (gin_next, gout_next))
-    gin_last, gout_last = (lax.ppermute(w, "seq", to_last) for w in (gin_last, gout_last))
-    grad_expert_in = gin_own + gin_last.astype(jnp.float32) + gin_next.astype(jnp.float32)
-    grad_expert_out = gout_own + gout_last.astype(jnp.float32) + gout_next.astype(jnp.float32)
     routed = jnp.dot(dispatch, returned, preferred_element_type=jnp.float32)
     combined, grad_mixed = routed[:, :D], routed[:, D:]
     output = (after_cross + gate_prob[:, None] * combined).astype(jnp.bfloat16)
@@ -951,22 +1025,18 @@
         lse_self,
         tiles,
     )
+    grad_keys, grad_values, gin_last, gout_last, gin_next, gout_next = lax.optimization_barrier(
+        (grad_keys, grad_values, gin_last, gout_last, gin_next, gout_next)
+    )
+    grad_expert_in = gin_own + gin_last.astype(jnp.float32) + gin_next.astype(jnp.float32)
+    grad_expert_out = gout_own + gout_last.astype(jnp.float32) + gout_next.astype(jnp.float32)
     grad_table = bias_gradient(near, sums)
-    grad_normed_part = (
-        input_grad(grad_keys, proj_in[1]) + input_grad(grad_values, proj_in[2])
-    ).astype(jnp.bfloat16)
-    grad_normed_own, grad_memory = ring_scatter(
-        [
-            grad_normed_part.reshape(n, token_count, D),
-            grad_memory_part.reshape(n, memory_count, D),
-        ],
-        n,
-        4,
-        jnp.float32,
-    )
-    grad_normed_self = input_grad(grad_self_query, proj_in[0]) + grad_normed_own
-    grad_token_part, grad_gain_self = rms_backward(tokens, gain_rows[0], grad_normed_self)
-    grad_in = (grad_after_self + grad_token_part).astype(jnp.bfloat16)
+    grad_normed_query = input_grad(grad_self_query, proj_in[0])
+    grad_normed_part = input_grad(grad_keys, proj_in[1]) + input_grad(grad_values, proj_in[2])
+    grad_gain_self = (
+        jnp.sum(grad_normed_part * normed_all.astype(jnp.float32), axis=0)
+        + jnp.sum(grad_normed_query * normed_self.astype(jnp.float32), axis=0)
+    ) / gain_rows[0]
 
     grads = jnp.stack(
         [
@@ -981,13 +1051,19 @@
         ]
     )
     grad_gains = jnp.stack([grad_gain_self, grad_gain_cross, grad_gain_mix])
-    grads, small = total_everywhere(
+    (grad_normed_own, grad_memory), grads, small = finish(
+        [
+            grad_normed_part.astype(jnp.bfloat16).reshape(n, token_count, D),
+            grad_memory_part.reshape(n, memory_count, D),
+        ],
         grads.reshape(-1, D),
         jnp.concatenate([grad_gains.reshape(-1), grad_table.reshape(-1), grad_router.reshape(-1)]),
         n,
         m,
-        5,
-    )
+        4,
+    )
+    grad_token_part, _ = rms_backward(tokens, gain_rows[0], grad_normed_query + grad_normed_own)
+    grad_in = (grad_after_self + grad_token_part).astype(jnp.bfloat16)
     grads = grads.reshape(-1, D, D).astype(jnp.float32)
     ends = (grad_gains.size, grad_gains.size + grad_table.size)
     return (

time: 795 us -> 689 us (0.87)
  Pallas kernels: 578 us -> 488 us
    pallas_call x2 -> x1, Pallas kernels: 244 us -> 147 us  [finish(): pl.pallas_call(functools.partial(finish_kernel, n, (few, many)), out_shap...]
    ppermute x2, starting transfers between devices: 11.5 us -> 1.74 us  [the longest x1 1.69 us: body(): gout_far = lax.ppermute(gout_far, 'seq', to_last)]
    unnamed x144 -> x208, local copies, waits for them, and re-layouts: 13.9 us -> 16.6 us
  transfers between devices with their start and end apart: 12 -> 12, of which waited for: 2 -> 3; matrix products, arithmetic and copies ran while one was open for 17% -> 11% of each run, Pallas kernels for 46% -> 37%
where the time goes in v3:
time: 689 us; the launch traced here: 682 us
  Pallas kernels  488 us (71%)
  matrix products  83.2 us (12%)
  local copies, waits for them, and re-layouts  36.4 us (5%)
  other arithmetic  34.3 us (5%)
  starting transfers between devices  19.3 us (3%)
  waiting for transfers between devices  18 us (3%)
    pallas_call x2, Pallas kernels, spread(): pl.pallas_call(functools.partial(spread_kernel, n, m, back), out_shape=ja...  148 us
    pallas_call x1, Pallas kernels, finish(): pl.pallas_call(functools.partial(finish_kernel, n, (few, many)), out_shap...  147 us
    pallas_call x1, Pallas kernels, ring_gather(): pl.pallas_call(functools.partial(gather_kernel, n, parts, count), out_sha...  62 us
    pallas_call x2, Pallas kernels, attend_back(): pl.pallas_call(functools.partial(attend_back_kernel, causal, block), grid...  57.5 us
    pallas_call x2, Pallas kernels, attend(): pl.pallas_call(functools.partial(attend_kernel, causal, block), grid=(PAI...  45.7 us
    dot_general x8, matrix products, input_grad(): jnp.einsum('te,de->td', upstream, matrix, preferred_element_type=jnp.floa...  29.6 us
    pallas_call x1, Pallas kernels, run_experts(): pl.pallas_call(expert_kernel, grid=(count,), out_shape=[jax.ShapeDtypeStr...  27.8 us
    dot_general x8, matrix products, weight_grad(): jnp.einsum('td,te->de', source, upstream, preferred_element_type=jnp.floa...  22.5 us
  transfers between devices with their start and end apart: 12, of which 3 were waited for; matrix products, arithmetic and copies ran while one was open for 11% of the time, Pallas kernels for 37%

profile of v3, /device:TPU:25, one launch (start us, length us, event | category | flops | bytes accessed | tf_op | source)
XLA Modules:
  0.0 681.5 jit_solution(10208374211849301028)
XLA Ops:
  5.4 62.0 %ring_gather.1 = (bf16[8,384,768]{2,1,0:T(8,128)(2,1)}, bf16[8,128,768]{2,1,0:T(8,128)(2,1)}) custom-call(bf16[384,768]{1,0:T(8,128)(2,1)} %fusion.25.refs_0_, bf16[128,768]{1,0:T(8,128)(2,1)} %bitcast.273), custom_call_target="tpu_custom_call" | custom-call | flops 60000002048 | tf_op jit(solution)/shard_map/ring_gather/pallas_call | solution.py:139
  73.8 2.9 convolution_convert_fusion.3.v_ref
  79.3 5.7 convolution_convert_fusion.v_ref
  85.0 5.5 convolution_convert_fusion.1.k_ref
  93.3 6.3 select_select_fusion.refs_0_
  99.6 34.9 %attend_self.1 = (bf16[384,768]{1,0:T(8,128)(2,1)S(1)}, f32[384,768]{1,0:T(8,128)S(1)}, f32[6,2,384]{2,1,0:T(2,128)S(1)}) custom-call(s32[1]{0:T(128)} %bitcast.1.s_ref, bf16[384,768]{1,0:T(8,128)(2,1)S(1)} %convolution_convert_fusion.16.q_ref, bf16[3072,768]{1,0:T(8,128)(2,1)} %convolution_convert_fusion.1.k_ref, ...), custom_call_target="tpu_custom_call" | custom-call | flops 40000000000 | tf_op jit(solution)/shard_map/attend_self/pallas_call | solution.py:633
  137.1 5.9 collective-permute-start.3
  145.1 10.8 %attend_cross.1 = (bf16[384,768]{1,0:T(8,128)(2,1)S(1)}, f32[384,768]{1,0:T(8,128)S(1)}, f32[6,2,384]{2,1,0:T(2,128)S(1)}) custom-call(s32[1]{0:T(128)} %bitcast.1.s_ref, bf16[384,768]{1,0:T(8,128)(2,1)S(1)} %convolution_convert_fusion.15.q_ref, bf16[1024,768]{1,0:T(8,128)(2,1)S(1)} %copy-done.17, bf16[1024,768]{1,0:T(8,128)(2,1)S(1)} %convolution_convert_fusion.3.v_ref), custom_call_target="tpu_custom_call" | custom-call | flops 10000000000 | tf_op jit(solution)/shard_map/attend_cross/pallas_call | solution.py:633
  161.1 5.7 collective-permute-done.2.refs_7_
  168.9 75.3 %spread.1.refs_0_ = bf16[2,4,128,1536]{3,2,1,0:T(8,128)(2,1)} custom-call(bf16[4,128,1536]{2,1,0:T(8,128)(2,1)} %bitcast.288), custom_call_target="tpu_custom_call" | custom-call | flops 70000001024 | tf_op jit(solution)/shard_map/spread/pallas_call | solution.py:498
  244.3 27.8 %run_experts.1 = (bf16[2,4,128,1536]{3,2,1,0:T(8,128)(2,1)}, f32[2,768,384]{2,1,0:T(8,128)}, f32[2,768,384]{2,1,0:T(8,128)}, bf16[2,768,384]{2,1,0:T(8,128)(2,1)...) custom-call(bf16[2,4,128,1536]{3,2,1,0:T(8,128)(2,1)} %spread.1.refs, ...), custom_call_target="tpu_custom_call" | custom-call | flops 28000000000 | tf_op jit(solution)/shard_map/run_experts/pallas_call | solution.py:840
  273.9 73.1 %spread_back.1 = bf16[2,4,128,1536]{3,2,1,0:T(8,128)(2,1)} custom-call(bf16[2,4,128,1536]{3,2,1,0:T(8,128)(2,1)} %get-tuple-element.71.x_ref), custom_call_target="tpu_custom_call" | custom-call | flops 70000001024 | tf_op jit(solution)/shard_map/spread_back/pallas_call | solution.py:498
  348.5 4.7 reduce_sum.184
  361.5 15.1 %attend_cross_back.1 = (bf16[384,768]{1,0:T(8,128)(2,1)S(1)}, bf16[1024,768]{1,0:T(8,128)(2,1)S(1)}, bf16[1024,768]{1,0:T(8,128)(2,1)S(1)}) custom-call(s32[1]{0:T(128)} %bitcast.1.s_ref, bf16[384,768]{1,0:T(8,128)(2,1)S(1)} %copy-done.9, bf16[1024,768]{1,0:T(8,128)(2,1)} %convolution_convert_fusion.4.k_ref, bf16[1024,768]{1,0:T(8,128)(2,1)} %copy-done.16, ...), custom_call_target="tpu_custom_call" | custom-call | flops 15000000512 | tf_op jit(solution)/shard_map/attend_cross_back/pallas_call | solution.py:756
  376.7 3.0 multiply_reduce_fusion.2
  382.1 42.4 %attend_self_back.1 = (bf16[384,768]{1,0:T(8,128)(2,1)S(1)}, bf16[3072,768]{1,0:T(8,128)(2,1)}, bf16[3072,768]{1,0:T(8,128)(2,1)}, f32[12,256,128]{2,1,0:T(8,128)S(1)}, f32[6,2,384]{2,1,0:T(2,128)S(1)}) custom-call(s32[1]{0:T(128)} %bitcast.1.s_ref, bf16[384,768]{1,0:T(8,128)(2,1)S(1)} %copy-done.13, bf16[3072,768]{1,0:T(8,128)(2,1)} %convolution_convert_fusion.1.k_ref, ...), custom_call_target="tpu_custom_call" | custom-call | flops 48000000000 | tf_op jit(solution)/shard_map/attend_self_back/pallas_call | solution.py:756
  426.4 3.0 copy.28
  430.7 6.7 collective-permute-start.9
  444.5 3.2 multiply_reduce_fusion.3
  447.7 2.8 fusion.41
  450.6 4.0 add_convert_fusion
  454.6 8.6 %collective-permute-done.9 = bf16[2,768,384]{2,1,0:T(8,128)(2,1)S(1)} collective-permute-done((bf16[2,768,384]{2,1,0:T(8,128)(2,1)}, bf16[2,768,384]{2,1,0:T(8,128)(2,1)S(1)}, u32[]{:S(2)}, u32[]{:S(2)}) %collective-permute-start.9) | collective-permute-done | bytes 1179680 | tf_op jit(solution)/shard_map/ppermute | solution.py:975
  463.2 3.7 collective-permute-done.10
  467.0 5.5 fusion.49
  472.5 5.2 fusion.20
  477.7 5.0 fusion.22
  493.2 9.7 %multiply_reduce_fusion = (f32[768]{0:T(1024)S(1)}, bf16[3072,768]{1,0:T(8,128)(2,1)}) fusion(bf16[8,384,768]{2,1,0:T(8,128)(2,1)S(1)} %bitcast.279, f32[3072,768]{1,0:T(8,128)S(1)} %fusion.49, bf16[3072,768]{1,0:T(8,128)(2,1)} %get-tuple-element.89, bf16[6,768,768]{2,1,0:T(8,128)(2,1)} %param.13), kind=kOutput, calls=%fused_computation | convolution fusion | flops 3635674368 | bytes 24775680 | tf_op jit(solution)/shard_map/te,de->td/dot_general | solution.py:867
  504.4 146.6 %finish.1 = (f32[384,768]{1,0:T(8,128)}, f32[128,768]{1,0:T(8,128)}, bf16[2,2,8,192,768]{4,3,2,1,0:T(8,128)(2,1)}, f32[2,2,8,16,128]{4,3,2,1,0:T(8,128)}) custom-call(bf16[8,384,768]{2,1,0:T(8,128)(2,1)} %bitcast.282, bf16[8,128,768]{2,1,0:T(8,128)(2,1)} %bitcast.287, bf16[2,2,8,192,768]{4,3,2,1,0:T(8,128)(2,1)} %bitcast.31.refs_2_, ...), custom_call_target="tpu_custom_call" | custom-call | flops 120000004096 | tf_op jit(solution)/shard_map/finish/pallas_call | solution.py:427
  652.4 4.7 slice.230
  657.1 4.6 slice.271
  663.2 6.6 slice.270
  675.1 6.2 convert_add_fusion
  (311 shorter events, 72.3 us)
Async XLA Ops:
  0.6 157.3 %copy-start = (bf16[768,8]{0,1:T(8,128)(2,1)S(1)}, bf16[768,8]{0,1:T(8,128)(2,1)}, u32[]{:S(2)}) copy-start(bf16[768,8]{0,1:T(8,128)(2,1)} %param.17) | copy-start | bytes 36868
  2.5 69.1 %copy-start.76 = (f32[384]{0:T(512)}, f32[384]{0:T(512)S(1)}, u32[]{:S(2)}) copy-start(f32[384]{0:T(512)S(1)} %fusion.168) | copy-start | bytes 4612
  3.2 64.1 %copy-start.68 = (f32[3,768]{1,0:T(4,128)}, f32[3,768]{1,0:T(4,128)S(1)}, u32[]{:S(2)}) copy-start(f32[3,768]{1,0:T(4,128)S(1)} %convert_element_type.465) | copy-start | bytes 27652
  3.3 68.3 %copy-start.58 = (f32[768]{0:T(1024)}, f32[768]{0:T(1024)S(1)}, u32[]{:S(2)}) copy-start(f32[768]{0:T(1024)S(1)} %get-tuple-element.122) | copy-start | bytes 9220
  3.3 139.7 %copy-start.80 = (f32[768]{0:T(1024)}, f32[768]{0:T(1024)S(1)}, u32[]{:S(2)}) copy-start(f32[768]{0:T(1024)S(1)} %get-tuple-element.121) | copy-start | bytes 9220
  3.3 153.9 %copy-start.60 = (f32[768]{0:T(1024)}, f32[768]{0:T(1024)S(1)}, u32[]{:S(2)}) copy-start(f32[768]{0:T(1024)S(1)} %get-tuple-element.120) | copy-start | bytes 9220
  5.4 65.0 %copy-start.71 = (f32[32,12]{0,1:T(8,128)S(1)}, f32[32,12]{0,1:T(8,128)}, u32[]{:S(2)}) copy-start(f32[32,12]{0,1:T(8,128)} %param.16) | copy-start | bytes 4612
  5.4 66.2 %copy-start.30 = (bf16[1,384,768]{2,1,0:T(8,128)(2,1)S(1)}, bf16[1,384,768]{2,1,0:T(8,128)(2,1)}, u32[]{:S(2)}) copy-start(bf16[1,384,768]{2,1,0:T(8,128)(2,1)} %param.11) | copy-start | bytes 1769476
  67.4 176.9 %collective-permute-start.5 = (bf16[2,768,384]{2,1,0:T(8,128)(2,1)}, bf16[2,768,384]{2,1,0:T(8,128)(2,1)}, u32[]{:S(2)}, u32[]{:S(2)}) collective-permute-start(bf16[2,768,384]{2,1,0:T(8,128)(2,1)} %refs_1_), channel_id=1, source_target_pairs={{0,8},{4,0},{8,12},{12,4},{16,24},{20,16},{24,28},{28,20},{1,9},{5... | collective-permute-start | bytes 3538952 | tf_op jit(solution)/shard_map/ppermute | solution.py:898
  68.7 67.6 %collective-permute-start = (bf16[2,768,384]{2,1,0:T(8,128)(2,1)}, bf16[2,768,384]{2,1,0:T(8,128)(2,1)}, u32[]{:S(2)}, u32[]{:S(2)}) collective-permute-start(bf16[2,768,384]{2,1,0:T(8,128)(2,1)} %refs_1_), channel_id=1, source_target_pairs={{0,4},{4,12},{8,0},{12,8},{16,20},{20,28},{24,16},{28,24},{1,5},{5... | collective-permute-start | bytes 3538952 | tf_op jit(solution)/shard_map/ppermute | solution.py:897
  68.9 175.4 %collective-permute-start.4 = (bf16[2,768,384]{2,1,0:T(8,128)(2,1)}, bf16[2,768,384]{2,1,0:T(8,128)(2,1)}, u32[]{:S(2)}, u32[]{:S(2)}) collective-permute-start(bf16[2,768,384]{2,1,0:T(8,128)(2,1)} %refs_2_), channel_id=1, source_target_pairs={{0,4},{4,12},{8,0},{12,8},{16,20},{20,28},{24,16},{28,24},{1,5},{5... | collective-permute-start | bytes 3538952 | tf_op jit(solution)/shard_map/ppermute | solution.py:897
  70.1 66.1 %collective-permute-start.1 = (bf16[2,768,384]{2,1,0:T(8,128)(2,1)}, bf16[2,768,384]{2,1,0:T(8,128)(2,1)}, u32[]{:S(2)}, u32[]{:S(2)}) collective-permute-start(bf16[2,768,384]{2,1,0:T(8,128)(2,1)} %refs_2_), channel_id=1, source_target_pairs={{0,8},{4,0},{8,12},{12,4},{16,24},{20,16},{24,28},{28,20},{1,9},{5... | collective-permute-start | bytes 3538952 | tf_op jit(solution)/shard_map/ppermute | solution.py:898
  73.7 25.9 %copy-start.12 = (bf16[384,768]{1,0:T(8,128)(2,1)}, bf16[384,768]{1,0:T(8,128)(2,1)S(1)}, u32[]{:S(2)}) copy-start(bf16[384,768]{1,0:T(8,128)(2,1)S(1)} %convolution_convert_fusion.16.q_ref) | copy-start | bytes 1769476
  76.7 68.4 %copy-start.16 = (bf16[1024,768]{1,0:T(8,128)(2,1)}, bf16[1024,768]{1,0:T(8,128)(2,1)S(1)}, u32[]{:S(2)}) copy-start(bf16[1024,768]{1,0:T(8,128)(2,1)S(1)} %convolution_convert_fusion.3.v_ref) | copy-start | bytes 4718596
  90.5 67.8 %copy-start.56 = (s32[384]{0:T(512)}, s32[384]{0:T(512)S(1)}, u32[]{:S(2)}) copy-start(s32[384]{0:T(512)S(1)} %reduce.38) | copy-start | bytes 4612
  99.6 35.0 %copy-start.4 = (f32[12,128,256]{2,1,0:T(8,128)}, f32[12,128,256]{2,1,0:T(8,128)S(1)}, u32[]{:S(2)}) copy-start(f32[12,128,256]{2,1,0:T(8,128)S(1)} %select_select_fusion.refs_0_) | copy-start | bytes 4718596
  99.6 36.7 %copy-start.32 = (bf16[2,768,768]{2,1,0:T(8,128)(2,1)S(1)}, bf16[2,768,768]{2,1,0:T(8,128)(2,1)}, u32[]{:S(2)}) copy-start(bf16[2,768,768]{2,1,0:T(8,128)(2,1)} %param.14) | copy-start | bytes 7077892
  135.2 23.6 %copy-start.64 = (s32[384]{0:T(512)}, s32[384]{0:T(512)S(1)}, u32[]{:S(2)}) copy-start(s32[384]{0:T(512)S(1)} %add_select_fusion) | copy-start | bytes 4612
  137.1 29.7 %collective-permute-start.2 = (bf16[2,768,384]{2,1,0:T(8,128)(2,1)}, bf16[2,768,384]{2,1,0:T(8,128)(2,1)S(1)}, u32[]{:S(2)}, u32[]{:S(2)}) collective-permute-start(bf16[2,768,384]{2,1,0:T(8,128)(2,1)} %collective-permute-done.refs_3_), channel_id=1, source_target_pairs={{0,4},{4,12},{8,0},{12,8},{16,20},{20,28},{24,16},{28,24},{1,5},{5... | collective-permute-start | bytes 3538952 | tf_op jit(solution)/shard_map/ppermute | solution.py:912
  137.1 30.7 %collective-permute-start.3 = (bf16[2,768,384]{2,1,0:T(8,128)(2,1)}, bf16[2,768,384]{2,1,0:T(8,128)(2,1)S(1)}, u32[]{:S(2)}, u32[]{:S(2)}) collective-permute-start(bf16[2,768,384]{2,1,0:T(8,128)(2,1)} %collective-permute-done.1.refs_6_), channel_id=1, source_target_pairs={{0,8},{4,0},{8,12},{12,4},{16,24},{20,16},{24,28},{28,20},{1,9},{5... | collective-permute-start | bytes 3538952 | tf_op jit(solution)/shard_map/ppermute | solution.py:913
  272.1 76.4 %collective-permute-start.6 = (bf16[2,768,384]{2,1,0:T(8,128)(2,1)}, bf16[2,768,384]{2,1,0:T(8,128)(2,1)S(1)}, u32[]{:S(2)}, u32[]{:S(2)}) collective-permute-start(bf16[2,768,384]{2,1,0:T(8,128)(2,1)} %get-tuple-element.72), channel_id=1, source_target_pairs={{0,4},{4,12},{8,0},{12,8},{16,20},{20,28},{24,16},{28,24},{1,5},{5... | collective-permute-start | bytes 3538952 | tf_op jit(solution)/shard_map/ppermute | solution.py:970
  272.2 76.3 %collective-permute-start.7 = (bf16[2,768,384]{2,1,0:T(8,128)(2,1)}, bf16[2,768,384]{2,1,0:T(8,128)(2,1)S(1)}, u32[]{:S(2)}, u32[]{:S(2)}) collective-permute-start(bf16[2,768,384]{2,1,0:T(8,128)(2,1)} %get-tuple-element.73), channel_id=1, source_target_pairs={{0,8},{4,0},{8,12},{12,4},{16,24},{20,16},{24,28},{28,20},{1,9},{5... | collective-permute-start | bytes 3538952 | tf_op jit(solution)/shard_map/ppermute | solution.py:971
  347.0 107.7 %collective-permute-start.8 = (bf16[2,768,384]{2,1,0:T(8,128)(2,1)}, bf16[2,768,384]{2,1,0:T(8,128)(2,1)}, u32[]{:S(2)}, u32[]{:S(2)}) collective-permute-start(bf16[2,768,384]{2,1,0:T(8,128)(2,1)} %get-tuple-element.83), channel_id=1, source_target_pairs={{0,8},{4,0},{8,12},{12,4},{16,24},{20,16},{24,28},{28,20},{1,9},{5... | collective-permute-start | bytes 3538952 | tf_op jit(solution)/shard_map/ppermute | solution.py:975
  348.5 106.1 %collective-permute-start.11 = (bf16[2,768,384]{2,1,0:T(8,128)(2,1)}, bf16[2,768,384]{2,1,0:T(8,128)(2,1)}, u32[]{:S(2)}, u32[]{:S(2)}) collective-permute-start(bf16[2,768,384]{2,1,0:T(8,128)(2,1)} %get-tuple-element.88), channel_id=1, source_target_pairs={{0,4},{4,12},{8,0},{12,8},{16,20},{20,28},{24,16},{28,24},{1,5},{5... | collective-permute-start | bytes 3538952 | tf_op jit(solution)/shard_map/ppermute | solution.py:974
  359.6 20.1 %copy-start.28 = (f32[384,768]{1,0:T(8,128)}, f32[384,768]{1,0:T(8,128)S(1)}, u32[]{:S(2)}) copy-start(f32[384,768]{1,0:T(8,128)S(1)} %convert_add_fusion.2) | copy-start | bytes 3538948
  380.1 44.5 %copy-start.25 = (f32[384,768]{1,0:T(8,128)}, f32[384,768]{1,0:T(8,128)S(1)}, u32[]{:S(2)}) copy-start(f32[384,768]{1,0:T(8,128)S(1)} %fusion.29) | copy-start | bytes 3538948
  430.7 32.5 %collective-permute-start.9 = (bf16[2,768,384]{2,1,0:T(8,128)(2,1)}, bf16[2,768,384]{2,1,0:T(8,128)(2,1)S(1)}, u32[]{:S(2)}, u32[]{:S(2)}) collective-permute-start(bf16[2,768,384]{2,1,0:T(8,128)(2,1)} %add.421), channel_id=1, source_target_pairs={{0,8},{4,0},{8,12},{12,4},{16,24},{20,16},{24,28},{28,20},{1,9},{5... | collective-permute-start | bytes 3538952 | tf_op jit(solution)/shard_map/ppermute | solution.py:975
  438.8 28.1 %collective-permute-start.10 = (bf16[2,768,384]{2,1,0:T(8,128)(2,1)}, bf16[2,768,384]{2,1,0:T(8,128)(2,1)}, u32[]{:S(2)}, u32[]{:S(2)}) collective-permute-start(bf16[2,768,384]{2,1,0:T(8,128)(2,1)} %add.422), channel_id=1, source_target_pairs={{0,4},{4,12},{8,0},{12,8},{16,20},{20,28},{24,16},{28,24},{1,5},{5... | collective-permute-start | bytes 3538952 | tf_op jit(solution)/shard_map/ppermute | solution.py:974
  444.5 22.4 %slice-start.9 = ((s8[4718592]{0:T(1024)(128)(4,1)}), s8[4194304]{0:T(1024)(128)(4,1)S(1)}, s32[]{:S(2)}) async-start(s8[4718592]{0:T(1024)(128)(4,1)} %bitcast.291), calls=%async_computation.9 | async-start | bytes 8388608
  447.7 19.2 %slice-start.10 = ((s8[4718592]{0:T(1024)(128)(4,1)}), s8[524288]{0:T(1024)(128)(4,1)S(1)}, s32[]{:S(2)}) async-start(s8[4718592]{0:T(1024)(128)(4,1)} %bitcast.291), calls=%async_computation.10 | async-start | bytes 1048576
  450.6 21.9 %slice-start.5 = ((s8[4718592]{0:T(1024)(128)(4,1)}), s8[4194304]{0:T(1024)(128)(4,1)S(1)}, s32[]{:S(2)}) async-start(s8[4718592]{0:T(1024)(128)(4,1)} %bitcast.278), calls=%async_computation.5 | async-start | bytes 8388608
  450.6 21.9 %slice-start.7 = ((s8[4718592]{0:T(1024)(128)(4,1)}), s8[4194304]{0:T(1024)(128)(4,1)S(1)}, s32[]{:S(2)}) async-start(s8[4718592]{0:T(1024)(128)(4,1)} %bitcast.289), calls=%async_computation.7 | async-start | bytes 8388608
  (83 other events, 320.7 us)

commit v4 on v3

--- a/solution.py
+++ b/solution.py
@@ -93,30 +93,34 @@
     return pos, at, ({"seq": at(pos + 1)}, {"seq": at(pos - 1)})
 
 
-def gather_kernel(n, parts, count, *refs):
-    sources, outs = refs[:count], refs[count : 2 * count]
-    own_sem, send_sem, recv_sem = refs[2 * count :]
+def gather_kernel(n, parts, *refs):
+    sources, proj_ref, outs = refs[:2], refs[2], refs[3:10]
+    lands, w_buf, bufs = refs[10:12], refs[12], refs[13:18]
+    own_sem, w_sem, send_sem, recv_sem, store_sem = refs[18:]
     pos, at, sides = seq_ring(n)
     me = at(pos)
     greet(sides)
-    own = [
-        pltpu.make_async_copy(sources[a], outs[a].at[me], own_sem.at[a]) for a in range(count)
+    own = [pltpu.make_async_copy(sources[a], lands[a].at[me], own_sem.at[a]) for a in range(2)]
+    weights = [
+        pltpu.make_async_copy(proj_ref.at[number], w_buf.at[i], w_sem.at[i])
+        for i, number in enumerate((0, 1, 2, 4, 5))
     ]
-    for copy in own:
-        copy.start()
-    started, latest = [], {}
-    for step in range(n - 1):
-        for a in range(count):
-            rows = sources[a].shape[0] // 2 // parts
-            for part in range(parts):
+    started, latest, stored = [], {}, []
+
+    def pass_on(step):
+        for part in range(parts):
+            for a in range(2):
+                rows = sources[a].shape[0] // 2 // parts
                 for way in range(2):
                     if step:
                         latest[a, way, part].wait_recv()
+                    if step == n - 1:
+                        continue
                     block = at(pos - step) if way == 0 else at(pos + step)
                     span = pl.ds((way * parts + part) * rows, rows)
                     copy = pltpu.make_async_remote_copy(
-                        src_ref=outs[a].at[block, span] if step else sources[a].at[span],
-                        dst_ref=outs[a].at[block, span],
+                        src_ref=lands[a].at[block, span] if step else sources[a].at[span],
+                        dst_ref=lands[a].at[block, span],
                         send_sem=send_sem.at[a, way, step, part],
                         recv_sem=recv_sem.at[a, way, step, part],
                         device_id=sides[way],
@@ -125,31 +129,68 @@
                     copy.start()
                     started.append(copy)
                     latest[a, way, part] = copy
-    for copy in latest.values():
-        copy.wait_recv()
+
+    def store(source, target, number, step, way):
+        copy = pltpu.make_async_copy(source, target, store_sem.at[number, step, way])
+        copy.start()
+        stored.append(copy)
+
+    def work(step):
+        blocks = (at(pos - step), at(pos + step))
+        for a in range(2):
+            half = sources[a].shape[0] // 2
+            spans = (pl.ds(0, half), pl.ds(half, half))
+            rows = jnp.concatenate([lands[a][blocks[way], spans[way], :] for way in range(2)], axis=0)
+            for i in range(2):
+                buf = bufs[1 + 2 * a + i]
+                made = dot_plain(rows, w_buf[1 + 2 * a + i]).astype(buf.dtype)
+                for way in range(2):
+                    buf[blocks[way], spans[way], :] = made[way * half : (way + 1) * half]
+            for way in range(2):
+                where = (blocks[way], spans[way])
+                store(lands[a].at[where], outs[a].at[where], a, step, way)
+                for i in range(2):
+                    number = 1 + 2 * a + i
+                    store(bufs[number].at[where], outs[2 + number].at[where], 2 + number, step, way)
+
+    pass_on(0)
+    for copy in own + weights:
+        copy.start()
+    for copy in own + weights:
+        copy.wait()
+    bufs[0][...] = dot_plain(lands[0][me], w_buf[0]).astype(bufs[0].dtype)
+    store(bufs[0], outs[2], 2, 0, 0)
+    work(0)
+    for step in range(1, n):
+        pass_on(step)
+        work(step)
     for copy in started:
         copy.wait_send()
-    for copy in own:
+    for copy in stored:
         copy.wait()
 
 
-def ring_gather(arrays, n, number, parts=2):
-    count = len(arrays)
-    copies = (count, 2, n - 1, parts)
+def gather_projected(tokens, memory_rows, proj_in, n, number, parts=2):
+    both = (tokens, memory_rows)
+    copies = (2, 2, n - 1, parts)
+    wide = [(n,) + x.shape for x in both]
+    shapes = wide + [tokens.shape] + [wide[0]] * 2 + [wide[1]] * 2
+    dma = pltpu.SemaphoreType.DMA
     return pl.pallas_call(
-        functools.partial(gather_kernel, n, parts, count),
-        out_shape=[jax.ShapeDtypeStruct((n,) + a.shape, a.dtype) for a in arrays],
-        in_specs=[ANY] * count,
-        out_specs=[ANY] * count,
-        scratch_shapes=[
-            pltpu.SemaphoreType.DMA((count,)),
-            pltpu.SemaphoreType.DMA(copies),
-            pltpu.SemaphoreType.DMA(copies),
-        ],
-        compiler_params=pltpu.CompilerParams(collective_id=number, has_side_effects=True),
+        functools.partial(gather_kernel, n, parts),
+        out_shape=[jax.ShapeDtypeStruct(shape, tokens.dtype) for shape in shapes],
+        in_specs=[ANY] * 3,
+        out_specs=[ANY] * 7,
+        scratch_shapes=[pltpu.VMEM(shape, tokens.dtype) for shape in wide]
+        + [pltpu.VMEM((5,) + proj_in.shape[1:], tokens.dtype)]
+        + [pltpu.VMEM(shape, tokens.dtype) for shape in shapes[2:]]
+        + [dma((2,)), dma((5,)), dma(copies), dma(copies), dma((7, n, 2))],
+        compiler_params=pltpu.CompilerParams(
+            collective_id=number, has_side_effects=True, vmem_limit_bytes=58 << 20
+        ),
         cost_estimate=cost(60),
-        name="ring_gather",
-    )(*arrays)
+        name="gather_projected",
+    )(tokens, memory_rows, proj_in)
 
 
 def scatter_kernel(n, parts, count, *refs):
@@ -271,11 +312,17 @@
     add = lambda *terms: functools.reduce(lambda u, v: u + v, [t.astype(jnp.float32) for t in terms])
     ways = range(2)
     lanes = [(a, way) for a in range(many) for way in ways]
-    rings = [(a, way) for a in range(few) for way in ways]
+    parts = 2
+    rings = [(a, way, part) for part in range(parts) for a in range(few) for way in ways]
 
     def span(ref, way):
         half = ref.shape[-2] // 2
         return pl.ds(way * half, half)
+
+    def piece(lane):
+        a, way, part = lane
+        rows = blocks[a].shape[-2] // 2 // parts
+        return pl.ds(way * parts * rows + part * rows, rows), pl.ds(part * rows, rows)
 
     pairs, own, crossing, ring = {}, {}, {}, {}
     for side in range(2):
@@ -288,7 +335,7 @@
                     xs[a].at[1 - core, place, where, rows],
                     twins[a].at[side, way, step],
                     pair_sem,
-                    (0, side) + lane + (step,),
+                    (0, side) + lane + (0, step),
                     peer,
                 )
                 own[side, lane, step] = fetch(
@@ -298,37 +345,42 @@
                 )
         if side == 0:
             for lane in rings:
-                a, way = lane
+                a, way, part = lane
+                wide, thin = piece(lane)
                 ring[lane] = push(
-                    blocks[a].at[block(way, 0), span(blocks[a], way)],
-                    got_bufs[a].at[way, 0],
+                    blocks[a].at[block(way, 0), wide],
+                    got_bufs[a].at[way, 0, thin],
                     far_sem,
                     lane + (0,),
                     sides[way],
                 )
-            near = {
-                (lane, step): fetch(
-                    blocks[lane[0]].at[block(lane[1], step), span(blocks[lane[0]], lane[1])],
-                    own_bufs[lane[0]].at[lane[1], step - 1],
-                    near_sem.at[lane + (step - 1,)],
-                )
-                for step in range(1, n)
-                for lane in rings
-            }
-
-    def scatter(step):
+            near = {}
+            for step in range(1, n):
+                for lane in rings:
+                    a, way, part = lane
+                    wide, thin = piece(lane)
+                    near[lane, step] = fetch(
+                        blocks[a].at[block(way, step), wide],
+                        own_bufs[a].at[way, step - 1, thin],
+                        near_sem.at[lane + (step - 1,)],
+                    )
+
+    def scatter(step, which):
         for lane in rings:
-            a, way = lane
+            a, way, part = lane
+            if part != which:
+                continue
+            wide, thin = piece(lane)
             near[lane, step].wait()
             ring[lane].wait_recv()
-            total = add(got_bufs[a][way, step - 1], own_bufs[a][way, step - 1])
+            total = add(got_bufs[a][way, step - 1, thin], own_bufs[a][way, step - 1, thin])
             if step == n - 1:
-                sums[a][span(sums[a], way)] = total.astype(sums[a].dtype)
+                sums[a][wide] = total.astype(sums[a].dtype)
             else:
-                got_bufs[a][way, step - 1] = total.astype(got_bufs[a].dtype)
+                got_bufs[a][way, step - 1, thin] = total.astype(got_bufs[a].dtype)
                 ring[lane] = push(
-                    got_bufs[a].at[way, step - 1],
-                    got_bufs[a].at[way, step],
+                    got_bufs[a].at[way, step - 1, thin],
+                    got_bufs[a].at[way, step, thin],
                     far_sem,
                     lane + (step,),
                     sides[way],
@@ -346,13 +398,15 @@
                 mines[a].at[0, way, step],
                 crosses[a].at[way, step],
                 cross_sem,
-                (0,) + lane + (step,),
+                (0,) + lane + (0, step),
                 over,
             )
-        if step == n // 2:
-            scatter(1)
+        if step >= n - 2:
+            scatter(1, step - n + 2)
     latest = {}
     for step in range(n):
+        if step + 2 < n:
+            scatter(step + 2, 0)
         for lane in lanes:
             a, way = lane
             own[1, lane, step].wait()
@@ -368,38 +422,67 @@
                     mines[a].at[1, way, step],
                     gots[a].at[way, step],
                     ring_sem,
-                    (0,) + lane + (step,),
+                    (0,) + lane + (0, step),
                     sides[way],
                 )
-        if 2 <= step + 2 < n:
-            scatter(step + 2)
+        if step + 2 < n:
+            scatter(step + 2, 1)
     keep, done = [], []
-
-    def hand_on(step):
-        for lane in lanes:
-            a, way = lane
-            crossing[lane, step].wait_recv()
-            where = at(pos - step) if way == 0 else at(pos + step)
-            place = outs[a].at[core, 1 - chip, where, span(outs[a], way)]
-            done.append(push(place, place, pair_sem, (1, 1) + lane + (step,), peer))
+    streams = []
+    for a, way in lanes:
+        half = xs[a].shape[-2] // 2
+        if half % 48 == 0:
+            some = half * 2 // 3
+            streams += [
+                (a, way, 0, way * half, some, False, True),
+                (a, way, 1, way * half + some, half - some, False, False),
+                (a, way, 2, way * half + some, half - some, True, False),
+            ]
+        else:
+            streams.append((a, way, 0, way * half, half, False, True))
+    latest, crossing = {}, {}
+
+    def target_of(stream, step, other):
+        a, way, number, first, size = stream[:5]
+        where = at(pos - step) if way == 0 else at(pos + step)
+        return outs[a].at[core, 1 - chip if other else chip, where, pl.ds(first, size)]
+
+    def hand_on(stream, step):
+        a, way, number = stream[:3]
+        crossing[stream, step].wait_recv()
+        target = target_of(stream, step, True)
+        done.append(push(target, target, pair_sem, (1, 1, a, way, number, step), peer))
 
     for step in range(n):
-        for lane in lanes:
-            a, way = lane
+        for stream in streams:
+            a, way, number, first, size, other, always = stream
             if step:
-                latest[lane].wait_recv()
-            where = at(pos - step) if way == 0 else at(pos + step)
-            target = outs[a].at[core, chip, where, span(outs[a], way)]
-            source = target if step else mines[a].at[1, way, n - 1]
+                latest[stream].wait_recv()
+            target = target_of(stream, step, other)
+            if step or other:
+                source = target
+            else:
+                source = mines[a].at[1, way, n - 1, pl.ds(first - way * (xs[a].shape[-2] // 2), size)]
+            if step == 0 and other:
+                crossing[streams[streams.index(stream) - 1], 0].wait_recv()
             if step < n - 1:
-                latest[lane] = push(source, target, ring_sem, (1,) + lane + (step,), sides[way])
-            crossing[lane, step] = push(source, target, cross_sem, (1,) + lane + (step,), over)
-            done.append(push(source, target, pair_sem, (1, 0) + lane + (step,), peer))
-            if step == 0:
-                keep.append(fetch(source, target, own_sem.at[(0,) + lane + (0,)]))
+                latest[stream] = push(
+                    source, target, ring_sem, (1, a, way, number, step), sides[way]
+                )
+            if not other and (always or step == 0):
+                crossing[stream, step] = push(
+                    source, target, cross_sem, (1, a, way, number, step), over
+                )
+            done.append(push(source, target, pair_sem, (1, 0, a, way, number, step), peer))
+            if step == 0 and not other:
+                keep.append(fetch(source, target, own_sem.at[0, a, way, number]))
         if step:
-            hand_on(step - 1)
-    hand_on(n - 1)
+            for stream in streams:
+                if stream[6]:
+                    hand_on(stream, step - 1)
+    for stream in streams:
+        if stream[6]:
+            hand_on(stream, n - 1)
     for copy in keep:
         copy.wait()
     for copy in done:
@@ -411,12 +494,12 @@
 def finish(blocks, rows_in, small, n, m, number):
     rows, cols = rows_in.shape
     each = rows // (4 * n)
-    if m != 4 or rows % (4 * n * 32) or small.size > 4 * n * 16 * TILE:
+    if m != 4 or rows % (4 * n * 32) or small.shape[0] > 4 * n * 16:
         return (
             ring_scatter(blocks, n, number, jnp.float32),
             *lax.psum((rows_in, small), ("seq", "exp")),
         )
-    padded = jnp.pad(small, (0, 4 * n * 16 * TILE - small.size))
+    padded = jnp.pad(small, ((0, 4 * n * 16 - small.shape[0]), (0, 0)))
     arrays = [rows_in.reshape(2, 2, n, each, cols), padded.reshape(2, 2, n, 16, TILE)]
     few, many = len(blocks), len(arrays)
     halves = [(x.shape[-2] // 2, x.shape[-1], x.dtype) for x in blocks + arrays]
@@ -434,12 +517,12 @@
         + two * 2
         + one * 2
         + [
-            dma((few, 2, n)),
-            dma((2, few, 2, n)),
+            dma((few, 2, 2, n)),
+            dma((2, few, 2, 2, n)),
             dma((2, many, 2, n)),
-            dma((2, 2, 2, many, 2, n)),
-            dma((2, 2, many, 2, n)),
-            dma((2, 2, many, 2, n)),
+            dma((2, 2, 2, many, 2, 3, n)),
+            dma((2, 2, many, 2, 3, n)),
+            dma((2, 2, many, 2, 3, n)),
         ],
         compiler_params=pltpu.CompilerParams(
             collective_id=number, has_side_effects=True, vmem_limit_bytes=58 << 20
@@ -447,68 +530,7 @@
         cost_estimate=cost(120),
         name="finish",
     )(*blocks, *arrays)
-    return results[:few], results[few].reshape(rows, cols), results[-1].reshape(-1)[: small.size]
-
-
-QUAD = 4
-
-
-def quad_moves(n):
-    ring = (0, 1, 3, 2)
-    step = lambda i, by: i - i % QUAD + ring[(ring.index(i % QUAD) + by) % QUAD]
-    return [(i, step(i, 1)) for i in range(n)], [(i, step(i, -1)) for i in range(n)]
-
-
-def spread_kernel(n, m, back, x_ref, out_ref, own_sem, send_sem, recv_sem):
-    seq, exp = lax.axis_index("seq"), lax.axis_index("exp")
-    groups = n // QUAD
-    moves = [(g, k) for g in reversed(range(groups)) for k in range(m) if g or k]
-
-    def target(g, k):
-        shift = n - g * QUAD if back else g * QUAD
-        return lax.rem(seq + shift, n), lax.rem(exp + k, m)
-
-    greet([dict(zip(("seq", "exp"), target(g, k))) for g, k in moves])
-    started = []
-    for g, k in moves:
-        to_seq, to_exp = target(g, k)
-        copy = pltpu.make_async_remote_copy(
-            src_ref=x_ref.at[g, to_exp] if back else x_ref.at[to_exp],
-            dst_ref=out_ref.at[g, exp],
-            send_sem=send_sem.at[g, k],
-            recv_sem=recv_sem.at[g, k],
-            device_id={"seq": to_seq, "exp": to_exp},
-            device_id_type=MESH,
-        )
-        copy.start()
-        started.append(copy)
-    own = pltpu.make_async_copy(
-        x_ref.at[0, exp] if back else x_ref.at[exp], out_ref.at[0, exp], own_sem
-    )
-    own.start()
-    for copy in started:
-        copy.wait_recv()
-    for copy in started:
-        copy.wait_send()
-    own.wait()
-
-
-def spread(x, n, m, back, number):
-    groups = n // QUAD
-    return pl.pallas_call(
-        functools.partial(spread_kernel, n, m, back),
-        out_shape=jax.ShapeDtypeStruct((groups,) + x.shape[-3:], x.dtype),
-        in_specs=[ANY],
-        out_specs=ANY,
-        scratch_shapes=[
-            pltpu.SemaphoreType.DMA,
-            pltpu.SemaphoreType.DMA((groups, m)),
-            pltpu.SemaphoreType.DMA((groups, m)),
-        ],
-        compiler_params=pltpu.CompilerParams(collective_id=number, has_side_effects=True),
-        cost_estimate=cost(70),
-        name="spread_back" if back else "spread",
-    )(x)
+    return results[:few], results[few].reshape(rows, cols), results[-1].reshape(-1, TILE)
 
 
 def dot_last(a, b):
@@ -548,11 +570,11 @@
     return jnp.concatenate(rows, axis=0)
 
 
-def edge_bias(tile_ref, rows):
+def edge_bias(tiles, rows):
     edge = []
     for h in range(2):
         first = jnp.concatenate(
-            [jnp.zeros((rows - TILE, TILE), jnp.float32), tile_ref[h][:, :TILE].T], axis=0
+            [jnp.zeros((rows - TILE, TILE), jnp.float32), tiles[h][:, :TILE].T], axis=0
         )
         edge += [first, jnp.zeros((rows, rows - TILE), jnp.float32)]
     return jnp.concatenate(edge, axis=1)
@@ -560,7 +582,7 @@
 
 def attend_kernel(causal, block, s_ref, q_ref, k_ref, v_ref, *refs):
     if causal:
-        tile_ref, low_ref, wide_ref, lse_ref, acc_ref, top_ref = refs
+        line_ref, low_ref, wide_ref, lse_ref, acc_ref, top_ref = refs
     else:
         low_ref, wide_ref, lse_ref, acc_ref, top_ref = refs
     rows = q_ref.shape[0]
@@ -589,15 +611,16 @@
     if causal:
         s = s_ref[0]
         count = rows // TILE
+        tiles = [bias_tile(line_ref, h) for h in range(2)]
         visit(
             pl.multiple_of(s * block, block),
-            jnp.concatenate([own_bias(tile_ref[h], count).T for h in range(2)], axis=1),
+            jnp.concatenate([own_bias(tiles[h], count).T for h in range(2)], axis=1),
             True,
         )
 
         @pl.when(s > 0)
         def _():
-            visit(pl.multiple_of((s - 1) * block, block), edge_bias(tile_ref, rows), False)
+            visit(pl.multiple_of((s - 1) * block, block), edge_bias(tiles, rows), False)
 
         def far(j, carry):
             visit(pl.multiple_of(j * block, block), None, False)
@@ -621,15 +644,15 @@
     lse_ref[0] = jnp.concatenate([lse[:, :rows], lse[:, rows:]], axis=0)
 
 
-def attend(seq_at, queries, keys, values, tiles):
+def attend(seq_at, queries, keys, values, lines):
     rows, total = queries.shape[0], keys.shape[0]
-    causal = tiles is not None
+    causal = lines is not None
     block = rows if causal else math.gcd(total, 512)
     pair = pl.BlockSpec((rows, TILE), lambda g: (0, g))
     long = pl.BlockSpec((total, TILE), lambda g: (0, g))
     extra, specs = [], []
     if causal:
-        extra, specs = [tiles], [pl.BlockSpec((2,) + tiles.shape[1:], lambda g: (g, 0, 0))]
+        extra, specs = [lines], [pl.BlockSpec((1,) + lines.shape[1:], lambda g: (g, 0, 0))]
     return pl.pallas_call(
         functools.partial(attend_kernel, causal, block),
         grid=(PAIRS,),
@@ -652,7 +675,7 @@
 
 def attend_back_kernel(causal, block, s_ref, q_ref, k_ref, v_ref, up_ref, wide_ref, lse_ref, *refs):
     if causal:
-        tile_ref, dq_ref, dk_ref, dv_ref, near_ref, sum_ref, acc_ref = refs
+        line_ref, dq_ref, dk_ref, dv_ref, near_ref, sum_ref, acc_ref = refs
     else:
         dq_ref, dk_ref, dv_ref, acc_ref = refs
     rows = q_ref.shape[0]
@@ -692,9 +715,10 @@
     if causal:
         s = s_ref[0]
         count = rows // TILE
+        tiles = [bias_tile(line_ref, h) for h in range(2)]
         ds = visit(
             pl.multiple_of(s * block, block),
-            jnp.concatenate([own_bias(tile_ref[h], count).T for h in range(2)], axis=1),
+            jnp.concatenate([own_bias(tiles[h], count).T for h in range(2)], axis=1),
             True,
         )
         for h in range(2):
@@ -709,7 +733,7 @@
 
         @pl.when(s > 0)
         def _():
-            ds = visit(pl.multiple_of((s - 1) * block, block), edge_bias(tile_ref, rows), False)
+            ds = visit(pl.multiple_of((s - 1) * block, block), edge_bias(tiles, rows), False)
             for h in range(2):
                 near_ref[h, :TILE] += ds[rows - TILE :, h * rows : h * rows + TILE].astype(
                     jnp.float32
@@ -738,16 +762,16 @@
     dq_ref[...] = (dq.T * scale_factor).astype(dq_ref.dtype)
 
 
-def attend_back(seq_at, queries, keys, values, upstream, wide, lse, tiles):
+def attend_back(seq_at, queries, keys, values, upstream, wide, lse, lines):
     rows, total = queries.shape[0], keys.shape[0]
-    causal = tiles is not None
+    causal = lines is not None
     block = rows if causal else math.gcd(total, 512)
     pair = pl.BlockSpec((rows, TILE), lambda g: (0, g))
     long = pl.BlockSpec((total, TILE), lambda g: (0, g))
     line = pl.BlockSpec((1, 2, rows), lambda g: (g, 0, 0))
     extra, specs, shapes, out_specs = [], [], [], []
     if causal:
-        extra, specs = [tiles], [pl.BlockSpec((2,) + tiles.shape[1:], lambda g: (g, 0, 0))]
+        extra, specs = [lines], [pl.BlockSpec((1,) + lines.shape[1:], lambda g: (g, 0, 0))]
         shapes = [
             jax.ShapeDtypeStruct((HEADS, 2 * TILE, TILE), jnp.float32),
             jax.ShapeDtypeStruct((PAIRS, 2, rows), jnp.float32),
@@ -771,17 +795,19 @@
     )(seq_at, queries, keys, values, upstream, wide, lse, *extra)
 
 
-def bias_tiles(bias_table):
-    distance = (
-        TILE
-        + jnp.arange(TILE, dtype=jnp.int32)[:, None]
-        - jnp.arange(2 * TILE, dtype=jnp.int32)[None, :]
-    )
+def bias_lines(bias_table):
+    at = jnp.arange(3 * TILE, dtype=jnp.int32)
+    distance = jnp.where(at <= 2 * TILE, TILE - at, 4 * TILE - at)
     table = (bias_table - bias_table[NBUCKET - 1 :]) * log2e
-    terms = jnp.broadcast_to(table[0][:, None, None], (HEADS, TILE, 2 * TILE))
+    terms = jnp.broadcast_to(table[0][:, None], (HEADS, 3 * TILE))
     for number, threshold in enumerate(bucket_edges()):
-        terms = jnp.where((distance >= threshold)[None], table[number + 1][:, None, None], terms)
-    return jnp.where((distance >= 0)[None], terms, masked_score)
+        terms = jnp.where((distance >= threshold)[None], table[number + 1][:, None], terms)
+    return jnp.where((distance >= 0)[None], terms, masked_score).reshape(PAIRS, 2, 3 * TILE)
+
+
+def bias_tile(line_ref, h):
+    line = jnp.broadcast_to(line_ref[0, h : h + 1, :], (TILE, 3 * TILE))
+    return pltpu.roll(line, 0, 1, stride=1, stride_axis=0)[:, : 2 * TILE]
 
 
 def bias_gradient(near, sums):
@@ -805,52 +831,222 @@
     return table + jnp.where(last, far[None, :], 0.0)
 
 
-def expert_kernel(*refs):
-    rows_ref, maps = refs[0], refs[1 : 1 + 2 * QUAD]
-    part_ref, grads = refs[1 + 2 * QUAD], refs[2 + 2 * QUAD :]
-    shape = rows_ref.shape
-    rows = rows_ref[...].reshape(shape[0] * shape[1] * shape[2], shape[3])
-    tokens, upstream = rows[:, :D], rows[:, D:]
+def expert_kernel(n, m, slots, *refs):
+    x_ref, maps, result_ref, grads = refs[0], refs[1:9], refs[9], refs[10:16]
+    rows, parts, backs, up_all, down_all, act_all, du_all = refs[16:23]
+    grad_bufs, far_bufs = refs[23:31], refs[31:33]
+    map_sem, own_sem, grad_sem, go_sem, back_sem, term_sem = refs[33:]
+    seq, exp = lax.axis_index("seq"), lax.axis_index("exp")
+    groups, count = n // QUAD, x_ref.shape[1] // slots
+    batch = max(1, 128 // slots)
+    far = [(g, k) for g in range(1, groups) for k in range(m)]
+    moves = far + [(0, k) for k in range(1, m)]
+    source_of = lambda k: lax.rem(exp + m - k, m)
+
+    def push(source, target, sems, g, k, to_seq, to_exp):
+        copy = pltpu.make_async_remote_copy(
+            src_ref=source,
+            dst_ref=target,
+            send_sem=sems.at[0, g, k],
+            recv_sem=sems.at[1, g, k],
+            device_id={"seq": to_seq, "exp": to_exp},
+            device_id_type=MESH,
+        )
+        copy.start()
+        return copy
+
+    def place(g, k):
+        return lax.rem(seq + g * QUAD, n), lax.rem(exp + k, m)
+
+    to_next, to_last = quad_moves(n)
+    side = {"next": look_up(seq, [b for _, b in to_next]), "last": look_up(seq, [b for _, b in to_last])}
+    greet(
+        [dict(zip(("seq", "exp"), place(g, k))) for g, k in moves]
+        + [{"seq": side["next"], "exp": exp}, {"seq": side["last"], "exp": exp}]
+    )
+    going = {}
+    for g, k in moves:
+        to_seq, to_exp = place(g, k)
+        going[g, k] = push(x_ref.at[to_exp], rows.at[g, exp], go_sem, g, k, to_seq, to_exp)
+    own = pltpu.make_async_copy(x_ref.at[exp], rows.at[0, exp], own_sem.at[0])
+    own.start()
+    fetched = []
+    for j in range(QUAD):
+        for at, (source, target) in enumerate(((maps[2 * j], up_all), (maps[2 * j + 1], down_all))):
+            copy = pltpu.make_async_copy(source, target.at[j], map_sem.at[at, j])
+            copy.start()
+            fetched.append(copy)
+    for copy in fetched:
+        copy.wait()
+    own.wait()
     slope = math.sqrt(2.0 / math.pi)
-    result = back = None
-    for j in range(QUAD):
-        up_map, down_map = maps[2 * j][0], maps[2 * j + 1][0]
-        u = dot_plain(tokens, up_map)
-        square = u * u
-        bend = jnp.tanh(slope * (u + 0.044715 * (square * u)))
-        half = 0.5 * (1.0 + bend)
-        act = (u * half).astype(tokens.dtype)
-        rise = half + 0.5 * u * (1.0 - bend * bend) * (slope * (1.0 + 3 * 0.044715 * square))
-        du = (dot_plain(upstream, down_map) * rise).astype(tokens.dtype)
-        y, dn = dot_last(act, down_map), dot_last(du, up_map)
-        result = y if result is None else result + y
-        back = dn if back is None else back + dn
-        for ref, left, right in ((grads[2 * j], tokens, du), (grads[2 * j + 1], upstream, act)):
-            ref[0] = dot_first(left, right).astype(ref.dtype)
-    part_ref[...] = (
-        jnp.concatenate([result, back], axis=1).astype(part_ref.dtype).reshape(part_ref.shape)
-    )
-
-
-def run_experts(rows, maps):
-    groups, m, slots, width = rows.shape
+    coming = {}
+
+    def work(g, first, last):
+        for k in range(first, last):
+            if g or k:
+                going[g, k].wait_recv()
+        size = (last - first) * slots
+        base = (g * m + first) * slots
+
+        def one(e, carry):
+            start = pl.multiple_of(e * slots, slots)
+            piece = jnp.concatenate(
+                [rows[g, source_of(k), pl.ds(start, slots), :] for k in range(first, last)], axis=0
+            )
+            tokens, upstream = piece[:, :D], piece[:, D:]
+            result = back = None
+            for j in range(QUAD):
+                up_map, down_map = up_all[j, e], down_all[j, e]
+                u = dot_plain(tokens, up_map)
+                square = u * u
+                bend = jnp.tanh(slope * (u + 0.044715 * (square * u)))
+                half = 0.5 * (1.0 + bend)
+                act = (u * half).astype(tokens.dtype)
+                rise = half + 0.5 * u * (1.0 - bend * bend) * (
+                    slope * (1.0 + 3 * 0.044715 * square)
+                )
+                du = (dot_plain(upstream, down_map) * rise).astype(tokens.dtype)
+                act_all[e, j, base : base + size] = act
+                du_all[e, j, base : base + size] = du
+                y, dn = dot_last(act, down_map), dot_last(du, up_map)
+                result = y if result is None else result + y
+                back = dn if back is None else back + dn
+            for i, k in enumerate(range(first, last)):
+                span = slice(i * slots, (i + 1) * slots)
+                where = (g, source_of(k), pl.ds(start, slots))
+                parts[where + (slice(0, D),)] = result[span].astype(parts.dtype)
+                parts[where + (slice(D, 2 * D),)] = back[span].astype(parts.dtype)
+            return carry
+
+        lax.fori_loop(0, count, one, 0)
+        for k in range(first, last):
+            if g or k:
+                source = source_of(k)
+                coming[g, k] = push(
+                    parts.at[g, source],
+                    backs.at[g, exp],
+                    back_sem,
+                    g,
+                    k,
+                    lax.rem(seq + n - g * QUAD, n),
+                    source,
+                )
+
+    work(0, 0, m)
+    for g in range(1, groups):
+        for first in range(0, m, batch):
+            work(g, first, min(m, first + batch))
+
+    total = groups * m * slots
+
+    def weigh(j):
+        def one(e, carry):
+            start = pl.multiple_of(e * slots, slots)
+            piece = jnp.concatenate(
+                [
+                    rows[g, source_of(k), pl.ds(start, slots), :]
+                    for g in range(groups)
+                    for k in range(m)
+                ],
+                axis=0,
+            )
+            tokens, upstream = piece[:, :D], piece[:, D:]
+            up_buf, down_buf = grad_bufs[2 * j], grad_bufs[2 * j + 1]
+            up_buf[e] = dot_first(tokens, du_all[e, j, :total]).astype(up_buf.dtype)
+            down_buf[e] = dot_first(upstream, act_all[e, j, :total]).astype(down_buf.dtype)
+            return carry
+
+        lax.fori_loop(0, count, one, 0)
+
+    def term(source, target, number, to):
+        return push(source, target, term_sem, 0, number, side[to], exp)
+
+    def store(source, number):
+        copy = pltpu.make_async_copy(source, grads[number], grad_sem.at[number])
+        copy.start()
+        return copy
+
+    weigh(3)
+    terms_out = [
+        term(grad_bufs[6], far_bufs[0], 0, "next"),
+        term(grad_bufs[7], far_bufs[1], 1, "last"),
+    ]
+    weigh(1)
+    weigh(2)
+    weigh(0)
+    stored = [
+        store(grad_bufs[i], number) for number, i in ((0, 0), (1, 1), (4, 2), (5, 5))
+    ]
+    for number, (buf, far_buf) in enumerate(((grad_bufs[4], far_bufs[0]), (grad_bufs[3], far_bufs[1]))):
+        terms_out[number].wait_recv()
+        buf[...] = (buf[...].astype(jnp.float32) + far_buf[...].astype(jnp.float32)).astype(buf.dtype)
+        stored.append(store(buf, 2 + number))
+    for k in range(m):
+        where = source_of(k)
+        terms = []
+        for g in range(groups):
+            back_k = (m - k) % m
+            if g == 0 and k == 0:
+                terms.append(parts[0, exp])
+            else:
+                coming[g, back_k].wait_recv()
+                terms.append(backs[g, where])
+        total_row = terms[0].astype(jnp.float32)
+        for term in terms[1:]:
+            total_row = total_row + term.astype(jnp.float32)
+        result_ref[where] = total_row.astype(result_ref.dtype)
+    for copy in stored:
+        copy.wait()
+    for copy in terms_out:
+        copy.wait_send()
+    for copies in (going, coming):
+        for copy in copies.values():
+            copy.wait_send()
+
+
+def run_experts(x, maps, n, m, slots, number):
+    groups = n // QUAD
     count, _, hidden = maps[0].shape
-    block = pl.BlockSpec((groups, m, slots // count, width), lambda e: (0, 0, e, 0))
-    weight = pl.BlockSpec((1, D, hidden), lambda e: (e, 0, 0))
+    total = groups * m * slots
+    big = pltpu.VMEM((groups,) + x.shape, x.dtype)
+    stack = pltpu.VMEM((QUAD,) + maps[0].shape, x.dtype)
+    kept = pltpu.VMEM((count, QUAD, total, hidden), x.dtype)
+    grads = [(w.shape, jnp.float32 if i < 2 else jnp.bfloat16) for i, w in enumerate(maps)]
+    dma = pltpu.SemaphoreType.DMA
     return pl.pallas_call(
-        expert_kernel,
-        grid=(count,),
-        out_shape=[jax.ShapeDtypeStruct(rows.shape, rows.dtype)]
+        functools.partial(expert_kernel, n, m, slots),
+        out_shape=[jax.ShapeDtypeStruct(x.shape, x.dtype)]
+        + [jax.ShapeDtypeStruct(shape, dtype) for shape, dtype in grads[:6]],
+        in_specs=[ANY] * (1 + len(maps)),
+        out_specs=[pl.BlockSpec(memory_space=pltpu.VMEM)] + [ANY] * 6,
+        scratch_shapes=[big] * 3
+        + [stack] * 2
+        + [kept] * 2
+        + [pltpu.VMEM(shape, dtype) for shape, dtype in grads + grads[6:]]
         + [
-            jax.ShapeDtypeStruct(w.shape, jnp.float32 if i < 2 else jnp.bfloat16)
-            for i, w in enumerate(maps)
+            dma((2, QUAD)),
+            dma((1,)),
+            dma((6,)),
+            dma((2, groups, m)),
+            dma((2, groups, m)),
+            dma((2, 1, 2)),
         ],
-        in_specs=[block] + [weight] * len(maps),
-        out_specs=[block] + [weight] * len(maps),
-        compiler_params=pltpu.CompilerParams(vmem_limit_bytes=58 << 20),
-        cost_estimate=cost(28),
+        compiler_params=pltpu.CompilerParams(
+            collective_id=number, has_side_effects=True, vmem_limit_bytes=60 << 20
+        ),
+        cost_estimate=cost(150),
         name="run_experts",
-    )(rows, *maps)
+    )(x, *maps)
+
+
+QUAD = 4
+
+
+def quad_moves(n):
+    ring = (0, 1, 3, 2)
+    step = lambda i, by: i - i % QUAD + ring[(ring.index(i % QUAD) + by) % QUAD]
+    return [(i, step(i, 1)) for i in range(n)], [(i, step(i, -1)) for i in range(n)]
 
 
 def project(source, matrix):
@@ -889,22 +1085,23 @@
     token_count = tokens.shape[0]
     seq_at = lax.axis_index("seq").astype(jnp.int32).reshape(1)
     normed_self = rms_apply(tokens, gain_rows[0]).astype(jnp.bfloat16)
-    tiles = bias_tiles(rel_bias)
-
-    normed_all, memory_all = ring_gather([normed_self, memory_rows], n, 1)
+    lines = bias_lines(rel_bias)
+
+    normed_all, memory_all, queries, key_all, value_all, memory_key_all, memory_value_all = (
+        gather_projected(normed_self, memory_rows, proj_in, n, 1)
+    )
     to_next, to_last = quad_moves(n)
     in_own, out_own, normed_all = lax.optimization_barrier((expert_in, expert_out, normed_all))
     in_last, out_last = (lax.ppermute(w, "seq", to_next) for w in (in_own, out_own))
     in_next, out_next = (lax.ppermute(w, "seq", to_last) for w in (in_own, out_own))
     normed_all = normed_all.reshape(n * token_count, D)
     memory_all = memory_all.reshape(n * memory_count, D)
-    queries = project(normed_self, proj_in[0])
-    key_all = project(normed_all, proj_in[1])
-    value_all = project(normed_all, proj_in[2])
-    memory_key_all = project(memory_all, proj_in[4])
-    memory_value_all = project(memory_all, proj_in[5])
+    key_all, value_all = (x.reshape(n * token_count, D) for x in (key_all, value_all))
+    memory_key_all, memory_value_all = (
+        x.reshape(n * memory_count, D) for x in (memory_key_all, memory_value_all)
+    )
     attended_self_low, attended_self, lse_self = attend(
-        seq_at, queries, key_all, value_all, tiles
+        seq_at, queries, key_all, value_all, lines
     )
     attended_self_low, in_last, out_next = lax.optimization_barrier(
         (attended_self_low, in_last, out_next)
@@ -963,18 +1160,11 @@
     )
     sent_rows, in_far, out_far = lax.optimization_barrier((sent_rows, in_far, out_far))
     maps = [in_own, out_own, in_last, out_last, in_next, out_next, in_far, out_far]
-    received = spread(sent_rows, n, m, False, 2)
-    parts, *terms = run_experts(received, maps)
-    returned = spread(parts, n, m, True, 3)
-    gin_own, gout_own, gin_last, gout_last, gin_next, gout_next, gin_far, gout_far = terms
-    gin_far = lax.ppermute(gin_far, "seq", to_next)
-    gout_far = lax.ppermute(gout_far, "seq", to_last)
-    returned, gin_far, gout_far = lax.optimization_barrier((returned, gin_far, gout_far))
-    gin_next, gout_last = gin_next + gin_far, gout_last + gout_far
-    gin_next, gout_next = (lax.ppermute(w, "seq", to_next) for w in (gin_next, gout_next))
-    gin_last, gout_last = (lax.ppermute(w, "seq", to_last) for w in (gin_last, gout_last))
-    returned = jnp.sum(returned.astype(jnp.float32), axis=0).astype(jnp.bfloat16)
+    returned, *terms = run_experts(sent_rows, maps, n, m, slots, 2)
     returned = returned.reshape(expert_count * slots, 2 * D)
+    gin_own, gout_own, gin_next, gout_last, gin_last, gout_next = terms
+    gout_next = lax.ppermute(gout_next, "seq", to_next)
+    gin_last = lax.ppermute(gin_last, "seq", to_last)
     routed = jnp.dot(dispatch, returned, preferred_element_type=jnp.float32)
     combined, grad_mixed = routed[:, :D], routed[:, D:]
     output = (after_cross + gate_prob[:, None] * combined).astype(jnp.bfloat16)
@@ -1003,6 +1193,11 @@
         lse_cross,
         None,
     )
+    grad_cross_query, gin_last, gout_next, gin_next, gout_last = lax.optimization_barrier(
+        (grad_cross_query, gin_last, gout_next, gin_next, gout_last)
+    )
+    gin_next = lax.ppermute(gin_next, "seq", to_next)
+    gout_last = lax.ppermute(gout_last, "seq", to_last)
     grad_query_cross = weight_grad(normed_cross, grad_cross_query)
     grad_self_part, grad_gain_cross = rms_backward(
         after_self, gain_rows[1], input_grad(grad_cross_query, proj_in[3])
@@ -1015,6 +1210,16 @@
     grad_self_low = grad_after_self.astype(jnp.bfloat16)
     grad_out_self = weight_grad(attended_self_low, grad_self_low)
     grad_attended_self = input_grad(grad_self_low, proj_out[0]).astype(jnp.bfloat16)
+    early = [
+        grad_query_cross,
+        weight_grad(memory_all, grad_memory_keys),
+        weight_grad(memory_all, grad_memory_values),
+        grad_out_self,
+        grad_out_cross,
+    ]
+    grad_attended_self, grad_memory_part, *early = lax.optimization_barrier(
+        (grad_attended_self, grad_memory_part, *early)
+    )
     grad_self_query, grad_keys, grad_values, near, sums = attend_back(
         seq_at,
         queries,
@@ -1023,49 +1228,55 @@
         grad_attended_self,
         attended_self,
         lse_self,
-        tiles,
-    )
-    grad_keys, grad_values, gin_last, gout_last, gin_next, gout_next = lax.optimization_barrier(
-        (grad_keys, grad_values, gin_last, gout_last, gin_next, gout_next)
+        lines,
+    )
+    grad_self_query, grad_keys, grad_values, near, sums, gout_last, gin_next = (
+        lax.optimization_barrier(
+            (grad_self_query, grad_keys, grad_values, near, sums, gout_last, gin_next)
+        )
     )
     grad_expert_in = gin_own + gin_last.astype(jnp.float32) + gin_next.astype(jnp.float32)
     grad_expert_out = gout_own + gout_last.astype(jnp.float32) + gout_next.astype(jnp.float32)
     grad_table = bias_gradient(near, sums)
     grad_normed_query = input_grad(grad_self_query, proj_in[0])
-    grad_normed_part = input_grad(grad_keys, proj_in[1]) + input_grad(grad_values, proj_in[2])
+    grad_normed_part = (
+        input_grad(grad_keys, proj_in[1]) + input_grad(grad_values, proj_in[2])
+    ).astype(jnp.bfloat16)
+    grad_normed_part = lax.optimization_barrier(grad_normed_part)
     grad_gain_self = (
-        jnp.sum(grad_normed_part * normed_all.astype(jnp.float32), axis=0)
+        jnp.sum(grad_normed_part.astype(jnp.float32) * normed_all.astype(jnp.float32), axis=0)
         + jnp.sum(grad_normed_query * normed_self.astype(jnp.float32), axis=0)
     ) / gain_rows[0]
 
-    grads = jnp.stack(
+    grads = jnp.concatenate(
         [
             weight_grad(normed_self, grad_self_query),
             weight_grad(normed_all, grad_keys),
             weight_grad(normed_all, grad_values),
-            grad_query_cross,
-            weight_grad(memory_all, grad_memory_keys),
-            weight_grad(memory_all, grad_memory_values),
-            grad_out_self,
-            grad_out_cross,
+            *early,
         ]
     )
     grad_gains = jnp.stack([grad_gain_self, grad_gain_cross, grad_gain_mix])
+    small = [
+        grad_gains.reshape(-1, TILE),
+        grad_router.T.reshape(-1, TILE),
+        jnp.pad(grad_table, ((0, 0), (0, TILE - HEADS))),
+    ]
+    ends = [small[0].shape[0], small[0].shape[0] + small[1].shape[0]]
     (grad_normed_own, grad_memory), grads, small = finish(
         [
-            grad_normed_part.astype(jnp.bfloat16).reshape(n, token_count, D),
+            grad_normed_part.reshape(n, token_count, D),
             grad_memory_part.reshape(n, memory_count, D),
         ],
-        grads.reshape(-1, D),
-        jnp.concatenate([grad_gains.reshape(-1), grad_table.reshape(-1), grad_router.reshape(-1)]),
+        grads,
+        jnp.concatenate(small),
         n,
         m,
         4,
     )
+    grads = grads.reshape(-1, D, D).astype(jnp.float32)
     grad_token_part, _ = rms_backward(tokens, gain_rows[0], grad_normed_query + grad_normed_own)
     grad_in = (grad_after_self + grad_token_part).astype(jnp.bfloat16)
-    grads = grads.reshape(-1, D, D).astype(jnp.float32)
-    ends = (grad_gains.size, grad_gains.size + grad_table.size)
     return (
         output.reshape(1, token_count, D),
         grad_in.reshape(1, token_count, D),
@@ -1073,8 +1284,8 @@
         grads[:6],
         grads[6:],
         small[: ends[0]].reshape(grad_gains.shape),
-        small[ends[0] : ends[1]].reshape(grad_table.shape),
-        small[ends[1] :].reshape(grad_router.shape),
+        small[ends[1] : ends[1] + NBUCKET, :HEADS],
+        small[ends[0] : ends[1]].reshape(expert_count, D).T,
         grad_expert_in,
         grad_expert_out,
         tally_counts,

time: 689 us -> 657 us (0.954)
  Pallas kernels: 488 us -> 470 us
  other arithmetic: 34.3 us -> 22 us
  starting transfers between devices: 19.3 us -> 8.09 us
  matrix products: 83.2 us -> 73.3 us
  waiting for transfers between devices: 18 us -> 27.1 us
    pallas_call x4 -> x2, Pallas kernels: 238 us -> 210 us  [the longest x1 145 us: run_experts(): pl.pallas_call(functools.partial(expert_kernel, n, m, slots), out_shape=[...]
    dot_general x6 -> x1, matrix products: 20.8 us -> 2.1 us  [project(): jnp.dot(source, matrix, preferred_element_type=jnp.float32)]
    ppermute x2 -> x4, waiting for transfers between devices: 0.01 us -> 16.6 us  [the longest x1 15.8 us: body(): gin_last = lax.ppermute(gin_last, 'seq', to_last)]
    pallas_call x1, Pallas kernels: 147 us -> 156 us  [finish(): pl.pallas_call(functools.partial(finish_kernel, n, (few, many)), out_shap...]
    ppermute x4 -> x2, starting transfers between devices: 9.76 us -> 1.63 us  [body(): lax.ppermute(w, 'seq', to_last)]
    unnamed x208 -> x206, local copies, waits for them, and re-layouts: 16.6 us -> 22.3 us
  transfers between devices with their start and end apart: 12 -> 10, of which waited for: 3 -> 5; matrix products, arithmetic and copies ran while one was open for 11% -> 4% of each run, Pallas kernels for 37% -> 14%
where the time goes in v4:
time: 657 us; the launch traced here: 645 us
  Pallas kernels  470 us (72%)
  matrix products  73.3 us (11%)
  local copies, waits for them, and re-layouts  42.9 us (7%)
  waiting for transfers between devices  27.1 us (4%)
  other arithmetic  22 us (3%)
  starting transfers between devices  8.09 us (1%)
    pallas_call x1, Pallas kernels, finish(): pl.pallas_call(functools.partial(finish_kernel, n, (few, many)), out_shap...  156 us
    pallas_call x1, Pallas kernels, run_experts(): pl.pallas_call(functools.partial(expert_kernel, n, m, slots), out_shape=[...  145 us
    pallas_call x1, Pallas kernels, gather_projected(): pl.pallas_call(functools.partial(gather_kernel, n, parts), out_shape=[jax...  65.4 us
    pallas_call x2, Pallas kernels, attend_back(): pl.pallas_call(functools.partial(attend_back_kernel, causal, block), grid...  58.3 us
    pallas_call x2, Pallas kernels, attend(): pl.pallas_call(functools.partial(attend_kernel, causal, block), grid=(PAI...  45.3 us
    dot_general x8, matrix products, input_grad(): jnp.einsum('te,de->td', upstream, matrix, preferred_element_type=jnp.floa...  32.4 us
    dot_general x8, matrix products, weight_grad(): jnp.einsum('td,te->de', source, upstream, preferred_element_type=jnp.floa...  28.9 us
    unnamed x206, local copies, waits for them, and re-layouts  22.3 us
  transfers between devices with their start and end apart: 10, of which 5 were waited for; matrix products, arithmetic and copies ran while one was open for 4% of the time, Pallas kernels for 14%

profile of v4, /device:TPU:25, one launch (start us, length us, event | category | flops | bytes accessed | tf_op | source)
XLA Modules:
  0.0 645.4 jit_solution(12860864533554406178)
XLA Ops:
  3.9 2.1 fusion.12.refs_0_
  6.0 65.4 %gather_projected.1 = (bf16[8,384,768]{2,1,0:T(8,128)(2,1)}, bf16[8,128,768]{2,1,0:T(8,128)(2,1)}, bf16[384,768]{1,0:T(8,128)(2,1)}, bf16[8,384,768]{2,1,0:T(8,1...) custom-call(bf16[384,768]{1,0:T(8,128)(2,1)} %fusion.12.refs_0_, ...), custom_call_target="tpu_custom_call" | custom-call | flops 60000002048 | tf_op jit(solution)/shard_map/gather_projected/pallas_call | solution.py:179
  82.0 34.9 %attend_self.1 = (bf16[384,768]{1,0:T(8,128)(2,1)S(1)}, f32[384,768]{1,0:T(8,128)S(1)}, f32[6,2,384]{2,1,0:T(2,128)S(1)}) custom-call(s32[1]{0:T(128)} %bitcast.1.s_ref, bf16[384,768]{1,0:T(8,128)(2,1)S(1)} %copy-done.16, bf16[3072,768]{1,0:T(8,128)(2,1)} %bitcast.217, bf16[3072,768]{1,0:T(8,128)(2,1)} %bitcast.219, f32[6,2,384]{2,1,0:T(2,128)S(1)} %select_select_fusion.refs_0_), custom_call_target="tpu_custom_call" | custom-call | flops 40000000000 | tf_op jit(solution)/shard_map/attend_self/pallas_call | solution.py:656
  118.6 4.1 collective-permute-done.1.refs_6_
  125.3 2.1 convolution_convert_fusion.11.q_ref
  127.6 10.4 %attend_cross.1 = (bf16[384,768]{1,0:T(8,128)(2,1)S(1)}, f32[384,768]{1,0:T(8,128)S(1)}, f32[6,2,384]{2,1,0:T(2,128)S(1)}) custom-call(s32[1]{0:T(128)} %bitcast.1.s_ref, bf16[384,768]{1,0:T(8,128)(2,1)S(1)} %convolution_convert_fusion.11.q_ref, bf16[1024,768]{1,0:T(8,128)(2,1)S(1)} %bitcast.192, bf16[1024,768]{1,0:T(8,128)(2,1)S(1)} %bitcast.194), custom_call_target="tpu_custom_call" | custom-call | flops 10000000000 | tf_op jit(solution)/shard_map/attend_cross/pallas_call | solution.py:656
  141.1 2.2 convolution_convert_fusion
  143.4 5.7 collective-permute-done.2.refs_7_
  150.8 145.0 %run_experts.1 = (bf16[4,128,1536]{2,1,0:T(8,128)(2,1)}, f32[2,768,384]{2,1,0:T(8,128)}, f32[2,768,384]{2,1,0:T(8,128)}, bf16[2,768,384]{2,1,0:T(8,128)(2,1)}, b...) custom-call(bf16[4,128,1536]{2,1,0:T(8,128)(2,1)} %bitcast.224, ...), custom_call_target="tpu_custom_call" | custom-call | flops 149999992832 | tf_op jit(solution)/shard_map/run_experts/pallas_call | solution.py:1017
  295.8 2.4 fusion.44
  304.0 15.0 %attend_cross_back.1 = (bf16[384,768]{1,0:T(8,128)(2,1)S(1)}, bf16[1024,768]{1,0:T(8,128)(2,1)S(1)}, bf16[1024,768]{1,0:T(8,128)(2,1)S(1)}) custom-call(s32[1]{0:T(128)} %bitcast.1.s_ref, bf16[384,768]{1,0:T(8,128)(2,1)S(1)} %copy-done.11, bf16[1024,768]{1,0:T(8,128)(2,1)} %bitcast.191, bf16[1024,768]{1,0:T(8,128)(2,1)} %bitcast.193, ...), custom_call_target="tpu_custom_call" | custom-call | flops 15000000512 | tf_op jit(solution)/shard_map/attend_cross_back/pallas_call | solution.py:780
  319.0 4.5 fusion.23
  323.5 2.5 convolution_convert_fusion.7
  328.0 3.2 convolution_convert_fusion.4
  331.2 2.5 convolution_convert_fusion.6
  333.7 3.9 add_convert_fusion.1
  337.7 15.8 %collective-permute-done.6 = bf16[2,768,384]{2,1,0:T(8,128)(2,1)} collective-permute-done((bf16[2,768,384]{2,1,0:T(8,128)(2,1)}, bf16[2,768,384]{2,1,0:T(8,128)(2,1)}, u32[]{:S(2)}, u32[]{:S(2)}) %collective-permute-start.6) | collective-permute-done | bytes 1179680 | tf_op jit(solution)/shard_map/ppermute | solution.py:1167
  354.3 1.9 convolution_convert_fusion.8
  356.2 2.2 multiply_reduce_fusion.2
  364.2 43.3 %attend_self_back.1 = (bf16[384,768]{1,0:T(8,128)(2,1)S(1)}, bf16[3072,768]{1,0:T(8,128)(2,1)}, bf16[3072,768]{1,0:T(8,128)(2,1)}, f32[12,256,128]{2,1,0:T(8,128)S(1)}, f32[6,2,384]{2,1,0:T(2,128)S(1)}) custom-call(s32[1]{0:T(128)} %bitcast.1.s_ref, bf16[384,768]{1,0:T(8,128)(2,1)S(1)} %copy-done.17, bf16[3072,768]{1,0:T(8,128)(2,1)} %bitcast.218, ...), custom_call_target="tpu_custom_call" | custom-call | flops 48000000000 | tf_op jit(solution)/shard_map/attend_self_back/pallas_call | solution.py:780
  409.2 3.0 multiply_reduce_fusion.3
  412.2 1.8 fusion.4
  415.4 2.3 fusion.37
  417.8 10.5 %fusion.17 = f32[3072,768]{1,0:T(8,128)} fusion(bf16[3072,768]{1,0:T(8,128)(2,1)} %get-tuple-element.111, bf16[6,768,768]{2,1,0:T(8,128)(2,1)} %refs_2_.1), kind=kOutput, calls=%fused_computation.48 | convolution fusion | flops 3623878656 | bytes 15335424 | tf_op jit(solution)/shard_map/te,de->td/dot_general | solution.py:1063
  428.3 7.6 %fusion.3 = bf16[6144,768]{1,0:T(8,128)(2,1)} fusion(bf16[6144,768]{1,0:T(8,128)(2,1)} %fusion.4, bf16[3072,768]{1,0:T(8,128)(2,1)S(1)} %bitcast.201, bf16[3072,768]{1,0:T(8,128)(2,1)} %get-tuple-element.110), kind=kOutput, calls=%fused_computation.23 | convolution fusion | flops 3624468480 | bytes 10616832 | tf_op jit(solution)/shard_map/td,te->de/dot_general | solution.py:1057
  435.9 7.5 %fusion.2 = bf16[6144,768]{1,0:T(8,128)(2,1)} fusion(bf16[6144,768]{1,0:T(8,128)(2,1)} %fusion.3, bf16[3072,768]{1,0:T(8,128)(2,1)S(1)} %bitcast.202, bf16[3072,768]{1,0:T(8,128)(2,1)} %get-tuple-element.111), kind=kOutput, calls=%fused_computation.21 | convolution fusion | flops 3624468480 | bytes 10616832 | tf_op jit(solution)/shard_map/td,te->de/dot_general | solution.py:1057
  443.4 7.1 %add_convert_fusion = bf16[3072,768]{1,0:T(8,128)(2,1)S(1)} fusion(f32[3072,768]{1,0:T(8,128)} %fusion.17, bf16[3072,768]{1,0:T(8,128)(2,1)S(1)} %bitcast.226, bf16[6,768,768]{2,1,0:T(8,128)(2,1)} %refs_2_.1), kind=kOutput, calls=%fused_computation.1 | convolution fusion | flops 3628597248 | bytes 20054016 | tf_op jit(solution)/shard_map/te,de->td/dot_general | solution.py:1063
  462.1 156.0 %finish.1 = (f32[384,768]{1,0:T(8,128)}, f32[128,768]{1,0:T(8,128)}, bf16[2,2,8,192,768]{4,3,2,1,0:T(8,128)(2,1)}, f32[2,2,8,16,128]{4,3,2,1,0:T(8,128)}) custom-call(bf16[8,384,768]{2,1,0:T(8,128)(2,1)} %bitcast.205, bf16[8,128,768]{2,1,0:T(8,128)(2,1)} %bitcast.223, bf16[2,2,8,192,768]{4,3,2,1,0:T(8,128)(2,1)} %bitcast.215, f32[2,2,8,16,128]{4,3,2,1,0:T(8,128)} %bitcast.207), custom_call_target="tpu_custom_call" | custom-call | flops 120000004096 | tf_op jit(solution)/shard_map/finish/pallas_call | solution.py:510
  620.4 4.8 slice.258
  626.5 6.6 %slice.257 = f32[6,768,768]{2,1,0:T(8,128)} slice(bf16[8,768,768]{2,1,0:T(8,128)(2,1)S(1)} %bitcast.196), slice={[0:6], [0:768], [0:768]} | slice | bytes 28311552 | tf_op jit(solution)/shard_map/slice | solution.py:1284
  638.2 3.6 convert_add_fusion.1
  641.8 3.3 convert_add_fusion.2
  (340 shorter events, 60.3 us)
Async XLA Ops:
  0.6 139.4 %copy-start = (bf16[768,8]{0,1:T(8,128)(2,1)S(1)}, bf16[768,8]{0,1:T(8,128)(2,1)}, u32[]{:S(2)}) copy-start(bf16[768,8]{0,1:T(8,128)(2,1)} %param.17) | copy-start | bytes 36868
  3.3 122.0 %copy-start.65 = (f32[768]{0:T(1024)}, f32[768]{0:T(1024)S(1)}, u32[]{:S(2)}) copy-start(f32[768]{0:T(1024)S(1)} %get-tuple-element.136) | copy-start | bytes 9220
  3.3 135.9 %copy-start.56 = (f32[768]{0:T(1024)}, f32[768]{0:T(1024)S(1)}, u32[]{:S(2)}) copy-start(f32[768]{0:T(1024)S(1)} %get-tuple-element.135) | copy-start | bytes 9220
  6.0 65.4 %copy-start.84 = (bf16[2,768,384]{2,1,0:T(8,128)(2,1)S(1)}, bf16[2,768,384]{2,1,0:T(8,128)(2,1)}, u32[]{:S(2)}) copy-start(bf16[2,768,384]{2,1,0:T(8,128)(2,1)} %refs_1_) | copy-start | bytes 3538948
  6.0 67.0 %copy-start.85 = (bf16[2,768,384]{2,1,0:T(8,128)(2,1)S(1)}, bf16[2,768,384]{2,1,0:T(8,128)(2,1)}, u32[]{:S(2)}) copy-start(bf16[2,768,384]{2,1,0:T(8,128)(2,1)} %refs_2_.2) | copy-start | bytes 3538948
  6.0 68.8 %copy-start.69 = (f32[32,12]{0,1:T(8,128)S(1)}, f32[32,12]{0,1:T(8,128)}, u32[]{:S(2)}) copy-start(f32[32,12]{0,1:T(8,128)} %param.16) | copy-start | bytes 4612
  6.0 72.5 %copy-start.82 = (s32[1,384,1]{1,2,0:T(1,128)S(1)}, s32[1,384,1]{1,2,0:T(1,128)}, u32[]{:S(2)}) copy-start(s32[1,384,1]{1,2,0:T(1,128)} %param.18) | copy-start | bytes 4612
  71.4 78.4 %collective-permute-start.5 = (bf16[2,768,384]{2,1,0:T(8,128)(2,1)S(1)}, bf16[2,768,384]{2,1,0:T(8,128)(2,1)}, u32[]{:S(2)}, u32[]{:S(2)}) collective-permute-start(bf16[2,768,384]{2,1,0:T(8,128)(2,1)S(1)} %copy-done.84), channel_id=1, source_target_pairs={{0,8},{4,0},{8,12},{12,4},{16,24},{20,16},{24,28},{28,20},{1,9},{5... | collective-permute-start | bytes 3538952 | tf_op jit(solution)/shard_map/ppermute | solution.py:1096
  72.7 45.9 %collective-permute-start = (bf16[2,768,384]{2,1,0:T(8,128)(2,1)S(1)}, bf16[2,768,384]{2,1,0:T(8,128)(2,1)}, u32[]{:S(2)}, u32[]{:S(2)}) collective-permute-start(bf16[2,768,384]{2,1,0:T(8,128)(2,1)S(1)} %copy-done.84), channel_id=1, source_target_pairs={{0,4},{4,12},{8,0},{12,8},{16,20},{20,28},{24,16},{28,24},{1,5},{5... | collective-permute-start | bytes 3538952 | tf_op jit(solution)/shard_map/ppermute | solution.py:1095
  72.9 77.9 %collective-permute-start.4 = (bf16[2,768,384]{2,1,0:T(8,128)(2,1)S(1)}, bf16[2,768,384]{2,1,0:T(8,128)(2,1)}, u32[]{:S(2)}, u32[]{:S(2)}) collective-permute-start(bf16[2,768,384]{2,1,0:T(8,128)(2,1)S(1)} %copy-done.85), channel_id=1, source_target_pairs={{0,4},{4,12},{8,0},{12,8},{16,20},{20,28},{24,16},{28,24},{1,5},{5... | collective-permute-start | bytes 3538952 | tf_op jit(solution)/shard_map/ppermute | solution.py:1095
  74.2 48.6 %collective-permute-start.1 = (bf16[2,768,384]{2,1,0:T(8,128)(2,1)S(1)}, bf16[2,768,384]{2,1,0:T(8,128)(2,1)}, u32[]{:S(2)}, u32[]{:S(2)}) collective-permute-start(bf16[2,768,384]{2,1,0:T(8,128)(2,1)S(1)} %copy-done.85), channel_id=1, source_target_pairs={{0,8},{4,0},{8,12},{12,4},{16,24},{20,16},{24,28},{28,20},{1,9},{5... | collective-permute-start | bytes 3538952 | tf_op jit(solution)/shard_map/ppermute | solution.py:1096
  78.5 61.8 %copy-start.52 = (s32[384]{0:T(512)}, s32[384]{0:T(512)S(1)}, u32[]{:S(2)}) copy-start(s32[384]{0:T(512)S(1)} %reduce.37) | copy-start | bytes 4612
  80.9 36.0 %copy-start.6 = (f32[6,2,384]{2,1,0:T(2,128)}, f32[6,2,384]{2,1,0:T(2,128)S(1)}, u32[]{:S(2)}) copy-start(f32[6,2,384]{2,1,0:T(2,128)S(1)} %select_select_fusion.refs_0_) | copy-start | bytes 55300
  82.0 40.7 %copy-start.27 = (bf16[1,384,768]{2,1,0:T(8,128)(2,1)S(1)}, bf16[1,384,768]{2,1,0:T(8,128)(2,1)}, u32[]{:S(2)}) copy-start(bf16[1,384,768]{2,1,0:T(8,128)(2,1)} %param.11) | copy-start | bytes 1769476
  82.0 40.7 %copy-start.30 = (bf16[2,768,768]{2,1,0:T(8,128)(2,1)S(1)}, bf16[2,768,768]{2,1,0:T(8,128)(2,1)}, u32[]{:S(2)}) copy-start(bf16[2,768,768]{2,1,0:T(8,128)(2,1)} %param.14) | copy-start | bytes 7077892
  117.5 23.5 %copy-start.60 = (s32[384]{0:T(512)}, s32[384]{0:T(512)S(1)}, u32[]{:S(2)}) copy-start(s32[384]{0:T(512)S(1)} %add_select_fusion) | copy-start | bytes 4612
  123.5 14.5 %copy-start.25 = (f32[384,768]{1,0:T(8,128)}, f32[384,768]{1,0:T(8,128)S(1)}, u32[]{:S(2)}) copy-start(f32[384,768]{1,0:T(8,128)S(1)} %get-tuple-element.175) | copy-start | bytes 3538948
  123.5 25.6 %collective-permute-start.2 = (bf16[2,768,384]{2,1,0:T(8,128)(2,1)}, bf16[2,768,384]{2,1,0:T(8,128)(2,1)S(1)}, u32[]{:S(2)}, u32[]{:S(2)}) collective-permute-start(bf16[2,768,384]{2,1,0:T(8,128)(2,1)} %collective-permute-done.refs_3_), channel_id=1, source_target_pairs={{0,4},{4,12},{8,0},{12,8},{16,20},{20,28},{24,16},{28,24},{1,5},{5... | collective-permute-start | bytes 3538952 | tf_op jit(solution)/shard_map/ppermute | solution.py:1109
  124.8 24.9 %collective-permute-start.3 = (bf16[2,768,384]{2,1,0:T(8,128)(2,1)}, bf16[2,768,384]{2,1,0:T(8,128)(2,1)S(1)}, u32[]{:S(2)}, u32[]{:S(2)}) collective-permute-start(bf16[2,768,384]{2,1,0:T(8,128)(2,1)} %collective-permute-done.1.refs_6_), channel_id=1, source_target_pairs={{0,8},{4,0},{8,12},{12,4},{16,24},{20,16},{24,28},{28,20},{1,9},{5... | collective-permute-start | bytes 3538952 | tf_op jit(solution)/shard_map/ppermute | solution.py:1110
  127.5 10.5 %copy-start.10 = (bf16[384,768]{1,0:T(8,128)(2,1)}, bf16[384,768]{1,0:T(8,128)(2,1)S(1)}, u32[]{:S(2)}) copy-start(bf16[384,768]{1,0:T(8,128)(2,1)S(1)} %convolution_convert_fusion.11.q_ref) | copy-start | bytes 1769476
  150.8 145.0 %copy-start.61 = (s32[384]{0:T(512)S(1)}, s32[384]{0:T(512)}, u32[]{:S(2)}) copy-start(s32[384]{0:T(512)} %copy-done.60) | copy-start | bytes 4612
  326.0 27.5 %collective-permute-start.6 = (bf16[2,768,384]{2,1,0:T(8,128)(2,1)}, bf16[2,768,384]{2,1,0:T(8,128)(2,1)}, u32[]{:S(2)}, u32[]{:S(2)}) collective-permute-start(bf16[2,768,384]{2,1,0:T(8,128)(2,1)} %get-tuple-element.91), channel_id=1, source_target_pairs={{0,8},{4,0},{8,12},{12,4},{16,24},{20,16},{24,28},{28,20},{1,9},{5... | collective-permute-start | bytes 3538952 | tf_op jit(solution)/shard_map/ppermute | solution.py:1167
  326.7 27.5 %collective-permute-start.7 = (bf16[2,768,384]{2,1,0:T(8,128)(2,1)}, bf16[2,768,384]{2,1,0:T(8,128)(2,1)}, u32[]{:S(2)}, u32[]{:S(2)}) collective-permute-start(bf16[2,768,384]{2,1,0:T(8,128)(2,1)} %get-tuple-element.92), channel_id=1, source_target_pairs={{0,4},{4,12},{8,0},{12,8},{16,20},{20,28},{24,16},{28,24},{1,5},{5... | collective-permute-start | bytes 3538952 | tf_op jit(solution)/shard_map/ppermute | solution.py:1166
  333.7 20.5 %copy-start.26 = (f32[384,768]{1,0:T(8,128)S(1)}, f32[384,768]{1,0:T(8,128)}, u32[]{:S(2)}) copy-start(f32[384,768]{1,0:T(8,128)} %copy-done.25) | copy-start | bytes 3538948
  333.7 20.5 %copy-start.66 = (f32[768]{0:T(1024)S(1)}, f32[768]{0:T(1024)}, u32[]{:S(2)}) copy-start(f32[768]{0:T(1024)} %copy-done.65) | copy-start | bytes 9220
  333.7 20.5 %copy-start.77 = (f32[384]{0:T(512)S(1)}, f32[384]{0:T(512)}, u32[]{:S(2)}) copy-start(f32[384]{0:T(512)} %copy-done.76) | copy-start | bytes 4612
  362.7 44.8 %collective-permute-start.8 = (bf16[2,768,384]{2,1,0:T(8,128)(2,1)S(1)}, bf16[2,768,384]{2,1,0:T(8,128)(2,1)}, u32[]{:S(2)}, u32[]{:S(2)}) collective-permute-start(bf16[2,768,384]{2,1,0:T(8,128)(2,1)S(1)} %copy-done.87), channel_id=1, source_target_pairs={{0,8},{4,0},{8,12},{12,4},{16,24},{20,16},{24,28},{28,20},{1,9},{5... | collective-permute-start | bytes 3538952 | tf_op jit(solution)/shard_map/ppermute | solution.py:1200
  363.2 44.3 %collective-permute-start.9 = (bf16[2,768,384]{2,1,0:T(8,128)(2,1)S(1)}, bf16[2,768,384]{2,1,0:T(8,128)(2,1)}, u32[]{:S(2)}, u32[]{:S(2)}) collective-permute-start(bf16[2,768,384]{2,1,0:T(8,128)(2,1)S(1)} %copy-done.86), channel_id=1, source_target_pairs={{0,4},{4,12},{8,0},{12,8},{16,20},{20,28},{24,16},{28,24},{1,5},{5... | collective-permute-start | bytes 3538952 | tf_op jit(solution)/shard_map/ppermute | solution.py:1199
  414.2 14.1 %slice-start = ((s8[4718592]{0:T(1024)(128)(4,1)}), s8[524288]{0:T(1024)(128)(4,1)S(1)}, s32[]{:S(2)}) async-start(s8[4718592]{0:T(1024)(128)(4,1)} %bitcast.199), calls=%async_computation | async-start | bytes 1048576
  417.8 10.5 %slice-start.1 = ((s8[4718592]{0:T(1024)(128)(4,1)}), s8[4194304]{0:T(1024)(128)(4,1)S(1)}, s32[]{:S(2)}) async-start(s8[4718592]{0:T(1024)(128)(4,1)} %bitcast.199), calls=%async_computation.1 | async-start | bytes 8388608
  428.3 15.1 %slice-start.4 = ((s8[4718592]{0:T(1024)(128)(4,1)}), s8[4194304]{0:T(1024)(128)(4,1)S(1)}, s32[]{:S(2)}) async-start(s8[4718592]{0:T(1024)(128)(4,1)} %bitcast.225), calls=%async_computation.4 | async-start | bytes 8388608
  435.9 14.6 %slice-start.2 = ((s8[4718592]{0:T(1024)(128)(4,1)}), s8[4194304]{0:T(1024)(128)(4,1)S(1)}, s32[]{:S(2)}) async-start(s8[4718592]{0:T(1024)(128)(4,1)} %bitcast.203), calls=%async_computation.2 | async-start | bytes 8388608
  (77 other events, 207.6 us)

commit v5 on v4

--- a/solution.py
+++ b/solution.py
@@ -580,6 +580,22 @@
     return jnp.concatenate(edge, axis=1)
 
 
+def each_far(s, block, act, times=3):
+    far = jnp.maximum(s - 1, 0)
+    bundles = far // times
+
+    def bundle(j, carry):
+        act(pl.multiple_of(j * times * block, block), times)
+        return carry
+
+    def single(j, carry):
+        act(pl.multiple_of(j * block, block), 1)
+        return carry
+
+    lax.fori_loop(0, bundles, bundle, 0)
+    lax.fori_loop(bundles * times, far, single, 0)
+
+
 def attend_kernel(causal, block, s_ref, q_ref, k_ref, v_ref, *refs):
     if causal:
         line_ref, low_ref, wide_ref, lse_ref, acc_ref, top_ref = refs
@@ -587,11 +603,11 @@
         low_ref, wide_ref, lse_ref, acc_ref, top_ref = refs
     rows = q_ref.shape[0]
     both = split_heads(q_ref[...])
-    ones = jnp.ones((16, block), v_ref.dtype)
-
-    def visit(start, bias, first):
-        keys = k_ref[pl.ds(start, block), :]
-        values = v_ref[pl.ds(start, block), :]
+
+    def visit(start, bias, first, times=1):
+        ones = jnp.ones((16, times * block), v_ref.dtype)
+        keys = k_ref[pl.ds(start, times * block), :]
+        values = v_ref[pl.ds(start, times * block), :]
         t = dot_last(keys, both) * (scale_factor * log2e)
         if bias is not None:
             t = t + bias
@@ -622,11 +638,7 @@
         def _():
             visit(pl.multiple_of((s - 1) * block, block), edge_bias(tiles, rows), False)
 
-        def far(j, carry):
-            visit(pl.multiple_of(j * block, block), None, False)
-            return carry
-
-        lax.fori_loop(0, s - 1, far, 0)
+        each_far(s, block, lambda start, times: visit(start, None, False, times))
     else:
         for j in range(k_ref.shape[0] // block):
             visit(j * block, None, j == 0)
@@ -647,7 +659,7 @@
 def attend(seq_at, queries, keys, values, lines):
     rows, total = queries.shape[0], keys.shape[0]
     causal = lines is not None
-    block = rows if causal else math.gcd(total, 512)
+    block = rows if causal else math.gcd(total, 1024)
     pair = pl.BlockSpec((rows, TILE), lambda g: (0, g))
     long = pl.BlockSpec((total, TILE), lambda g: (0, g))
     extra, specs = [], []
@@ -691,20 +703,20 @@
         axis=1,
     )
     lse = jnp.concatenate([lse_ref[0, :1], lse_ref[0, 1:]], axis=1)
-    ones = jnp.ones((16, block), k_ref.dtype)
-
-    def visit(start, bias, first):
-        keys = k_ref[pl.ds(start, block), :]
-        values = v_ref[pl.ds(start, block), :]
+
+    def visit(start, bias, first, times=1):
+        ones = jnp.ones((16, times * block), k_ref.dtype)
+        keys = k_ref[pl.ds(start, times * block), :]
+        values = v_ref[pl.ds(start, times * block), :]
         t = dot_last(keys, both) * (scale_factor * log2e)
         if bias is not None:
             t = t + bias
         p = jnp.exp2(t - lse)
         ds = (p * (dot_last(values, up_both) - delta)).astype(keys.dtype)
-        dv_ref[pl.ds(start, block), :] = dot_plain(p.astype(keys.dtype), up_both).astype(
+        dv_ref[pl.ds(start, times * block), :] = dot_plain(p.astype(keys.dtype), up_both).astype(
             dv_ref.dtype
         )
-        dk_ref[pl.ds(start, block), :] = (dot_plain(ds, both) * scale_factor).astype(dk_ref.dtype)
+        dk_ref[pl.ds(start, times * block), :] = (dot_plain(ds, both) * scale_factor).astype(dk_ref.dtype)
         part = dot_plain(jnp.concatenate([keys.T, ones], axis=0), ds)
         if first:
             acc_ref[...] = part
@@ -739,11 +751,7 @@
                     jnp.float32
                 )
 
-        def far(j, carry):
-            visit(pl.multiple_of(j * block, block), None, False)
-            return carry
-
-        lax.fori_loop(0, s - 1, far, 0)
+        each_far(s, block, lambda start, times: visit(start, None, False, times))
 
         def beyond(j, carry):
             start = pl.multiple_of(j * block, block)
@@ -765,7 +773,7 @@
 def attend_back(seq_at, queries, keys, values, upstream, wide, lse, lines):
     rows, total = queries.shape[0], keys.shape[0]
     causal = lines is not None
-    block = rows if causal else math.gcd(total, 512)
+    block = rows if causal else math.gcd(total, 1024)
     pair = pl.BlockSpec((rows, TILE), lambda g: (0, g))
     long = pl.BlockSpec((total, TILE), lambda g: (0, g))
     line = pl.BlockSpec((1, 2, rows), lambda g: (g, 0, 0))
@@ -793,6 +801,56 @@
         cost_estimate=cost(48 if causal else 15),
         name="attend_self_back" if causal else "attend_cross_back",
     )(seq_at, queries, keys, values, upstream, wide, lse, *extra)
+
+
+def token_back_kernel(x_ref, dk_ref, dv_ref, wk_ref, wv_ref, dx_ref, gk_ref, gv_ref, gain_ref, k_acc, v_acc):
+    x, dk, dv = x_ref[...], dk_ref[...], dv_ref[...]
+    dx = dot_last(dk, wk_ref[0]) + dot_last(dv, wv_ref[0])
+    dx_ref[...] = dx.astype(dx_ref.dtype)
+    gain = jnp.sum(dx * x.astype(jnp.float32), axis=0, keepdims=True)
+    gk, gv = dot_first(x, dk), dot_first(x, dv)
+    step, last = pl.program_id(0), pl.num_programs(0) - 1
+
+    @pl.when(step == 0)
+    def _():
+        gain_ref[...] = gain
+        k_acc[...] = gk
+        v_acc[...] = gv
+
+    @pl.when(step > 0)
+    def _():
+        gain_ref[...] += gain
+        k_acc[...] += gk
+        v_acc[...] += gv
+
+    @pl.when(step == last)
+    def _():
+        gk_ref[...] = k_acc[...].astype(gk_ref.dtype)
+        gv_ref[...] = v_acc[...].astype(gv_ref.dtype)
+
+
+def token_back(tokens, grad_keys, grad_values, proj_in, rows, first, name):
+    total = tokens.shape[0]
+    block = pl.BlockSpec((rows, D), lambda i: (i, 0))
+    weight = lambda number: pl.BlockSpec((1, D, D), lambda i: (number, 0, 0))
+    whole = lambda r: pl.BlockSpec((r, D), lambda i: (0, 0))
+    grad = jax.ShapeDtypeStruct((D, D), tokens.dtype)
+    return pl.pallas_call(
+        token_back_kernel,
+        grid=(total // rows,),
+        out_shape=[
+            jax.ShapeDtypeStruct(tokens.shape, tokens.dtype),
+            grad,
+            grad,
+            jax.ShapeDtypeStruct((1, D), jnp.float32),
+        ],
+        in_specs=[block] * 3 + [weight(first), weight(first + 1)],
+        out_specs=[block, whole(D), whole(D), whole(1)],
+        scratch_shapes=[pltpu.VMEM((D, D), jnp.float32)] * 2,
+        compiler_params=pltpu.CompilerParams(vmem_limit_bytes=48 << 20),
+        cost_estimate=cost(18 if total > 2048 else 8),
+        name=name,
+    )(tokens, grad_keys, grad_values, proj_in, proj_in)
 
 
 def bias_lines(bias_table):
@@ -1203,23 +1261,19 @@
         after_self, gain_rows[1], input_grad(grad_cross_query, proj_in[3])
     )
     grad_after_self = grad_after_cross + grad_self_part
-    grad_memory_part = (
-        input_grad(grad_memory_keys, proj_in[4]) + input_grad(grad_memory_values, proj_in[5])
-    ).astype(jnp.bfloat16)
+    grad_memory_part, grad_key_cross, grad_value_cross, _ = token_back(
+        memory_all,
+        grad_memory_keys,
+        grad_memory_values,
+        proj_in,
+        math.gcd(n * memory_count, 512),
+        4,
+        "memory_back",
+    )
 
     grad_self_low = grad_after_self.astype(jnp.bfloat16)
     grad_out_self = weight_grad(attended_self_low, grad_self_low)
     grad_attended_self = input_grad(grad_self_low, proj_out[0]).astype(jnp.bfloat16)
-    early = [
-        grad_query_cross,
-        weight_grad(memory_all, grad_memory_keys),
-        weight_grad(memory_all, grad_memory_values),
-        grad_out_self,
-        grad_out_cross,
-    ]
-    grad_attended_self, grad_memory_part, *early = lax.optimization_barrier(
-        (grad_attended_self, grad_memory_part, *early)
-    )
     grad_self_query, grad_keys, grad_values, near, sums = attend_back(
         seq_at,
         queries,
@@ -1239,21 +1293,24 @@
     grad_expert_out = gout_own + gout_last.astype(jnp.float32) + gout_next.astype(jnp.float32)
     grad_table = bias_gradient(near, sums)
     grad_normed_query = input_grad(grad_self_query, proj_in[0])
-    grad_normed_part = (
-        input_grad(grad_keys, proj_in[1]) + input_grad(grad_values, proj_in[2])
-    ).astype(jnp.bfloat16)
-    grad_normed_part = lax.optimization_barrier(grad_normed_part)
+    grad_normed_part, grad_key_self, grad_value_self, grad_gain_part = token_back(
+        normed_all, grad_keys, grad_values, proj_in, 2 * token_count, 1, "token_back"
+    )
     grad_gain_self = (
-        jnp.sum(grad_normed_part.astype(jnp.float32) * normed_all.astype(jnp.float32), axis=0)
+        grad_gain_part[0]
         + jnp.sum(grad_normed_query * normed_self.astype(jnp.float32), axis=0)
     ) / gain_rows[0]
 
     grads = jnp.concatenate(
         [
             weight_grad(normed_self, grad_self_query),
-            weight_grad(normed_all, grad_keys),
-            weight_grad(normed_all, grad_values),
-            *early,
+            grad_key_self,
+            grad_value_self,
+            grad_query_cross,
+            grad_key_cross,
+            grad_value_cross,
+            grad_out_self,
+            grad_out_cross,
         ]
     )
     grad_gains = jnp.stack([grad_gain_self, grad_gain_cross, grad_gain_mix])

time: 657 us -> 621 us (0.945)
  matrix products: 73.3 us -> 26.8 us
  Pallas kernels: 470 us -> 489 us
  waiting for transfers between devices: 27.1 us -> 17.7 us
    pallas_call x0 -> x2, Pallas kernels: none -> 30.8 us  [token_back(): pl.pallas_call(token_back_kernel, grid=(total // rows,), out_shape=[jax.S...]
    dot_general x8 -> x4, matrix products: 32.4 us -> 7.32 us  [input_grad(): jnp.einsum('te,de->td', upstream, matrix, preferred_element_type=jnp.floa...]
    dot_general x8 -> x4, matrix products: 28.9 us -> 7.42 us  [weight_grad(): jnp.einsum('td,te->de', source, upstream, preferred_element_type=jnp.floa...]
    ppermute x1, waiting for transfers between devices: 15.8 us -> 0.01 us  [body(): gin_last = lax.ppermute(gin_last, 'seq', to_last)]
    unnamed x206 -> x186, local copies, waits for them, and re-layouts: 22.3 us -> 25.5 us
  transfers between devices with their start and end apart: 10 -> 10, of which waited for: 5 -> 3; matrix products, arithmetic and copies ran while one was open for 4% -> 2% of each run, Pallas kernels for 14% -> 17%
where the time goes in v5:
time: 621 us; the launch traced here: 609 us
  Pallas kernels  489 us (79%)
  local copies, waits for them, and re-layouts  44.7 us (7%)
  matrix products  26.8 us (4%)
  other arithmetic  21.1 us (3%)
  waiting for transfers between devices  17.7 us (3%)
  starting transfers between devices  7.62 us (1%)
    pallas_call x1, Pallas kernels, finish(): pl.pallas_call(functools.partial(finish_kernel, n, (few, many)), out_shap...  153 us
    pallas_call x1, Pallas kernels, run_experts(): pl.pallas_call(functools.partial(expert_kernel, n, m, slots), out_shape=[...  145 us
    pallas_call x1, Pallas kernels, gather_projected(): pl.pallas_call(functools.partial(gather_kernel, n, parts), out_shape=[jax...  65.3 us
    pallas_call x2, Pallas kernels, attend_back(): pl.pallas_call(functools.partial(attend_back_kernel, causal, block), grid...  55.8 us
    pallas_call x2, Pallas kernels, attend(): pl.pallas_call(functools.partial(attend_kernel, causal, block), grid=(PAI...  39.1 us
    pallas_call x2, Pallas kernels, token_back(): pl.pallas_call(token_back_kernel, grid=(total // rows,), out_shape=[jax.S...  30.8 us
    unnamed x186, local copies, waits for them, and re-layouts  25.5 us
  transfers between devices with their start and end apart: 10, of which 3 were waited for; matrix products, arithmetic and copies ran while one was open for 2% of the time, Pallas kernels for 17%

profile of v5, /device:TPU:25, one launch (start us, length us, event | category | flops | bytes accessed | tf_op | source)
XLA Modules:
  0.0 608.9 jit_solution(12808220371425211219)
XLA Ops:
  3.9 2.1 fusion.13.refs_0_
  6.0 65.3 %gather_projected.1 = (bf16[8,384,768]{2,1,0:T(8,128)(2,1)}, bf16[8,128,768]{2,1,0:T(8,128)(2,1)}, bf16[384,768]{1,0:T(8,128)(2,1)}, bf16[8,384,768]{2,1,0:T(8,1...) custom-call(bf16[384,768]{1,0:T(8,128)(2,1)} %fusion.13.refs_0_, ...), custom_call_target="tpu_custom_call" | custom-call | flops 60000002048 | tf_op jit(solution)/shard_map/gather_projected/pallas_call | solution.py:179
  82.0 29.7 %attend_self.1 = (bf16[384,768]{1,0:T(8,128)(2,1)S(1)}, f32[384,768]{1,0:T(8,128)S(1)}, f32[6,2,384]{2,1,0:T(2,128)S(1)}) custom-call(s32[1]{0:T(128)} %bitcast.1.s_ref, bf16[384,768]{1,0:T(8,128)(2,1)S(1)} %copy-done.23, bf16[3072,768]{1,0:T(8,128)(2,1)} %bitcast.188, bf16[3072,768]{1,0:T(8,128)(2,1)} %bitcast.190, f32[6,2,384]{2,1,0:T(2,128)S(1)} %select_select_fusion.refs_0_), custom_call_target="tpu_custom_call" | custom-call | flops 40000000000 | tf_op jit(solution)/shard_map/attend_self/pallas_call | solution.py:668
  113.3 9.6 %collective-permute-done.1.refs_6_ = bf16[2,768,384]{2,1,0:T(8,128)(2,1)} collective-permute-done((bf16[2,768,384]{2,1,0:T(8,128)(2,1)}, bf16[2,768,384]{2,1,0:T(8,128)(2,1)}, u32[]{:S(2)}, u32[]{:S(2)}) %collective-permute-start.1) | collective-permute-done | bytes 1179680 | tf_op jit(solution)/shard_map/ppermute | solution.py:1154
  123.7 1.3 collective-permute-start.2
  125.2 2.1 convolution_convert_fusion.7.q_ref
  127.4 9.4 %attend_cross.1 = (bf16[384,768]{1,0:T(8,128)(2,1)S(1)}, f32[384,768]{1,0:T(8,128)S(1)}, f32[6,2,384]{2,1,0:T(2,128)S(1)}) custom-call(s32[1]{0:T(128)} %bitcast.1.s_ref, bf16[384,768]{1,0:T(8,128)(2,1)S(1)} %convolution_convert_fusion.7.q_ref, bf16[1024,768]{1,0:T(8,128)(2,1)S(1)} %bitcast.168, bf16[1024,768]{1,0:T(8,128)(2,1)S(1)} %bitcast.170), custom_call_target="tpu_custom_call" | custom-call | flops 10000000000 | tf_op jit(solution)/shard_map/attend_cross/pallas_call | solution.py:668
  139.5 2.2 convolution_convert_fusion
  141.8 7.2 %collective-permute-done.2.refs_7_ = bf16[2,768,384]{2,1,0:T(8,128)(2,1)S(1)} collective-permute-done((bf16[2,768,384]{2,1,0:T(8,128)(2,1)}, bf16[2,768,384]{2,1,0:T(8,128)(2,1)S(1)}, u32[]{:S(2)}, u32[]{:S(2)}) %collective-permute-start.2) | collective-permute-done | bytes 1179680 | tf_op jit(solution)/shard_map/ppermute | solution.py:1167
  150.9 145.0 %run_experts.1 = (bf16[4,128,1536]{2,1,0:T(8,128)(2,1)}, f32[2,768,384]{2,1,0:T(8,128)}, f32[2,768,384]{2,1,0:T(8,128)}, bf16[2,768,384]{2,1,0:T(8,128)(2,1)}, b...) custom-call(bf16[4,128,1536]{2,1,0:T(8,128)(2,1)} %bitcast.193, ...), custom_call_target="tpu_custom_call" | custom-call | flops 149999992832 | tf_op jit(solution)/shard_map/run_experts/pallas_call | solution.py:1075
  296.0 2.4 fusion.35
  304.8 15.2 %attend_cross_back.1 = (bf16[384,768]{1,0:T(8,128)(2,1)S(1)}, bf16[1024,768]{1,0:T(8,128)(2,1)S(1)}, bf16[1024,768]{1,0:T(8,128)(2,1)S(1)}) custom-call(s32[1]{0:T(128)} %bitcast.1.s_ref, bf16[384,768]{1,0:T(8,128)(2,1)S(1)} %copy-done.18, bf16[1024,768]{1,0:T(8,128)(2,1)} %bitcast.167, bf16[1024,768]{1,0:T(8,128)(2,1)} %bitcast.169, ...), custom_call_target="tpu_custom_call" | custom-call | flops 15000000512 | tf_op jit(solution)/shard_map/attend_cross_back/pallas_call | solution.py:788
  322.7 9.1 %memory_back.1 = (bf16[1024,768]{1,0:T(8,128)(2,1)S(1)}, bf16[768,768]{1,0:T(8,128)(2,1)S(1)}, bf16[768,768]{1,0:T(8,128)(2,1)S(1)}, f32[1,768]{1,0:T(1,128)}) custom-call(bf16[1024,768]{1,0:T(8,128)(2,1)S(1)} %bitcast.166, bf16[1024,768]{1,0:T(8,128)(2,1)} %copy-done.19, bf16[1024,768]{1,0:T(8,128)(2,1)} %copy-done.20, bf16[6,768,768]{2,1,0:T(8,128)(2,1)} %wv_ref.3, ...), custom_call_target="tpu_custom_call" | custom-call | flops 8000000000 | tf_op jit(solution)/shard_map/memory_back/pallas_call | solution.py:838
  331.9 3.0 multiply_reduce_fusion.1
  335.3 1.3 copy-done.37
  339.1 40.6 %attend_self_back.1 = (bf16[384,768]{1,0:T(8,128)(2,1)S(1)}, bf16[3072,768]{1,0:T(8,128)(2,1)}, bf16[3072,768]{1,0:T(8,128)(2,1)}, f32[12,256,128]{2,1,0:T(8,128)S(1)}, f32[6,2,384]{2,1,0:T(2,128)S(1)}) custom-call(s32[1]{0:T(128)} %bitcast.1.s_ref, bf16[384,768]{1,0:T(8,128)(2,1)S(1)} %copy-done.24, bf16[3072,768]{1,0:T(8,128)(2,1)} %bitcast.189, ...), custom_call_target="tpu_custom_call" | custom-call | flops 48000000000 | tf_op jit(solution)/shard_map/attend_self_back/pallas_call | solution.py:788
  379.9 1.5 pad.21
  381.4 2.9 multiply_reduce_fusion.2
  384.4 1.8 fusion.2
  386.4 2.8 copy.28
  389.3 2.3 fusion.28
  391.6 21.7 %token_back.1 = (bf16[3072,768]{1,0:T(8,128)(2,1)}, bf16[768,768]{1,0:T(8,128)(2,1)S(1)}, bf16[768,768]{1,0:T(8,128)(2,1)S(1)}, f32[1,768]{1,0:T(1,128)S(1)}) custom-call(bf16[3072,768]{1,0:T(8,128)(2,1)} %bitcast.187, bf16[3072,768]{1,0:T(8,128)(2,1)} %get-tuple-element.107.dk_ref, bf16[3072,768]{1,0:T(8,128)(2,1)} %get-tuple-element.108.dv_ref, ...), custom_call_target="tpu_custom_call" | custom-call | flops 17999998976 | tf_op jit(solution)/shard_map/token_back/pallas_call | solution.py:838
  415.8 2.4 constant_dynamic-update-slice_fusion.3
  420.1 1.9 fusion.3
  425.0 1.8 fusion.4
  426.8 1.8 fusion.5
  428.6 153.1 %finish.1 = (f32[384,768]{1,0:T(8,128)}, f32[128,768]{1,0:T(8,128)}, bf16[2,2,8,192,768]{4,3,2,1,0:T(8,128)(2,1)}, f32[2,2,8,16,128]{4,3,2,1,0:T(8,128)}) custom-call(bf16[8,384,768]{2,1,0:T(8,128)(2,1)} %bitcast.192, bf16[8,128,768]{2,1,0:T(8,128)(2,1)} %bitcast.171, bf16[2,2,8,192,768]{4,3,2,1,0:T(8,128)(2,1)} %bitcast.185, f32[2,2,8,16,128]{4,3,2,1,0:T(8,128)} %bitcast.177), custom_call_target="tpu_custom_call" | custom-call | flops 120000004096 | tf_op jit(solution)/shard_map/finish/pallas_call | solution.py:510
  583.9 4.6 slice.242
  588.5 1.5 copy-done.25
  590.0 6.6 %slice.241 = f32[6,768,768]{2,1,0:T(8,128)} slice(bf16[8,768,768]{2,1,0:T(8,128)(2,1)S(1)} %bitcast.173), slice={[0:6], [0:768], [0:768]} | slice | bytes 28311552 | tf_op jit(solution)/shard_map/slice | solution.py:1341
  601.0 4.2 convert_add_fusion.1
  605.2 3.4 convert_add_fusion.2
  (308 shorter events, 47.2 us)
Async XLA Ops:
  0.6 137.8 %copy-start = (bf16[768,8]{0,1:T(8,128)(2,1)S(1)}, bf16[768,8]{0,1:T(8,128)(2,1)}, u32[]{:S(2)}) copy-start(bf16[768,8]{0,1:T(8,128)(2,1)} %param.17) | copy-start | bytes 36868
  1.9 69.4 %copy-start.73 = (f32[384]{0:T(512)}, f32[384]{0:T(512)S(1)}, u32[]{:S(2)}) copy-start(f32[384]{0:T(512)S(1)} %fusion.129) | copy-start | bytes 4612
  3.3 121.9 %copy-start.77 = (f32[768]{0:T(1024)}, f32[768]{0:T(1024)S(1)}, u32[]{:S(2)}) copy-start(f32[768]{0:T(1024)S(1)} %get-tuple-element.136) | copy-start | bytes 9220
  3.3 134.4 %copy-start.57 = (f32[768]{0:T(1024)}, f32[768]{0:T(1024)S(1)}, u32[]{:S(2)}) copy-start(f32[768]{0:T(1024)S(1)} %get-tuple-element.135) | copy-start | bytes 9220
  6.0 68.7 %copy-start.68 = (f32[32,12]{0,1:T(8,128)S(1)}, f32[32,12]{0,1:T(8,128)}, u32[]{:S(2)}) copy-start(f32[32,12]{0,1:T(8,128)} %param.16) | copy-start | bytes 4612
  6.0 72.5 %copy-start.83 = (s32[1,384,1]{1,2,0:T(1,128)S(1)}, s32[1,384,1]{1,2,0:T(1,128)}, u32[]{:S(2)}) copy-start(s32[1,384,1]{1,2,0:T(1,128)} %param.18) | copy-start | bytes 4612
  71.3 78.6 %collective-permute-start.5 = (bf16[2,768,384]{2,1,0:T(8,128)(2,1)}, bf16[2,768,384]{2,1,0:T(8,128)(2,1)}, u32[]{:S(2)}, u32[]{:S(2)}) collective-permute-start(bf16[2,768,384]{2,1,0:T(8,128)(2,1)} %refs_1_), channel_id=1, source_target_pairs={{0,8},{4,0},{8,12},{12,4},{16,24},{20,16},{24,28},{28,20},{1,9},{5... | collective-permute-start | bytes 3538952 | tf_op jit(solution)/shard_map/ppermute | solution.py:1154
  72.6 40.7 %collective-permute-start = (bf16[2,768,384]{2,1,0:T(8,128)(2,1)}, bf16[2,768,384]{2,1,0:T(8,128)(2,1)}, u32[]{:S(2)}, u32[]{:S(2)}) collective-permute-start(bf16[2,768,384]{2,1,0:T(8,128)(2,1)} %refs_1_), channel_id=1, source_target_pairs={{0,4},{4,12},{8,0},{12,8},{16,20},{20,28},{24,16},{28,24},{1,5},{5... | collective-permute-start | bytes 3538952 | tf_op jit(solution)/shard_map/ppermute | solution.py:1153
  72.8 78.1 %collective-permute-start.4 = (bf16[2,768,384]{2,1,0:T(8,128)(2,1)}, bf16[2,768,384]{2,1,0:T(8,128)(2,1)}, u32[]{:S(2)}, u32[]{:S(2)}) collective-permute-start(bf16[2,768,384]{2,1,0:T(8,128)(2,1)} %refs_2_.2), channel_id=1, source_target_pairs={{0,4},{4,12},{8,0},{12,8},{16,20},{20,28},{24,16},{28,24},{1,5},{5... | collective-permute-start | bytes 3538952 | tf_op jit(solution)/shard_map/ppermute | solution.py:1153
  74.1 48.8 %collective-permute-start.1 = (bf16[2,768,384]{2,1,0:T(8,128)(2,1)}, bf16[2,768,384]{2,1,0:T(8,128)(2,1)}, u32[]{:S(2)}, u32[]{:S(2)}) collective-permute-start(bf16[2,768,384]{2,1,0:T(8,128)(2,1)} %refs_2_.2), channel_id=1, source_target_pairs={{0,8},{4,0},{8,12},{12,4},{16,24},{20,16},{24,28},{28,20},{1,9},{5... | collective-permute-start | bytes 3538952 | tf_op jit(solution)/shard_map/ppermute | solution.py:1154
  78.5 60.3 %copy-start.53 = (s32[384]{0:T(512)}, s32[384]{0:T(512)S(1)}, u32[]{:S(2)}) copy-start(s32[384]{0:T(512)S(1)} %reduce.37) | copy-start | bytes 4612
  80.9 30.8 %copy-start.9 = (f32[6,2,384]{2,1,0:T(2,128)}, f32[6,2,384]{2,1,0:T(2,128)S(1)}, u32[]{:S(2)}) copy-start(f32[6,2,384]{2,1,0:T(2,128)S(1)} %select_select_fusion.refs_0_) | copy-start | bytes 55300
  82.0 40.9 %copy-start.33 = (bf16[1,384,768]{2,1,0:T(8,128)(2,1)S(1)}, bf16[1,384,768]{2,1,0:T(8,128)(2,1)}, u32[]{:S(2)}) copy-start(bf16[1,384,768]{2,1,0:T(8,128)(2,1)} %param.11) | copy-start | bytes 1769476
  82.0 40.9 %copy-start.35 = (bf16[2,768,768]{2,1,0:T(8,128)(2,1)S(1)}, bf16[2,768,768]{2,1,0:T(8,128)(2,1)}, u32[]{:S(2)}) copy-start(bf16[2,768,768]{2,1,0:T(8,128)(2,1)} %param.14) | copy-start | bytes 7077892
  111.6 12.0 %copy-start.7 = (bf16[384,768]{1,0:T(8,128)(2,1)}, bf16[384,768]{1,0:T(8,128)(2,1)S(1)}, u32[]{:S(2)}) copy-start(bf16[384,768]{1,0:T(8,128)(2,1)S(1)} %get-tuple-element.78) | copy-start | bytes 1769476
  111.7 12.0 %copy-start.21 = (f32[384,768]{1,0:T(8,128)}, f32[384,768]{1,0:T(8,128)S(1)}, u32[]{:S(2)}) copy-start(f32[384,768]{1,0:T(8,128)S(1)} %get-tuple-element.96.wide_ref) | copy-start | bytes 3538948
  112.2 27.2 %copy-start.61 = (s32[384]{0:T(512)}, s32[384]{0:T(512)S(1)}, u32[]{:S(2)}) copy-start(s32[384]{0:T(512)S(1)} %add_select_fusion) | copy-start | bytes 4612
  123.6 13.2 %copy-start.42 = (f32[384,768]{1,0:T(8,128)}, f32[384,768]{1,0:T(8,128)S(1)}, u32[]{:S(2)}) copy-start(f32[384,768]{1,0:T(8,128)S(1)} %get-tuple-element.175) | copy-start | bytes 3538948
  123.7 25.3 %collective-permute-start.2 = (bf16[2,768,384]{2,1,0:T(8,128)(2,1)}, bf16[2,768,384]{2,1,0:T(8,128)(2,1)S(1)}, u32[]{:S(2)}, u32[]{:S(2)}) collective-permute-start(bf16[2,768,384]{2,1,0:T(8,128)(2,1)} %collective-permute-done.refs_3_), channel_id=1, source_target_pairs={{0,4},{4,12},{8,0},{12,8},{16,20},{20,28},{24,16},{28,24},{1,5},{5... | collective-permute-start | bytes 3538952 | tf_op jit(solution)/shard_map/ppermute | solution.py:1167
  125.0 24.9 %collective-permute-start.3 = (bf16[2,768,384]{2,1,0:T(8,128)(2,1)}, bf16[2,768,384]{2,1,0:T(8,128)(2,1)S(1)}, u32[]{:S(2)}, u32[]{:S(2)}) collective-permute-start(bf16[2,768,384]{2,1,0:T(8,128)(2,1)} %collective-permute-done.1.refs_6_), channel_id=1, source_target_pairs={{0,8},{4,0},{8,12},{12,4},{16,24},{20,16},{24,28},{28,20},{1,9},{5... | collective-permute-start | bytes 3538952 | tf_op jit(solution)/shard_map/ppermute | solution.py:1168
  127.3 9.5 %copy-start.17 = (bf16[384,768]{1,0:T(8,128)(2,1)}, bf16[384,768]{1,0:T(8,128)(2,1)S(1)}, u32[]{:S(2)}) copy-start(bf16[384,768]{1,0:T(8,128)(2,1)S(1)} %convolution_convert_fusion.7.q_ref) | copy-start | bytes 1769476
  150.9 145.0 %copy-start.62 = (s32[384]{0:T(512)S(1)}, s32[384]{0:T(512)}, u32[]{:S(2)}) copy-start(s32[384]{0:T(512)} %copy-done.61) | copy-start | bytes 4612
  303.4 28.4 %collective-permute-start.6 = (bf16[2,768,384]{2,1,0:T(8,128)(2,1)}, bf16[2,768,384]{2,1,0:T(8,128)(2,1)}, u32[]{:S(2)}, u32[]{:S(2)}) collective-permute-start(bf16[2,768,384]{2,1,0:T(8,128)(2,1)} %get-tuple-element.91), channel_id=1, source_target_pairs={{0,8},{4,0},{8,12},{12,4},{16,24},{20,16},{24,28},{28,20},{1,9},{5... | collective-permute-start | bytes 3538952 | tf_op jit(solution)/shard_map/ppermute | solution.py:1225
  303.6 28.2 %collective-permute-start.7 = (bf16[2,768,384]{2,1,0:T(8,128)(2,1)}, bf16[2,768,384]{2,1,0:T(8,128)(2,1)}, u32[]{:S(2)}, u32[]{:S(2)}) collective-permute-start(bf16[2,768,384]{2,1,0:T(8,128)(2,1)} %get-tuple-element.92), channel_id=1, source_target_pairs={{0,4},{4,12},{8,0},{12,8},{16,20},{20,28},{24,16},{28,24},{1,5},{5... | collective-permute-start | bytes 3538952 | tf_op jit(solution)/shard_map/ppermute | solution.py:1224
  304.8 17.5 %copy-start.39 = (bf16[384,768]{1,0:T(8,128)(2,1)S(1)}, bf16[384,768]{1,0:T(8,128)(2,1)}, u32[]{:S(2)}) copy-start(bf16[384,768]{1,0:T(8,128)(2,1)} %copy-done.38) | copy-start | bytes 1769476
  304.8 17.8 %copy-start.11 = (bf16[8,128,768]{2,1,0:T(8,128)(2,1)S(1)}, bf16[8,128,768]{2,1,0:T(8,128)(2,1)}, u32[]{:S(2)}) copy-start(bf16[8,128,768]{2,1,0:T(8,128)(2,1)} %get-tuple-element.110) | copy-start | bytes 4718596
  322.3 9.5 %copy-start.15 = (bf16[384,768]{1,0:T(8,128)(2,1)}, bf16[384,768]{1,0:T(8,128)(2,1)S(1)}, u32[]{:S(2)}) copy-start(bf16[384,768]{1,0:T(8,128)(2,1)S(1)} %get-tuple-element.95) | copy-start | bytes 1769476
  322.7 9.1 %copy-start.43 = (f32[384,768]{1,0:T(8,128)S(1)}, f32[384,768]{1,0:T(8,128)}, u32[]{:S(2)}) copy-start(f32[384,768]{1,0:T(8,128)} %copy-done.42) | copy-start | bytes 3538948
  322.7 9.1 %copy-start.78 = (f32[768]{0:T(1024)S(1)}, f32[768]{0:T(1024)}, u32[]{:S(2)}) copy-start(f32[768]{0:T(1024)} %copy-done.77) | copy-start | bytes 9220
  322.7 9.1 %copy-start.80 = (f32[384]{0:T(512)S(1)}, f32[384]{0:T(512)}, u32[]{:S(2)}) copy-start(f32[384]{0:T(512)} %copy-done.79) | copy-start | bytes 4612
  337.6 42.1 %collective-permute-start.8 = (bf16[2,768,384]{2,1,0:T(8,128)(2,1)S(1)}, bf16[2,768,384]{2,1,0:T(8,128)(2,1)}, u32[]{:S(2)}, u32[]{:S(2)}) collective-permute-start(bf16[2,768,384]{2,1,0:T(8,128)(2,1)S(1)} %copy-done.86), channel_id=1, source_target_pairs={{0,8},{4,0},{8,12},{12,4},{16,24},{20,16},{24,28},{28,20},{1,9},{5... | collective-permute-start | bytes 3538952 | tf_op jit(solution)/shard_map/ppermute | solution.py:1258
  337.9 41.8 %collective-permute-start.9 = (bf16[2,768,384]{2,1,0:T(8,128)(2,1)S(1)}, bf16[2,768,384]{2,1,0:T(8,128)(2,1)}, u32[]{:S(2)}, u32[]{:S(2)}) collective-permute-start(bf16[2,768,384]{2,1,0:T(8,128)(2,1)S(1)} %copy-done.85), channel_id=1, source_target_pairs={{0,4},{4,12},{8,0},{12,8},{16,20},{20,28},{24,16},{28,24},{1,5},{5... | collective-permute-start | bytes 3538952 | tf_op jit(solution)/shard_map/ppermute | solution.py:1257
  (67 other events, 157.7 us)

commit v6 on v5

--- a/solution.py
+++ b/solution.py
@@ -335,7 +335,7 @@
                     xs[a].at[1 - core, place, where, rows],
                     twins[a].at[side, way, step],
                     pair_sem,
-                    (0, side) + lane + (0, step),
+                    (0, side) + lane + (step,),
                     peer,
                 )
                 own[side, lane, step] = fetch(
@@ -398,15 +398,12 @@
                 mines[a].at[0, way, step],
                 crosses[a].at[way, step],
                 cross_sem,
-                (0,) + lane + (0, step),
+                (0,) + lane + (step,),
                 over,
             )
-        if step >= n - 2:
-            scatter(1, step - n + 2)
     latest = {}
+    waiting = [(step, part) for step in range(1, n) for part in range(parts)]
     for step in range(n):
-        if step + 2 < n:
-            scatter(step + 2, 0)
         for lane in lanes:
             a, way = lane
             own[1, lane, step].wait()
@@ -422,67 +419,45 @@
                     mines[a].at[1, way, step],
                     gots[a].at[way, step],
                     ring_sem,
-                    (0,) + lane + (0, step),
+                    (0,) + lane + (step,),
                     sides[way],
                 )
-        if step + 2 < n:
-            scatter(step + 2, 1)
+        if waiting:
+            scatter(*waiting.pop(0))
     keep, done = [], []
-    streams = []
-    for a, way in lanes:
-        half = xs[a].shape[-2] // 2
-        if half % 48 == 0:
-            some = half * 2 // 3
-            streams += [
-                (a, way, 0, way * half, some, False, True),
-                (a, way, 1, way * half + some, half - some, False, False),
-                (a, way, 2, way * half + some, half - some, True, False),
-            ]
-        else:
-            streams.append((a, way, 0, way * half, half, False, True))
     latest, crossing = {}, {}
 
-    def target_of(stream, step, other):
-        a, way, number, first, size = stream[:5]
+    def target_of(lane, step, place):
+        a, way = lane
         where = at(pos - step) if way == 0 else at(pos + step)
-        return outs[a].at[core, 1 - chip if other else chip, where, pl.ds(first, size)]
-
-    def hand_on(stream, step):
-        a, way, number = stream[:3]
-        crossing[stream, step].wait_recv()
-        target = target_of(stream, step, True)
-        done.append(push(target, target, pair_sem, (1, 1, a, way, number, step), peer))
+        return outs[a].at[core, place, where, span(outs[a], way)]
+
+    def hand_on(step):
+        for lane in lanes:
+            crossing[lane, step].wait_recv()
+            target = target_of(lane, step, 1 - chip)
+            done.append(push(target, target, pair_sem, (1, 1) + lane + (step,), peer))
 
     for step in range(n):
-        for stream in streams:
-            a, way, number, first, size, other, always = stream
+        for lane in lanes:
+            a, way = lane
             if step:
-                latest[stream].wait_recv()
-            target = target_of(stream, step, other)
-            if step or other:
-                source = target
-            else:
-                source = mines[a].at[1, way, n - 1, pl.ds(first - way * (xs[a].shape[-2] // 2), size)]
-            if step == 0 and other:
-                crossing[streams[streams.index(stream) - 1], 0].wait_recv()
+                latest[lane].wait_recv()
+            target = target_of(lane, step, chip)
+            source = target if step else mines[a].at[1, way, n - 1]
             if step < n - 1:
-                latest[stream] = push(
-                    source, target, ring_sem, (1, a, way, number, step), sides[way]
-                )
-            if not other and (always or step == 0):
-                crossing[stream, step] = push(
-                    source, target, cross_sem, (1, a, way, number, step), over
-                )
-            done.append(push(source, target, pair_sem, (1, 0, a, way, number, step), peer))
-            if step == 0 and not other:
-                keep.append(fetch(source, target, own_sem.at[0, a, way, number]))
+                latest[lane] = push(source, target, ring_sem, (1,) + lane + (step,), sides[way])
+            crossing[lane, step] = push(source, target, cross_sem, (1,) + lane + (step,), over)
+            done.append(push(source, target, pair_sem, (1, 0) + lane + (step,), peer))
+            if step == 0:
+                keep.append(fetch(source, target, own_sem.at[(0,) + lane + (0,)]))
+        if waiting:
+            scatter(*waiting.pop(0))
         if step:
-            for stream in streams:
-                if stream[6]:
-                    hand_on(stream, step - 1)
-    for stream in streams:
-        if stream[6]:
-            hand_on(stream, n - 1)
+            hand_on(step - 1)
+    hand_on(n - 1)
+    while waiting:
+        scatter(*waiting.pop(0))
     for copy in keep:
         copy.wait()
     for copy in done:
@@ -520,9 +495,9 @@
             dma((few, 2, 2, n)),
             dma((2, few, 2, 2, n)),
             dma((2, many, 2, n)),
-            dma((2, 2, 2, many, 2, 3, n)),
-            dma((2, 2, many, 2, 3, n)),
-            dma((2, 2, many, 2, 3, n)),
+            dma((2, 2, 2, many, 2, n)),
+            dma((2, 2, many, 2, n)),
+            dma((2, 2, many, 2, n)),
         ],
         compiler_params=pltpu.CompilerParams(
             collective_id=number, has_side_effects=True, vmem_limit_bytes=58 << 20
@@ -803,54 +778,116 @@
     )(seq_at, queries, keys, values, upstream, wide, lse, *extra)
 
 
-def token_back_kernel(x_ref, dk_ref, dv_ref, wk_ref, wv_ref, dx_ref, gk_ref, gv_ref, gain_ref, k_acc, v_acc):
+def key_value_back(x_ref, dk_ref, dv_ref, wk_ref, wv_ref, dx_ref):
     x, dk, dv = x_ref[...], dk_ref[...], dv_ref[...]
     dx = dot_last(dk, wk_ref[0]) + dot_last(dv, wv_ref[0])
     dx_ref[...] = dx.astype(dx_ref.dtype)
     gain = jnp.sum(dx * x.astype(jnp.float32), axis=0, keepdims=True)
-    gk, gv = dot_first(x, dk), dot_first(x, dv)
-    step, last = pl.program_id(0), pl.num_programs(0) - 1
-
+    return gain, dot_first(x, dk), dot_first(x, dv)
+
+
+def add_up(step, last, made, totals, outs):
     @pl.when(step == 0)
     def _():
-        gain_ref[...] = gain
-        k_acc[...] = gk
-        v_acc[...] = gv
+        for total, term in zip(totals, made):
+            total[...] = term
+
+    @pl.when(step > 0)
+    def _():
+        for total, term in zip(totals, made):
+            total[...] += term
+
+    @pl.when(step == last)
+    def _():
+        for out, total in zip(outs, totals):
+            out[...] = total[...].astype(out.dtype)
+
+
+def memory_back_kernel(x_ref, dk_ref, dv_ref, wk_ref, wv_ref, dx_ref, grad_ref, k_acc, v_acc):
+    _, gk, gv = key_value_back(x_ref, dk_ref, dv_ref, wk_ref, wv_ref, dx_ref)
+    outs = [grad_ref.at[0], grad_ref.at[1]]
+    add_up(pl.program_id(0), pl.num_programs(0) - 1, (gk, gv), (k_acc, v_acc), outs)
+
+
+def token_back_kernel(*refs):
+    x_ref, dk_ref, dv_ref, wk_ref, wv_ref, own_ref, dq_ref, wq_ref = refs[:8]
+    terms, (dx_ref, grad_ref, gain_ref, query_ref), sums = refs[8:14], refs[14:18], refs[18:20]
+    k_acc, v_acc = refs[20:]
+    step, last = pl.program_id(0), pl.num_programs(0) - 1
+    for i, out in enumerate(sums):
+        own, *others = terms[3 * i : 3 * i + 3]
+        total = own[...]
+        for other in others:
+            total = total + other[...].astype(jnp.float32)
+        out[...] = total
+    gain, gk, gv = key_value_back(x_ref, dk_ref, dv_ref, wk_ref, wv_ref, dx_ref)
+    add_up(step, last, (gk, gv), (k_acc, v_acc), [grad_ref.at[1], grad_ref.at[2]])
+
+    @pl.when(step == 0)
+    def _():
+        own, dq = own_ref[...], dq_ref[...]
+        back = dot_last(dq, wq_ref[0])
+        query_ref[...] = back
+        gain_ref[...] = gain + jnp.sum(back * own.astype(jnp.float32), axis=0, keepdims=True)
+        grad_ref[0] = dot_first(own, dq).astype(grad_ref.dtype)
 
     @pl.when(step > 0)
     def _():
         gain_ref[...] += gain
-        k_acc[...] += gk
-        v_acc[...] += gv
-
-    @pl.when(step == last)
-    def _():
-        gk_ref[...] = k_acc[...].astype(gk_ref.dtype)
-        gv_ref[...] = v_acc[...].astype(gv_ref.dtype)
-
-
-def token_back(tokens, grad_keys, grad_values, proj_in, rows, first, name):
+
+
+def memory_back(tokens, grad_keys, grad_values, proj_in):
     total = tokens.shape[0]
+    rows = math.gcd(total, 512)
     block = pl.BlockSpec((rows, D), lambda i: (i, 0))
     weight = lambda number: pl.BlockSpec((1, D, D), lambda i: (number, 0, 0))
-    whole = lambda r: pl.BlockSpec((r, D), lambda i: (0, 0))
-    grad = jax.ShapeDtypeStruct((D, D), tokens.dtype)
     return pl.pallas_call(
-        token_back_kernel,
+        memory_back_kernel,
         grid=(total // rows,),
         out_shape=[
             jax.ShapeDtypeStruct(tokens.shape, tokens.dtype),
-            grad,
-            grad,
-            jax.ShapeDtypeStruct((1, D), jnp.float32),
+            jax.ShapeDtypeStruct((2, D, D), tokens.dtype),
         ],
-        in_specs=[block] * 3 + [weight(first), weight(first + 1)],
-        out_specs=[block, whole(D), whole(D), whole(1)],
+        in_specs=[block] * 3 + [weight(4), weight(5)],
+        out_specs=[block, pl.BlockSpec((2, D, D), lambda i: (0, 0, 0))],
         scratch_shapes=[pltpu.VMEM((D, D), jnp.float32)] * 2,
         compiler_params=pltpu.CompilerParams(vmem_limit_bytes=48 << 20),
-        cost_estimate=cost(18 if total > 2048 else 8),
-        name=name,
+        cost_estimate=cost(8),
+        name="memory_back",
     )(tokens, grad_keys, grad_values, proj_in, proj_in)
+
+
+def token_back(tokens, grad_keys, grad_values, own, grad_queries, proj_in, terms):
+    steps = tokens.shape[0] // (2 * own.shape[0])
+    block = pl.BlockSpec((2 * own.shape[0], D), lambda i: (i, 0))
+    weight = lambda number: pl.BlockSpec((1, D, D), lambda i: (number, 0, 0))
+    whole = pl.BlockSpec(own.shape, lambda i: (0, 0))
+    count, _, hidden = terms[0].shape
+    expert = pl.BlockSpec((count, D // steps, hidden), lambda i: (0, i, 0))
+    return pl.pallas_call(
+        token_back_kernel,
+        grid=(steps,),
+        out_shape=[
+            jax.ShapeDtypeStruct(tokens.shape, tokens.dtype),
+            jax.ShapeDtypeStruct((8, D, D), tokens.dtype),
+            jax.ShapeDtypeStruct((1, D), jnp.float32),
+            jax.ShapeDtypeStruct(own.shape, jnp.float32),
+        ]
+        + [jax.ShapeDtypeStruct(terms[0].shape, jnp.float32)] * 2,
+        in_specs=[block] * 3 + [weight(1), weight(2), whole, whole, weight(0)] + [expert] * 6,
+        out_specs=[
+            block,
+            pl.BlockSpec((3, D, D), lambda i: (0, 0, 0)),
+            pl.BlockSpec((1, D), lambda i: (0, 0)),
+            whole,
+            expert,
+            expert,
+        ],
+        scratch_shapes=[pltpu.VMEM((D, D), jnp.float32)] * 2,
+        compiler_params=pltpu.CompilerParams(vmem_limit_bytes=56 << 20),
+        cost_estimate=cost(24),
+        name="token_back",
+    )(tokens, grad_keys, grad_values, proj_in, proj_in, own, grad_queries, proj_in, *terms)
 
 
 def bias_lines(bias_table):
@@ -890,10 +927,10 @@
 
 
 def expert_kernel(n, m, slots, *refs):
-    x_ref, maps, result_ref, grads = refs[0], refs[1:9], refs[9], refs[10:16]
-    rows, parts, backs, up_all, down_all, act_all, du_all = refs[16:23]
-    grad_bufs, far_bufs = refs[23:31], refs[31:33]
-    map_sem, own_sem, grad_sem, go_sem, back_sem, term_sem = refs[33:]
+    x_ref, maps, result_ref, grads = refs[0], refs[1:7], refs[7], refs[8:14]
+    rows, parts, backs, up_all, down_all, act_all, du_all = refs[14:21]
+    grad_bufs, far_bufs = refs[21:29], refs[29:31]
+    map_sem, own_sem, grad_sem, go_sem, back_sem, term_sem, far_sem = refs[31:]
     seq, exp = lax.axis_index("seq"), lax.axis_index("exp")
     groups, count = n // QUAD, x_ref.shape[1] // slots
     batch = max(1, 128 // slots)
@@ -929,13 +966,18 @@
     own = pltpu.make_async_copy(x_ref.at[exp], rows.at[0, exp], own_sem.at[0])
     own.start()
     fetched = []
-    for j in range(QUAD):
+    for j in range(1, QUAD):
+        j = j % (QUAD - 1)
         for at, (source, target) in enumerate(((maps[2 * j], up_all), (maps[2 * j + 1], down_all))):
             copy = pltpu.make_async_copy(source, target.at[j], map_sem.at[at, j])
             copy.start()
             fetched.append(copy)
     for copy in fetched:
         copy.wait()
+    far_maps = [
+        push(up_all.at[1], up_all.at[3], far_sem, 0, 0, side["next"], exp),
+        push(down_all.at[2], down_all.at[3], far_sem, 0, 1, side["last"], exp),
+    ]
     own.wait()
     slope = math.sqrt(2.0 / math.pi)
     coming = {}
@@ -991,6 +1033,8 @@
                     source,
                 )
 
+    for copy in far_maps:
+        copy.wait_recv()
     work(0, 0, m)
     for g in range(1, groups):
         for first in range(0, m, batch):
@@ -1056,7 +1100,7 @@
         result_ref[where] = total_row.astype(result_ref.dtype)
     for copy in stored:
         copy.wait()
-    for copy in terms_out:
+    for copy in terms_out + far_maps:
         copy.wait_send()
     for copies in (going, coming):
         for copy in copies.values():
@@ -1070,7 +1114,7 @@
     big = pltpu.VMEM((groups,) + x.shape, x.dtype)
     stack = pltpu.VMEM((QUAD,) + maps[0].shape, x.dtype)
     kept = pltpu.VMEM((count, QUAD, total, hidden), x.dtype)
-    grads = [(w.shape, jnp.float32 if i < 2 else jnp.bfloat16) for i, w in enumerate(maps)]
+    grads = [(maps[0].shape, jnp.float32 if i < 2 else jnp.bfloat16) for i in range(2 * QUAD)]
     dma = pltpu.SemaphoreType.DMA
     return pl.pallas_call(
         functools.partial(expert_kernel, n, m, slots),
@@ -1088,6 +1132,7 @@
             dma((6,)),
             dma((2, groups, m)),
             dma((2, groups, m)),
+            dma((2, 1, 2)),
             dma((2, 1, 2)),
         ],
         compiler_params=pltpu.CompilerParams(
@@ -1161,11 +1206,6 @@
     attended_self_low, attended_self, lse_self = attend(
         seq_at, queries, key_all, value_all, lines
     )
-    attended_self_low, in_last, out_next = lax.optimization_barrier(
-        (attended_self_low, in_last, out_next)
-    )
-    in_far = lax.ppermute(in_last, "seq", to_next)
-    out_far = lax.ppermute(out_next, "seq", to_last)
     after_self = tokens + jnp.dot(
         attended_self_low, proj_out[0], preferred_element_type=jnp.float32
     )
@@ -1216,8 +1256,7 @@
         .astype(jnp.bfloat16)
         .reshape(m, local_experts * slots, 2 * D)
     )
-    sent_rows, in_far, out_far = lax.optimization_barrier((sent_rows, in_far, out_far))
-    maps = [in_own, out_own, in_last, out_last, in_next, out_next, in_far, out_far]
+    maps = [in_own, out_own, in_last, out_last, in_next, out_next]
     returned, *terms = run_experts(sent_rows, maps, n, m, slots, 2)
     returned = returned.reshape(expert_count * slots, 2 * D)
     gin_own, gout_own, gin_next, gout_last, gin_last, gout_next = terms
@@ -1261,14 +1300,8 @@
         after_self, gain_rows[1], input_grad(grad_cross_query, proj_in[3])
     )
     grad_after_self = grad_after_cross + grad_self_part
-    grad_memory_part, grad_key_cross, grad_value_cross, _ = token_back(
-        memory_all,
-        grad_memory_keys,
-        grad_memory_values,
-        proj_in,
-        math.gcd(n * memory_count, 512),
-        4,
-        "memory_back",
+    grad_memory_part, grads_cross = memory_back(
+        memory_all, grad_memory_keys, grad_memory_values, proj_in
     )
 
     grad_self_low = grad_after_self.astype(jnp.bfloat16)
@@ -1289,30 +1322,28 @@
             (grad_self_query, grad_keys, grad_values, near, sums, gout_last, gin_next)
         )
     )
-    grad_expert_in = gin_own + gin_last.astype(jnp.float32) + gin_next.astype(jnp.float32)
-    grad_expert_out = gout_own + gout_last.astype(jnp.float32) + gout_next.astype(jnp.float32)
     grad_table = bias_gradient(near, sums)
-    grad_normed_query = input_grad(grad_self_query, proj_in[0])
-    grad_normed_part, grad_key_self, grad_value_self, grad_gain_part = token_back(
-        normed_all, grad_keys, grad_values, proj_in, 2 * token_count, 1, "token_back"
-    )
-    grad_gain_self = (
-        grad_gain_part[0]
-        + jnp.sum(grad_normed_query * normed_self.astype(jnp.float32), axis=0)
-    ) / gain_rows[0]
-
-    grads = jnp.concatenate(
-        [
-            weight_grad(normed_self, grad_self_query),
-            grad_key_self,
-            grad_value_self,
-            grad_query_cross,
-            grad_key_cross,
-            grad_value_cross,
-            grad_out_self,
-            grad_out_cross,
-        ]
-    )
+    (
+        grad_normed_part,
+        grads,
+        grad_gain_part,
+        grad_normed_query,
+        grad_expert_in,
+        grad_expert_out,
+    ) = token_back(
+        normed_all,
+        grad_keys,
+        grad_values,
+        normed_self,
+        grad_self_query,
+        proj_in,
+        [gin_own, gin_last, gin_next, gout_own, gout_last, gout_next],
+    )
+    grad_gain_self = grad_gain_part[0] / gain_rows[0]
+
+    grads = lax.dynamic_update_slice(grads, grads_cross, (4, 0, 0))
+    for number, grad in ((3, grad_query_cross), (6, grad_out_self), (7, grad_out_cross)):
+        grads = lax.dynamic_update_slice(grads, grad[None], (number, 0, 0))
     grad_gains = jnp.stack([grad_gain_self, grad_gain_cross, grad_gain_mix])
     small = [
         grad_gains.reshape(-1, TILE),
@@ -1325,7 +1356,7 @@
             grad_normed_part.reshape(n, token_count, D),
             grad_memory_part.reshape(n, memory_count, D),
         ],
-        grads,
+        grads.reshape(-1, D),
         jnp.concatenate(small),
         n,
         m,

time: 621 us -> 581 us (0.936)
  waiting for transfers between devices: 17.7 us -> 0.02 us
  Pallas kernels: 489 us -> 479 us
  other arithmetic: 21.1 us -> 13.6 us
    pallas_call x1, Pallas kernels: 153 us -> 136 us  [finish(): pl.pallas_call(functools.partial(finish_kernel, n, (few, many)), out_shap...]
    ppermute x2, waiting for transfers between devices: 9.56 us -> 0.01 us  [body(): lax.ppermute(w, 'seq', to_last)]
    ppermute x2 -> x0, waiting for transfers between devices: 8.15 us -> none  [the longest x1 7.16 us: body(): in_far = lax.ppermute(in_last, 'seq', to_next)]
    add x2 -> x0, other arithmetic: 7.63 us -> none  [the longest x1 4.2 us: body(): gout_own + gout_last.astype(jnp.float32) + gout_next.astype(jnp.float32)]
    unnamed x186 -> x170, local copies, waits for them, and re-layouts: 25.5 us -> 20.7 us
  transfers between devices with their start and end apart: 10 -> 8, of which waited for: 3 -> 0; matrix products, arithmetic and copies ran while one was open for 2% -> 3% of each run, Pallas kernels for 17% -> 18%
where the time goes in v6:
time: 581 us; the launch traced here: 572 us
  Pallas kernels  479 us (82%)
  local copies, waits for them, and re-layouts  46.5 us (8%)
  matrix products  22 us (4%)
  other arithmetic  13.6 us (2%)
  starting transfers between devices  8.78 us (2%)
    pallas_call x1, Pallas kernels, run_experts(): pl.pallas_call(functools.partial(expert_kernel, n, m, slots), out_shape=[...  146 us
    pallas_call x1, Pallas kernels, finish(): pl.pallas_call(functools.partial(finish_kernel, n, (few, many)), out_shap...  136 us
    pallas_call x1, Pallas kernels, gather_projected(): pl.pallas_call(functools.partial(gather_kernel, n, parts), out_shape=[jax...  65.3 us
    pallas_call x2, Pallas kernels, attend_back(): pl.pallas_call(functools.partial(attend_back_kernel, causal, block), grid...  55.6 us
    pallas_call x2, Pallas kernels, attend(): pl.pallas_call(functools.partial(attend_kernel, causal, block), grid=(PAI...  38.7 us
    pallas_call x1, Pallas kernels, token_back(): pl.pallas_call(token_back_kernel, grid=(steps,), out_shape=[jax.ShapeDtyp...  27 us
    unnamed x170, local copies, waits for them, and re-layouts  20.7 us
  transfers between devices with their start and end apart: 8, of which 0 were waited for; matrix products, arithmetic and copies ran while one was open for 3% of the time, Pallas kernels for 18%

profile of v6, /device:TPU:25, one launch (start us, length us, event | category | flops | bytes accessed | tf_op | source)
XLA Modules:
  0.0 571.6 jit_solution(12944686384276902788)
XLA Ops:
  3.9 2.1 fusion.15.refs_0_.refs_5_
  5.9 65.3 %gather_projected.1 = (bf16[8,384,768]{2,1,0:T(8,128)(2,1)}, bf16[8,128,768]{2,1,0:T(8,128)(2,1)}, bf16[384,768]{1,0:T(8,128)(2,1)}, bf16[8,384,768]{2,1,0:T(8,1...) custom-call(bf16[384,768]{1,0:T(8,128)(2,1)} %fusion.15.refs_0_.refs_5_, ...), custom_call_target="tpu_custom_call" | custom-call | flops 60000002048 | tf_op jit(solution)/shard_map/gather_projected/pallas_call | solution.py:179
  81.5 29.7 %attend_self.1 = (bf16[384,768]{1,0:T(8,128)(2,1)S(1)}, f32[384,768]{1,0:T(8,128)S(1)}, f32[6,2,384]{2,1,0:T(2,128)S(1)}) custom-call(s32[1]{0:T(128)} %bitcast.1.s_ref, bf16[384,768]{1,0:T(8,128)(2,1)S(1)} %copy-done.20, bf16[3072,768]{1,0:T(8,128)(2,1)} %bitcast.192, bf16[3072,768]{1,0:T(8,128)(2,1)} %bitcast.194, f32[6,2,384]{2,1,0:T(2,128)S(1)} %select_select_fusion.refs_0_), custom_call_target="tpu_custom_call" | custom-call | flops 40000000000 | tf_op jit(solution)/shard_map/attend_self/pallas_call | solution.py:643
  112.5 2.4 convolution_convert_fusion.6.q_ref
  115.1 9.0 %attend_cross.1 = (bf16[384,768]{1,0:T(8,128)(2,1)S(1)}, f32[384,768]{1,0:T(8,128)S(1)}, f32[6,2,384]{2,1,0:T(2,128)S(1)}) custom-call(s32[1]{0:T(128)} %bitcast.1.s_ref, bf16[384,768]{1,0:T(8,128)(2,1)S(1)} %convolution_convert_fusion.6.q_ref, bf16[1024,768]{1,0:T(8,128)(2,1)S(1)} %bitcast.172, bf16[1024,768]{1,0:T(8,128)(2,1)S(1)} %bitcast.174), custom_call_target="tpu_custom_call" | custom-call | flops 10000000000 | tf_op jit(solution)/shard_map/attend_cross/pallas_call | solution.py:643
  127.5 2.2 convolution_convert_fusion
  130.9 146.4 %run_experts.1 = (bf16[4,128,1536]{2,1,0:T(8,128)(2,1)}, f32[2,768,384]{2,1,0:T(8,128)}, f32[2,768,384]{2,1,0:T(8,128)}, bf16[2,768,384]{2,1,0:T(8,128)(2,1)}, b...) custom-call(bf16[4,128,1536]{2,1,0:T(8,128)(2,1)} %bitcast.197, ...), custom_call_target="tpu_custom_call" | custom-call | flops 149999992832 | tf_op jit(solution)/shard_map/run_experts/pallas_call | solution.py:1119
  277.4 2.4 fusion.34
  284.7 4.0 collective-permute-start.4
  288.8 15.2 %attend_cross_back.1 = (bf16[384,768]{1,0:T(8,128)(2,1)S(1)}, bf16[1024,768]{1,0:T(8,128)(2,1)S(1)}, bf16[1024,768]{1,0:T(8,128)(2,1)S(1)}) custom-call(s32[1]{0:T(128)} %bitcast.1.s_ref, bf16[384,768]{1,0:T(8,128)(2,1)S(1)} %copy-done.13, bf16[1024,768]{1,0:T(8,128)(2,1)} %bitcast.171, bf16[1024,768]{1,0:T(8,128)(2,1)} %bitcast.173, ...), custom_call_target="tpu_custom_call" | custom-call | flops 15000000512 | tf_op jit(solution)/shard_map/attend_cross_back/pallas_call | solution.py:763
  306.6 1.4 copy-done.15
  308.0 9.7 %memory_back.1 = (bf16[1024,768]{1,0:T(8,128)(2,1)S(1)}, bf16[2,768,768]{2,1,0:T(8,128)(2,1)}) custom-call(bf16[1024,768]{1,0:T(8,128)(2,1)S(1)} %bitcast.170, bf16[1024,768]{1,0:T(8,128)(2,1)S(1)} %copy-done.15, bf16[1024,768]{1,0:T(8,128)(2,1)} %copy-done.16, bf16[6,768,768]{2,1,0:T(8,128)(2,1)} %wv_ref.1, bf16[6,768,768]{2,1,0:T(8,128)(2,1)} %wv_ref.1), custom_call_target="tpu_custom_call" | custom-call | flops 8000000000 | tf_op jit(solution)/shard_map/memory_back/pallas_call | solution.py:844
  317.8 2.7 multiply_reduce_fusion.1
  323.3 1.5 collective-permute-start.6
  324.8 40.4 %attend_self_back.1 = (bf16[384,768]{1,0:T(8,128)(2,1)S(1)}, bf16[3072,768]{1,0:T(8,128)(2,1)}, bf16[3072,768]{1,0:T(8,128)(2,1)}, f32[12,256,128]{2,1,0:T(8,128)S(1)}, f32[6,2,384]{2,1,0:T(2,128)S(1)}) custom-call(s32[1]{0:T(128)} %bitcast.1.s_ref, bf16[384,768]{1,0:T(8,128)(2,1)S(1)} %copy-done.21, bf16[3072,768]{1,0:T(8,128)(2,1)} %bitcast.193, ...), custom_call_target="tpu_custom_call" | custom-call | flops 48000000000 | tf_op jit(solution)/shard_map/attend_self_back/pallas_call | solution.py:763
  367.6 1.6 pad.21
  369.1 27.0 %token_back.1 = (bf16[3072,768]{1,0:T(8,128)(2,1)}, bf16[8,768,768]{2,1,0:T(8,128)(2,1)}, f32[1,768]{1,0:T(1,128)}, f32[384,768]{1,0:T(8,128)}, f32[2,768,384]{2,1,0:T(8,128)}, /*index=5*/f32[2,768,384]{2,1,0:T(8,128)}) custom-call(bf16[3072,768]{1,0:T(8,128)(2,1)} %bitcast.191, bf16[3072,768]{1,0:T(8,128)(2,1)} %get-tuple-element.95.refs_1_, ...), custom_call_target="tpu_custom_call" | custom-call | flops 24000000000 | tf_op jit(solution)/shard_map/token_back/pallas_call | solution.py:867
  397.1 2.8 copy.28
  400.0 2.3 fusion.27
  403.1 3.3 constant_dynamic-update-slice_fusion
  406.4 1.9 fusion.3
  408.3 1.8 fusion.5
  410.2 1.8 fusion.7
  412.0 136.0 %finish.1 = (f32[384,768]{1,0:T(8,128)}, f32[128,768]{1,0:T(8,128)}, bf16[2,2,8,192,768]{4,3,2,1,0:T(8,128)(2,1)}, f32[2,2,8,16,128]{4,3,2,1,0:T(8,128)}) custom-call(bf16[8,384,768]{2,1,0:T(8,128)(2,1)} %bitcast.196, bf16[8,128,768]{2,1,0:T(8,128)(2,1)} %bitcast.175, bf16[2,2,8,192,768]{4,3,2,1,0:T(8,128)(2,1)} %bitcast.189, f32[2,2,8,16,128]{4,3,2,1,0:T(8,128)} %bitcast.181), custom_call_target="tpu_custom_call" | custom-call | flops 120000004096 | tf_op jit(solution)/shard_map/finish/pallas_call | solution.py:485
  549.4 1.3 slice.240
  550.7 1.3 slice.241
  552.0 4.6 slice.238
  556.6 1.5 copy-done.22
  558.2 6.6 %slice.237 = f32[6,768,768]{2,1,0:T(8,128)} slice(bf16[8,768,768]{2,1,0:T(8,128)(2,1)S(1)} %bitcast.177), slice={[0:6], [0:768], [0:768]} | slice | bytes 28311552 | tf_op jit(solution)/shard_map/slice | solution.py:1372
  567.4 1.3 reshape.927
  568.7 1.4 copy.26
  570.1 1.3 reshape.928
  (285 shorter events, 37.3 us)
Async XLA Ops:
  0.6 125.1 %copy-start = (bf16[768,8]{0,1:T(8,128)(2,1)S(1)}, bf16[768,8]{0,1:T(8,128)(2,1)}, u32[]{:S(2)}) copy-start(bf16[768,8]{0,1:T(8,128)(2,1)} %param.17) | copy-start | bytes 36868
  3.2 68.1 %copy-start.59 = (f32[3,768]{1,0:T(4,128)}, f32[3,768]{1,0:T(4,128)S(1)}, u32[]{:S(2)}) copy-start(f32[3,768]{1,0:T(4,128)S(1)} %convert_element_type.403) | copy-start | bytes 27652
  3.3 109.2 %copy-start.71 = (f32[768]{0:T(1024)}, f32[768]{0:T(1024)S(1)}, u32[]{:S(2)}) copy-start(f32[768]{0:T(1024)S(1)} %get-tuple-element.126) | copy-start | bytes 9220
  3.3 121.7 %copy-start.51 = (f32[768]{0:T(1024)}, f32[768]{0:T(1024)S(1)}, u32[]{:S(2)}) copy-start(f32[768]{0:T(1024)S(1)} %get-tuple-element.125) | copy-start | bytes 9220
  5.9 68.8 %copy-start.62 = (f32[32,12]{0,1:T(8,128)S(1)}, f32[32,12]{0,1:T(8,128)}, u32[]{:S(2)}) copy-start(f32[32,12]{0,1:T(8,128)} %param.16) | copy-start | bytes 4612
  5.9 70.1 %copy-start.77 = (s32[1,384,1]{1,2,0:T(1,128)S(1)}, s32[1,384,1]{1,2,0:T(1,128)}, u32[]{:S(2)}) copy-start(s32[1,384,1]{1,2,0:T(1,128)} %param.18) | copy-start | bytes 4612
  71.3 59.6 %collective-permute-start.2 = (bf16[2,768,384]{2,1,0:T(8,128)(2,1)}, bf16[2,768,384]{2,1,0:T(8,128)(2,1)}, u32[]{:S(2)}, u32[]{:S(2)}) collective-permute-start(bf16[2,768,384]{2,1,0:T(8,128)(2,1)} %refs_1_), channel_id=1, source_target_pairs={{0,8},{4,0},{8,12},{12,4},{16,24},{20,16},{24,28},{28,20},{1,9},{5... | collective-permute-start | bytes 3538952 | tf_op jit(solution)/shard_map/ppermute | solution.py:1199
  72.6 58.3 %collective-permute-start = (bf16[2,768,384]{2,1,0:T(8,128)(2,1)}, bf16[2,768,384]{2,1,0:T(8,128)(2,1)}, u32[]{:S(2)}, u32[]{:S(2)}) collective-permute-start(bf16[2,768,384]{2,1,0:T(8,128)(2,1)} %refs_1_), channel_id=1, source_target_pairs={{0,4},{4,12},{8,0},{12,8},{16,20},{20,28},{24,16},{28,24},{1,5},{5... | collective-permute-start | bytes 3538952 | tf_op jit(solution)/shard_map/ppermute | solution.py:1198
  72.8 58.0 %collective-permute-start.3 = (bf16[2,768,384]{2,1,0:T(8,128)(2,1)}, bf16[2,768,384]{2,1,0:T(8,128)(2,1)}, u32[]{:S(2)}, u32[]{:S(2)}) collective-permute-start(bf16[2,768,384]{2,1,0:T(8,128)(2,1)} %refs_2_.2), channel_id=1, source_target_pairs={{0,8},{4,0},{8,12},{12,4},{16,24},{20,16},{24,28},{28,20},{1,9},{5... | collective-permute-start | bytes 3538952 | tf_op jit(solution)/shard_map/ppermute | solution.py:1199
  74.0 56.8 %collective-permute-start.1 = (bf16[2,768,384]{2,1,0:T(8,128)(2,1)}, bf16[2,768,384]{2,1,0:T(8,128)(2,1)}, u32[]{:S(2)}, u32[]{:S(2)}) collective-permute-start(bf16[2,768,384]{2,1,0:T(8,128)(2,1)} %refs_2_.2), channel_id=1, source_target_pairs={{0,4},{4,12},{8,0},{12,8},{16,20},{20,28},{24,16},{28,24},{1,5},{5... | collective-permute-start | bytes 3538952 | tf_op jit(solution)/shard_map/ppermute | solution.py:1198
  76.0 50.1 %copy-start.47 = (s32[384]{0:T(512)}, s32[384]{0:T(512)S(1)}, u32[]{:S(2)}) copy-start(s32[384]{0:T(512)S(1)} %reduce.37) | copy-start | bytes 4612
  77.3 50.3 %copy-start.53 = (s32[384]{0:T(512)}, s32[384]{0:T(512)S(1)}, u32[]{:S(2)}) copy-start(s32[384]{0:T(512)S(1)} %add_select_fusion) | copy-start | bytes 4612
  80.4 30.7 %copy-start.6 = (f32[6,2,384]{2,1,0:T(2,128)}, f32[6,2,384]{2,1,0:T(2,128)S(1)}, u32[]{:S(2)}) copy-start(f32[6,2,384]{2,1,0:T(2,128)S(1)} %select_select_fusion.refs_0_) | copy-start | bytes 55300
  81.5 29.7 %copy-start.29 = (bf16[1,384,768]{2,1,0:T(8,128)(2,1)S(1)}, bf16[1,384,768]{2,1,0:T(8,128)(2,1)}, u32[]{:S(2)}) copy-start(bf16[1,384,768]{2,1,0:T(8,128)(2,1)} %param.11) | copy-start | bytes 1769476
  81.5 29.7 %copy-start.31 = (bf16[2,768,768]{2,1,0:T(8,128)(2,1)S(1)}, bf16[2,768,768]{2,1,0:T(8,128)(2,1)}, u32[]{:S(2)}) copy-start(bf16[2,768,768]{2,1,0:T(8,128)(2,1)} %param.14) | copy-start | bytes 7077892
  112.4 11.7 %copy-start.38 = (f32[384,768]{1,0:T(8,128)}, f32[384,768]{1,0:T(8,128)S(1)}, u32[]{:S(2)}) copy-start(f32[384,768]{1,0:T(8,128)S(1)} %get-tuple-element.165) | copy-start | bytes 3538948
  114.9 9.2 %copy-start.12 = (bf16[384,768]{1,0:T(8,128)(2,1)}, bf16[384,768]{1,0:T(8,128)(2,1)S(1)}, u32[]{:S(2)}) copy-start(bf16[384,768]{1,0:T(8,128)(2,1)S(1)} %convolution_convert_fusion.6.q_ref) | copy-start | bytes 1769476
  130.9 146.5 %copy-start.54 = (s32[384]{0:T(512)S(1)}, s32[384]{0:T(512)}, u32[]{:S(2)}) copy-start(s32[384]{0:T(512)} %copy-done.53) | copy-start | bytes 4612
  284.7 33.0 %collective-permute-start.4 = (bf16[2,768,384]{2,1,0:T(8,128)(2,1)}, bf16[2,768,384]{2,1,0:T(8,128)(2,1)}, u32[]{:S(2)}, u32[]{:S(2)}) collective-permute-start(bf16[2,768,384]{2,1,0:T(8,128)(2,1)} %get-tuple-element.80), channel_id=1, source_target_pairs={{0,8},{4,0},{8,12},{12,4},{16,24},{20,16},{24,28},{28,20},{1,9},{5... | collective-permute-start | bytes 3538952 | tf_op jit(solution)/shard_map/ppermute | solution.py:1264
  288.8 29.0 %collective-permute-start.5 = (bf16[2,768,384]{2,1,0:T(8,128)(2,1)}, bf16[2,768,384]{2,1,0:T(8,128)(2,1)}, u32[]{:S(2)}, u32[]{:S(2)}) collective-permute-start(bf16[2,768,384]{2,1,0:T(8,128)(2,1)} %get-tuple-element.81), channel_id=1, source_target_pairs={{0,4},{4,12},{8,0},{12,8},{16,20},{20,28},{24,16},{28,24},{1,5},{5... | collective-permute-start | bytes 3538952 | tf_op jit(solution)/shard_map/ppermute | solution.py:1263
  288.8 17.5 %copy-start.35 = (bf16[384,768]{1,0:T(8,128)(2,1)S(1)}, bf16[384,768]{1,0:T(8,128)(2,1)}, u32[]{:S(2)}) copy-start(bf16[384,768]{1,0:T(8,128)(2,1)} %copy-done.34) | copy-start | bytes 1769476
  288.8 17.8 %copy-start.8 = (bf16[8,128,768]{2,1,0:T(8,128)(2,1)S(1)}, bf16[8,128,768]{2,1,0:T(8,128)(2,1)}, u32[]{:S(2)}) copy-start(bf16[8,128,768]{2,1,0:T(8,128)(2,1)} %get-tuple-element.106) | copy-start | bytes 4718596
  308.0 9.7 %copy-start.39 = (f32[384,768]{1,0:T(8,128)S(1)}, f32[384,768]{1,0:T(8,128)}, u32[]{:S(2)}) copy-start(f32[384,768]{1,0:T(8,128)} %copy-done.38) | copy-start | bytes 3538948
  308.0 9.8 %copy-start.72 = (f32[768]{0:T(1024)S(1)}, f32[768]{0:T(1024)}, u32[]{:S(2)}) copy-start(f32[768]{0:T(1024)} %copy-done.71) | copy-start | bytes 9220
  308.0 9.8 %copy-start.74 = (f32[384]{0:T(512)S(1)}, f32[384]{0:T(512)}, u32[]{:S(2)}) copy-start(f32[384]{0:T(512)} %copy-done.73) | copy-start | bytes 4612
  323.3 42.7 %collective-permute-start.6 = (bf16[2,768,384]{2,1,0:T(8,128)(2,1)S(1)}, bf16[2,768,384]{2,1,0:T(8,128)(2,1)S(1)}, u32[]{:S(2)}, u32[]{:S(2)}) collective-permute-start(bf16[2,768,384]{2,1,0:T(8,128)(2,1)S(1)} %copy-done.80), channel_id=1, source_target_pairs={{0,8},{4,0},{8,12},{12,4},{16,24},{20,16},{24,28},{28,20},{1,9},{5... | collective-permute-start | bytes 3538952 | tf_op jit(solution)/shard_map/ppermute | solution.py:1297
  324.7 41.3 %collective-permute-start.7 = (bf16[2,768,384]{2,1,0:T(8,128)(2,1)S(1)}, bf16[2,768,384]{2,1,0:T(8,128)(2,1)S(1)}, u32[]{:S(2)}, u32[]{:S(2)}) collective-permute-start(bf16[2,768,384]{2,1,0:T(8,128)(2,1)S(1)} %copy-done.79), channel_id=1, source_target_pairs={{0,4},{4,12},{8,0},{12,8},{16,20},{20,28},{24,16},{28,24},{1,5},{5... | collective-permute-start | bytes 3538952 | tf_op jit(solution)/shard_map/ppermute | solution.py:1296
  558.1 6.6 %copy-start.44 = (f32[128,768]{1,0:T(8,128)S(1)}, f32[128,768]{1,0:T(8,128)}, u32[]{:S(2)}) copy-start(f32[128,768]{1,0:T(8,128)} %get-tuple-element.116) | copy-start | bytes 1179652
  558.1 7.3 %copy-start.30 = (bf16[1,384,768]{2,1,0:T(8,128)(2,1)S(1)}, bf16[1,384,768]{2,1,0:T(8,128)(2,1)}, u32[]{:S(2)}) copy-start(bf16[1,384,768]{2,1,0:T(8,128)(2,1)} %param.11) | copy-start | bytes 1769476
  558.1 7.3 %copy-start.41 = (f32[384,768]{1,0:T(8,128)S(1)}, f32[384,768]{1,0:T(8,128)}, u32[]{:S(2)}) copy-start(f32[384,768]{1,0:T(8,128)} %get-tuple-element.104) | copy-start | bytes 3538948
  558.1 7.3 %copy-start.42 = (f32[384,768]{1,0:T(8,128)S(1)}, f32[384,768]{1,0:T(8,128)}, u32[]{:S(2)}) copy-start(f32[384,768]{1,0:T(8,128)} %get-tuple-element.115) | copy-start | bytes 3538948
  558.1 7.3 %copy-start.50 = (f32[768]{0:T(1024)S(1)}, f32[768]{0:T(1024)}, u32[]{:S(2)}) copy-start(f32[768]{0:T(1024)} %copy-done.49) | copy-start | bytes 9220
  (59 other events, 123.0 us)

commit v7 on v6

--- a/solution.py
+++ b/solution.py
@@ -662,7 +662,7 @@
 
 def attend_back_kernel(causal, block, s_ref, q_ref, k_ref, v_ref, up_ref, wide_ref, lse_ref, *refs):
     if causal:
-        line_ref, dq_ref, dk_ref, dv_ref, near_ref, sum_ref, acc_ref = refs
+        line_ref, dq_ref, dk_ref, dv_ref, bias_ref, sum_ref, acc_ref, near_ref = refs
     else:
         dq_ref, dk_ref, dv_ref, acc_ref = refs
     rows = q_ref.shape[0]
@@ -735,6 +735,18 @@
             return carry
 
         lax.fori_loop(s + 1, k_ref.shape[0] // block, beyond, 0)
+        turn = (
+            lax.broadcasted_iota(jnp.int32, (TILE, TILE), 0)
+            + lax.broadcasted_iota(jnp.int32, (TILE, TILE), 1)
+            == TILE - 1
+        ).astype(jnp.float32)
+        diagonals = []
+        for h in range(2):
+            near = jnp.dot(turn, near_ref[h].T, precision=highest, preferred_element_type=jnp.float32)
+            near = jnp.concatenate([near, jnp.zeros((TILE, TILE), jnp.float32)], axis=1)
+            near = pltpu.roll(near, 0, 1, stride=1, stride_axis=0)
+            diagonals.append(jnp.sum(near, axis=0, keepdims=True))
+        bias_ref[0] = jnp.concatenate(diagonals, axis=0)
         sum_ref[0] = jnp.concatenate(
             [acc_ref[TILE : TILE + 1, :rows], acc_ref[TILE : TILE + 1, rows:]], axis=0
         )
@@ -752,14 +764,15 @@
     pair = pl.BlockSpec((rows, TILE), lambda g: (0, g))
     long = pl.BlockSpec((total, TILE), lambda g: (0, g))
     line = pl.BlockSpec((1, 2, rows), lambda g: (g, 0, 0))
-    extra, specs, shapes, out_specs = [], [], [], []
+    extra, specs, shapes, out_specs, scratch = [], [], [], [], []
     if causal:
         extra, specs = [lines], [pl.BlockSpec((1,) + lines.shape[1:], lambda g: (g, 0, 0))]
         shapes = [
-            jax.ShapeDtypeStruct((HEADS, 2 * TILE, TILE), jnp.float32),
+            jax.ShapeDtypeStruct((PAIRS, 2, 3 * TILE), jnp.float32),
             jax.ShapeDtypeStruct((PAIRS, 2, rows), jnp.float32),
         ]
-        out_specs = [pl.BlockSpec((2, 2 * TILE, TILE), lambda g: (g, 0, 0)), line]
+        out_specs = [pl.BlockSpec((1, 2, 3 * TILE), lambda g: (g, 0, 0)), line]
+        scratch = [pltpu.VMEM((2, 2 * TILE, TILE), jnp.float32)]
     return pl.pallas_call(
         functools.partial(attend_back_kernel, causal, block),
         grid=(PAIRS,),
@@ -771,7 +784,7 @@
         + shapes,
         in_specs=[SMEM, pair, long, long, pair, pair, line] + specs,
         out_specs=[pair, long, long] + out_specs,
-        scratch_shapes=[pltpu.VMEM((TILE + 16, 2 * rows), jnp.float32)],
+        scratch_shapes=[pltpu.VMEM((TILE + 16, 2 * rows), jnp.float32)] + scratch,
         compiler_params=pltpu.CompilerParams(vmem_limit_bytes=48 << 20),
         cost_estimate=cost(48 if causal else 15),
         name="attend_self_back" if causal else "attend_cross_back",
@@ -779,49 +792,48 @@
 
 
 def key_value_back(x_ref, dk_ref, dv_ref, wk_ref, wv_ref, dx_ref):
-    x, dk, dv = x_ref[...], dk_ref[...], dv_ref[...]
-    dx = dot_last(dk, wk_ref[0]) + dot_last(dv, wv_ref[0])
+    x, both = x_ref[...], jnp.concatenate([dk_ref[...], dv_ref[...]], axis=1)
+    dx = dot_last(both, jnp.concatenate([wk_ref[0], wv_ref[0]], axis=1))
     dx_ref[...] = dx.astype(dx_ref.dtype)
     gain = jnp.sum(dx * x.astype(jnp.float32), axis=0, keepdims=True)
-    return gain, dot_first(x, dk), dot_first(x, dv)
-
-
-def add_up(step, last, made, totals, outs):
+    return gain, dot_first(x, both)
+
+
+def add_up(step, last, made, total, outs):
     @pl.when(step == 0)
     def _():
-        for total, term in zip(totals, made):
-            total[...] = term
+        total[...] = made
 
     @pl.when(step > 0)
     def _():
-        for total, term in zip(totals, made):
-            total[...] += term
+        total[...] += made
 
     @pl.when(step == last)
     def _():
-        for out, total in zip(outs, totals):
-            out[...] = total[...].astype(out.dtype)
-
-
-def memory_back_kernel(x_ref, dk_ref, dv_ref, wk_ref, wv_ref, dx_ref, grad_ref, k_acc, v_acc):
-    _, gk, gv = key_value_back(x_ref, dk_ref, dv_ref, wk_ref, wv_ref, dx_ref)
+        for i, out in enumerate(outs):
+            out[...] = total[:, i * D : (i + 1) * D].astype(out.dtype)
+
+
+def memory_back_kernel(x_ref, dk_ref, dv_ref, wk_ref, wv_ref, dx_ref, grad_ref, acc_ref):
+    _, made = key_value_back(x_ref, dk_ref, dv_ref, wk_ref, wv_ref, dx_ref)
     outs = [grad_ref.at[0], grad_ref.at[1]]
-    add_up(pl.program_id(0), pl.num_programs(0) - 1, (gk, gv), (k_acc, v_acc), outs)
+    add_up(pl.program_id(0), pl.num_programs(0) - 1, made, acc_ref, outs)
 
 
 def token_back_kernel(*refs):
     x_ref, dk_ref, dv_ref, wk_ref, wv_ref, own_ref, dq_ref, wq_ref = refs[:8]
-    terms, (dx_ref, grad_ref, gain_ref, query_ref), sums = refs[8:14], refs[14:18], refs[18:20]
-    k_acc, v_acc = refs[20:]
+    terms, others, cross_ref = refs[8:14], refs[14:20], refs[20]
+    (dx_ref, grad_ref, gain_ref, query_ref), sums = refs[21:25], refs[25:27]
+    acc_ref = refs[27]
     step, last = pl.program_id(0), pl.num_programs(0) - 1
     for i, out in enumerate(sums):
-        own, *others = terms[3 * i : 3 * i + 3]
-        total = own[...]
-        for other in others:
-            total = total + other[...].astype(jnp.float32)
+        first, *rest = terms[3 * i : 3 * i + 3]
+        total = first[...]
+        for term in rest:
+            total = total + term[...].astype(jnp.float32)
         out[...] = total
-    gain, gk, gv = key_value_back(x_ref, dk_ref, dv_ref, wk_ref, wv_ref, dx_ref)
-    add_up(step, last, (gk, gv), (k_acc, v_acc), [grad_ref.at[1], grad_ref.at[2]])
+    gain, made = key_value_back(x_ref, dk_ref, dv_ref, wk_ref, wv_ref, dx_ref)
+    add_up(step, last, made, acc_ref, [grad_ref.at[1], grad_ref.at[2]])
 
     @pl.when(step == 0)
     def _():
@@ -830,10 +842,18 @@
         query_ref[...] = back
         gain_ref[...] = gain + jnp.sum(back * own.astype(jnp.float32), axis=0, keepdims=True)
         grad_ref[0] = dot_first(own, dq).astype(grad_ref.dtype)
+        grad_ref[4:6] = cross_ref[...]
 
     @pl.when(step > 0)
     def _():
         gain_ref[...] += gain
+
+    for i, number in enumerate((3, 6, 7)):
+
+        @pl.when(step == jnp.minimum(i + 1, last))
+        def _(i=i, number=number):
+            product = dot_first(others[2 * i][...], others[2 * i + 1][...])
+            grad_ref[number] = product.astype(grad_ref.dtype)
 
 
 def memory_back(tokens, grad_keys, grad_values, proj_in):
@@ -850,18 +870,20 @@
         ],
         in_specs=[block] * 3 + [weight(4), weight(5)],
         out_specs=[block, pl.BlockSpec((2, D, D), lambda i: (0, 0, 0))],
-        scratch_shapes=[pltpu.VMEM((D, D), jnp.float32)] * 2,
+        scratch_shapes=[pltpu.VMEM((D, 2 * D), jnp.float32)],
         compiler_params=pltpu.CompilerParams(vmem_limit_bytes=48 << 20),
         cost_estimate=cost(8),
         name="memory_back",
     )(tokens, grad_keys, grad_values, proj_in, proj_in)
 
 
-def token_back(tokens, grad_keys, grad_values, own, grad_queries, proj_in, terms):
+def token_back(tokens, grad_keys, grad_values, own, grad_queries, proj_in, terms, others, grads_cross):
     steps = tokens.shape[0] // (2 * own.shape[0])
     block = pl.BlockSpec((2 * own.shape[0], D), lambda i: (i, 0))
-    weight = lambda number: pl.BlockSpec((1, D, D), lambda i: (number, 0, 0))
-    whole = pl.BlockSpec(own.shape, lambda i: (0, 0))
+    once = pl.Buffered(1)
+    weight = lambda number: pl.BlockSpec((1, D, D), lambda i: (number, 0, 0), pipeline_mode=once)
+    whole = pl.BlockSpec(own.shape, lambda i: (0, 0), pipeline_mode=once)
+    pair = pl.BlockSpec((2, D, D), lambda i: (0, 0, 0), pipeline_mode=once)
     count, _, hidden = terms[0].shape
     expert = pl.BlockSpec((count, D // steps, hidden), lambda i: (0, i, 0))
     return pl.pallas_call(
@@ -874,20 +896,36 @@
             jax.ShapeDtypeStruct(own.shape, jnp.float32),
         ]
         + [jax.ShapeDtypeStruct(terms[0].shape, jnp.float32)] * 2,
-        in_specs=[block] * 3 + [weight(1), weight(2), whole, whole, weight(0)] + [expert] * 6,
+        in_specs=[block] * 3
+        + [weight(1), weight(2), whole, whole, weight(0)]
+        + [expert] * 6
+        + [whole] * 6
+        + [pair],
         out_specs=[
             block,
-            pl.BlockSpec((3, D, D), lambda i: (0, 0, 0)),
+            pl.BlockSpec((8, D, D), lambda i: (0, 0, 0), pipeline_mode=once),
             pl.BlockSpec((1, D), lambda i: (0, 0)),
-            whole,
+            pl.BlockSpec(own.shape, lambda i: (0, 0)),
             expert,
             expert,
         ],
-        scratch_shapes=[pltpu.VMEM((D, D), jnp.float32)] * 2,
+        scratch_shapes=[pltpu.VMEM((D, 2 * D), jnp.float32)],
         compiler_params=pltpu.CompilerParams(vmem_limit_bytes=56 << 20),
-        cost_estimate=cost(24),
+        cost_estimate=cost(28),
         name="token_back",
-    )(tokens, grad_keys, grad_values, proj_in, proj_in, own, grad_queries, proj_in, *terms)
+    )(
+        tokens,
+        grad_keys,
+        grad_values,
+        proj_in,
+        proj_in,
+        own,
+        grad_queries,
+        proj_in,
+        *terms,
+        *others,
+        grads_cross,
+    )
 
 
 def bias_lines(bias_table):
@@ -905,25 +943,21 @@
     return pltpu.roll(line, 0, 1, stride=1, stride_axis=0)[:, : 2 * TILE]
 
 
-def bias_gradient(near, sums):
-    distance = (
-        TILE
-        + jnp.arange(TILE, dtype=jnp.int32)[None, :]
-        - jnp.arange(2 * TILE, dtype=jnp.int32)[:, None]
-    )
+def bias_gradient(diagonals, sums):
+    distance = 2 * TILE - 1 - jnp.arange(3 * TILE, dtype=jnp.int32)
     bucket = jnp.zeros(distance.shape, jnp.int32)
     for threshold in bucket_edges():
         bucket = bucket + (distance >= threshold).astype(jnp.int32)
-    onehot = (
-        bucket.reshape(-1)[None, :] == jnp.arange(NBUCKET, dtype=jnp.int32)[:, None]
-    ).astype(jnp.float32)
-    flat = near.reshape(HEADS, -1)
+    buckets = jnp.arange(NBUCKET, dtype=jnp.int32)[:, None]
+    flat = diagonals.reshape(HEADS, -1)
+    far = jnp.sum(sums, axis=-1).reshape(HEADS) - jnp.sum(flat, axis=-1)
     table = lax.dot_general(
-        onehot, flat, (((1,), (1,)), ((), ())), precision=highest
-    )
-    far = jnp.sum(sums, axis=-1).reshape(HEADS) - jnp.sum(flat, axis=-1)
-    last = jnp.arange(NBUCKET, dtype=jnp.int32)[:, None] == NBUCKET - 1
-    return table + jnp.where(last, far[None, :], 0.0)
+        (bucket[None, :] == buckets).astype(jnp.float32),
+        flat,
+        (((1,), (1,)), ((), ())),
+        precision=highest,
+    )
+    return table + jnp.where(buckets == NBUCKET - 1, far[None, :], 0.0)
 
 
 def expert_kernel(n, m, slots, *refs):
@@ -1152,14 +1186,52 @@
     return [(i, step(i, 1)) for i in range(n)], [(i, step(i, -1)) for i in range(n)]
 
 
+def present_kernel(grad_ref, small_ref, in_ref, out_ref, gain_ref, table_ref, router_ref):
+    step = pl.program_id(0)
+    value = grad_ref[...].astype(jnp.float32)
+
+    @pl.when(step < 6)
+    def _():
+        in_ref[...] = value
+
+    @pl.when(step >= 6)
+    def _():
+        out_ref[...] = value
+
+    @pl.when(step == 0)
+    def _():
+        experts = router_ref.shape[1]
+        each = experts + 8
+        pieces = D // TILE
+        lines = jnp.concatenate(
+            [small_ref[i * each : (i + 1) * each, :] for i in range(pieces)], axis=1
+        )
+        router_ref[...] = lines[:experts].T
+        gain_ref[...] = lines[experts : experts + 3]
+        table_ref[...] = small_ref[pieces * each : pieces * each + NBUCKET, :HEADS]
+
+
+def present(grads, small, experts):
+    whole = lambda shape: pl.BlockSpec(shape, lambda i: (0, 0))
+    shapes = [(6, D, D), (2, D, D), (3, D), (NBUCKET, HEADS), (D, experts)]
+    return pl.pallas_call(
+        present_kernel,
+        grid=(8,),
+        out_shape=[jax.ShapeDtypeStruct(shape, jnp.float32) for shape in shapes],
+        in_specs=[pl.BlockSpec((1, D, D), lambda i: (i, 0, 0)), whole(small.shape)],
+        out_specs=[
+            pl.BlockSpec((1, D, D), lambda i: (jnp.minimum(i, 5), 0, 0)),
+            pl.BlockSpec((1, D, D), lambda i: (jnp.maximum(i - 6, 0), 0, 0)),
+        ]
+        + [whole(shape) for shape in shapes[2:]],
+        compiler_params=pltpu.CompilerParams(vmem_limit_bytes=48 << 20),
+        cost_estimate=cost(8),
+        name="present",
+    )(grads, small)
+
+
 def project(source, matrix):
     return jnp.dot(source, matrix, preferred_element_type=jnp.float32).astype(jnp.bfloat16)
-
-
-def weight_grad(source, upstream):
-    return jnp.einsum("td,te->de", source, upstream, preferred_element_type=jnp.float32).astype(
-        jnp.bfloat16
-    )
 
 
 def input_grad(upstream, matrix):
@@ -1278,7 +1350,6 @@
     grad_after_cross = grad_top + grad_cross_part
 
     grad_cross_low = grad_after_cross.astype(jnp.bfloat16)
-    grad_out_cross = weight_grad(attended_cross_low, grad_cross_low)
     grad_attended_cross = input_grad(grad_cross_low, proj_out[1]).astype(jnp.bfloat16)
     grad_cross_query, grad_memory_keys, grad_memory_values = attend_back(
         seq_at,
@@ -1295,7 +1366,6 @@
     )
     gin_next = lax.ppermute(gin_next, "seq", to_next)
     gout_last = lax.ppermute(gout_last, "seq", to_last)
-    grad_query_cross = weight_grad(normed_cross, grad_cross_query)
     grad_self_part, grad_gain_cross = rms_backward(
         after_self, gain_rows[1], input_grad(grad_cross_query, proj_in[3])
     )
@@ -1305,7 +1375,6 @@
     )
 
     grad_self_low = grad_after_self.astype(jnp.bfloat16)
-    grad_out_self = weight_grad(attended_self_low, grad_self_low)
     grad_attended_self = input_grad(grad_self_low, proj_out[0]).astype(jnp.bfloat16)
     grad_self_query, grad_keys, grad_values, near, sums = attend_back(
         seq_at,
@@ -1338,19 +1407,24 @@
         grad_self_query,
         proj_in,
         [gin_own, gin_last, gin_next, gout_own, gout_last, gout_next],
+        [
+            normed_cross,
+            grad_cross_query,
+            attended_self_low,
+            grad_self_low,
+            attended_cross_low,
+            grad_cross_low,
+        ],
+        grads_cross,
     )
     grad_gain_self = grad_gain_part[0] / gain_rows[0]
 
-    grads = lax.dynamic_update_slice(grads, grads_cross, (4, 0, 0))
-    for number, grad in ((3, grad_query_cross), (6, grad_out_self), (7, grad_out_cross)):
-        grads = lax.dynamic_update_slice(grads, grad[None], (number, 0, 0))
     grad_gains = jnp.stack([grad_gain_self, grad_gain_cross, grad_gain_mix])
-    small = [
-        grad_gains.reshape(-1, TILE),
-        grad_router.T.reshape(-1, TILE),
-        jnp.pad(grad_table, ((0, 0), (0, TILE - HEADS))),
-    ]
-    ends = [small[0].shape[0], small[0].shape[0] + small[1].shape[0]]
+    lines = jnp.concatenate(
+        [grad_router.T, grad_gains, jnp.zeros((8 - grad_gains.shape[0], D), jnp.float32)]
+    )
+    small = [lines[:, i * TILE : (i + 1) * TILE] for i in range(D // TILE)]
+    small.append(jnp.pad(grad_table, ((0, 0), (0, TILE - HEADS))))
     (grad_normed_own, grad_memory), grads, small = finish(
         [
             grad_normed_part.reshape(n, token_count, D),
@@ -1362,18 +1436,14 @@
         m,
         4,
     )
-    grads = grads.reshape(-1, D, D).astype(jnp.float32)
+    wide = present(grads.reshape(8, D, D), small, expert_count)
     grad_token_part, _ = rms_backward(tokens, gain_rows[0], grad_normed_query + grad_normed_own)
     grad_in = (grad_after_self + grad_token_part).astype(jnp.bfloat16)
     return (
         output.reshape(1, token_count, D),
         grad_in.reshape(1, token_count, D),
         grad_memory.astype(jnp.bfloat16).reshape(1, memory_count, D),
-        grads[:6],
-        grads[6:],
-        small[: ends[0]].reshape(grad_gains.shape),
-        small[ends[1] : ends[1] + NBUCKET, :HEADS],
-        small[ends[0] : ends[1]].reshape(expert_count, D).T,
+        *wide,
         grad_expert_in,
         grad_expert_out,
         tally_counts,

time: 581 us -> 568 us (0.978)
  local copies, waits for them, and re-layouts: 46.5 us -> 15.3 us
  Pallas kernels: 479 us -> 500 us
  matrix products: 22 us -> 14 us
    slice x6 -> x8, local copies, waits for them, and re-layouts: 15.4 us -> 0.82 us  [the longest x7 0.6 us: body(): small = [lines[:, i * TILE:(i + 1) * TILE] for i in range(D // TILE)]]
    pallas_call x0 -> x1, Pallas kernels: none -> 12 us  [present(): pl.pallas_call(present_kernel, grid=(8,), out_shape=[jax.ShapeDtypeStruct...]
    unnamed x170 -> x153, local copies, waits for them, and re-layouts: 20.7 us -> 9.78 us
    dot_general x4 -> x1, matrix products: 7.85 us -> 0.15 us  [bias_gradient(): lax.dot_general((bucket[None, :] == buckets).astype(jnp.float32), flat, (...]
    pallas_call x1, Pallas kernels: 27 us -> 33.4 us  [token_back(): pl.pallas_call(token_back_kernel, grid=(steps,), out_shape=[jax.ShapeDtyp...]
  transfers between devices with their start and end apart: 8 -> 8, of which waited for: 0 -> 1; matrix products, arithmetic and copies ran while one was open for 3% -> 3% of each run, Pallas kernels for 18% -> 19%
where the time goes in v7:
time: 568 us; the launch traced here: 559 us
  Pallas kernels  500 us (88%)
  other arithmetic  18.4 us (3%)
  local copies, waits for them, and re-layouts  15.3 us (3%)
  matrix products  14 us (2%)
  starting transfers between devices  8.08 us (1%)
    pallas_call x1, Pallas kernels, run_experts(): pl.pallas_call(functools.partial(expert_kernel, n, m, slots), out_shape=[...  147 us
    pallas_call x1, Pallas kernels, finish(): pl.pallas_call(functools.partial(finish_kernel, n, (few, many)), out_shap...  136 us
    pallas_call x1, Pallas kernels, gather_projected(): pl.pallas_call(functools.partial(gather_kernel, n, parts), out_shape=[jax...  65.4 us
    pallas_call x2, Pallas kernels, attend_back(): pl.pallas_call(functools.partial(attend_back_kernel, causal, block), grid...  58.3 us
    pallas_call x2, Pallas kernels, attend(): pl.pallas_call(functools.partial(attend_kernel, causal, block), grid=(PAI...  38.7 us
    pallas_call x1, Pallas kernels, token_back(): pl.pallas_call(token_back_kernel, grid=(steps,), out_shape=[jax.ShapeDtyp...  33.4 us
    pallas_call x1, Pallas kernels, present(): pl.pallas_call(present_kernel, grid=(8,), out_shape=[jax.ShapeDtypeStruct...  12 us
  transfers between devices with their start and end apart: 8, of which 1 were waited for; matrix products, arithmetic and copies ran while one was open for 3% of the time, Pallas kernels for 19%

profile of v7, /device:TPU:25, one launch (start us, length us, event | category | flops | bytes accessed | tf_op | source)
XLA Modules:
  0.0 558.7 jit_solution(12731351925430356820)
XLA Ops:
  0.7 1.3 fusion.5
  3.3 2.1 fusion.7.refs_0_.refs_5_
  5.4 65.4 %gather_projected.1 = (bf16[8,384,768]{2,1,0:T(8,128)(2,1)}, bf16[8,128,768]{2,1,0:T(8,128)(2,1)}, bf16[384,768]{1,0:T(8,128)(2,1)}, bf16[8,384,768]{2,1,0:T(8,1...) custom-call(bf16[384,768]{1,0:T(8,128)(2,1)} %fusion.7.refs_0_.refs_5_, ...), custom_call_target="tpu_custom_call" | custom-call | flops 60000002048 | tf_op jit(solution)/shard_map/gather_projected/pallas_call | solution.py:179
  70.8 1.3 collective-permute-start.2
  72.3 1.2 collective-permute-start.3
  79.0 1.1 reduce-window.6
  81.1 1.1 copy-done.16
  82.1 29.6 %attend_self.1 = (bf16[384,768]{1,0:T(8,128)(2,1)S(1)}, f32[384,768]{1,0:T(8,128)S(1)}, f32[6,2,384]{2,1,0:T(2,128)S(1)}) custom-call(s32[1]{0:T(128)} %bitcast.1.s_ref, bf16[384,768]{1,0:T(8,128)(2,1)S(1)} %copy-done.16, bf16[3072,768]{1,0:T(8,128)(2,1)} %bitcast.102, bf16[3072,768]{1,0:T(8,128)(2,1)} %bitcast.104, f32[6,2,384]{2,1,0:T(2,128)S(1)} %select_select_fusion.refs_0_), custom_call_target="tpu_custom_call" | custom-call | flops 40000000000 | tf_op jit(solution)/shard_map/attend_self/pallas_call | solution.py:643
  112.9 2.6 convolution_convert_fusion.3.q_ref
  115.6 9.0 %attend_cross.1 = (bf16[384,768]{1,0:T(8,128)(2,1)S(1)}, f32[384,768]{1,0:T(8,128)S(1)}, f32[6,2,384]{2,1,0:T(2,128)S(1)}) custom-call(s32[1]{0:T(128)} %bitcast.1.s_ref, bf16[384,768]{1,0:T(8,128)(2,1)S(1)} %convolution_convert_fusion.3.q_ref, bf16[1024,768]{1,0:T(8,128)(2,1)S(1)} %bitcast.88, bf16[1024,768]{1,0:T(8,128)(2,1)S(1)} %bitcast.90), custom_call_target="tpu_custom_call" | custom-call | flops 10000000000 | tf_op jit(solution)/shard_map/attend_cross/pallas_call | solution.py:643
  127.4 2.2 convolution_convert_fusion
  129.7 146.9 %run_experts.1 = (bf16[4,128,1536]{2,1,0:T(8,128)(2,1)}, f32[2,768,384]{2,1,0:T(8,128)}, f32[2,768,384]{2,1,0:T(8,128)}, bf16[2,768,384]{2,1,0:T(8,128)(2,1)}, b...) custom-call(bf16[4,128,1536]{2,1,0:T(8,128)(2,1)} %bitcast.107, ...), custom_call_target="tpu_custom_call" | custom-call | flops 149999992832 | tf_op jit(solution)/shard_map/run_experts/pallas_call | solution.py:1153
  276.7 2.4 fusion.25
  279.1 1.0 fusion.4
  280.2 1.0 multiply_reduce_fusion
  281.6 1.3 copy-done.32
  283.8 3.6 collective-permute-start.4
  287.4 15.3 %attend_cross_back.1 = (bf16[384,768]{1,0:T(8,128)(2,1)S(1)}, bf16[1024,768]{1,0:T(8,128)(2,1)S(1)}, bf16[1024,768]{1,0:T(8,128)(2,1)S(1)}) custom-call(s32[1]{0:T(128)} %bitcast.1.s_ref, bf16[384,768]{1,0:T(8,128)(2,1)S(1)} %copy-done.13, bf16[1024,768]{1,0:T(8,128)(2,1)} %bitcast.87, bf16[1024,768]{1,0:T(8,128)(2,1)} %bitcast.89, ...), custom_call_target="tpu_custom_call" | custom-call | flops 15000000512 | tf_op jit(solution)/shard_map/attend_cross_back/pallas_call | solution.py:776
  302.8 1.1 copy-done.14
  304.3 9.7 %memory_back.1 = (bf16[1024,768]{1,0:T(8,128)(2,1)S(1)}, bf16[2,768,768]{2,1,0:T(8,128)(2,1)}) custom-call(bf16[1024,768]{1,0:T(8,128)(2,1)S(1)} %bitcast.86, bf16[1024,768]{1,0:T(8,128)(2,1)S(1)} %get-tuple-element.110.dk_ref, bf16[1024,768]{1,0:T(8,128)(2,1)} %copy-done.14, bf16[6,768,768]{2,1,0:T(8,128)(2,1)} %refs_7_.1, bf16[6,768,768]{2,1,0:T(8,128)(2,1)} %refs_7_.1), custom_call_target="tpu_custom_call" | custom-call | flops 8000000000 | tf_op jit(solution)/shard_map/memory_back/pallas_call | solution.py:864
  314.5 2.1 multiply_reduce_fusion.1
  316.7 1.6 fusion.124
  319.8 1.5 collective-permute-start.6
  321.3 43.0 %attend_self_back.1 = (bf16[384,768]{1,0:T(8,128)(2,1)S(1)}, bf16[3072,768]{1,0:T(8,128)(2,1)}, bf16[3072,768]{1,0:T(8,128)(2,1)}, f32[6,2,384]{2,1,0:T(2,128)S(1)}, f32[6,2,384]{2,1,0:T(2,128)S(1)}) custom-call(s32[1]{0:T(128)} %bitcast.1.s_ref, bf16[384,768]{1,0:T(8,128)(2,1)S(1)} %copy-done.17, bf16[3072,768]{1,0:T(8,128)(2,1)} %bitcast.103, ...), custom_call_target="tpu_custom_call" | custom-call | flops 48000000000 | tf_op jit(solution)/shard_map/attend_self_back/pallas_call | solution.py:776
  364.2 0.8 copy-done.15
  365.1 1.0 copy-done.72
  366.5 33.4 %token_back.1 = (bf16[3072,768]{1,0:T(8,128)(2,1)}, bf16[8,768,768]{2,1,0:T(8,128)(2,1)}, f32[1,768]{1,0:T(1,128)}, f32[384,768]{1,0:T(8,128)}, f32[2,768,384]{2,1,0:T(8,128)}, /*index=5*/f32[2,768,384]{2,1,0:T(8,128)}) custom-call(bf16[3072,768]{1,0:T(8,128)(2,1)} %bitcast.101, bf16[3072,768]{1,0:T(8,128)(2,1)} %get-tuple-element.100.refs_1_, ...), custom_call_target="tpu_custom_call" | custom-call | flops 28000000000 | tf_op jit(solution)/shard_map/token_back/pallas_call | solution.py:889
  402.8 136.1 %finish.1 = (f32[384,768]{1,0:T(8,128)}, f32[128,768]{1,0:T(8,128)}, bf16[2,2,8,192,768]{4,3,2,1,0:T(8,128)(2,1)}, f32[2,2,8,16,128]{4,3,2,1,0:T(8,128)}) custom-call(bf16[8,384,768]{2,1,0:T(8,128)(2,1)} %bitcast.106, bf16[8,128,768]{2,1,0:T(8,128)(2,1)} %bitcast.91, bf16[2,2,8,192,768]{4,3,2,1,0:T(8,128)(2,1)} %bitcast.99, f32[2,2,8,16,128]{4,3,2,1,0:T(8,128)} %bitcast.94), custom_call_target="tpu_custom_call" | custom-call | flops 120000004096 | tf_op jit(solution)/shard_map/finish/pallas_call | solution.py:485
  538.9 1.7 convert_bitcast_fusion
  540.6 1.6 fusion.8
  542.3 12.0 %present.1 = (f32[6,768,768]{2,1,0:T(8,128)}, f32[2,768,768]{2,1,0:T(8,128)}, f32[3,768]{1,0:T(4,128)}, f32[32,12]{1,0:T(8,128)S(1)}, f32[768,8]{1,0:T(8,128)S(1)}) custom-call(bf16[8,768,768]{2,1,0:T(8,128)(2,1)} %bitcast.100, f32[512,128]{1,0:T(8,128)S(1)} %bitcast.92), custom_call_target="tpu_custom_call" | custom-call | flops 8000000000 | tf_op jit(solution)/shard_map/present/pallas_call | solution.py:1217
  555.7 2.5 fusion.27
  (266 shorter events, 19.9 us)
Async XLA Ops:
  0.6 125.7 %copy-start = (bf16[768,8]{0,1:T(8,128)(2,1)S(1)}, bf16[768,8]{0,1:T(8,128)(2,1)}, u32[]{:S(2)}) copy-start(bf16[768,8]{0,1:T(8,128)(2,1)} %param.17) | copy-start | bytes 36868
  3.2 67.6 %copy-start.51 = (f32[3,768]{1,0:T(4,128)}, f32[3,768]{1,0:T(4,128)S(1)}, u32[]{:S(2)}) copy-start(f32[3,768]{1,0:T(4,128)S(1)} %convert_element_type.299) | copy-start | bytes 27652
  3.2 67.5 %copy-start.41 = (f32[768]{0:T(1024)}, f32[768]{0:T(1024)S(1)}, u32[]{:S(2)}) copy-start(f32[768]{0:T(1024)S(1)} %get-tuple-element.159) | copy-start | bytes 9220
  3.2 109.4 %copy-start.52 = (f32[768]{0:T(1024)}, f32[768]{0:T(1024)S(1)}, u32[]{:S(2)}) copy-start(f32[768]{0:T(1024)S(1)} %get-tuple-element.158) | copy-start | bytes 9220
  3.3 122.9 %copy-start.39 = (f32[768]{0:T(1024)}, f32[768]{0:T(1024)S(1)}, u32[]{:S(2)}) copy-start(f32[768]{0:T(1024)S(1)} %get-tuple-element.157) | copy-start | bytes 9220
  5.4 65.4 %copy-start.69 = (bf16[2,768,384]{2,1,0:T(8,128)(2,1)S(1)}, bf16[2,768,384]{2,1,0:T(8,128)(2,1)}, u32[]{:S(2)}) copy-start(bf16[2,768,384]{2,1,0:T(8,128)(2,1)} %refs_1_) | copy-start | bytes 3538948
  5.4 69.9 %copy-start.56 = (f32[32,12]{0,1:T(8,128)S(1)}, f32[32,12]{0,1:T(8,128)}, u32[]{:S(2)}) copy-start(f32[32,12]{0,1:T(8,128)} %param.16) | copy-start | bytes 4612
  5.4 73.6 %copy-start.68 = (s32[1,384,1]{1,2,0:T(1,128)S(1)}, s32[1,384,1]{1,2,0:T(1,128)}, u32[]{:S(2)}) copy-start(s32[1,384,1]{1,2,0:T(1,128)} %param.18) | copy-start | bytes 4612
  70.8 58.9 %collective-permute-start.2 = (bf16[2,768,384]{2,1,0:T(8,128)(2,1)S(1)}, bf16[2,768,384]{2,1,0:T(8,128)(2,1)}, u32[]{:S(2)}, u32[]{:S(2)}) collective-permute-start(bf16[2,768,384]{2,1,0:T(8,128)(2,1)S(1)} %copy-done.69), channel_id=1, source_target_pairs={{0,8},{4,0},{8,12},{12,4},{16,24},{20,16},{24,28},{28,20},{1,9},{5... | collective-permute-start | bytes 3538952 | tf_op jit(solution)/shard_map/ppermute | solution.py:1271
  72.1 57.6 %collective-permute-start = (bf16[2,768,384]{2,1,0:T(8,128)(2,1)S(1)}, bf16[2,768,384]{2,1,0:T(8,128)(2,1)}, u32[]{:S(2)}, u32[]{:S(2)}) collective-permute-start(bf16[2,768,384]{2,1,0:T(8,128)(2,1)S(1)} %copy-done.69), channel_id=1, source_target_pairs={{0,4},{4,12},{8,0},{12,8},{16,20},{20,28},{24,16},{28,24},{1,5},{5... | collective-permute-start | bytes 3538952 | tf_op jit(solution)/shard_map/ppermute | solution.py:1270
  72.3 57.4 %collective-permute-start.3 = (bf16[2,768,384]{2,1,0:T(8,128)(2,1)}, bf16[2,768,384]{2,1,0:T(8,128)(2,1)}, u32[]{:S(2)}, u32[]{:S(2)}) collective-permute-start(bf16[2,768,384]{2,1,0:T(8,128)(2,1)} %refs_2_.2), channel_id=1, source_target_pairs={{0,8},{4,0},{8,12},{12,4},{16,24},{20,16},{24,28},{28,20},{1,9},{5... | collective-permute-start | bytes 3538952 | tf_op jit(solution)/shard_map/ppermute | solution.py:1271
  73.5 56.2 %collective-permute-start.1 = (bf16[2,768,384]{2,1,0:T(8,128)(2,1)}, bf16[2,768,384]{2,1,0:T(8,128)(2,1)}, u32[]{:S(2)}, u32[]{:S(2)}) collective-permute-start(bf16[2,768,384]{2,1,0:T(8,128)(2,1)} %refs_2_.2), channel_id=1, source_target_pairs={{0,4},{4,12},{8,0},{12,8},{16,20},{20,28},{24,16},{28,24},{1,5},{5... | collective-permute-start | bytes 3538952 | tf_op jit(solution)/shard_map/ppermute | solution.py:1270
  79.0 47.7 %copy-start.37 = (s32[384]{0:T(512)}, s32[384]{0:T(512)S(1)}, u32[]{:S(2)}) copy-start(s32[384]{0:T(512)S(1)} %reduce.37) | copy-start | bytes 4612
  81.1 30.7 %copy-start.3 = (f32[6,2,384]{2,1,0:T(2,128)}, f32[6,2,384]{2,1,0:T(2,128)S(1)}, u32[]{:S(2)}) copy-start(f32[6,2,384]{2,1,0:T(2,128)S(1)} %select_select_fusion.refs_0_) | copy-start | bytes 55300
  82.1 29.7 %copy-start.22 = (bf16[1,384,768]{2,1,0:T(8,128)(2,1)S(1)}, bf16[1,384,768]{2,1,0:T(8,128)(2,1)}, u32[]{:S(2)}) copy-start(bf16[1,384,768]{2,1,0:T(8,128)(2,1)} %param.11) | copy-start | bytes 1769476
  82.1 29.7 %copy-start.31 = (bf16[2,768,768]{2,1,0:T(8,128)(2,1)S(1)}, bf16[2,768,768]{2,1,0:T(8,128)(2,1)}, u32[]{:S(2)}) copy-start(bf16[2,768,768]{2,1,0:T(8,128)(2,1)} %param.14) | copy-start | bytes 7077892
  112.6 12.0 %copy-start.20 = (f32[384,768]{1,0:T(8,128)}, f32[384,768]{1,0:T(8,128)S(1)}, u32[]{:S(2)}) copy-start(f32[384,768]{1,0:T(8,128)S(1)} %get-tuple-element.205) | copy-start | bytes 3538948
  129.7 146.9 %copy-start.48 = (s32[384]{0:T(512)S(1)}, s32[384]{0:T(512)}, u32[]{:S(2)}) copy-start(s32[384]{0:T(512)} %copy-done.47) | copy-start | bytes 4612
  283.8 30.2 %collective-permute-start.4 = (bf16[2,768,384]{2,1,0:T(8,128)(2,1)}, bf16[2,768,384]{2,1,0:T(8,128)(2,1)}, u32[]{:S(2)}, u32[]{:S(2)}) collective-permute-start(bf16[2,768,384]{2,1,0:T(8,128)(2,1)} %get-tuple-element.85), channel_id=1, source_target_pairs={{0,8},{4,0},{8,12},{12,4},{16,24},{20,16},{24,28},{28,20},{1,9},{5... | collective-permute-start | bytes 3538952 | tf_op jit(solution)/shard_map/ppermute | solution.py:1336
  287.4 27.0 %collective-permute-start.5 = (bf16[2,768,384]{2,1,0:T(8,128)(2,1)}, bf16[2,768,384]{2,1,0:T(8,128)(2,1)}, u32[]{:S(2)}, u32[]{:S(2)}) collective-permute-start(bf16[2,768,384]{2,1,0:T(8,128)(2,1)} %get-tuple-element.86), channel_id=1, source_target_pairs={{0,4},{4,12},{8,0},{12,8},{16,20},{20,28},{24,16},{28,24},{1,5},{5... | collective-permute-start | bytes 3538952 | tf_op jit(solution)/shard_map/ppermute | solution.py:1335
  287.4 16.5 %copy-start.27 = (bf16[384,768]{1,0:T(8,128)(2,1)S(1)}, bf16[384,768]{1,0:T(8,128)(2,1)}, u32[]{:S(2)}) copy-start(bf16[384,768]{1,0:T(8,128)(2,1)} %copy-done.26) | copy-start | bytes 1769476
  287.4 16.8 %copy-start.5 = (bf16[8,128,768]{2,1,0:T(8,128)(2,1)S(1)}, bf16[8,128,768]{2,1,0:T(8,128)(2,1)}, u32[]{:S(2)}) copy-start(bf16[8,128,768]{2,1,0:T(8,128)(2,1)} %get-tuple-element.109) | copy-start | bytes 4718596
  303.9 10.5 %copy-start.10 = (bf16[384,768]{1,0:T(8,128)(2,1)}, bf16[384,768]{1,0:T(8,128)(2,1)S(1)}, u32[]{:S(2)}) copy-start(bf16[384,768]{1,0:T(8,128)(2,1)S(1)} %get-tuple-element.89.refs_15_) | copy-start | bytes 1769476
  319.8 45.3 %collective-permute-start.6 = (bf16[2,768,384]{2,1,0:T(8,128)(2,1)S(1)}, bf16[2,768,384]{2,1,0:T(8,128)(2,1)S(1)}, u32[]{:S(2)}, u32[]{:S(2)}) collective-permute-start(bf16[2,768,384]{2,1,0:T(8,128)(2,1)S(1)} %copy-done.71), channel_id=1, source_target_pairs={{0,8},{4,0},{8,12},{12,4},{16,24},{20,16},{24,28},{28,20},{1,9},{5... | collective-permute-start | bytes 3538952 | tf_op jit(solution)/shard_map/ppermute | solution.py:1368
  321.3 43.8 %collective-permute-start.7 = (bf16[2,768,384]{2,1,0:T(8,128)(2,1)S(1)}, bf16[2,768,384]{2,1,0:T(8,128)(2,1)S(1)}, u32[]{:S(2)}, u32[]{:S(2)}) collective-permute-start(bf16[2,768,384]{2,1,0:T(8,128)(2,1)S(1)} %copy-done.70), channel_id=1, source_target_pairs={{0,4},{4,12},{8,0},{12,8},{16,20},{20,28},{24,16},{28,24},{1,5},{5... | collective-permute-start | bytes 3538952 | tf_op jit(solution)/shard_map/ppermute | solution.py:1367
  366.5 34.5 %copy-start.67 = (s32[384]{0:T(512)S(1)}, s32[384]{0:T(512)}, u32[]{:S(2)}) copy-start(s32[384]{0:T(512)} %convert_add_fusion.2) | copy-start | bytes 4612
  366.5 34.5 %copy-start.74 = (pred[32]{0:T(512)(128)(4,1)S(1)}, pred[32]{0:T(512)(128)(4,1)}, u32[]{:S(2)}) copy-start(pred[32]{0:T(512)(128)(4,1)} %iota_compare_fusion.8) | copy-start | bytes 100
  402.8 137.8 %copy-start.23 = (bf16[1,384,768]{2,1,0:T(8,128)(2,1)S(1)}, bf16[1,384,768]{2,1,0:T(8,128)(2,1)}, u32[]{:S(2)}) copy-start(bf16[1,384,768]{2,1,0:T(8,128)(2,1)} %param.11) | copy-start | bytes 1769476
  402.8 137.8 %copy-start.29 = (f32[384,768]{1,0:T(8,128)S(1)}, f32[384,768]{1,0:T(8,128)}, u32[]{:S(2)}) copy-start(f32[384,768]{1,0:T(8,128)} %get-tuple-element.113) | copy-start | bytes 3538948
  402.8 137.8 %copy-start.42 = (f32[768]{0:T(1024)S(1)}, f32[768]{0:T(1024)}, u32[]{:S(2)}) copy-start(f32[768]{0:T(1024)} %copy-done.41) | copy-start | bytes 9220
  542.3 13.4 %copy-start.28 = (f32[384,768]{1,0:T(8,128)S(1)}, f32[384,768]{1,0:T(8,128)}, u32[]{:S(2)}) copy-start(f32[384,768]{1,0:T(8,128)} %get-tuple-element.195) | copy-start | bytes 3538948
  542.3 13.4 %copy-start.60 = (f32[384]{0:T(512)S(1)}, f32[384]{0:T(512)}, u32[]{:S(2)}) copy-start(f32[384]{0:T(512)} %copy-done.59) | copy-start | bytes 4612
  (51 other events, 125.1 us)

commit v8 on v7

--- a/solution.py
+++ b/solution.py
@@ -994,9 +994,14 @@
         + [{"seq": side["next"], "exp": exp}, {"seq": side["last"], "exp": exp}]
     )
     going = {}
-    for g, k in moves:
-        to_seq, to_exp = place(g, k)
-        going[g, k] = push(x_ref.at[to_exp], rows.at[g, exp], go_sem, g, k, to_seq, to_exp)
+
+    def go(some):
+        for g, k in some:
+            to_seq, to_exp = place(g, k)
+            going[g, k] = push(x_ref.at[to_exp], rows.at[g, exp], go_sem, g, k, to_seq, to_exp)
+
+    early = far[: len(far) // 2]
+    go(early + moves[len(far) :])
     own = pltpu.make_async_copy(x_ref.at[exp], rows.at[0, exp], own_sem.at[0])
     own.start()
     fetched = []
@@ -1067,6 +1072,9 @@
                     source,
                 )
 
+    for move in early:
+        going[move].wait_send()
+    go(far[len(early) :])
     for copy in far_maps:
         copy.wait_recv()
     work(0, 0, m)
@@ -1136,9 +1144,10 @@
         copy.wait()
     for copy in terms_out + far_maps:
         copy.wait_send()
-    for copies in (going, coming):
-        for copy in copies.values():
-            copy.wait_send()
+    for move in moves[len(early) :]:
+        going[move].wait_send()
+    for copy in coming.values():
+        copy.wait_send()
 
 
 def run_experts(x, maps, n, m, slots, number):

time: 568 us -> 560 us (0.986)
  Pallas kernels: 500 us -> 492 us
    pallas_call x1, Pallas kernels: 147 us -> 138 us  [run_experts(): pl.pallas_call(functools.partial(expert_kernel, n, m, slots), out_shape=[...]
where the time goes in v8:
time: 560 us; the launch traced here: 551 us
  Pallas kernels  492 us (88%)
  other arithmetic  18.4 us (3%)
  local copies, waits for them, and re-layouts  15.3 us (3%)
  matrix products  13.9 us (2%)
  starting transfers between devices  7.76 us (1%)
    pallas_call x1, Pallas kernels, run_experts(): pl.pallas_call(functools.partial(expert_kernel, n, m, slots), out_shape=[...  138 us
    pallas_call x1, Pallas kernels, finish(): pl.pallas_call(functools.partial(finish_kernel, n, (few, many)), out_shap...  137 us
    pallas_call x1, Pallas kernels, gather_projected(): pl.pallas_call(functools.partial(gather_kernel, n, parts), out_shape=[jax...  65.4 us
    pallas_call x2, Pallas kernels, attend_back(): pl.pallas_call(functools.partial(attend_back_kernel, causal, block), grid...  58.3 us
    pallas_call x2, Pallas kernels, attend(): pl.pallas_call(functools.partial(attend_kernel, causal, block), grid=(PAI...  38.7 us
    pallas_call x1, Pallas kernels, token_back(): pl.pallas_call(token_back_kernel, grid=(steps,), out_shape=[jax.ShapeDtyp...  33.4 us
    pallas_call x1, Pallas kernels, present(): pl.pallas_call(present_kernel, grid=(8,), out_shape=[jax.ShapeDtypeStruct...  12 us
  transfers between devices with their start and end apart: 8, of which 1 were waited for; matrix products, arithmetic and copies ran while one was open for 3% of the time, Pallas kernels for 19%

profile of v8, /device:TPU:25, one launch (start us, length us, event | category | flops | bytes accessed | tf_op | source)
XLA Modules:
  0.0 550.6 jit_solution(10169524268272887407)
XLA Ops:
  0.7 1.3 fusion.5
  3.3 2.1 fusion.7.refs_0_.refs_5_
  5.4 65.4 %gather_projected.1 = (bf16[8,384,768]{2,1,0:T(8,128)(2,1)}, bf16[8,128,768]{2,1,0:T(8,128)(2,1)}, bf16[384,768]{1,0:T(8,128)(2,1)}, bf16[8,384,768]{2,1,0:T(8,1...) custom-call(bf16[384,768]{1,0:T(8,128)(2,1)} %fusion.7.refs_0_.refs_5_, ...), custom_call_target="tpu_custom_call" | custom-call | flops 60000002048 | tf_op jit(solution)/shard_map/gather_projected/pallas_call | solution.py:179
  70.8 1.3 collective-permute-start.2
  72.3 1.2 collective-permute-start.3
  79.0 1.1 reduce-window.6
  81.1 1.1 copy-done.16
  82.1 29.6 %attend_self.1 = (bf16[384,768]{1,0:T(8,128)(2,1)S(1)}, f32[384,768]{1,0:T(8,128)S(1)}, f32[6,2,384]{2,1,0:T(2,128)S(1)}) custom-call(s32[1]{0:T(128)} %bitcast.1.s_ref, bf16[384,768]{1,0:T(8,128)(2,1)S(1)} %copy-done.16, bf16[3072,768]{1,0:T(8,128)(2,1)} %bitcast.102, bf16[3072,768]{1,0:T(8,128)(2,1)} %bitcast.104, f32[6,2,384]{2,1,0:T(2,128)S(1)} %select_select_fusion.refs_0_), custom_call_target="tpu_custom_call" | custom-call | flops 40000000000 | tf_op jit(solution)/shard_map/attend_self/pallas_call | solution.py:643
  112.9 2.6 convolution_convert_fusion.3.q_ref
  115.6 9.0 %attend_cross.1 = (bf16[384,768]{1,0:T(8,128)(2,1)S(1)}, f32[384,768]{1,0:T(8,128)S(1)}, f32[6,2,384]{2,1,0:T(2,128)S(1)}) custom-call(s32[1]{0:T(128)} %bitcast.1.s_ref, bf16[384,768]{1,0:T(8,128)(2,1)S(1)} %convolution_convert_fusion.3.q_ref, bf16[1024,768]{1,0:T(8,128)(2,1)S(1)} %bitcast.88, bf16[1024,768]{1,0:T(8,128)(2,1)S(1)} %bitcast.90), custom_call_target="tpu_custom_call" | custom-call | flops 10000000000 | tf_op jit(solution)/shard_map/attend_cross/pallas_call | solution.py:643
  127.4 2.2 convolution_convert_fusion
  129.7 138.2 %run_experts.1 = (bf16[4,128,1536]{2,1,0:T(8,128)(2,1)}, f32[2,768,384]{2,1,0:T(8,128)}, f32[2,768,384]{2,1,0:T(8,128)}, bf16[2,768,384]{2,1,0:T(8,128)(2,1)}, b...) custom-call(bf16[4,128,1536]{2,1,0:T(8,128)(2,1)} %bitcast.107, ...), custom_call_target="tpu_custom_call" | custom-call | flops 149999992832 | tf_op jit(solution)/shard_map/run_experts/pallas_call | solution.py:1162
  268.0 2.3 fusion.25
  270.4 1.0 fusion.4
  271.5 1.0 multiply_reduce_fusion
  272.9 1.3 copy-done.32
  275.1 3.3 collective-permute-start.4
  278.4 15.3 %attend_cross_back.1 = (bf16[384,768]{1,0:T(8,128)(2,1)S(1)}, bf16[1024,768]{1,0:T(8,128)(2,1)S(1)}, bf16[1024,768]{1,0:T(8,128)(2,1)S(1)}) custom-call(s32[1]{0:T(128)} %bitcast.1.s_ref, bf16[384,768]{1,0:T(8,128)(2,1)S(1)} %copy-done.13, bf16[1024,768]{1,0:T(8,128)(2,1)} %bitcast.87, bf16[1024,768]{1,0:T(8,128)(2,1)} %bitcast.89, ...), custom_call_target="tpu_custom_call" | custom-call | flops 15000000512 | tf_op jit(solution)/shard_map/attend_cross_back/pallas_call | solution.py:776
  293.7 1.1 copy-done.14
  295.3 9.7 %memory_back.1 = (bf16[1024,768]{1,0:T(8,128)(2,1)S(1)}, bf16[2,768,768]{2,1,0:T(8,128)(2,1)}) custom-call(bf16[1024,768]{1,0:T(8,128)(2,1)S(1)} %bitcast.86, bf16[1024,768]{1,0:T(8,128)(2,1)S(1)} %get-tuple-element.110.dk_ref, bf16[1024,768]{1,0:T(8,128)(2,1)} %copy-done.14, bf16[6,768,768]{2,1,0:T(8,128)(2,1)} %refs_7_.1, bf16[6,768,768]{2,1,0:T(8,128)(2,1)} %refs_7_.1), custom_call_target="tpu_custom_call" | custom-call | flops 8000000000 | tf_op jit(solution)/shard_map/memory_back/pallas_call | solution.py:864
  305.0 0.9 collective-permute-done.5.refs_13_
  305.9 2.1 multiply_reduce_fusion.1
  308.1 1.6 fusion.124
  311.2 1.1 collective-permute-start.6
  312.7 42.9 %attend_self_back.1 = (bf16[384,768]{1,0:T(8,128)(2,1)S(1)}, bf16[3072,768]{1,0:T(8,128)(2,1)}, bf16[3072,768]{1,0:T(8,128)(2,1)}, f32[6,2,384]{2,1,0:T(2,128)S(1)}, f32[6,2,384]{2,1,0:T(2,128)S(1)}) custom-call(s32[1]{0:T(128)} %bitcast.1.s_ref, bf16[384,768]{1,0:T(8,128)(2,1)S(1)} %copy-done.17, bf16[3072,768]{1,0:T(8,128)(2,1)} %bitcast.103, ...), custom_call_target="tpu_custom_call" | custom-call | flops 48000000000 | tf_op jit(solution)/shard_map/attend_self_back/pallas_call | solution.py:776
  356.5 1.0 copy-done.72
  357.9 33.4 %token_back.1 = (bf16[3072,768]{1,0:T(8,128)(2,1)}, bf16[8,768,768]{2,1,0:T(8,128)(2,1)}, f32[1,768]{1,0:T(1,128)}, f32[384,768]{1,0:T(8,128)}, f32[2,768,384]{2,1,0:T(8,128)}, /*index=5*/f32[2,768,384]{2,1,0:T(8,128)}) custom-call(bf16[3072,768]{1,0:T(8,128)(2,1)} %bitcast.101, bf16[3072,768]{1,0:T(8,128)(2,1)} %get-tuple-element.100.refs_1_, ...), custom_call_target="tpu_custom_call" | custom-call | flops 28000000000 | tf_op jit(solution)/shard_map/token_back/pallas_call | solution.py:889
  394.1 136.6 %finish.1 = (f32[384,768]{1,0:T(8,128)}, f32[128,768]{1,0:T(8,128)}, bf16[2,2,8,192,768]{4,3,2,1,0:T(8,128)(2,1)}, f32[2,2,8,16,128]{4,3,2,1,0:T(8,128)}) custom-call(bf16[8,384,768]{2,1,0:T(8,128)(2,1)} %bitcast.106, bf16[8,128,768]{2,1,0:T(8,128)(2,1)} %bitcast.91, bf16[2,2,8,192,768]{4,3,2,1,0:T(8,128)(2,1)} %bitcast.99, f32[2,2,8,16,128]{4,3,2,1,0:T(8,128)} %bitcast.94), custom_call_target="tpu_custom_call" | custom-call | flops 120000004096 | tf_op jit(solution)/shard_map/finish/pallas_call | solution.py:485
  530.8 1.7 convert_bitcast_fusion
  532.5 1.6 fusion.8
  534.2 12.0 %present.1 = (f32[6,768,768]{2,1,0:T(8,128)}, f32[2,768,768]{2,1,0:T(8,128)}, f32[3,768]{1,0:T(4,128)}, f32[32,12]{1,0:T(8,128)S(1)}, f32[768,8]{1,0:T(8,128)S(1)}) custom-call(bf16[8,768,768]{2,1,0:T(8,128)(2,1)} %bitcast.100, f32[512,128]{1,0:T(8,128)S(1)} %bitcast.92), custom_call_target="tpu_custom_call" | custom-call | flops 8000000000 | tf_op jit(solution)/shard_map/present/pallas_call | solution.py:1226
  547.6 2.5 fusion.27
  (266 shorter events, 20.6 us)
Async XLA Ops:
  0.6 125.7 %copy-start = (bf16[768,8]{0,1:T(8,128)(2,1)S(1)}, bf16[768,8]{0,1:T(8,128)(2,1)}, u32[]{:S(2)}) copy-start(bf16[768,8]{0,1:T(8,128)(2,1)} %param.17) | copy-start | bytes 36868
  3.2 67.6 %copy-start.51 = (f32[3,768]{1,0:T(4,128)}, f32[3,768]{1,0:T(4,128)S(1)}, u32[]{:S(2)}) copy-start(f32[3,768]{1,0:T(4,128)S(1)} %convert_element_type.299) | copy-start | bytes 27652
  3.2 67.5 %copy-start.41 = (f32[768]{0:T(1024)}, f32[768]{0:T(1024)S(1)}, u32[]{:S(2)}) copy-start(f32[768]{0:T(1024)S(1)} %get-tuple-element.159) | copy-start | bytes 9220
  3.2 109.4 %copy-start.52 = (f32[768]{0:T(1024)}, f32[768]{0:T(1024)S(1)}, u32[]{:S(2)}) copy-start(f32[768]{0:T(1024)S(1)} %get-tuple-element.158) | copy-start | bytes 9220
  3.3 122.9 %copy-start.39 = (f32[768]{0:T(1024)}, f32[768]{0:T(1024)S(1)}, u32[]{:S(2)}) copy-start(f32[768]{0:T(1024)S(1)} %get-tuple-element.157) | copy-start | bytes 9220
  5.4 65.4 %copy-start.69 = (bf16[2,768,384]{2,1,0:T(8,128)(2,1)S(1)}, bf16[2,768,384]{2,1,0:T(8,128)(2,1)}, u32[]{:S(2)}) copy-start(bf16[2,768,384]{2,1,0:T(8,128)(2,1)} %refs_1_) | copy-start | bytes 3538948
  5.4 69.9 %copy-start.56 = (f32[32,12]{0,1:T(8,128)S(1)}, f32[32,12]{0,1:T(8,128)}, u32[]{:S(2)}) copy-start(f32[32,12]{0,1:T(8,128)} %param.16) | copy-start | bytes 4612
  5.4 73.6 %copy-start.68 = (s32[1,384,1]{1,2,0:T(1,128)S(1)}, s32[1,384,1]{1,2,0:T(1,128)}, u32[]{:S(2)}) copy-start(s32[1,384,1]{1,2,0:T(1,128)} %param.18) | copy-start | bytes 4612
  70.8 58.9 %collective-permute-start.2 = (bf16[2,768,384]{2,1,0:T(8,128)(2,1)S(1)}, bf16[2,768,384]{2,1,0:T(8,128)(2,1)}, u32[]{:S(2)}, u32[]{:S(2)}) collective-permute-start(bf16[2,768,384]{2,1,0:T(8,128)(2,1)S(1)} %copy-done.69), channel_id=1, source_target_pairs={{0,8},{4,0},{8,12},{12,4},{16,24},{20,16},{24,28},{28,20},{1,9},{5... | collective-permute-start | bytes 3538952 | tf_op jit(solution)/shard_map/ppermute | solution.py:1280
  72.1 57.6 %collective-permute-start = (bf16[2,768,384]{2,1,0:T(8,128)(2,1)S(1)}, bf16[2,768,384]{2,1,0:T(8,128)(2,1)}, u32[]{:S(2)}, u32[]{:S(2)}) collective-permute-start(bf16[2,768,384]{2,1,0:T(8,128)(2,1)S(1)} %copy-done.69), channel_id=1, source_target_pairs={{0,4},{4,12},{8,0},{12,8},{16,20},{20,28},{24,16},{28,24},{1,5},{5... | collective-permute-start | bytes 3538952 | tf_op jit(solution)/shard_map/ppermute | solution.py:1279
  72.3 57.4 %collective-permute-start.3 = (bf16[2,768,384]{2,1,0:T(8,128)(2,1)}, bf16[2,768,384]{2,1,0:T(8,128)(2,1)}, u32[]{:S(2)}, u32[]{:S(2)}) collective-permute-start(bf16[2,768,384]{2,1,0:T(8,128)(2,1)} %refs_2_.2), channel_id=1, source_target_pairs={{0,8},{4,0},{8,12},{12,4},{16,24},{20,16},{24,28},{28,20},{1,9},{5... | collective-permute-start | bytes 3538952 | tf_op jit(solution)/shard_map/ppermute | solution.py:1280
  73.5 56.2 %collective-permute-start.1 = (bf16[2,768,384]{2,1,0:T(8,128)(2,1)}, bf16[2,768,384]{2,1,0:T(8,128)(2,1)}, u32[]{:S(2)}, u32[]{:S(2)}) collective-permute-start(bf16[2,768,384]{2,1,0:T(8,128)(2,1)} %refs_2_.2), channel_id=1, source_target_pairs={{0,4},{4,12},{8,0},{12,8},{16,20},{20,28},{24,16},{28,24},{1,5},{5... | collective-permute-start | bytes 3538952 | tf_op jit(solution)/shard_map/ppermute | solution.py:1279
  79.0 47.7 %copy-start.37 = (s32[384]{0:T(512)}, s32[384]{0:T(512)S(1)}, u32[]{:S(2)}) copy-start(s32[384]{0:T(512)S(1)} %reduce.37) | copy-start | bytes 4612
  81.1 30.7 %copy-start.3 = (f32[6,2,384]{2,1,0:T(2,128)}, f32[6,2,384]{2,1,0:T(2,128)S(1)}, u32[]{:S(2)}) copy-start(f32[6,2,384]{2,1,0:T(2,128)S(1)} %select_select_fusion.refs_0_) | copy-start | bytes 55300
  82.1 29.7 %copy-start.22 = (bf16[1,384,768]{2,1,0:T(8,128)(2,1)S(1)}, bf16[1,384,768]{2,1,0:T(8,128)(2,1)}, u32[]{:S(2)}) copy-start(bf16[1,384,768]{2,1,0:T(8,128)(2,1)} %param.11) | copy-start | bytes 1769476
  82.1 29.7 %copy-start.31 = (bf16[2,768,768]{2,1,0:T(8,128)(2,1)S(1)}, bf16[2,768,768]{2,1,0:T(8,128)(2,1)}, u32[]{:S(2)}) copy-start(bf16[2,768,768]{2,1,0:T(8,128)(2,1)} %param.14) | copy-start | bytes 7077892
  112.6 12.0 %copy-start.20 = (f32[384,768]{1,0:T(8,128)}, f32[384,768]{1,0:T(8,128)S(1)}, u32[]{:S(2)}) copy-start(f32[384,768]{1,0:T(8,128)S(1)} %get-tuple-element.205) | copy-start | bytes 3538948
  129.7 138.2 %copy-start.48 = (s32[384]{0:T(512)S(1)}, s32[384]{0:T(512)}, u32[]{:S(2)}) copy-start(s32[384]{0:T(512)} %copy-done.47) | copy-start | bytes 4612
  275.1 29.9 %collective-permute-start.4 = (bf16[2,768,384]{2,1,0:T(8,128)(2,1)}, bf16[2,768,384]{2,1,0:T(8,128)(2,1)}, u32[]{:S(2)}, u32[]{:S(2)}) collective-permute-start(bf16[2,768,384]{2,1,0:T(8,128)(2,1)} %get-tuple-element.85), channel_id=1, source_target_pairs={{0,8},{4,0},{8,12},{12,4},{16,24},{20,16},{24,28},{28,20},{1,9},{5... | collective-permute-start | bytes 3538952 | tf_op jit(solution)/shard_map/ppermute | solution.py:1345
  278.4 27.5 %collective-permute-start.5 = (bf16[2,768,384]{2,1,0:T(8,128)(2,1)}, bf16[2,768,384]{2,1,0:T(8,128)(2,1)}, u32[]{:S(2)}, u32[]{:S(2)}) collective-permute-start(bf16[2,768,384]{2,1,0:T(8,128)(2,1)} %get-tuple-element.86), channel_id=1, source_target_pairs={{0,4},{4,12},{8,0},{12,8},{16,20},{20,28},{24,16},{28,24},{1,5},{5... | collective-permute-start | bytes 3538952 | tf_op jit(solution)/shard_map/ppermute | solution.py:1344
  278.4 16.5 %copy-start.27 = (bf16[384,768]{1,0:T(8,128)(2,1)S(1)}, bf16[384,768]{1,0:T(8,128)(2,1)}, u32[]{:S(2)}) copy-start(bf16[384,768]{1,0:T(8,128)(2,1)} %copy-done.26) | copy-start | bytes 1769476
  278.4 16.8 %copy-start.5 = (bf16[8,128,768]{2,1,0:T(8,128)(2,1)S(1)}, bf16[8,128,768]{2,1,0:T(8,128)(2,1)}, u32[]{:S(2)}) copy-start(bf16[8,128,768]{2,1,0:T(8,128)(2,1)} %get-tuple-element.109) | copy-start | bytes 4718596
  294.9 11.0 %copy-start.10 = (bf16[384,768]{1,0:T(8,128)(2,1)}, bf16[384,768]{1,0:T(8,128)(2,1)S(1)}, u32[]{:S(2)}) copy-start(bf16[384,768]{1,0:T(8,128)(2,1)S(1)} %get-tuple-element.89.refs_15_) | copy-start | bytes 1769476
  311.2 45.3 %collective-permute-start.6 = (bf16[2,768,384]{2,1,0:T(8,128)(2,1)S(1)}, bf16[2,768,384]{2,1,0:T(8,128)(2,1)S(1)}, u32[]{:S(2)}, u32[]{:S(2)}) collective-permute-start(bf16[2,768,384]{2,1,0:T(8,128)(2,1)S(1)} %copy-done.71), channel_id=1, source_target_pairs={{0,8},{4,0},{8,12},{12,4},{16,24},{20,16},{24,28},{28,20},{1,9},{5... | collective-permute-start | bytes 3538952 | tf_op jit(solution)/shard_map/ppermute | solution.py:1377
  312.3 44.2 %collective-permute-start.7 = (bf16[2,768,384]{2,1,0:T(8,128)(2,1)S(1)}, bf16[2,768,384]{2,1,0:T(8,128)(2,1)S(1)}, u32[]{:S(2)}, u32[]{:S(2)}) collective-permute-start(bf16[2,768,384]{2,1,0:T(8,128)(2,1)S(1)} %copy-done.70), channel_id=1, source_target_pairs={{0,4},{4,12},{8,0},{12,8},{16,20},{20,28},{24,16},{28,24},{1,5},{5... | collective-permute-start | bytes 3538952 | tf_op jit(solution)/shard_map/ppermute | solution.py:1376
  357.9 34.5 %copy-start.67 = (s32[384]{0:T(512)S(1)}, s32[384]{0:T(512)}, u32[]{:S(2)}) copy-start(s32[384]{0:T(512)} %convert_add_fusion.2) | copy-start | bytes 4612
  357.9 34.5 %copy-start.74 = (pred[32]{0:T(512)(128)(4,1)S(1)}, pred[32]{0:T(512)(128)(4,1)}, u32[]{:S(2)}) copy-start(pred[32]{0:T(512)(128)(4,1)} %iota_compare_fusion.8) | copy-start | bytes 100
  394.1 138.3 %copy-start.23 = (bf16[1,384,768]{2,1,0:T(8,128)(2,1)S(1)}, bf16[1,384,768]{2,1,0:T(8,128)(2,1)}, u32[]{:S(2)}) copy-start(bf16[1,384,768]{2,1,0:T(8,128)(2,1)} %param.11) | copy-start | bytes 1769476
  394.1 138.3 %copy-start.29 = (f32[384,768]{1,0:T(8,128)S(1)}, f32[384,768]{1,0:T(8,128)}, u32[]{:S(2)}) copy-start(f32[384,768]{1,0:T(8,128)} %get-tuple-element.113) | copy-start | bytes 3538948
  394.1 138.3 %copy-start.42 = (f32[768]{0:T(1024)S(1)}, f32[768]{0:T(1024)}, u32[]{:S(2)}) copy-start(f32[768]{0:T(1024)} %copy-done.41) | copy-start | bytes 9220
  534.2 13.4 %copy-start.28 = (f32[384,768]{1,0:T(8,128)S(1)}, f32[384,768]{1,0:T(8,128)}, u32[]{:S(2)}) copy-start(f32[384,768]{1,0:T(8,128)} %get-tuple-element.195) | copy-start | bytes 3538948
  534.2 13.4 %copy-start.60 = (f32[384]{0:T(512)S(1)}, f32[384]{0:T(512)}, u32[]{:S(2)}) copy-start(f32[384]{0:T(512)} %copy-done.59) | copy-start | bytes 4612
  (51 other events, 126.2 us)

commit v9 on v8

--- a/solution.py
+++ b/solution.py
@@ -325,6 +325,16 @@
         return pl.ds(way * parts * rows + part * rows, rows), pl.ds(part * rows, rows)
 
     pairs, own, crossing, ring = {}, {}, {}, {}
+    for lane in rings:
+        a, way, part = lane
+        wide, thin = piece(lane)
+        ring[lane] = push(
+            blocks[a].at[block(way, 0), wide],
+            got_bufs[a].at[way, 0, thin],
+            far_sem,
+            lane + (0,),
+            sides[way],
+        )
     for side in range(2):
         for step in range(n):
             for lane in lanes:
@@ -344,16 +354,6 @@
                     own_sem.at[(side,) + lane + (step,)],
                 )
         if side == 0:
-            for lane in rings:
-                a, way, part = lane
-                wide, thin = piece(lane)
-                ring[lane] = push(
-                    blocks[a].at[block(way, 0), wide],
-                    got_bufs[a].at[way, 0, thin],
-                    far_sem,
-                    lane + (0,),
-                    sides[way],
-                )
             near = {}
             for step in range(1, n):
                 for lane in rings:

time: 560 us -> 560 us (level)
  no operation moved by 1% of the time
where the time goes in v9:
time: 560 us; the launch traced here: 550 us
  Pallas kernels  492 us (88%)
  other arithmetic  18.4 us (3%)
  local copies, waits for them, and re-layouts  15.3 us (3%)
  matrix products  13.9 us (2%)
  starting transfers between devices  7.76 us (1%)
    pallas_call x1, Pallas kernels, run_experts(): pl.pallas_call(functools.partial(expert_kernel, n, m, slots), out_shape=[...  138 us
    pallas_call x1, Pallas kernels, finish(): pl.pallas_call(functools.partial(finish_kernel, n, (few, many)), out_shap...  136 us
    pallas_call x1, Pallas kernels, gather_projected(): pl.pallas_call(functools.partial(gather_kernel, n, parts), out_shape=[jax...  65.4 us
    pallas_call x2, Pallas kernels, attend_back(): pl.pallas_call(functools.partial(attend_back_kernel, causal, block), grid...  58.3 us
    pallas_call x2, Pallas kernels, attend(): pl.pallas_call(functools.partial(attend_kernel, causal, block), grid=(PAI...  38.7 us
    pallas_call x1, Pallas kernels, token_back(): pl.pallas_call(token_back_kernel, grid=(steps,), out_shape=[jax.ShapeDtyp...  33.4 us
    pallas_call x1, Pallas kernels, present(): pl.pallas_call(present_kernel, grid=(8,), out_shape=[jax.ShapeDtypeStruct...  12 us
  transfers between devices with their start and end apart: 8, of which 1 were waited for; matrix products, arithmetic and copies ran while one was open for 3% of the time, Pallas kernels for 19%

profile of v9, /device:TPU:25, one launch (start us, length us, event | category | flops | bytes accessed | tf_op | source)
XLA Modules:
  0.0 550.4 jit_solution(13721759388496260481)
XLA Ops:
  0.7 1.3 fusion.5
  3.3 2.1 fusion.7.refs_0_.refs_5_
  5.4 65.4 %gather_projected.1 = (bf16[8,384,768]{2,1,0:T(8,128)(2,1)}, bf16[8,128,768]{2,1,0:T(8,128)(2,1)}, bf16[384,768]{1,0:T(8,128)(2,1)}, bf16[8,384,768]{2,1,0:T(8,1...) custom-call(bf16[384,768]{1,0:T(8,128)(2,1)} %fusion.7.refs_0_.refs_5_, ...), custom_call_target="tpu_custom_call" | custom-call | flops 60000002048 | tf_op jit(solution)/shard_map/gather_projected/pallas_call | solution.py:179
  70.8 1.3 collective-permute-start.2
  72.3 1.2 collective-permute-start.3
  79.0 1.1 reduce-window.6
  81.1 1.1 copy-done.16
  82.1 29.6 %attend_self.1 = (bf16[384,768]{1,0:T(8,128)(2,1)S(1)}, f32[384,768]{1,0:T(8,128)S(1)}, f32[6,2,384]{2,1,0:T(2,128)S(1)}) custom-call(s32[1]{0:T(128)} %bitcast.1.s_ref, bf16[384,768]{1,0:T(8,128)(2,1)S(1)} %copy-done.16, bf16[3072,768]{1,0:T(8,128)(2,1)} %bitcast.102, bf16[3072,768]{1,0:T(8,128)(2,1)} %bitcast.104, f32[6,2,384]{2,1,0:T(2,128)S(1)} %select_select_fusion.refs_0_), custom_call_target="tpu_custom_call" | custom-call | flops 40000000000 | tf_op jit(solution)/shard_map/attend_self/pallas_call | solution.py:643
  112.9 2.6 convolution_convert_fusion.3.q_ref
  115.6 9.0 %attend_cross.1 = (bf16[384,768]{1,0:T(8,128)(2,1)S(1)}, f32[384,768]{1,0:T(8,128)S(1)}, f32[6,2,384]{2,1,0:T(2,128)S(1)}) custom-call(s32[1]{0:T(128)} %bitcast.1.s_ref, bf16[384,768]{1,0:T(8,128)(2,1)S(1)} %convolution_convert_fusion.3.q_ref, bf16[1024,768]{1,0:T(8,128)(2,1)S(1)} %bitcast.88, bf16[1024,768]{1,0:T(8,128)(2,1)S(1)} %bitcast.90), custom_call_target="tpu_custom_call" | custom-call | flops 10000000000 | tf_op jit(solution)/shard_map/attend_cross/pallas_call | solution.py:643
  127.4 2.2 convolution_convert_fusion
  129.7 138.2 %run_experts.1 = (bf16[4,128,1536]{2,1,0:T(8,128)(2,1)}, f32[2,768,384]{2,1,0:T(8,128)}, f32[2,768,384]{2,1,0:T(8,128)}, bf16[2,768,384]{2,1,0:T(8,128)(2,1)}, b...) custom-call(bf16[4,128,1536]{2,1,0:T(8,128)(2,1)} %bitcast.107, ...), custom_call_target="tpu_custom_call" | custom-call | flops 149999992832 | tf_op jit(solution)/shard_map/run_experts/pallas_call | solution.py:1162
  268.0 2.3 fusion.25
  270.4 1.0 fusion.4
  271.5 1.0 multiply_reduce_fusion
  272.9 1.3 copy-done.32
  275.1 3.3 collective-permute-start.4
  278.4 15.3 %attend_cross_back.1 = (bf16[384,768]{1,0:T(8,128)(2,1)S(1)}, bf16[1024,768]{1,0:T(8,128)(2,1)S(1)}, bf16[1024,768]{1,0:T(8,128)(2,1)S(1)}) custom-call(s32[1]{0:T(128)} %bitcast.1.s_ref, bf16[384,768]{1,0:T(8,128)(2,1)S(1)} %copy-done.13, bf16[1024,768]{1,0:T(8,128)(2,1)} %bitcast.87, bf16[1024,768]{1,0:T(8,128)(2,1)} %bitcast.89, ...), custom_call_target="tpu_custom_call" | custom-call | flops 15000000512 | tf_op jit(solution)/shard_map/attend_cross_back/pallas_call | solution.py:776
  293.7 1.1 copy-done.14
  295.3 9.7 %memory_back.1 = (bf16[1024,768]{1,0:T(8,128)(2,1)S(1)}, bf16[2,768,768]{2,1,0:T(8,128)(2,1)}) custom-call(bf16[1024,768]{1,0:T(8,128)(2,1)S(1)} %bitcast.86, bf16[1024,768]{1,0:T(8,128)(2,1)S(1)} %get-tuple-element.110.dk_ref, bf16[1024,768]{1,0:T(8,128)(2,1)} %copy-done.14, bf16[6,768,768]{2,1,0:T(8,128)(2,1)} %refs_7_.1, bf16[6,768,768]{2,1,0:T(8,128)(2,1)} %refs_7_.1), custom_call_target="tpu_custom_call" | custom-call | flops 8000000000 | tf_op jit(solution)/shard_map/memory_back/pallas_call | solution.py:864
  305.0 0.9 collective-permute-done.5.refs_13_
  305.9 2.1 multiply_reduce_fusion.1
  308.1 1.6 fusion.124
  311.2 1.1 collective-permute-start.6
  312.7 42.9 %attend_self_back.1 = (bf16[384,768]{1,0:T(8,128)(2,1)S(1)}, bf16[3072,768]{1,0:T(8,128)(2,1)}, bf16[3072,768]{1,0:T(8,128)(2,1)}, f32[6,2,384]{2,1,0:T(2,128)S(1)}, f32[6,2,384]{2,1,0:T(2,128)S(1)}) custom-call(s32[1]{0:T(128)} %bitcast.1.s_ref, bf16[384,768]{1,0:T(8,128)(2,1)S(1)} %copy-done.17, bf16[3072,768]{1,0:T(8,128)(2,1)} %bitcast.103, ...), custom_call_target="tpu_custom_call" | custom-call | flops 48000000000 | tf_op jit(solution)/shard_map/attend_self_back/pallas_call | solution.py:776
  356.5 1.0 copy-done.72
  357.9 33.4 %token_back.1 = (bf16[3072,768]{1,0:T(8,128)(2,1)}, bf16[8,768,768]{2,1,0:T(8,128)(2,1)}, f32[1,768]{1,0:T(1,128)}, f32[384,768]{1,0:T(8,128)}, f32[2,768,384]{2,1,0:T(8,128)}, /*index=5*/f32[2,768,384]{2,1,0:T(8,128)}) custom-call(bf16[3072,768]{1,0:T(8,128)(2,1)} %bitcast.101, bf16[3072,768]{1,0:T(8,128)(2,1)} %get-tuple-element.100.refs_1_, ...), custom_call_target="tpu_custom_call" | custom-call | flops 28000000000 | tf_op jit(solution)/shard_map/token_back/pallas_call | solution.py:889
  394.1 136.4 %finish.1 = (f32[384,768]{1,0:T(8,128)}, f32[128,768]{1,0:T(8,128)}, bf16[2,2,8,192,768]{4,3,2,1,0:T(8,128)(2,1)}, f32[2,2,8,16,128]{4,3,2,1,0:T(8,128)}) custom-call(bf16[8,384,768]{2,1,0:T(8,128)(2,1)} %bitcast.106, bf16[8,128,768]{2,1,0:T(8,128)(2,1)} %bitcast.91, bf16[2,2,8,192,768]{4,3,2,1,0:T(8,128)(2,1)} %bitcast.99, f32[2,2,8,16,128]{4,3,2,1,0:T(8,128)} %bitcast.94), custom_call_target="tpu_custom_call" | custom-call | flops 120000004096 | tf_op jit(solution)/shard_map/finish/pallas_call | solution.py:485
  530.6 1.7 convert_bitcast_fusion
  532.3 1.6 fusion.8
  534.0 12.0 %present.1 = (f32[6,768,768]{2,1,0:T(8,128)}, f32[2,768,768]{2,1,0:T(8,128)}, f32[3,768]{1,0:T(4,128)}, f32[32,12]{1,0:T(8,128)S(1)}, f32[768,8]{1,0:T(8,128)S(1)}) custom-call(bf16[8,768,768]{2,1,0:T(8,128)(2,1)} %bitcast.100, f32[512,128]{1,0:T(8,128)S(1)} %bitcast.92), custom_call_target="tpu_custom_call" | custom-call | flops 8000000000 | tf_op jit(solution)/shard_map/present/pallas_call | solution.py:1226
  547.4 2.5 fusion.27
  (266 shorter events, 20.6 us)
Async XLA Ops:
  0.6 125.7 %copy-start = (bf16[768,8]{0,1:T(8,128)(2,1)S(1)}, bf16[768,8]{0,1:T(8,128)(2,1)}, u32[]{:S(2)}) copy-start(bf16[768,8]{0,1:T(8,128)(2,1)} %param.17) | copy-start | bytes 36868
  3.2 67.6 %copy-start.51 = (f32[3,768]{1,0:T(4,128)}, f32[3,768]{1,0:T(4,128)S(1)}, u32[]{:S(2)}) copy-start(f32[3,768]{1,0:T(4,128)S(1)} %convert_element_type.299) | copy-start | bytes 27652
  3.2 67.5 %copy-start.41 = (f32[768]{0:T(1024)}, f32[768]{0:T(1024)S(1)}, u32[]{:S(2)}) copy-start(f32[768]{0:T(1024)S(1)} %get-tuple-element.159) | copy-start | bytes 9220
  3.2 109.4 %copy-start.52 = (f32[768]{0:T(1024)}, f32[768]{0:T(1024)S(1)}, u32[]{:S(2)}) copy-start(f32[768]{0:T(1024)S(1)} %get-tuple-element.158) | copy-start | bytes 9220
  3.3 122.9 %copy-start.39 = (f32[768]{0:T(1024)}, f32[768]{0:T(1024)S(1)}, u32[]{:S(2)}) copy-start(f32[768]{0:T(1024)S(1)} %get-tuple-element.157) | copy-start | bytes 9220
  5.4 65.4 %copy-start.69 = (bf16[2,768,384]{2,1,0:T(8,128)(2,1)S(1)}, bf16[2,768,384]{2,1,0:T(8,128)(2,1)}, u32[]{:S(2)}) copy-start(bf16[2,768,384]{2,1,0:T(8,128)(2,1)} %refs_1_) | copy-start | bytes 3538948
  5.4 69.9 %copy-start.56 = (f32[32,12]{0,1:T(8,128)S(1)}, f32[32,12]{0,1:T(8,128)}, u32[]{:S(2)}) copy-start(f32[32,12]{0,1:T(8,128)} %param.16) | copy-start | bytes 4612
  5.4 73.6 %copy-start.68 = (s32[1,384,1]{1,2,0:T(1,128)S(1)}, s32[1,384,1]{1,2,0:T(1,128)}, u32[]{:S(2)}) copy-start(s32[1,384,1]{1,2,0:T(1,128)} %param.18) | copy-start | bytes 4612
  70.8 58.9 %collective-permute-start.2 = (bf16[2,768,384]{2,1,0:T(8,128)(2,1)S(1)}, bf16[2,768,384]{2,1,0:T(8,128)(2,1)}, u32[]{:S(2)}, u32[]{:S(2)}) collective-permute-start(bf16[2,768,384]{2,1,0:T(8,128)(2,1)S(1)} %copy-done.69), channel_id=1, source_target_pairs={{0,8},{4,0},{8,12},{12,4},{16,24},{20,16},{24,28},{28,20},{1,9},{5... | collective-permute-start | bytes 3538952 | tf_op jit(solution)/shard_map/ppermute | solution.py:1280
  72.1 57.6 %collective-permute-start = (bf16[2,768,384]{2,1,0:T(8,128)(2,1)S(1)}, bf16[2,768,384]{2,1,0:T(8,128)(2,1)}, u32[]{:S(2)}, u32[]{:S(2)}) collective-permute-start(bf16[2,768,384]{2,1,0:T(8,128)(2,1)S(1)} %copy-done.69), channel_id=1, source_target_pairs={{0,4},{4,12},{8,0},{12,8},{16,20},{20,28},{24,16},{28,24},{1,5},{5... | collective-permute-start | bytes 3538952 | tf_op jit(solution)/shard_map/ppermute | solution.py:1279
  72.3 57.4 %collective-permute-start.3 = (bf16[2,768,384]{2,1,0:T(8,128)(2,1)}, bf16[2,768,384]{2,1,0:T(8,128)(2,1)}, u32[]{:S(2)}, u32[]{:S(2)}) collective-permute-start(bf16[2,768,384]{2,1,0:T(8,128)(2,1)} %refs_2_.2), channel_id=1, source_target_pairs={{0,8},{4,0},{8,12},{12,4},{16,24},{20,16},{24,28},{28,20},{1,9},{5... | collective-permute-start | bytes 3538952 | tf_op jit(solution)/shard_map/ppermute | solution.py:1280
  73.5 56.2 %collective-permute-start.1 = (bf16[2,768,384]{2,1,0:T(8,128)(2,1)}, bf16[2,768,384]{2,1,0:T(8,128)(2,1)}, u32[]{:S(2)}, u32[]{:S(2)}) collective-permute-start(bf16[2,768,384]{2,1,0:T(8,128)(2,1)} %refs_2_.2), channel_id=1, source_target_pairs={{0,4},{4,12},{8,0},{12,8},{16,20},{20,28},{24,16},{28,24},{1,5},{5... | collective-permute-start | bytes 3538952 | tf_op jit(solution)/shard_map/ppermute | solution.py:1279
  79.0 47.7 %copy-start.37 = (s32[384]{0:T(512)}, s32[384]{0:T(512)S(1)}, u32[]{:S(2)}) copy-start(s32[384]{0:T(512)S(1)} %reduce.37) | copy-start | bytes 4612
  81.1 30.7 %copy-start.3 = (f32[6,2,384]{2,1,0:T(2,128)}, f32[6,2,384]{2,1,0:T(2,128)S(1)}, u32[]{:S(2)}) copy-start(f32[6,2,384]{2,1,0:T(2,128)S(1)} %select_select_fusion.refs_0_) | copy-start | bytes 55300
  82.1 29.7 %copy-start.22 = (bf16[1,384,768]{2,1,0:T(8,128)(2,1)S(1)}, bf16[1,384,768]{2,1,0:T(8,128)(2,1)}, u32[]{:S(2)}) copy-start(bf16[1,384,768]{2,1,0:T(8,128)(2,1)} %param.11) | copy-start | bytes 1769476
  82.1 29.7 %copy-start.31 = (bf16[2,768,768]{2,1,0:T(8,128)(2,1)S(1)}, bf16[2,768,768]{2,1,0:T(8,128)(2,1)}, u32[]{:S(2)}) copy-start(bf16[2,768,768]{2,1,0:T(8,128)(2,1)} %param.14) | copy-start | bytes 7077892
  112.6 12.0 %copy-start.20 = (f32[384,768]{1,0:T(8,128)}, f32[384,768]{1,0:T(8,128)S(1)}, u32[]{:S(2)}) copy-start(f32[384,768]{1,0:T(8,128)S(1)} %get-tuple-element.205) | copy-start | bytes 3538948
  129.7 138.2 %copy-start.48 = (s32[384]{0:T(512)S(1)}, s32[384]{0:T(512)}, u32[]{:S(2)}) copy-start(s32[384]{0:T(512)} %copy-done.47) | copy-start | bytes 4612
  275.1 29.9 %collective-permute-start.4 = (bf16[2,768,384]{2,1,0:T(8,128)(2,1)}, bf16[2,768,384]{2,1,0:T(8,128)(2,1)}, u32[]{:S(2)}, u32[]{:S(2)}) collective-permute-start(bf16[2,768,384]{2,1,0:T(8,128)(2,1)} %get-tuple-element.85), channel_id=1, source_target_pairs={{0,8},{4,0},{8,12},{12,4},{16,24},{20,16},{24,28},{28,20},{1,9},{5... | collective-permute-start | bytes 3538952 | tf_op jit(solution)/shard_map/ppermute | solution.py:1345
  278.4 27.5 %collective-permute-start.5 = (bf16[2,768,384]{2,1,0:T(8,128)(2,1)}, bf16[2,768,384]{2,1,0:T(8,128)(2,1)}, u32[]{:S(2)}, u32[]{:S(2)}) collective-permute-start(bf16[2,768,384]{2,1,0:T(8,128)(2,1)} %get-tuple-element.86), channel_id=1, source_target_pairs={{0,4},{4,12},{8,0},{12,8},{16,20},{20,28},{24,16},{28,24},{1,5},{5... | collective-permute-start | bytes 3538952 | tf_op jit(solution)/shard_map/ppermute | solution.py:1344
  278.4 16.5 %copy-start.27 = (bf16[384,768]{1,0:T(8,128)(2,1)S(1)}, bf16[384,768]{1,0:T(8,128)(2,1)}, u32[]{:S(2)}) copy-start(bf16[384,768]{1,0:T(8,128)(2,1)} %copy-done.26) | copy-start | bytes 1769476
  278.4 16.8 %copy-start.5 = (bf16[8,128,768]{2,1,0:T(8,128)(2,1)S(1)}, bf16[8,128,768]{2,1,0:T(8,128)(2,1)}, u32[]{:S(2)}) copy-start(bf16[8,128,768]{2,1,0:T(8,128)(2,1)} %get-tuple-element.109) | copy-start | bytes 4718596
  294.9 11.0 %copy-start.10 = (bf16[384,768]{1,0:T(8,128)(2,1)}, bf16[384,768]{1,0:T(8,128)(2,1)S(1)}, u32[]{:S(2)}) copy-start(bf16[384,768]{1,0:T(8,128)(2,1)S(1)} %get-tuple-element.89.refs_15_) | copy-start | bytes 1769476
  311.2 45.3 %collective-permute-start.6 = (bf16[2,768,384]{2,1,0:T(8,128)(2,1)S(1)}, bf16[2,768,384]{2,1,0:T(8,128)(2,1)S(1)}, u32[]{:S(2)}, u32[]{:S(2)}) collective-permute-start(bf16[2,768,384]{2,1,0:T(8,128)(2,1)S(1)} %copy-done.71), channel_id=1, source_target_pairs={{0,8},{4,0},{8,12},{12,4},{16,24},{20,16},{24,28},{28,20},{1,9},{5... | collective-permute-start | bytes 3538952 | tf_op jit(solution)/shard_map/ppermute | solution.py:1377
  312.3 44.2 %collective-permute-start.7 = (bf16[2,768,384]{2,1,0:T(8,128)(2,1)S(1)}, bf16[2,768,384]{2,1,0:T(8,128)(2,1)S(1)}, u32[]{:S(2)}, u32[]{:S(2)}) collective-permute-start(bf16[2,768,384]{2,1,0:T(8,128)(2,1)S(1)} %copy-done.70), channel_id=1, source_target_pairs={{0,4},{4,12},{8,0},{12,8},{16,20},{20,28},{24,16},{28,24},{1,5},{5... | collective-permute-start | bytes 3538952 | tf_op jit(solution)/shard_map/ppermute | solution.py:1376
  357.9 34.5 %copy-start.67 = (s32[384]{0:T(512)S(1)}, s32[384]{0:T(512)}, u32[]{:S(2)}) copy-start(s32[384]{0:T(512)} %convert_add_fusion.2) | copy-start | bytes 4612
  357.9 34.5 %copy-start.74 = (pred[32]{0:T(512)(128)(4,1)S(1)}, pred[32]{0:T(512)(128)(4,1)}, u32[]{:S(2)}) copy-start(pred[32]{0:T(512)(128)(4,1)} %iota_compare_fusion.8) | copy-start | bytes 100
  394.1 138.2 %copy-start.23 = (bf16[1,384,768]{2,1,0:T(8,128)(2,1)S(1)}, bf16[1,384,768]{2,1,0:T(8,128)(2,1)}, u32[]{:S(2)}) copy-start(bf16[1,384,768]{2,1,0:T(8,128)(2,1)} %param.11) | copy-start | bytes 1769476
  394.1 138.2 %copy-start.29 = (f32[384,768]{1,0:T(8,128)S(1)}, f32[384,768]{1,0:T(8,128)}, u32[]{:S(2)}) copy-start(f32[384,768]{1,0:T(8,128)} %get-tuple-element.113) | copy-start | bytes 3538948
  394.1 138.2 %copy-start.42 = (f32[768]{0:T(1024)S(1)}, f32[768]{0:T(1024)}, u32[]{:S(2)}) copy-start(f32[768]{0:T(1024)} %copy-done.41) | copy-start | bytes 9220
  534.0 13.4 %copy-start.28 = (f32[384,768]{1,0:T(8,128)S(1)}, f32[384,768]{1,0:T(8,128)}, u32[]{:S(2)}) copy-start(f32[384,768]{1,0:T(8,128)} %get-tuple-element.195) | copy-start | bytes 3538948
  534.0 13.4 %copy-start.60 = (f32[384]{0:T(512)S(1)}, f32[384]{0:T(512)}, u32[]{:S(2)}) copy-start(f32[384]{0:T(512)} %copy-done.59) | copy-start | bytes 4612
  (51 other events, 126.2 us)
